TPU v7x, 32 devices: a whole 2x2x4 slice. The times are simulated.
32 devices in a mesh: expert: 4 (over z), dp: 8 (over y, x, core).
Axes of the slice: x: 2, y: 2, z: 4, core: 2. Of those that a mesh axis runs over, the one named last changes fastest.
Arguments:
- tokens: bfloat16 [1024, 2048], P('dp'), may hold values from -6 to 6
- cotangent: bfloat16 [1024, 2048], P('dp'), may hold values from -6 to 6
- expert_ids: int32 [1024, 4], P('dp'), may hold values from 0 to 7, all different within a row; in each aligned block of 64 rows (0 to 63, 64 to 127, ...) at most 64 rows name the same one
- gate_probs: bfloat16 [1024, 4], P('dp'), may hold values from 0.049804688 to 0.29882812
- weights: bfloat16 [3, 1536, 4096], P(None, 'dp', 'expert'), may hold values from -0.125 to 0.125
- first_moment: bfloat16 [3, 1536, 4096], P(None, 'dp', 'expert'), may hold values from -4 to 4
- second_moment: bfloat16 [3, 1536, 4096], P(None, 'dp', 'expert'), may hold values from 0.099609375 to 1
Outputs:
- new_first: bfloat16 [3, 1536, 4096], P(None, 'dp', 'expert')
- new_second: bfloat16 [3, 1536, 4096], P(None, 'dp', 'expert')
- update: bfloat16 [3, 1536, 4096], P(None, 'dp', 'expert')
Inputs may be any that keep to these rules, and one draw needn't show every extreme that they name: `expert_ids`: each token names 4 different experts. Split the tokens in order into aligned blocks of 64 tokens: within a block no expert is named by more than 64 tokens, and in every draw some expert is named by exactly 64 tokens of some block.
All inputs are finite; a program needn't handle non-finite values.
Results may differ from a plain program's by a relative error of at most 0.0068.
Values may be sent and summed in bfloat16 or wider, within the bound.
No kernel may reach another device: no remote copies, remote signals or barrier semaphores. Data moves between devices by JAX's collectives and lax.ppermute only.
A program may use at most 64 MiB of HBM per device.

v0:
```python
import jax
import jax.numpy as jnp
from jax import lax
from jax.sharding import PartitionSpec as P

beta_one = 0.9
beta_two = 0.95
step_count = 10
epsilon = 1e-08


def from_partner(value, axis, distance):
    mask = 2**distance
    pairs = [(source, source ^ mask) for source in range(lax.axis_size(axis))]
    return lax.ppermute(value, axis, pairs)


def contract_last(left, right):
    return lax.dot_general(
        left, right, (((1,), (1,)), ((), ())), preferred_element_type=jnp.float32
    )


def contract_first(left, right):
    return lax.dot_general(
        left, right, (((0,), (0,)), ((), ())), preferred_element_type=jnp.float32
    )


def split_halves(grad, replica, width_half):
    keep = lax.dynamic_slice_in_dim(grad, replica * width_half, width_half, grad.ndim - 1)
    give = lax.dynamic_slice_in_dim(grad, (1 - replica) * width_half, width_half, grad.ndim - 1)
    return (keep, give)


def route_block(block_ids, block_gates, group, n_data, capacity):
    count = block_ids.shape[0]
    top = block_ids.shape[1]
    target = block_ids - group * n_data
    inside = block_ids // n_data == group
    onehot = (
        (target[:, :, None] == jnp.arange(n_data, dtype=jnp.int32)[None, None, :])
        & inside[:, :, None]
    ).astype(jnp.int32)
    per_token = jnp.sum(onehot, axis=1)
    earlier = jnp.cumsum(per_token, axis=0) - per_token
    rank = jnp.sum(onehot * earlier[:, None, :], axis=2)
    total_slots = n_data * capacity
    slot = jnp.where(inside, target * capacity + rank, total_slots).reshape(-1)
    token_of = jnp.broadcast_to(jnp.arange(count, dtype=jnp.int32)[:, None], (count, top)).reshape(
        -1
    )
    table = jnp.full((total_slots,), count, jnp.int32).at[slot].set(token_of, mode="drop")
    gate_slot = (
        jnp.zeros((total_slots,), jnp.bfloat16).at[slot].set(block_gates.reshape(-1), mode="drop")
    )
    return (table, gate_slot)


def per_device(tokens, cotangent, expert_ids, gate_probs, weights, first_moment, second_moment):
    n_expert = lax.axis_size("expert")
    n_data = lax.axis_size("dp")
    slices = min(4, n_expert // 2)
    place = lax.axis_index("expert")
    replica = place % 2
    group = place // (2 * slices)
    groups = n_expert // (2 * slices)
    experts_total = groups * n_data
    half = tokens.shape[0] // 2
    width_half = weights.shape[2]
    top = expert_ids.shape[1]
    capacity = max(2, 2 * half * top // experts_total)
    start = replica * half
    own_ids = lax.dynamic_slice_in_dim(expert_ids, start, half, 0)
    own_gates = lax.dynamic_slice_in_dim(gate_probs, start, half, 0)
    table, gate_slot = route_block(own_ids, own_gates, group, n_data, capacity)
    source_tokens = lax.dynamic_slice_in_dim(tokens, start, half, 0)
    source_cot = lax.dynamic_slice_in_dim(cotangent, start, half, 0)
    columns = source_tokens.shape[1]
    padded_tokens = jnp.concatenate([source_tokens, jnp.zeros((1, columns), jnp.bfloat16)], 0)
    padded_cot = jnp.concatenate([source_cot, jnp.zeros((1, columns), jnp.bfloat16)], 0)
    send_rows = padded_tokens[table].reshape(n_data, -1, columns)
    send_cot = padded_cot[table].reshape(n_data, -1, columns)
    send_gates = gate_slot.reshape(n_data, -1)
    rows_in, gates_in = (
        lax.all_to_all(send_rows, "dp", split_axis=0, concat_axis=0, tiled=True),
        lax.all_to_all(send_gates, "dp", split_axis=0, concat_axis=0, tiled=True),
    )
    rows = rows_in.reshape(-1, columns)
    gate_rows = gates_in.reshape(-1).astype(jnp.float32)
    partner = from_partner(weights, "expert", 0)
    lower = jnp.where(replica == 0, weights, partner)
    upper = jnp.where(replica == 0, partner, weights)
    full = jnp.concatenate([lower, upper], 2)
    hg = contract_last(rows, full[0])
    hu = contract_last(rows, full[1])
    sig = jax.nn.sigmoid(hg)
    act = (hg * sig * hu).astype(jnp.bfloat16)
    cot_in = lax.all_to_all(send_cot, "dp", split_axis=0, concat_axis=0, tiled=True)
    cots = cot_in.reshape(-1, columns)
    dz = (gate_rows[:, None] * cots.astype(jnp.float32)).astype(jnp.bfloat16)
    dact = contract_last(dz, full[2])
    grad_down = contract_first(act, dz)
    dhg = (dact * hu * sig * (1.0 + hg * (1.0 - sig))).astype(jnp.bfloat16)
    dhu = (dact * hg * sig).astype(jnp.bfloat16)
    grad_gate = contract_first(dhg, rows)
    grad_up = contract_first(dhu, rows)
    stacked = jnp.stack([grad_gate, grad_up, grad_down])
    keep, give = split_halves(stacked, replica, width_half)
    total = keep + from_partner(give, "expert", 0)
    moment_one = beta_one * first_moment.astype(jnp.float32) + (1.0 - beta_one) * total
    moment_two = beta_two * second_moment.astype(jnp.float32) + (1.0 - beta_two) * total * total
    step = (
        moment_one
        / (1.0 - beta_one**step_count)
        / (jnp.sqrt(moment_two / (1.0 - beta_two**step_count)) + epsilon)
    )
    return (
        moment_one.astype(jnp.bfloat16),
        moment_two.astype(jnp.bfloat16),
        step.astype(jnp.bfloat16),
    )


def solution(mesh):
    in_specs = (
        P("dp", None),
        P("dp", None),
        P("dp", None),
        P("dp", None),
        P(None, "dp", "expert"),
        P(None, "dp", "expert"),
        P(None, "dp", "expert"),
    )
    out_specs = (P(None, "dp", "expert"), P(None, "dp", "expert"), P(None, "dp", "expert"))
    return jax.shard_map(
        per_device, mesh=mesh, in_specs=in_specs, out_specs=out_specs, check_vma=False
    )
```

profile of v0, /device:TPU:0, one launch (start us, length us, event | category | flops | bytes accessed | tf_op | source)
XLA Modules:
  0.0 148.6 jit_solution(15473388083497676365)
XLA Ops:
  2.5 0.8 add_select_fusion.1
  3.8 2.2 %scatter_custom_fusion = bf16[512]{0:T(512)(128)(2,1)S(1)} fusion(s32[256]{0:T(256)S(1)} %bitcast.39, bf16[256]{0:T(256)(128)(2,1)S(1)} %reshape.117, bf16[]{:T(256)} %constant.33.clone.1), kind=kCustom, calls=%fused_computation.64 | custom fusion | bytes 1026 | tf_op jit(solution)/shard_map/scatter | solution.py:55
  6.6 5.2 %all-to-all-start = ((bf16[8,1,64]{2,1,0:T(2,128)(2,1)}), bf16[8,1,64]{2,1,0:T(2,128)(2,1)S(1)}, u32[]{:S(2)}, u32[]{:S(2)}) async-start(bf16[8,1,64]{2,1,0:T(2,128)(2,1)} %all_to_all.16), calls=%async_computation | async-start | bytes 8192 | tf_op jit(solution)/shard_map/all_to_all | solution.py:87
  11.9 1.4 scatter_custom_fusion.1
  13.3 1.1 constant_dynamic-slice_fusion
  14.5 3.3 %gather_fusion.1 = bf16[512,2048]{1,0:T(8,128)(2,1)} fusion(bf16[65,2048]{1,0:T(8,128)(2,1)S(1)} %concatenate.11, s32[1024]{0:T(1024)S(1)} %pad_clamp_fusion), kind=kCustom, calls=%fused_computation.1 | custom fusion | bytes 4196352 | tf_op jit(solution)/shard_map/gather | solution.py:82
  17.8 4.2 %all-to-all-start.2 = ((bf16[8,64,2048]{2,1,0:T(8,128)(2,1)}), bf16[8,64,2048]{2,1,0:T(8,128)(2,1)S(1)}, u32[]{:S(2)}, u32[]{:S(2)}) async-start(bf16[8,64,2048]{2,1,0:T(8,128)(2,1)} %bitcast.36), calls=%async_computation.2 | async-start | bytes 4194304 | tf_op jit(solution)/shard_map/all_to_all | solution.py:86
  22.0 1.6 %collective-permute-start = (bf16[3,192,1024]{2,1,0:T(8,128)(2,1)}, bf16[3,192,1024]{2,1,0:T(8,128)(2,1)}, u32[]{:S(2)}, u32[]{:S(2)}) collective-permute-start(bf16[3,192,1024]{2,1,0:T(8,128)(2,1)} %param.11), channel_id=1, source_target_pairs={{0,8},{8,0},{16,24},{24,16},{1,9},{9,1},{17,25},{25,17},{2,10},{10... | collective-permute-start | bytes 3538952 | tf_op jit(solution)/shard_map/ppermute | solution.py:15
  23.6 3.3 %gather_fusion = bf16[512,2048]{1,0:T(8,128)(2,1)} fusion(bf16[65,2048]{1,0:T(8,128)(2,1)S(1)} %concatenate.9, s32[1024]{0:T(1024)S(1)} %pad_clamp_fusion), kind=kCustom, calls=%fused_computation | custom fusion | bytes 4196352 | tf_op jit(solution)/shard_map/gather | solution.py:83
  26.9 21.7 %all-to-all-done.2 = bf16[8,64,2048]{2,1,0:T(8,128)(2,1)S(1)} async-done(((bf16[8,64,2048]{2,1,0:T(8,128)(2,1)}), bf16[8,64,2048]{2,1,0:T(8,128)(2,1)S(1)}, u32[]{:S(2)}, u32[]{:S(2)}) %all-to-all-start.2) | async-done | bytes 2097184 | tf_op jit(solution)/shard_map/all_to_all | solution.py:86
  48.6 4.5 %all-to-all-start.1 = ((bf16[8,64,2048]{2,1,0:T(8,128)(2,1)}), bf16[8,64,2048]{2,1,0:T(8,128)(2,1)}, u32[]{:S(2)}, u32[]{:S(2)}) async-start(bf16[8,64,2048]{2,1,0:T(8,128)(2,1)} %bitcast.35), calls=%async_computation.1 | async-start | bytes 4194304 | tf_op jit(solution)/shard_map/all_to_all | solution.py:99
  53.3 1.8 %broadcast_select_fusion = (bf16[3,192,1024]{2,1,0:T(8,128)(2,1)S(1)}, bf16[3,192,1024]{2,1,0:T(8,128)(2,1)S(1)}) fusion(bf16[3,192,1024]{2,1,0:T(8,128)(2,1)} %collective-permute-done, bf16[3,192,1024]{2,1,0:T(8,128)(2,1)} %param.11, pred[]{:T(512)S(6)} %eq.30), kind=kLoop, calls=%fused_computation.22 | loop fusion | flops 1179648 | bytes 4718593 | tf_op jit(solution)/shard_map/jit(_where)/select_n | solution.py:93
  55.1 1.6 %fusion.13 = f32[512,192]{0,1:T(8,128)} fusion(bf16[512,2048]{1,0:T(8,128)(2,1)S(1)} %bitcast.31, bf16[3,192,1024]{2,1,0:T(8,128)(2,1)S(1)} %get-tuple-element.7, bf16[3,192,1024]{2,1,0:T(8,128)(2,1)S(1)} %get-tuple-element.8), kind=kOutput, calls=%fused_computation.32 | convolution fusion | flops 404226048 | bytes 4849664 | tf_op jit(solution)/shard_map/dot_general | solution.py:19
  56.7 1.6 %fusion.6 = f32[512,192]{0,1:T(8,128)} fusion(bf16[512,2048]{1,0:T(8,128)(2,1)S(1)} %bitcast.32, bf16[3,192,1024]{2,1,0:T(8,128)(2,1)S(1)} %get-tuple-element.8, bf16[3,192,1024]{2,1,0:T(8,128)(2,1)S(1)} %get-tuple-element.7), kind=kOutput, calls=%fused_computation.26 | convolution fusion | flops 404226048 | bytes 4849664 | tf_op jit(solution)/shard_map/dot_general | solution.py:19
  58.3 21.4 %all-to-all-done.1 = bf16[8,64,2048]{2,1,0:T(8,128)(2,1)} async-done(((bf16[8,64,2048]{2,1,0:T(8,128)(2,1)}), bf16[8,64,2048]{2,1,0:T(8,128)(2,1)}, u32[]{:S(2)}, u32[]{:S(2)}) %all-to-all-start.1) | async-done | bytes 2097184 | tf_op jit(solution)/shard_map/all_to_all | solution.py:99
  79.6 2.1 %multiply_convert_fusion = bf16[8,64,2048]{2,1,0:T(8,128)(2,1)S(1)} fusion(f32[8,64]{1,0:T(8,128)S(1)} %bitcast.38, bf16[8,64,2048]{2,1,0:T(8,128)(2,1)} %all-to-all-done.1), kind=kLoop, calls=%fused_computation.7 | loop fusion | flops 3145728 | bytes 4196352 | tf_op jit(solution)/shard_map/convert_element_type | solution.py:101
  81.7 0.8 fusion.10
  84.4 2.0 %fusion = bf16[512,2048]{1,0:T(8,128)(2,1)S(1)} fusion(f32[512]{0:T(512)S(1)} %reshape.95, bf16[8,64,2048]{2,1,0:T(8,128)(2,1)} %all-to-all-done.1), kind=kLoop, calls=%fused_computation.6 | loop fusion | flops 3145728 | bytes 4196352 | tf_op jit(solution)/shard_map/convert_element_type | solution.py:101
  87.6 1.8 %constant_dynamic-slice_fusion.3 = f32[3,192,1024]{2,1,0:T(8,128)} fusion(f32[3,192,2048]{2,1,0:T(8,128)S(1)} %pad_maximum_fusion, s32[]{:T(128)S(6)} %select_n.70), kind=kLoop, calls=%fused_computation.61 | loop fusion | bytes 4718596 | tf_op jit(solution)/shard_map/dynamic_slice | solution.py:32
  89.4 1.4 copy-done.1
  90.7 1.6 %collective-permute-start.1 = (f32[3,192,1024]{2,1,0:T(8,128)}, f32[3,192,1024]{2,1,0:T(8,128)}, u32[]{:S(2)}, u32[]{:S(2)}) collective-permute-start(f32[3,192,1024]{2,1,0:T(8,128)} %constant_dynamic-slice_fusion.3), channel_id=1, source_target_pairs={{0,8},{8,0},{16,24},{24,16},{1,9},{9,1},{17,25},{25,17},{2,10},{10... | collective-permute-start | bytes 7077896 | tf_op jit(solution)/shard_map/ppermute | solution.py:15
  92.3 48.7 %collective-permute-done.1 = f32[3,192,1024]{2,1,0:T(8,128)} collective-permute-done((f32[3,192,1024]{2,1,0:T(8,128)}, f32[3,192,1024]{2,1,0:T(8,128)}, u32[]{:S(2)}, u32[]{:S(2)}) %collective-permute-start.1) | collective-permute-done | bytes 2359328 | tf_op jit(solution)/shard_map/ppermute | solution.py:15
  141.0 5.2 %divide_convert_fusion = (bf16[3,192,1024]{2,1,0:T(8,128)(2,1)}, f32[3,192,1024]{2,1,0:T(8,128)S(1)}) fusion(bf16[3,192,1024]{2,1,0:T(8,128)(2,1)S(1)} %copy-done.5, bf16[3,192,1024]{2,1,0:T(8,128)(2,1)S(1)} %copy-done.6, f32[3,192,1024]{2,1,0:T(8,128)} %collective-permute-done.1, f32[3,192,2048]{2,1,0:T(8,128)} %copy-done.1, s32[]{:T(128)S(6)} %select_n.69), kind=kLoop, calls=%fused_computation.17 | loop fusion | flops 8847360 | bytes 10616836 | tf_op jit(solution)/shard_map/convert_element_type | solution.py:121
  146.2 2.4 %fusion.3 = (bf16[3,192,1024]{2,1,0:T(8,128)(2,1)}, bf16[3,192,1024]{2,1,0:T(8,128)(2,1)}) fusion(f32[3,192,1024]{2,1,0:T(8,128)S(1)} %get-tuple-element.4, bf16[3,192,1024]{2,1,0:T(8,128)(2,1)S(1)} %copy-done.6, bf16[3,192,1024]{2,1,0:T(8,128)(2,1)S(1)} %copy-done.5), kind=kLoop, calls=%fused_computation.21 | loop fusion | flops 6488064 | bytes 7077888 | tf_op jit(solution)/shard_map/convert_element_type | solution.py:120
  (45 shorter events, 6.3 us)
Async XLA Ops:
  0.6 2.8 %copy-start = (bf16[128,4]{0,1:T(4,128)(2,1)S(1)}, bf16[128,4]{0,1:T(4,128)(2,1)}, u32[]{:S(2)}) copy-start(bf16[128,4]{0,1:T(4,128)(2,1)} %param.10) | copy-start | bytes 3076
  6.6 11.1 %all-to-all-start = ((bf16[8,1,64]{2,1,0:T(2,128)(2,1)}), bf16[8,1,64]{2,1,0:T(2,128)(2,1)S(1)}, u32[]{:S(2)}, u32[]{:S(2)}) async-start(bf16[8,1,64]{2,1,0:T(2,128)(2,1)} %all_to_all.16), calls=%async_computation | async-start | bytes 8192 | tf_op jit(solution)/shard_map/all_to_all | solution.py:87
  17.8 30.8 %all-to-all-start.2 = ((bf16[8,64,2048]{2,1,0:T(8,128)(2,1)}), bf16[8,64,2048]{2,1,0:T(8,128)(2,1)S(1)}, u32[]{:S(2)}, u32[]{:S(2)}) async-start(bf16[8,64,2048]{2,1,0:T(8,128)(2,1)} %bitcast.36), calls=%async_computation.2 | async-start | bytes 4194304 | tf_op jit(solution)/shard_map/all_to_all | solution.py:86
  22.0 31.3 %collective-permute-start = (bf16[3,192,1024]{2,1,0:T(8,128)(2,1)}, bf16[3,192,1024]{2,1,0:T(8,128)(2,1)}, u32[]{:S(2)}, u32[]{:S(2)}) collective-permute-start(bf16[3,192,1024]{2,1,0:T(8,128)(2,1)} %param.11), channel_id=1, source_target_pairs={{0,8},{8,0},{16,24},{24,16},{1,9},{9,1},{17,25},{25,17},{2,10},{10... | collective-permute-start | bytes 3538952 | tf_op jit(solution)/shard_map/ppermute | solution.py:15
  48.6 31.0 %all-to-all-start.1 = ((bf16[8,64,2048]{2,1,0:T(8,128)(2,1)}), bf16[8,64,2048]{2,1,0:T(8,128)(2,1)}, u32[]{:S(2)}, u32[]{:S(2)}) async-start(bf16[8,64,2048]{2,1,0:T(8,128)(2,1)} %bitcast.35), calls=%async_computation.1 | async-start | bytes 4194304 | tf_op jit(solution)/shard_map/all_to_all | solution.py:99
  55.1 1.6 %copy-start.2 = (bf16[3,192,1024]{2,1,0:T(8,128)(2,1)}, bf16[3,192,1024]{2,1,0:T(8,128)(2,1)S(1)}, u32[]{:S(2)}) copy-start(bf16[3,192,1024]{2,1,0:T(8,128)(2,1)S(1)} %get-tuple-element.8) | copy-start | bytes 3538948
  79.6 2.1 %copy-start.3 = (bf16[3,192,1024]{2,1,0:T(8,128)(2,1)S(1)}, bf16[3,192,1024]{2,1,0:T(8,128)(2,1)}, u32[]{:S(2)}) copy-start(bf16[3,192,1024]{2,1,0:T(8,128)(2,1)} %copy-done.2) | copy-start | bytes 3538948
  81.7 1.0 copy-start.4
  82.7 1.0 copy-start.7
  87.6 3.1 %copy-start.1 = (f32[3,192,2048]{2,1,0:T(8,128)}, f32[3,192,2048]{2,1,0:T(8,128)S(1)}, u32[]{:S(2)}) copy-start(f32[3,192,2048]{2,1,0:T(8,128)S(1)} %pad_maximum_fusion) | copy-start | bytes 14155780
  87.6 53.4 %copy-start.5 = (bf16[3,192,1024]{2,1,0:T(8,128)(2,1)S(1)}, bf16[3,192,1024]{2,1,0:T(8,128)(2,1)}, u32[]{:S(2)}) copy-start(bf16[3,192,1024]{2,1,0:T(8,128)(2,1)} %param.12) | copy-start | bytes 3538948
  87.6 53.4 %copy-start.6 = (bf16[3,192,1024]{2,1,0:T(8,128)(2,1)S(1)}, bf16[3,192,1024]{2,1,0:T(8,128)(2,1)}, u32[]{:S(2)}) copy-start(bf16[3,192,1024]{2,1,0:T(8,128)(2,1)} %param.13) | copy-start | bytes 3538948
  90.7 50.2 %collective-permute-start.1 = (f32[3,192,1024]{2,1,0:T(8,128)}, f32[3,192,1024]{2,1,0:T(8,128)}, u32[]{:S(2)}, u32[]{:S(2)}) collective-permute-start(f32[3,192,1024]{2,1,0:T(8,128)} %constant_dynamic-slice_fusion.3), channel_id=1, source_target_pairs={{0,8},{8,0},{16,24},{24,16},{1,9},{9,1},{17,25},{25,17},{2,10},{10... | collective-permute-start | bytes 7077896 | tf_op jit(solution)/shard_map/ppermute | solution.py:15
where the time goes:
time: 150 us; the launch traced here: 149 us
  waiting for transfers between devices  91.7 us (61%)
  starting transfers between devices  17.1 us (11%)
  local copies, waits for them, and re-layouts  16.5 us (11%)
  other arithmetic  16.5 us (11%)
  matrix products  5.92 us (4%)
    ppermute x2, waiting for transfers between devices, from_partner(): return lax.ppermute(value, axis, pairs)  48.7 us
    all_to_all x1, waiting for transfers between devices, per_device(): lax.all_to_all(send_rows, 'dp', split_axis=0, concat_axis=0, tiled=True)  21.7 us
    all_to_all x1, waiting for transfers between devices, per_device(): lax.all_to_all(send_cot, 'dp', split_axis=0, concat_axis=0, tiled=True)  21.4 us
    convert_element_type x1, other arithmetic, per_device(): step.astype(jnp.bfloat16)  5.24 us
    all_to_all x1, starting transfers between devices, per_device(): lax.all_to_all(send_gates, 'dp', split_axis=0, concat_axis=0, tiled=True)  5.17 us
    all_to_all x1, starting transfers between devices, per_device(): lax.all_to_all(send_cot, 'dp', split_axis=0, concat_axis=0, tiled=True)  4.54 us
    all_to_all x1, starting transfers between devices, per_device(): lax.all_to_all(send_rows, 'dp', split_axis=0, concat_axis=0, tiled=True)  4.2 us
    convert_element_type x2, other arithmetic, per_device(): dz = (gate_rows[:, None] * cots.astype(jnp.float32)).astype(jnp.bfloat16)  4.08 us
  transfers between devices with their start and end apart: 5, of which 3 were waited for; matrix products, arithmetic and copies ran while one was open for 10% of the time, Pallas kernels for 0%

commit v1 on v0

--- a/solution.py
+++ b/solution.py
@@ -1,6 +1,10 @@
+import functools
+
 import jax
 import jax.numpy as jnp
 from jax import lax
+from jax.experimental import pallas as pl
+from jax.experimental.pallas import tpu as pltpu
 from jax.sharding import PartitionSpec as P
 
 beta_one = 0.9
@@ -57,7 +61,7 @@
     return (table, gate_slot)
 
 
-def per_device(tokens, cotangent, expert_ids, gate_probs, weights, first_moment, second_moment):
+def routed_plan(tokens, cotangent, expert_ids, gate_probs, weights, first_moment, second_moment):
     n_expert = lax.axis_size("expert")
     n_data = lax.axis_size("dp")
     slices = min(4, n_expert // 2)
@@ -122,6 +126,278 @@
     )
 
 
+VMEM_LIMIT = 48 * 1024 * 1024
+
+
+def params():
+    return pltpu.CompilerParams(vmem_limit_bytes=VMEM_LIMIT)
+
+
+def cost(flops, moved):
+    return pl.CostEstimate(flops=flops, bytes_accessed=moved, transcendentals=0)
+
+
+def whole():
+    return pl.BlockSpec(memory_space=pltpu.VMEM)
+
+
+def pack_kernel(replica_ref, ids_ref, gates_ref, tokens_ref, cot_ref, x_ref, y_ref):
+    count = tokens_ref.shape[0]
+    x_ref[...] = tokens_ref[...]
+    y_ref[0:count, :] = cot_ref[...]
+    ids = ids_ref[...]
+    gates = gates_ref[...].astype(jnp.float32)
+    slots = y_ref.shape[0] - count
+    row = lax.broadcasted_iota(jnp.int32, (slots, count), 0)
+    gate = jnp.zeros((slots, count), jnp.float32)
+    for k in range(ids.shape[0]):
+        gate = gate + jnp.where(row == ids[k : k + 1, :], gates[k : k + 1, :], 0.0)
+    y_ref[count:, :] = jnp.zeros((slots, y_ref.shape[1]), jnp.bfloat16)
+    y_ref[count:, 0:count] = gate.astype(jnp.bfloat16)
+
+
+def pack_own(replica, ids, gates, tokens, cotangent, width, slots):
+    count, top = ids.shape
+    column = lambda i, replica_ref: (0, replica_ref[0])
+    start = lambda i, replica_ref: (0, 0)
+    return pl.pallas_call(
+        pack_kernel,
+        grid_spec=pltpu.PrefetchScalarGridSpec(
+            num_scalar_prefetch=1,
+            grid=(1,),
+            in_specs=[
+                pl.BlockSpec((top, count), start),
+                pl.BlockSpec((top, count), start),
+                pl.BlockSpec((count, width), column),
+                pl.BlockSpec((count, width), column),
+            ],
+            out_specs=[
+                pl.BlockSpec((count, width), start),
+                pl.BlockSpec((count + slots, width), start),
+            ],
+        ),
+        out_shape=[
+            jax.ShapeDtypeStruct((count, width), jnp.bfloat16),
+            jax.ShapeDtypeStruct((count + slots, width), jnp.bfloat16),
+        ],
+        compiler_params=params(),
+        cost_estimate=cost(1000, 8 * count * width),
+    )(replica.reshape(1), ids.T, gates.T, tokens, cotangent)
+
+
+def joined(refs, count):
+    parts = [ref[0:count, :] for ref in refs]
+    return parts[0] if len(parts) == 1 else jnp.concatenate(parts, 0)
+
+
+def partial_kernel(n, first, last, count, w_ref, *refs):
+    blocks, (own_ref, send_ref) = refs[:n], refs[n:]
+    mats, hidden, width = w_ref.shape
+    left = w_ref[first:last].reshape((last - first) * hidden, width)
+    value = contract_last(left, joined(blocks, count))
+    own_ref[...] = value
+    send_ref[...] = value.astype(jnp.bfloat16)
+
+
+def partials(weights, blocks, first, last, count):
+    hidden, width = weights.shape[1:]
+    shape = ((last - first) * hidden, count * len(blocks))
+    return pl.pallas_call(
+        functools.partial(partial_kernel, len(blocks), first, last, count),
+        in_specs=[whole()] * (1 + len(blocks)),
+        out_specs=[whole()] * 2,
+        out_shape=[
+            jax.ShapeDtypeStruct(shape, jnp.float32),
+            jax.ShapeDtypeStruct(shape, jnp.bfloat16),
+        ],
+        compiler_params=params(),
+        cost_estimate=cost(
+            2 * shape[0] * shape[1] * width, 2 * (shape[0] + shape[1]) * width + 6 * shape[0] * shape[1]
+        ),
+    )(weights, *blocks)
+
+
+def gate_row(expert_ref, y_refs, count):
+    rows = []
+    for ref in y_refs:
+        held = ref[count:, 0:count].astype(jnp.float32)
+        index = lax.broadcasted_iota(jnp.int32, held.shape, 0)
+        rows.append(jnp.sum(jnp.where(index == expert_ref[0], held, 0.0), 0, keepdims=True))
+    return rows[0] if len(rows) == 1 else jnp.concatenate(rows, 1)
+
+
+def hidden_grads(gate, own_gu, got_gu, own_d, got_d):
+    hidden = own_d.shape[0]
+    gu = own_gu[...] + got_gu[...].astype(jnp.float32)
+    hg, hu = gu[0:hidden], gu[hidden:]
+    dact = gate * (own_d[...] + got_d[...].astype(jnp.float32))
+    sig = jax.nn.sigmoid(hg)
+    silu = hg * sig
+    act = (gate * (silu * hu)).astype(jnp.bfloat16)
+    dhg = (dact * hu * sig * (1.0 + hg * (1.0 - sig))).astype(jnp.bfloat16)
+    dhu = (dact * silu).astype(jnp.bfloat16)
+    return dhg, dhu, act
+
+
+def plain(left, right):
+    return lax.dot_general(
+        left, right, (((1,), (0,)), ((), ())), preferred_element_type=jnp.float32
+    )
+
+
+def grad_kernel(n, count, has_acc, expert_ref, own_gu, got_gu, own_d, got_d, *refs):
+    xs, ys = refs[:n], refs[n : 2 * n]
+    out_ref = refs[-1]
+    gate = gate_row(expert_ref, ys, count)
+    dhg, dhu, act = hidden_grads(gate, own_gu, got_gu, own_d, got_d)
+    x = joined(xs, count)
+    y = joined(ys, count)
+    for m, (left, right) in enumerate(((dhg, x), (dhu, x), (act, y))):
+        value = plain(left, right)
+        out_ref[m] = value + refs[2 * n][m] if has_acc else value
+
+
+def smem():
+    return pl.BlockSpec(memory_space=pltpu.SMEM)
+
+
+def add_grads(expert, part, xs, ys, acc, count, width):
+    n = len(xs)
+    hidden = part[2].shape[0]
+    shape = (3, hidden, width)
+    operands = [expert, *part, *xs, *ys] + ([] if acc is None else [acc])
+    return pl.pallas_call(
+        functools.partial(grad_kernel, n, count, acc is not None),
+        in_specs=[smem()] + [whole()] * (len(operands) - 1),
+        out_specs=whole(),
+        out_shape=jax.ShapeDtypeStruct(shape, jnp.float32),
+        input_output_aliases={} if acc is None else {len(operands) - 1: 0},
+        compiler_params=params(),
+        cost_estimate=cost(6 * hidden * width * n * count, 8 * 3 * hidden * width),
+    )(*operands)
+
+
+def last_kernel(n, count, expert_ref, own_gu, got_gu, own_d, got_d, *refs):
+    xs, ys = refs[:n], refs[n : 2 * n]
+    acc_ref, first_ref, second_ref = refs[2 * n : 2 * n + 3]
+    one_ref, two_ref, step_ref, left_ref = refs[2 * n + 3 :]
+    m = pl.program_id(1)
+
+    @pl.when((m == 0) & (pl.program_id(0) == 0))
+    def _():
+        gate = gate_row(expert_ref, ys, count)
+        dhg, dhu, act = hidden_grads(gate, own_gu, got_gu, own_d, got_d)
+        left_ref[0] = dhg
+        left_ref[1] = dhu
+        left_ref[2] = act
+
+    def finish(right):
+        grad = acc_ref[0] + plain(left_ref[m], right)
+        moment_one = beta_one * first_ref[0].astype(jnp.float32) + (1.0 - beta_one) * grad
+        moment_two = beta_two * second_ref[0].astype(jnp.float32) + (1.0 - beta_two) * grad * grad
+        one_ref[0] = moment_one.astype(jnp.bfloat16)
+        two_ref[0] = moment_two.astype(jnp.bfloat16)
+        scaled = moment_two * (1.0 / (1.0 - beta_two**step_count))
+        below = scaled * lax.rsqrt(scaled) + epsilon
+        step = moment_one * (1.0 / (1.0 - beta_one**step_count)) / below
+        step_ref[0] = step.astype(jnp.bfloat16)
+
+    @pl.when(m < 2)
+    def _():
+        finish(joined(xs, count))
+
+    @pl.when(m == 2)
+    def _():
+        finish(joined(ys, count))
+
+
+def last_grads(expert, part, xs, ys, acc, first_moment, second_moment, count, columns):
+    n = len(xs)
+    mats, hidden, width = first_moment.shape
+    tile = pl.BlockSpec((1, hidden, columns), lambda j, m: (m, 0, j))
+    out = jax.ShapeDtypeStruct(first_moment.shape, jnp.bfloat16)
+    flat = lambda value: pl.BlockSpec(value.shape, lambda j, m: (0, 0))
+    strip = lambda value: pl.BlockSpec((value.shape[0], columns), lambda j, m: (0, j))
+    gates_in = [flat(value) for value in part]
+    return pl.pallas_call(
+        functools.partial(last_kernel, n, count),
+        grid=(width // columns, mats),
+        in_specs=[smem()]
+        + gates_in
+        + [strip(value) for value in xs]
+        + [strip(value) for value in ys]
+        + [tile] * 3,
+        out_specs=[tile] * 3,
+        out_shape=[out] * 3,
+        scratch_shapes=[pltpu.VMEM((mats, hidden, n * count), jnp.bfloat16)],
+        compiler_params=params(),
+        cost_estimate=cost(6 * hidden * width * n * count, 24 * hidden * width * mats),
+    )(expert, *part, *xs, *ys, acc, first_moment, second_moment)
+
+
+def from_masked(value, axis, mask):
+    pairs = [(source, source ^ mask) for source in range(lax.axis_size(axis))]
+    return lax.ppermute(value, axis, pairs)
+
+
+def dense_plan(tokens, cotangent, expert_ids, gate_probs, weights, first_moment, second_moment):
+    n_expert = lax.axis_size("expert")
+    n_data = lax.axis_size("dp")
+    slices = min(4, n_expert // 2)
+    place = lax.axis_index("expert")
+    replica = place % 2
+    group = place // (2 * slices)
+    groups = n_expert // (2 * slices)
+    experts_total = groups * n_data
+    expert = (group * n_data + lax.axis_index("dp")).astype(jnp.int32).reshape(1)
+    count = tokens.shape[0]
+    width = weights.shape[2]
+    slots = -(-experts_total // 16) * 16
+    x_own, y_own = pack_own(
+        replica.astype(jnp.int32), expert_ids, gate_probs, tokens, cotangent, width, slots
+    )
+    xs = {0: x_own}
+    ys = {0: y_own}
+    far = [mask for mask in range(2, n_data, 2)]
+    for mask in far:
+        xs[mask] = from_masked(x_own, "dp", mask)
+        ys[mask] = from_masked(y_own, "dp", mask)
+    for mask in [0] + far:
+        xs[mask + 1] = from_masked(xs[mask], "dp", 1)
+        ys[mask + 1] = from_masked(ys[mask], "dp", 1)
+    near = [mask for mask in far if mask & (mask - 1) == 0]
+    rest = [mask for mask in far if mask & (mask - 1)]
+    chunks = [[0, 1], [m + c for m in near for c in (0, 1)], [m + c for m in rest for c in (0, 1)]]
+    chunks = [chunk for chunk in chunks if chunk]
+    acc = None
+    for number, chunk in enumerate(chunks):
+        x_chunk = [xs[m] for m in chunk]
+        y_chunk = [ys[m] for m in chunk]
+        own_gu, send_gu = partials(weights, x_chunk, 0, 2, count)
+        own_d, send_d = partials(weights, y_chunk, 2, 3, count)
+        got_gu = from_masked(send_gu, "expert", 1)
+        got_d = from_masked(send_d, "expert", 1)
+        part = (own_gu, got_gu, own_d, got_d)
+        if number < len(chunks) - 1:
+            acc = add_grads(expert, part, x_chunk, y_chunk, acc, count, width)
+    return tuple(
+        last_grads(expert, part, x_chunk, y_chunk, acc, first_moment, second_moment, count, width // 2)
+    )
+
+
+def per_device(tokens, cotangent, expert_ids, gate_probs, weights, first_moment, second_moment):
+    n_expert = lax.axis_size("expert")
+    n_data = lax.axis_size("dp")
+    slices = min(4, n_expert // 2)
+    experts_total = n_expert // (2 * slices) * n_data
+    half = tokens.shape[0] // 2
+    dense = 2 * half * expert_ids.shape[1] // experts_total >= half
+    plan = dense_plan if dense and n_data in (4, 8) else routed_plan
+    return plan(
+        tokens, cotangent, expert_ids, gate_probs, weights, first_moment, second_moment
+    )
+
+
 def solution(mesh):
     in_specs = (
         P("dp", None),

time: 150 us -> 82.8 us (0.55)
  waiting for transfers between devices: 91.7 us -> 29.4 us
  Pallas kernels: 0 us -> 18.4 us
  other arithmetic: 16.5 us -> 0 us
  matrix products: 5.92 us -> 0 us
  local copies, waits for them, and re-layouts: 16.5 us -> 13.1 us
  starting transfers between devices: 17.1 us -> 20.4 us
    all_to_all x3 -> x0, waiting for transfers between devices: 43.1 us -> none  [the longest x1 21.7 us: per_device(): lax.all_to_all(send_rows, 'dp', split_axis=0, concat_axis=0, tiled=True)]
    ppermute x2 -> x20, waiting for transfers between devices: 48.7 us -> 29.4 us  [from_masked(): return lax.ppermute(value, axis, pairs)]
    pallas_call x0 -> x10, Pallas kernels: none -> 18.4 us  [the longest x1 6.41 us: last_grads(): pl.pallas_call(functools.partial(last_kernel, n, count), grid=(width // c...]
    ppermute x2 -> x20, starting transfers between devices: 3.15 us -> 20.4 us  [from_masked(): return lax.ppermute(value, axis, pairs)]
    all_to_all x3 -> x0, starting transfers between devices: 13.9 us -> none  [the longest x1 5.17 us: per_device(): lax.all_to_all(send_gates, 'dp', split_axis=0, concat_axis=0, tiled=True)]
    convert_element_type x6 -> x0, other arithmetic: 11.7 us -> none  [the longest x1 5.24 us: per_device(): step.astype(jnp.bfloat16)]
    unnamed x16 -> x62, local copies, waits for them, and re-layouts: 1.91 us -> 13.1 us
    gather x2 -> x0, local copies, waits for them, and re-layouts: 6.62 us -> none  [the longest x1 3.32 us: per_device(): send_cot = padded_cot[table].reshape(n_data, -1, columns)]
  transfers between devices with their start and end apart: 5 -> 20, of which waited for: 3 -> 4; matrix products, arithmetic and copies ran while one was open for 10% -> 0% of each run, Pallas kernels for 0% -> 15%
where the time goes in v1:
time: 82.8 us; the launch traced here: 82.2 us
  waiting for transfers between devices  29.4 us (36%)
  starting transfers between devices  20.4 us (25%)
  Pallas kernels  18.4 us (22%)
  local copies, waits for them, and re-layouts  13.1 us (16%)
  between operations  0.86 us (1%)
    ppermute x20, waiting for transfers between devices, from_masked(): return lax.ppermute(value, axis, pairs)  29.4 us
    ppermute x20, starting transfers between devices, from_masked(): return lax.ppermute(value, axis, pairs)  20.4 us
    unnamed x62, local copies, waits for them, and re-layouts  13.1 us
    pallas_call x1, Pallas kernels, last_grads(): pl.pallas_call(functools.partial(last_kernel, n, count), grid=(width // c...  6.41 us
    pallas_call x6, Pallas kernels, partials(): pl.pallas_call(functools.partial(partial_kernel, len(blocks), first, last...  6 us
    pallas_call x2, Pallas kernels, add_grads(): pl.pallas_call(functools.partial(grad_kernel, n, count, acc is not None),...  5.92 us
  transfers between devices with their start and end apart: 20, of which 4 were waited for; matrix products, arithmetic and copies ran while one was open for 0% of the time, Pallas kernels for 15%

profile of v1, /device:TPU:0, one launch (start us, length us, event | category | flops | bytes accessed | tf_op | source)
XLA Modules:
  0.0 82.2 jit_solution(14911803225361576823)
XLA Ops:
  0.7 1.0 %copy-done.15 = bf16[128,2048]{1,0:T(8,128)(2,1)S(1)} copy-done((bf16[128,2048]{1,0:T(8,128)(2,1)S(1)}, bf16[128,2048]{1,0:T(8,128)(2,1)}, u32[]{:S(2)}) %copy-start.15) | copy-done | bytes 524312
  1.7 1.0 %copy-done.16 = bf16[128,2048]{1,0:T(8,128)(2,1)S(1)} copy-done((bf16[128,2048]{1,0:T(8,128)(2,1)S(1)}, bf16[128,2048]{1,0:T(8,128)(2,1)}, u32[]{:S(2)}) %copy-start.16) | copy-done | bytes 524312
  4.7 2.6 %collective-permute-start.6 = (bf16[128,1024]{1,0:T(8,128)(2,1)S(1)}, bf16[128,1024]{1,0:T(8,128)(2,1)S(1)}, u32[]{:S(2)}, u32[]{:S(2)}) collective-permute-start(bf16[128,1024]{1,0:T(8,128)(2,1)S(1)} %get-tuple-element.17.refs_0_), channel_id=1, source_target_pairs={{0,2},{1,3},{2,0},{3,1},{4,6},{5,7},{6,4},{7,5},{8,10},{9,11},{10,... | collective-permute-start | bytes 786440 | tf_op jit(solution)/shard_map/ppermute | solution.py:340
  7.3 2.0 %collective-permute-start.8 = (bf16[128,1024]{1,0:T(8,128)(2,1)S(1)}, bf16[128,1024]{1,0:T(8,128)(2,1)S(1)}, u32[]{:S(2)}, u32[]{:S(2)}) collective-permute-start(bf16[128,1024]{1,0:T(8,128)(2,1)S(1)} %get-tuple-element.17.refs_0_), channel_id=1, source_target_pairs={{0,4},{1,5},{2,6},{3,7},{4,0},{5,1},{6,2},{7,3},{8,12},{9,13},{10,... | collective-permute-start | bytes 786440 | tf_op jit(solution)/shard_map/ppermute | solution.py:340
  9.3 1.4 %collective-permute-start = (bf16[128,1024]{1,0:T(8,128)(2,1)S(1)}, bf16[128,1024]{1,0:T(8,128)(2,1)S(1)}, u32[]{:S(2)}, u32[]{:S(2)}) collective-permute-start(bf16[128,1024]{1,0:T(8,128)(2,1)S(1)} %get-tuple-element.17.refs_0_), channel_id=1, source_target_pairs={{0,6},{1,7},{2,4},{3,5},{4,2},{5,3},{6,0},{7,1},{8,14},{9,15},{10,... | collective-permute-start | bytes 786440 | tf_op jit(solution)/shard_map/ppermute | solution.py:340
  10.7 1.5 %collective-permute-start.13 = (bf16[144,1024]{1,0:T(8,128)(2,1)S(1)}, bf16[144,1024]{1,0:T(8,128)(2,1)S(1)}, u32[]{:S(2)}, u32[]{:S(2)}) collective-permute-start(bf16[144,1024]{1,0:T(8,128)(2,1)S(1)} %get-tuple-element.20.refs_0_.refs_2_), channel_id=1, source_target_pairs={{0,4},{1,5},{2,6},{3,7},{4,0},{5,1},{6,2},{7,3},{8,12},{9,13},{10,... | collective-permute-start | bytes 884744 | tf_op jit(solution)/shard_map/ppermute | solution.py:340
  12.2 2.1 %collective-permute-done.6.refs_0_ = bf16[128,1024]{1,0:T(8,128)(2,1)S(1)} collective-permute-done((bf16[128,1024]{1,0:T(8,128)(2,1)S(1)}, bf16[128,1024]{1,0:T(8,128)(2,1)S(1)}, u32[]{:S(2)}, u32[]{:S(2)}) %collective-permute-start.6) | collective-permute-done | bytes 262176 | tf_op jit(solution)/shard_map/ppermute | solution.py:340
  14.4 2.9 %collective-permute-start.3 = (bf16[144,1024]{1,0:T(8,128)(2,1)S(1)}, bf16[144,1024]{1,0:T(8,128)(2,1)S(1)}, u32[]{:S(2)}, u32[]{:S(2)}) collective-permute-start(bf16[144,1024]{1,0:T(8,128)(2,1)S(1)} %get-tuple-element.20.refs_0_.refs_2_), channel_id=1, source_target_pairs={{0,6},{1,7},{2,4},{3,5},{4,2},{5,3},{6,0},{7,1},{8,14},{9,15},{10,... | collective-permute-start | bytes 884744 | tf_op jit(solution)/shard_map/ppermute | solution.py:340
  17.3 10.5 %collective-permute-done.refs_0_ = bf16[128,1024]{1,0:T(8,128)(2,1)S(1)} collective-permute-done((bf16[128,1024]{1,0:T(8,128)(2,1)S(1)}, bf16[128,1024]{1,0:T(8,128)(2,1)S(1)}, u32[]{:S(2)}, u32[]{:S(2)}) %collective-permute-start) | collective-permute-done | bytes 262176 | tf_op jit(solution)/shard_map/ppermute | solution.py:340
  28.4 5.5 %collective-permute-done.13.refs_2_.refs_6_ = bf16[144,1024]{1,0:T(8,128)(2,1)S(1)} collective-permute-done((bf16[144,1024]{1,0:T(8,128)(2,1)S(1)}, bf16[144,1024]{1,0:T(8,128)(2,1)S(1)}, u32[]{:S(2)}, u32[]{:S(2)}) %collective-permute-start.13) | collective-permute-done | bytes 294944 | tf_op jit(solution)/shard_map/ppermute | solution.py:340
  34.9 1.3 %copy-done = bf16[3,192,1024]{2,1,0:T(8,128)(2,1)S(1)} copy-done((bf16[3,192,1024]{2,1,0:T(8,128)(2,1)S(1)}, bf16[3,192,1024]{2,1,0:T(8,128)(2,1)}, u32[]{:S(2)}) %copy-start) | copy-done | bytes 1179672
  36.2 1.4 %shard_map.97 = (f32[384,512]{1,0:T(8,128)S(1)}, bf16[384,512]{1,0:T(8,128)(2,1)}) custom-call(bf16[3,192,1024]{2,1,0:T(8,128)(2,1)S(1)} %copy-done, bf16[128,1024]{1,0:T(8,128)(2,1)S(1)} %collective-permute-done.6.refs_0_, bf16[128,1024]{1,0:T(8,128)(2,1)S(1)} %collective-permute-done.7.refs_1_, bf16[128,1024]{1,0:T(8,128)(2,1)S(1)} %collective-permute-done.8.refs_2_, ...), custom_call_target="tpu_custom_call" | custom-call | flops 402653184 | bytes 3014656 | tf_op jit(solution)/shard_map/pallas_call | solution.py:205
  38.4 1.8 %collective-permute-start.10 = (bf16[384,512]{1,0:T(8,128)(2,1)}, bf16[384,512]{1,0:T(8,128)(2,1)}, u32[]{:S(2)}, u32[]{:S(2)}) collective-permute-start(bf16[384,512]{1,0:T(8,128)(2,1)} %get-tuple-element.24), channel_id=1, source_target_pairs={{0,8},{8,0},{16,24},{24,16},{1,9},{9,1},{17,25},{25,17},{2,10},{10... | collective-permute-start | bytes 1179656 | tf_op jit(solution)/shard_map/ppermute | solution.py:340
  40.2 1.1 %shard_map.99 = (f32[384,256]{1,0:T(8,128)S(1)}, bf16[384,256]{1,0:T(8,128)(2,1)}) custom-call(bf16[3,192,1024]{2,1,0:T(8,128)(2,1)S(1)} %copy-done.1, bf16[128,1024]{1,0:T(8,128)(2,1)S(1)} %get-tuple-element.17.refs_0_, bf16[128,1024]{1,0:T(8,128)(2,1)S(1)} %collective-permute-done.16.refs_1_), custom_call_target="tpu_custom_call" | custom-call | flops 201326592 | bytes 1900544 | tf_op jit(solution)/shard_map/pallas_call | solution.py:205
  41.6 1.2 %shard_map.98 = (f32[192,512]{1,0:T(8,128)S(1)}, bf16[192,512]{1,0:T(8,128)(2,1)}) custom-call(bf16[3,192,1024]{2,1,0:T(8,128)(2,1)S(1)} %copy-done.1, bf16[144,1024]{1,0:T(8,128)(2,1)S(1)} %collective-permute-done.11.refs_0_.refs_4_, bf16[144,1024]{1,0:T(8,128)(2,1)S(1)} %collective-permute-done.12.refs_1_.refs_5_, ...), custom_call_target="tpu_custom_call" | custom-call | flops 201326592 | bytes 2031616 | tf_op jit(solution)/shard_map/pallas_call | solution.py:205
  42.8 1.9 %collective-permute-start.15 = (bf16[192,512]{1,0:T(8,128)(2,1)}, bf16[192,512]{1,0:T(8,128)(2,1)}, u32[]{:S(2)}, u32[]{:S(2)}) collective-permute-start(bf16[192,512]{1,0:T(8,128)(2,1)} %get-tuple-element.26), channel_id=1, source_target_pairs={{0,8},{8,0},{16,24},{24,16},{1,9},{9,1},{17,25},{25,17},{2,10},{10... | collective-permute-start | bytes 589832 | tf_op jit(solution)/shard_map/ppermute | solution.py:340
  45.3 1.1 %shard_map.95 = (f32[384,256]{1,0:T(8,128)S(1)}, bf16[384,256]{1,0:T(8,128)(2,1)}) custom-call(bf16[3,192,1024]{2,1,0:T(8,128)(2,1)S(1)} %copy-done.1, bf16[128,1024]{1,0:T(8,128)(2,1)S(1)} %collective-permute-done.refs_0_, bf16[128,1024]{1,0:T(8,128)(2,1)S(1)} %collective-permute-done.1.refs_1_), custom_call_target="tpu_custom_call" | custom-call | flops 201326592 | bytes 1900544 | tf_op jit(solution)/shard_map/pallas_call | solution.py:205
  46.4 1.9 %collective-permute-start.2 = (bf16[384,256]{1,0:T(8,128)(2,1)}, bf16[384,256]{1,0:T(8,128)(2,1)}, u32[]{:S(2)}, u32[]{:S(2)}) collective-permute-start(bf16[384,256]{1,0:T(8,128)(2,1)} %get-tuple-element.19), channel_id=1, source_target_pairs={{0,8},{8,0},{16,24},{24,16},{1,9},{9,1},{17,25},{25,17},{2,10},{10... | collective-permute-start | bytes 589832 | tf_op jit(solution)/shard_map/ppermute | solution.py:340
  50.0 11.2 %collective-permute-done.19.got_d = bf16[192,256]{1,0:T(8,128)(2,1)S(1)} collective-permute-done((bf16[192,256]{1,0:T(8,128)(2,1)S(1)}, bf16[192,256]{1,0:T(8,128)(2,1)S(1)}, u32[]{:S(2)}, u32[]{:S(2)}) %collective-permute-start.19) | collective-permute-done | bytes 98336 | tf_op jit(solution)/shard_map/ppermute | solution.py:340
  61.8 1.8 %collective-permute-start.5 = (bf16[192,256]{1,0:T(8,128)(2,1)}, bf16[192,256]{1,0:T(8,128)(2,1)S(1)}, u32[]{:S(2)}, u32[]{:S(2)}) collective-permute-start(bf16[192,256]{1,0:T(8,128)(2,1)} %get-tuple-element.22), channel_id=1, source_target_pairs={{0,8},{8,0},{16,24},{24,16},{1,9},{9,1},{17,25},{25,17},{2,10},{10... | collective-permute-start | bytes 294920 | tf_op jit(solution)/shard_map/ppermute | solution.py:340
  68.3 1.5 %shard_map.101.refs_8_ = f32[3,192,1024]{2,1,0:T(8,128)S(1)} custom-call(s32[1]{0:T(128)} %bitcast.expert_ref, f32[384,256]{1,0:T(8,128)S(1)} %copy-done.20, bf16[384,256]{1,0:T(8,128)(2,1)} %collective-permute-done.17.got_gu, f32[192,256]{1,0:T(8,128)S(1)} %copy-done.24, bf16[192,256]{1,0:T(8,128)(2,1)S(1)} %copy-done.28, bf16[128,1024]{1,0:T(8,128)(2,1)S(1)} %copy-done.6, ...), custom_call_target="tpu_custom_call" | custom-call | flops 301989888 | bytes 4718592 | tf_op jit(solution)/shard_map/pallas_call | solution.py:269
  69.9 1.4 %copy-done.2 = f32[3,192,1024]{2,1,0:T(8,128)} copy-done((f32[3,192,1024]{2,1,0:T(8,128)}, f32[3,192,1024]{2,1,0:T(8,128)S(1)}, u32[]{:S(2)}) %copy-start.2) | copy-done | bytes 2359320
  71.3 4.4 %shard_map.102.refs_4_ = f32[3,192,1024]{2,1,0:T(8,128)} custom-call(s32[1]{0:T(128)} %bitcast.expert_ref, f32[384,512]{1,0:T(8,128)S(1)} %copy-done.14, bf16[384,512]{1,0:T(8,128)(2,1)} %collective-permute-done.10.got_gu, f32[192,512]{1,0:T(8,128)S(1)} %copy-done.18, ...), custom_call_target="tpu_custom_call", output_to_operand_aliasing={{}: (13, {})} | custom-call | flops 603979776 | bytes 4718592 | tf_op jit(solution)/shard_map/pallas_call | solution.py:269
  75.8 6.4 %shard_map.103 = (bf16[3,192,1024]{2,1,0:T(8,128)(2,1)}, bf16[3,192,1024]{2,1,0:T(8,128)(2,1)}, bf16[3,192,1024]{2,1,0:T(8,128)(2,1)}) custom-call(s32[1]{0:T(128)} %bitcast.expert_ref, f32[384,256]{1,0:T(8,128)S(1)} %copy-done.22, bf16[384,256]{1,0:T(8,128)(2,1)} %collective-permute-done.2.got_gu, f32[192,256]{1,0:T(8,128)S(1)} %copy-done.26, ...), custom_call_target="tpu_custom_call" | custom-call | flops 301989888 | bytes 14155776 | tf_op jit(solution)/shard_map/pallas_call | solution.py:322
  (88 shorter events, 12.4 us)
Async XLA Ops:
  4.1 37.2 %copy-start.5 = (bf16[128,1024]{1,0:T(8,128)(2,1)}, bf16[128,1024]{1,0:T(8,128)(2,1)S(1)}, u32[]{:S(2)}) copy-start(bf16[128,1024]{1,0:T(8,128)(2,1)S(1)} %get-tuple-element.17.refs_0_) | copy-start | bytes 786436
  4.1 6.6 %collective-permute-start.16 = (bf16[128,1024]{1,0:T(8,128)(2,1)S(1)}, bf16[128,1024]{1,0:T(8,128)(2,1)S(1)}, u32[]{:S(2)}, u32[]{:S(2)}) collective-permute-start(bf16[128,1024]{1,0:T(8,128)(2,1)S(1)} %get-tuple-element.17.refs_0_), channel_id=1, source_target_pairs={{0,1},{1,0},{2,3},{3,2},{4,5},{5,4},{6,7},{7,6},{8,9},{9,8},{10,11... | collective-permute-start | bytes 786440 | tf_op jit(solution)/shard_map/ppermute | solution.py:340
  4.7 9.7 %collective-permute-start.6 = (bf16[128,1024]{1,0:T(8,128)(2,1)S(1)}, bf16[128,1024]{1,0:T(8,128)(2,1)S(1)}, u32[]{:S(2)}, u32[]{:S(2)}) collective-permute-start(bf16[128,1024]{1,0:T(8,128)(2,1)S(1)} %get-tuple-element.17.refs_0_), channel_id=1, source_target_pairs={{0,2},{1,3},{2,0},{3,1},{4,6},{5,7},{6,4},{7,5},{8,10},{9,11},{10,... | collective-permute-start | bytes 786440 | tf_op jit(solution)/shard_map/ppermute | solution.py:340
  7.2 20.6 %collective-permute-start.11 = (bf16[144,1024]{1,0:T(8,128)(2,1)S(1)}, bf16[144,1024]{1,0:T(8,128)(2,1)S(1)}, u32[]{:S(2)}, u32[]{:S(2)}) collective-permute-start(bf16[144,1024]{1,0:T(8,128)(2,1)S(1)} %get-tuple-element.20.refs_0_.refs_2_), channel_id=1, source_target_pairs={{0,2},{1,3},{2,0},{3,1},{4,6},{5,7},{6,4},{7,5},{8,10},{9,11},{10,... | collective-permute-start | bytes 884744 | tf_op jit(solution)/shard_map/ppermute | solution.py:340
  7.3 10.0 %collective-permute-start.8 = (bf16[128,1024]{1,0:T(8,128)(2,1)S(1)}, bf16[128,1024]{1,0:T(8,128)(2,1)S(1)}, u32[]{:S(2)}, u32[]{:S(2)}) collective-permute-start(bf16[128,1024]{1,0:T(8,128)(2,1)S(1)} %get-tuple-element.17.refs_0_), channel_id=1, source_target_pairs={{0,4},{1,5},{2,6},{3,7},{4,0},{5,1},{6,2},{7,3},{8,12},{9,13},{10,... | collective-permute-start | bytes 786440 | tf_op jit(solution)/shard_map/ppermute | solution.py:340
  9.3 18.6 %collective-permute-start = (bf16[128,1024]{1,0:T(8,128)(2,1)S(1)}, bf16[128,1024]{1,0:T(8,128)(2,1)S(1)}, u32[]{:S(2)}, u32[]{:S(2)}) collective-permute-start(bf16[128,1024]{1,0:T(8,128)(2,1)S(1)} %get-tuple-element.17.refs_0_), channel_id=1, source_target_pairs={{0,6},{1,7},{2,4},{3,5},{4,2},{5,3},{6,0},{7,1},{8,14},{9,15},{10,... | collective-permute-start | bytes 786440 | tf_op jit(solution)/shard_map/ppermute | solution.py:340
  10.7 30.6 %copy-start.7 = (bf16[128,1024]{1,0:T(8,128)(2,1)}, bf16[128,1024]{1,0:T(8,128)(2,1)S(1)}, u32[]{:S(2)}) copy-start(bf16[128,1024]{1,0:T(8,128)(2,1)S(1)} %collective-permute-done.16.refs_1_) | copy-start | bytes 786436
  10.7 23.2 %collective-permute-start.13 = (bf16[144,1024]{1,0:T(8,128)(2,1)S(1)}, bf16[144,1024]{1,0:T(8,128)(2,1)S(1)}, u32[]{:S(2)}, u32[]{:S(2)}) collective-permute-start(bf16[144,1024]{1,0:T(8,128)(2,1)S(1)} %get-tuple-element.20.refs_0_.refs_2_), channel_id=1, source_target_pairs={{0,4},{1,5},{2,6},{3,7},{4,0},{5,1},{6,2},{7,3},{8,12},{9,13},{10,... | collective-permute-start | bytes 884744 | tf_op jit(solution)/shard_map/ppermute | solution.py:340
  14.4 19.5 %collective-permute-start.3 = (bf16[144,1024]{1,0:T(8,128)(2,1)S(1)}, bf16[144,1024]{1,0:T(8,128)(2,1)S(1)}, u32[]{:S(2)}, u32[]{:S(2)}) collective-permute-start(bf16[144,1024]{1,0:T(8,128)(2,1)S(1)} %get-tuple-element.20.refs_0_.refs_2_), channel_id=1, source_target_pairs={{0,6},{1,7},{2,4},{3,5},{4,2},{5,3},{6,0},{7,1},{8,14},{9,15},{10,... | collective-permute-start | bytes 884744 | tf_op jit(solution)/shard_map/ppermute | solution.py:340
  17.3 17.1 %collective-permute-start.7 = (bf16[128,1024]{1,0:T(8,128)(2,1)S(1)}, bf16[128,1024]{1,0:T(8,128)(2,1)S(1)}, u32[]{:S(2)}, u32[]{:S(2)}) collective-permute-start(bf16[128,1024]{1,0:T(8,128)(2,1)S(1)} %collective-permute-done.6.refs_0_), channel_id=1, source_target_pairs={{0,1},{1,0},{2,3},{3,2},{4,5},{5,4},{6,7},{7,6},{8,9},{9,8},{10,11... | collective-permute-start | bytes 786440 | tf_op jit(solution)/shard_map/ppermute | solution.py:340
  27.8 17.5 %copy-start.9 = (bf16[128,1024]{1,0:T(8,128)(2,1)}, bf16[128,1024]{1,0:T(8,128)(2,1)S(1)}, u32[]{:S(2)}) copy-start(bf16[128,1024]{1,0:T(8,128)(2,1)S(1)} %collective-permute-done.refs_0_) | copy-start | bytes 786436
  27.8 6.6 %collective-permute-start.9 = (bf16[128,1024]{1,0:T(8,128)(2,1)S(1)}, bf16[128,1024]{1,0:T(8,128)(2,1)S(1)}, u32[]{:S(2)}, u32[]{:S(2)}) collective-permute-start(bf16[128,1024]{1,0:T(8,128)(2,1)S(1)} %collective-permute-done.8.refs_2_), channel_id=1, source_target_pairs={{0,1},{1,0},{2,3},{3,2},{4,5},{5,4},{6,7},{7,6},{8,9},{9,8},{10,11... | collective-permute-start | bytes 786440 | tf_op jit(solution)/shard_map/ppermute | solution.py:340
  27.8 10.6 %collective-permute-start.12 = (bf16[144,1024]{1,0:T(8,128)(2,1)S(1)}, bf16[144,1024]{1,0:T(8,128)(2,1)S(1)}, u32[]{:S(2)}, u32[]{:S(2)}) collective-permute-start(bf16[144,1024]{1,0:T(8,128)(2,1)S(1)} %collective-permute-done.11.refs_0_.refs_4_), channel_id=1, source_target_pairs={{0,1},{1,0},{2,3},{3,2},{4,5},{5,4},{6,7},{7,6},{8,9},{9,8},{10,11... | collective-permute-start | bytes 884744 | tf_op jit(solution)/shard_map/ppermute | solution.py:340
  33.9 7.4 %collective-permute-start.14 = (bf16[144,1024]{1,0:T(8,128)(2,1)S(1)}, bf16[144,1024]{1,0:T(8,128)(2,1)S(1)}, u32[]{:S(2)}, u32[]{:S(2)}) collective-permute-start(bf16[144,1024]{1,0:T(8,128)(2,1)S(1)} %collective-permute-done.13.refs_2_.refs_6_), channel_id=1, source_target_pairs={{0,1},{1,0},{2,3},{3,2},{4,5},{5,4},{6,7},{7,6},{8,9},{9,8},{10,11... | collective-permute-start | bytes 884744 | tf_op jit(solution)/shard_map/ppermute | solution.py:340
  33.9 8.9 %collective-permute-start.18 = (bf16[144,1024]{1,0:T(8,128)(2,1)S(1)}, bf16[144,1024]{1,0:T(8,128)(2,1)S(1)}, u32[]{:S(2)}, u32[]{:S(2)}) collective-permute-start(bf16[144,1024]{1,0:T(8,128)(2,1)S(1)} %get-tuple-element.20.refs_0_.refs_2_), channel_id=1, source_target_pairs={{0,1},{1,0},{2,3},{3,2},{4,5},{5,4},{6,7},{7,6},{8,9},{9,8},{10,11... | collective-permute-start | bytes 884744 | tf_op jit(solution)/shard_map/ppermute | solution.py:340
  34.4 12.0 %collective-permute-start.4 = (bf16[144,1024]{1,0:T(8,128)(2,1)S(1)}, bf16[144,1024]{1,0:T(8,128)(2,1)S(1)}, u32[]{:S(2)}, u32[]{:S(2)}) collective-permute-start(bf16[144,1024]{1,0:T(8,128)(2,1)S(1)} %collective-permute-done.3.refs_0_.refs_2_), channel_id=1, source_target_pairs={{0,1},{1,0},{2,3},{3,2},{4,5},{5,4},{6,7},{7,6},{8,9},{9,8},{10,11... | collective-permute-start | bytes 884744 | tf_op jit(solution)/shard_map/ppermute | solution.py:340
  34.5 10.5 %collective-permute-start.1 = (bf16[128,1024]{1,0:T(8,128)(2,1)S(1)}, bf16[128,1024]{1,0:T(8,128)(2,1)S(1)}, u32[]{:S(2)}, u32[]{:S(2)}) collective-permute-start(bf16[128,1024]{1,0:T(8,128)(2,1)S(1)} %collective-permute-done.refs_0_), channel_id=1, source_target_pairs={{0,1},{1,0},{2,3},{3,2},{4,5},{5,4},{6,7},{7,6},{8,9},{9,8},{10,11... | collective-permute-start | bytes 786440 | tf_op jit(solution)/shard_map/ppermute | solution.py:340
  38.4 32.8 %collective-permute-start.10 = (bf16[384,512]{1,0:T(8,128)(2,1)}, bf16[384,512]{1,0:T(8,128)(2,1)}, u32[]{:S(2)}, u32[]{:S(2)}) collective-permute-start(bf16[384,512]{1,0:T(8,128)(2,1)} %get-tuple-element.24), channel_id=1, source_target_pairs={{0,8},{8,0},{16,24},{24,16},{1,9},{9,1},{17,25},{25,17},{2,10},{10... | collective-permute-start | bytes 1179656 | tf_op jit(solution)/shard_map/ppermute | solution.py:340
  41.3 22.2 %collective-permute-start.17 = (bf16[384,256]{1,0:T(8,128)(2,1)}, bf16[384,256]{1,0:T(8,128)(2,1)}, u32[]{:S(2)}, u32[]{:S(2)}) collective-permute-start(bf16[384,256]{1,0:T(8,128)(2,1)} %get-tuple-element.28), channel_id=1, source_target_pairs={{0,8},{8,0},{16,24},{24,16},{1,9},{9,1},{17,25},{25,17},{2,10},{10... | collective-permute-start | bytes 589832 | tf_op jit(solution)/shard_map/ppermute | solution.py:340
  42.8 28.4 %collective-permute-start.15 = (bf16[192,512]{1,0:T(8,128)(2,1)}, bf16[192,512]{1,0:T(8,128)(2,1)}, u32[]{:S(2)}, u32[]{:S(2)}) collective-permute-start(bf16[192,512]{1,0:T(8,128)(2,1)} %get-tuple-element.26), channel_id=1, source_target_pairs={{0,8},{8,0},{16,24},{24,16},{1,9},{9,1},{17,25},{25,17},{2,10},{10... | collective-permute-start | bytes 589832 | tf_op jit(solution)/shard_map/ppermute | solution.py:340
  45.1 16.1 %collective-permute-start.19 = (bf16[192,256]{1,0:T(8,128)(2,1)S(1)}, bf16[192,256]{1,0:T(8,128)(2,1)S(1)}, u32[]{:S(2)}, u32[]{:S(2)}) collective-permute-start(bf16[192,256]{1,0:T(8,128)(2,1)S(1)} %get-tuple-element.30), channel_id=1, source_target_pairs={{0,8},{8,0},{16,24},{24,16},{1,9},{9,1},{17,25},{25,17},{2,10},{10... | collective-permute-start | bytes 294920 | tf_op jit(solution)/shard_map/ppermute | solution.py:340
  46.4 14.7 %copy-start.21 = (f32[384,256]{1,0:T(8,128)}, f32[384,256]{1,0:T(8,128)S(1)}, u32[]{:S(2)}) copy-start(f32[384,256]{1,0:T(8,128)S(1)} %get-tuple-element.18.own_gu) | copy-start | bytes 1179652
  46.4 29.3 %collective-permute-start.2 = (bf16[384,256]{1,0:T(8,128)(2,1)}, bf16[384,256]{1,0:T(8,128)(2,1)}, u32[]{:S(2)}, u32[]{:S(2)}) collective-permute-start(bf16[384,256]{1,0:T(8,128)(2,1)} %get-tuple-element.19), channel_id=1, source_target_pairs={{0,8},{8,0},{16,24},{24,16},{1,9},{9,1},{17,25},{25,17},{2,10},{10... | collective-permute-start | bytes 589832 | tf_op jit(solution)/shard_map/ppermute | solution.py:340
  61.8 13.9 %collective-permute-start.5 = (bf16[192,256]{1,0:T(8,128)(2,1)}, bf16[192,256]{1,0:T(8,128)(2,1)S(1)}, u32[]{:S(2)}, u32[]{:S(2)}) collective-permute-start(bf16[192,256]{1,0:T(8,128)(2,1)} %get-tuple-element.22), channel_id=1, source_target_pairs={{0,8},{8,0},{16,24},{24,16},{1,9},{9,1},{17,25},{25,17},{2,10},{10... | collective-permute-start | bytes 294920 | tf_op jit(solution)/shard_map/ppermute | solution.py:340
  (27 other events, 63.2 us)

commit v2 on v0

--- a/solution.py
+++ b/solution.py
@@ -1,6 +1,10 @@
+import functools
+
 import jax
 import jax.numpy as jnp
 from jax import lax
+from jax.experimental import pallas as pl
+from jax.experimental.pallas import tpu as pltpu
 from jax.sharding import PartitionSpec as P
 
 beta_one = 0.9
@@ -57,7 +61,7 @@
     return (table, gate_slot)
 
 
-def per_device(tokens, cotangent, expert_ids, gate_probs, weights, first_moment, second_moment):
+def routed_plan(tokens, cotangent, expert_ids, gate_probs, weights, first_moment, second_moment):
     n_expert = lax.axis_size("expert")
     n_data = lax.axis_size("dp")
     slices = min(4, n_expert // 2)
@@ -122,6 +126,274 @@
     )
 
 
+VMEM_LIMIT = 16 * 1024 * 1024
+
+
+def params():
+    return pltpu.CompilerParams(vmem_limit_bytes=VMEM_LIMIT)
+
+
+def cost(flops, moved):
+    return pl.CostEstimate(flops=flops, bytes_accessed=moved, transcendentals=0)
+
+
+def whole():
+    return pl.BlockSpec(memory_space=pltpu.VMEM)
+
+
+def in_hbm():
+    return pl.BlockSpec(memory_space=pltpu.HBM)
+
+
+def smem():
+    return pl.BlockSpec(memory_space=pltpu.SMEM)
+
+
+def pack_kernel(
+    replica_ref, ids_hbm, gates_hbm, tokens_ref, cot_ref, out_ref, ids_ref, gates_ref, sems
+):
+    count = tokens_ref.shape[0]
+    width = out_ref.shape[1]
+    columns = pl.ds(pl.multiple_of(replica_ref[0] * width, width), width)
+    copies = [
+        pltpu.make_async_copy(ids_hbm, ids_ref, sems.at[0]),
+        pltpu.make_async_copy(gates_hbm, gates_ref, sems.at[1]),
+        pltpu.make_async_copy(tokens_ref.at[:, columns], out_ref.at[0:count, :], sems.at[2]),
+        pltpu.make_async_copy(cot_ref.at[:, columns], out_ref.at[count : 2 * count, :], sems.at[3]),
+    ]
+    for copy in copies:
+        copy.start()
+    copies[0].wait()
+    copies[1].wait()
+    ids = ids_ref[...]
+    gates = gates_ref[...].astype(jnp.float32)
+    slots = out_ref.shape[0] - 2 * count
+    row = lax.broadcasted_iota(jnp.int32, (slots, count), 0)
+    gate = jnp.zeros((slots, count), jnp.float32)
+    for k in range(ids.shape[0]):
+        gate = gate + jnp.where(row == ids[k : k + 1, :], gates[k : k + 1, :], 0.0)
+    out_ref[2 * count :, 0:count] = gate.astype(jnp.bfloat16)
+    out_ref[2 * count :, count:] = jnp.zeros((slots, width - count), jnp.bfloat16)
+    copies[2].wait()
+    copies[3].wait()
+
+
+def pack_own(replica, ids, gates, tokens, cotangent, width, slots):
+    count, top = ids.shape
+    return pl.pallas_call(
+        pack_kernel,
+        in_specs=[smem()] + [in_hbm()] * 4,
+        out_specs=whole(),
+        out_shape=jax.ShapeDtypeStruct((2 * count + slots, width), jnp.bfloat16),
+        scratch_shapes=[
+            pltpu.VMEM((top, count), ids.dtype),
+            pltpu.VMEM((top, count), gates.dtype),
+            pltpu.SemaphoreType.DMA((4,)),
+        ],
+        compiler_params=params(),
+        cost_estimate=cost(1000, 8 * count * width),
+    )(replica.reshape(1), ids.T, gates.T, tokens, cotangent)
+
+
+def joined(refs, first, count):
+    parts = [ref[first : first + count, :] for ref in refs]
+    return parts[0] if len(parts) == 1 else jnp.concatenate(parts, 0)
+
+
+def partial_kernel(n, count, w_ref, after_ref, *refs):
+    blocks, (own_ref, send_ref, token_ref) = refs[:n], refs[n:]
+    mats, hidden, width = w_ref.shape
+    gu = contract_last(w_ref[0:2].reshape(2 * hidden, width), joined(blocks, 0, count))
+    own_ref[0 : 2 * hidden] = gu
+    send_ref[0 : 2 * hidden] = gu.astype(jnp.bfloat16)
+    down = contract_last(w_ref[2], joined(blocks, count, count))
+    own_ref[2 * hidden :] = down
+    send_ref[2 * hidden :] = down.astype(jnp.bfloat16)
+    token_ref[...] = jnp.zeros_like(token_ref)
+
+
+def partials(weights, after, blocks, count):
+    mats, hidden, width = weights.shape
+    shape = (mats * hidden, count * len(blocks))
+    return pl.pallas_call(
+        functools.partial(partial_kernel, len(blocks), count),
+        in_specs=[whole()] * (2 + len(blocks)),
+        out_specs=[whole()] * 3,
+        out_shape=[
+            jax.ShapeDtypeStruct(shape, jnp.float32),
+            jax.ShapeDtypeStruct(shape, jnp.bfloat16),
+            jax.ShapeDtypeStruct((8, 128), jnp.float32),
+        ],
+        compiler_params=params(),
+        cost_estimate=cost(2 * shape[0] * shape[1] * width, 6 * shape[0] * shape[1]),
+    )(weights, after, *blocks)
+
+
+def gate_row(expert_ref, blocks, count):
+    rows = []
+    for ref in blocks:
+        held = ref[2 * count :, 0:count].astype(jnp.float32)
+        index = lax.broadcasted_iota(jnp.int32, held.shape, 0)
+        rows.append(jnp.sum(jnp.where(index == expert_ref[0], held, 0.0), 0, keepdims=True))
+    return rows[0] if len(rows) == 1 else jnp.concatenate(rows, 1)
+
+
+def hidden_grads(gate, own, got):
+    total = own[...] + got[...].astype(jnp.float32)
+    hidden = total.shape[0] // 3
+    hg, hu = total[0:hidden], total[hidden : 2 * hidden]
+    dact = gate * total[2 * hidden :]
+    sig = jax.nn.sigmoid(hg)
+    silu = hg * sig
+    act = (gate * (silu * hu)).astype(jnp.bfloat16)
+    dhg = (dact * hu * sig * (1.0 + hg * (1.0 - sig))).astype(jnp.bfloat16)
+    dhu = (dact * silu).astype(jnp.bfloat16)
+    return dhg, dhu, act
+
+
+def plain(left, right):
+    return lax.dot_general(
+        left, right, (((1,), (0,)), ((), ())), preferred_element_type=jnp.float32
+    )
+
+
+def grad_kernel(n, count, has_acc, expert_ref, after_ref, own, got, *refs):
+    blocks = refs[:n]
+    out_ref, token_ref = refs[-2:]
+    dhg, dhu, act = hidden_grads(gate_row(expert_ref, blocks, count), own, got)
+    x = joined(blocks, 0, count)
+    y = joined(blocks, count, count)
+    for m, (left, right) in enumerate(((dhg, x), (dhu, x), (act, y))):
+        value = plain(left, right)
+        out_ref[m] = value + refs[n][m] if has_acc else value
+    token_ref[...] = jnp.zeros_like(token_ref)
+
+
+def add_grads(expert, after, own, got, blocks, acc, count):
+    n = len(blocks)
+    width = blocks[0].shape[1]
+    shape = (3, own.shape[0] // 3, width)
+    operands = [expert, after, own, got, *blocks] + ([] if acc is None else [acc])
+    return pl.pallas_call(
+        functools.partial(grad_kernel, n, count, acc is not None),
+        in_specs=[smem()] + [whole()] * (len(operands) - 1),
+        out_specs=[whole()] * 2,
+        out_shape=[
+            jax.ShapeDtypeStruct(shape, jnp.float32),
+            jax.ShapeDtypeStruct((8, 128), jnp.float32),
+        ],
+        input_output_aliases={} if acc is None else {len(operands) - 1: 0},
+        compiler_params=params(),
+        cost_estimate=cost(2 * own.shape[0] * width * n * count, 8 * own.shape[0] * width),
+    )(*operands)
+
+
+def last_kernel(n, count, expert_ref, own, got, *refs):
+    blocks = refs[:n]
+    acc_ref, first_ref, second_ref, one_ref, two_ref, step_ref, left_ref = refs[n:]
+    m = pl.program_id(1)
+
+    @pl.when((m == 0) & (pl.program_id(0) == 0))
+    def _():
+        dhg, dhu, act = hidden_grads(gate_row(expert_ref, blocks, count), own, got)
+        left_ref[0] = dhg
+        left_ref[1] = dhu
+        left_ref[2] = act
+
+    def finish(right):
+        grad = acc_ref[0] + plain(left_ref[m], right)
+        moment_one = beta_one * first_ref[0].astype(jnp.float32) + (1.0 - beta_one) * grad
+        moment_two = beta_two * second_ref[0].astype(jnp.float32) + (1.0 - beta_two) * grad * grad
+        one_ref[0] = moment_one.astype(jnp.bfloat16)
+        two_ref[0] = moment_two.astype(jnp.bfloat16)
+        scaled = moment_two * (1.0 / (1.0 - beta_two**step_count))
+        below = scaled * lax.rsqrt(scaled) + epsilon
+        step = moment_one * (1.0 / (1.0 - beta_one**step_count)) / below
+        step_ref[0] = step.astype(jnp.bfloat16)
+
+    @pl.when(m < 2)
+    def _():
+        finish(joined(blocks, 0, count))
+
+    @pl.when(m == 2)
+    def _():
+        finish(joined(blocks, count, count))
+
+
+def last_grads(expert, own, got, blocks, acc, first_moment, second_moment, count, columns):
+    n = len(blocks)
+    mats, hidden, width = first_moment.shape
+    tile = pl.BlockSpec((1, hidden, columns), lambda j, m: (m, 0, j))
+    out = jax.ShapeDtypeStruct(first_moment.shape, jnp.bfloat16)
+    strip = lambda value: pl.BlockSpec((value.shape[0], columns), lambda j, m: (0, j))
+    return pl.pallas_call(
+        functools.partial(last_kernel, n, count),
+        grid=(width // columns, mats),
+        in_specs=[smem(), whole(), whole()] + [strip(value) for value in blocks] + [tile] * 3,
+        out_specs=[tile] * 3,
+        out_shape=[out] * 3,
+        scratch_shapes=[pltpu.VMEM((mats, hidden, n * count), jnp.bfloat16)],
+        compiler_params=params(),
+        cost_estimate=cost(6 * hidden * width * n * count, 24 * hidden * width * mats),
+    )(expert, own, got, *blocks, acc, first_moment, second_moment)
+
+
+def from_masked(value, axis, mask):
+    pairs = [(source, source ^ mask) for source in range(lax.axis_size(axis))]
+    return lax.ppermute(value, axis, pairs)
+
+
+def dense_plan(tokens, cotangent, expert_ids, gate_probs, weights, first_moment, second_moment):
+    n_data = lax.axis_size("dp")
+    place = lax.axis_index("expert")
+    core = lax.axis_index("dp") % 2
+    slices = min(4, lax.axis_size("expert") // 2)
+    expert = (place // (2 * slices) * n_data + lax.axis_index("dp")).astype(jnp.int32).reshape(1)
+    experts_total = lax.axis_size("expert") // (2 * slices) * n_data
+    count = tokens.shape[0]
+    width = weights.shape[2]
+    slots = -(-experts_total // 16) * 16
+    own = pack_own(
+        (place % 2).astype(jnp.int32), expert_ids, gate_probs, tokens, cotangent, width, slots
+    )
+    over_x = from_masked(own, "dp", 2)
+    over_y = from_masked(own, "dp", 4)
+    onward = [(p, p ^ 4 if p % 2 == 0 else p ^ 2) for p in range(n_data)]
+    far = lax.ppermute(jnp.where(core == 0, over_x, over_y), "dp", onward)
+    chunks = [
+        [block for mine in group for block in (mine, from_masked(mine, "dp", 1))]
+        for group in ([own], [over_x, over_y], [far])
+    ]
+    token = jnp.zeros((8, 128), jnp.float32)
+    parts = []
+    acc = None
+    for number, blocks in enumerate(chunks):
+        mine, send, token = partials(weights, token, blocks, count)
+        parts.append((mine, from_masked(send, "expert", 1)))
+        if number > 0:
+            acc, token = add_grads(
+                expert, token, *parts[number - 1], chunks[number - 1], acc, count
+            )
+    return tuple(
+        last_grads(
+            expert, *parts[-1], chunks[-1], acc, first_moment, second_moment, count, width // 2
+        )
+    )
+
+
+def per_device(tokens, cotangent, expert_ids, gate_probs, weights, first_moment, second_moment):
+    n_expert = lax.axis_size("expert")
+    n_data = lax.axis_size("dp")
+    slices = min(4, n_expert // 2)
+    experts_total = n_expert // (2 * slices) * n_data
+    half = tokens.shape[0] // 2
+    dense = 2 * half * expert_ids.shape[1] // experts_total >= half
+    plan = dense_plan if dense and n_data == 8 else routed_plan
+    return plan(
+        tokens, cotangent, expert_ids, gate_probs, weights, first_moment, second_moment
+    )
+
+
 def solution(mesh):
     in_specs = (
         P("dp", None),

time: 150 us -> 68.1 us (0.45)
  waiting for transfers between devices: 91.7 us -> 34 us
  other arithmetic: 16.5 us -> 0.06 us
  Pallas kernels: 0 us -> 15.1 us
  local copies, waits for them, and re-layouts: 16.5 us -> 7.41 us
  starting transfers between devices: 17.1 us -> 10.3 us
  matrix products: 5.92 us -> 0 us
    all_to_all x3 -> x0, waiting for transfers between devices: 43.1 us -> none  [the longest x1 21.7 us: per_device(): lax.all_to_all(send_rows, 'dp', split_axis=0, concat_axis=0, tiled=True)]
    pallas_call x0 -> x7, Pallas kernels: none -> 15.1 us  [the longest x1 5.86 us: last_grads(): pl.pallas_call(functools.partial(last_kernel, n, count), grid=(width // c...]
    ppermute x2 -> x10, waiting for transfers between devices: 48.7 us -> 34 us  [the longest x9 26.4 us: from_masked(): return lax.ppermute(value, axis, pairs)]
    all_to_all x3 -> x0, starting transfers between devices: 13.9 us -> none  [the longest x1 5.17 us: per_device(): lax.all_to_all(send_gates, 'dp', split_axis=0, concat_axis=0, tiled=True)]
    convert_element_type x6 -> x0, other arithmetic: 11.7 us -> none  [the longest x1 5.24 us: per_device(): step.astype(jnp.bfloat16)]
    ppermute x2 -> x10, starting transfers between devices: 3.15 us -> 10.3 us  [the longest x9 8.7 us: from_masked(): return lax.ppermute(value, axis, pairs)]
    gather x2 -> x0, local copies, waits for them, and re-layouts: 6.62 us -> none  [the longest x1 3.32 us: per_device(): send_cot = padded_cot[table].reshape(n_data, -1, columns)]
    dot_general x6 -> x0, matrix products: 5.92 us -> none  [the longest x3 4.04 us: contract_last(): lax.dot_general(left, right, (((1,), (1,)), ((), ())), preferred_element_...]
  transfers between devices with their start and end apart: 5 -> 10, of which waited for: 3 -> 6; matrix products, arithmetic and copies ran while one was open for 10% -> 0% of each run, Pallas kernels for 0% -> 13%
where the time goes in v2:
time: 68.1 us; the launch traced here: 67.6 us
  waiting for transfers between devices  34 us (50%)
  Pallas kernels  15.1 us (22%)
  starting transfers between devices  10.3 us (15%)
  local copies, waits for them, and re-layouts  7.41 us (11%)
  between operations  0.76 us (1%)
    ppermute x9, waiting for transfers between devices, from_masked(): return lax.ppermute(value, axis, pairs)  26.4 us
    ppermute x9, starting transfers between devices, from_masked(): return lax.ppermute(value, axis, pairs)  8.7 us
    ppermute x1, waiting for transfers between devices, dense_plan(): far = lax.ppermute(jnp.where(core == 0, over_x, over_y), 'dp', onward)  7.6 us
    unnamed x30, local copies, waits for them, and re-layouts  7.41 us
    pallas_call x1, Pallas kernels, last_grads(): pl.pallas_call(functools.partial(last_kernel, n, count), grid=(width // c...  5.86 us
    pallas_call x3, Pallas kernels, partials(): pl.pallas_call(functools.partial(partial_kernel, len(blocks), count), in_...  4.9 us
    pallas_call x2, Pallas kernels, add_grads(): pl.pallas_call(functools.partial(grad_kernel, n, count, acc is not None),...  4.22 us
    ppermute x1, starting transfers between devices, dense_plan(): far = lax.ppermute(jnp.where(core == 0, over_x, over_y), 'dp', onward)  1.58 us
  transfers between devices with their start and end apart: 10, of which 6 were waited for; matrix products, arithmetic and copies ran while one was open for 0% of the time, Pallas kernels for 13%

profile of v2, /device:TPU:0, one launch (start us, length us, event | category | flops | bytes accessed | tf_op | source)
XLA Modules:
  0.0 67.6 jit_solution(4033904274921776947)
XLA Ops:
  0.7 1.0 %copy-done.11 = bf16[128,2048]{1,0:T(8,128)(2,1)S(1)} copy-done((bf16[128,2048]{1,0:T(8,128)(2,1)S(1)}, bf16[128,2048]{1,0:T(8,128)(2,1)}, u32[]{:S(2)}) %copy-start.11) | copy-done | bytes 524312
  1.7 1.0 %copy-done.12 = bf16[128,2048]{1,0:T(8,128)(2,1)S(1)} copy-done((bf16[128,2048]{1,0:T(8,128)(2,1)S(1)}, bf16[128,2048]{1,0:T(8,128)(2,1)}, u32[]{:S(2)}) %copy-start.12) | copy-done | bytes 524312
  2.7 0.7 %copy-done.13 = s32[128,4]{0,1:T(4,128)S(1)} copy-done((s32[128,4]{0,1:T(4,128)S(1)}, s32[128,4]{0,1:T(4,128)}, u32[]{:S(2)}) %copy-start.13) | copy-done | bytes 2072
  4.2 3.0 %collective-permute-start.1 = (bf16[272,1024]{1,0:T(8,128)(2,1)S(1)}, bf16[272,1024]{1,0:T(8,128)(2,1)S(1)}, u32[]{:S(2)}, u32[]{:S(2)}) collective-permute-start(bf16[272,1024]{1,0:T(8,128)(2,1)S(1)} %shard_map.94.refs_0_), channel_id=1, source_target_pairs={{0,2},{1,3},{2,0},{3,1},{4,6},{5,7},{6,4},{7,5},{8,10},{9,11},{10,... | collective-permute-start | bytes 1671176 | tf_op jit(solution)/shard_map/ppermute | solution.py:343
  7.2 1.5 %collective-permute-start.3 = (bf16[272,1024]{1,0:T(8,128)(2,1)S(1)}, bf16[272,1024]{1,0:T(8,128)(2,1)S(1)}, u32[]{:S(2)}, u32[]{:S(2)}) collective-permute-start(bf16[272,1024]{1,0:T(8,128)(2,1)S(1)} %shard_map.94.refs_0_), channel_id=1, source_target_pairs={{0,4},{1,5},{2,6},{3,7},{4,0},{5,1},{6,2},{7,3},{8,12},{9,13},{10,... | collective-permute-start | bytes 1671176 | tf_op jit(solution)/shard_map/ppermute | solution.py:343
  8.7 11.1 %collective-permute-done.1.refs_0_ = bf16[272,1024]{1,0:T(8,128)(2,1)S(1)} collective-permute-done((bf16[272,1024]{1,0:T(8,128)(2,1)S(1)}, bf16[272,1024]{1,0:T(8,128)(2,1)S(1)}, u32[]{:S(2)}, u32[]{:S(2)}) %collective-permute-start.1) | collective-permute-done | bytes 557088 | tf_op jit(solution)/shard_map/ppermute | solution.py:343
  19.8 1.5 %collective-permute-done.3.refs_2_ = bf16[272,1024]{1,0:T(8,128)(2,1)S(1)} collective-permute-done((bf16[272,1024]{1,0:T(8,128)(2,1)S(1)}, bf16[272,1024]{1,0:T(8,128)(2,1)S(1)}, u32[]{:S(2)}, u32[]{:S(2)}) %collective-permute-start.3) | collective-permute-done | bytes 557088 | tf_op jit(solution)/shard_map/ppermute | solution.py:343
  21.4 1.6 %collective-permute-start.6 = (bf16[272,1024]{1,0:T(8,128)(2,1)S(1)}, bf16[272,1024]{1,0:T(8,128)(2,1)}, u32[]{:S(2)}, u32[]{:S(2)}) collective-permute-start(bf16[272,1024]{1,0:T(8,128)(2,1)S(1)} %broadcast_select_fusion), channel_id=1, source_target_pairs={{0,4},{1,3},{2,6},{3,1},{4,0},{5,7},{6,2},{7,5},{8,12},{9,11},{10,... | collective-permute-start | bytes 1671176 | tf_op jit(solution)/shard_map/ppermute | solution.py:362
  23.5 7.6 %collective-permute-done.6.refs_0_ = bf16[272,1024]{1,0:T(8,128)(2,1)} collective-permute-done((bf16[272,1024]{1,0:T(8,128)(2,1)S(1)}, bf16[272,1024]{1,0:T(8,128)(2,1)}, u32[]{:S(2)}, u32[]{:S(2)}) %collective-permute-start.6) | collective-permute-done | bytes 557088 | tf_op jit(solution)/shard_map/ppermute | solution.py:362
  31.1 1.3 %shard_map.95 = (f32[576,256]{1,0:T(8,128)S(1)}, bf16[576,256]{1,0:T(8,128)(2,1)}, f32[8,128]{1,0:T(8,128)S(1)}) custom-call(bf16[3,192,1024]{2,1,0:T(8,128)(2,1)S(1)} %copy-done, f32[8,128]{1,0:T(8,128)S(1)} %broadcast_in_dim.3.after_ref, bf16[272,1024]{1,0:T(8,128)(2,1)S(1)} %shard_map.94.refs_0_, bf16[272,1024]{1,0:T(8,128)(2,1)S(1)} %collective-permute-done.refs_1_), custom_call_target="tpu_custom_call" | custom-call | flops 301989888 | bytes 884736 | tf_op jit(solution)/shard_map/pallas_call | solution.py:218
  32.4 0.8 %copy-done.9 = f32[576,256]{1,0:T(8,128)} copy-done((f32[576,256]{1,0:T(8,128)}, f32[576,256]{1,0:T(8,128)S(1)}, u32[]{:S(2)}) %copy-start.9) | copy-done | bytes 589848
  33.2 1.6 %collective-permute-start.5 = (bf16[576,256]{1,0:T(8,128)(2,1)}, bf16[576,256]{1,0:T(8,128)(2,1)}, u32[]{:S(2)}, u32[]{:S(2)}) collective-permute-start(bf16[576,256]{1,0:T(8,128)(2,1)} %get-tuple-element.18), channel_id=1, source_target_pairs={{0,8},{8,0},{16,24},{24,16},{1,9},{9,1},{17,25},{25,17},{2,10},{10... | collective-permute-start | bytes 884744 | tf_op jit(solution)/shard_map/ppermute | solution.py:343
  34.8 1.7 %shard_map.96 = (f32[576,512]{1,0:T(8,128)S(1)}, bf16[576,512]{1,0:T(8,128)(2,1)}, f32[8,128]{1,0:T(8,128)S(1)}) custom-call(bf16[3,192,1024]{2,1,0:T(8,128)(2,1)S(1)} %copy-done, f32[8,128]{1,0:T(8,128)S(1)} %get-tuple-element.15.after_ref, bf16[272,1024]{1,0:T(8,128)(2,1)S(1)} %collective-permute-done.1.refs_0_, ...), custom_call_target="tpu_custom_call" | custom-call | flops 603979776 | bytes 1769472 | tf_op jit(solution)/shard_map/pallas_call | solution.py:218
  36.5 1.0 %copy-done.7 = f32[576,512]{1,0:T(8,128)} copy-done((f32[576,512]{1,0:T(8,128)}, f32[576,512]{1,0:T(8,128)S(1)}, u32[]{:S(2)}) %copy-start.7) | copy-done | bytes 1179672
  38.0 5.3 %collective-permute-done.5.got = bf16[576,256]{1,0:T(8,128)(2,1)} collective-permute-done((bf16[576,256]{1,0:T(8,128)(2,1)}, bf16[576,256]{1,0:T(8,128)(2,1)}, u32[]{:S(2)}, u32[]{:S(2)}) %collective-permute-start.5) | collective-permute-done | bytes 294944 | tf_op jit(solution)/shard_map/ppermute | solution.py:343
  43.3 1.1 %copy-done.4 = bf16[272,1024]{1,0:T(8,128)(2,1)S(1)} copy-done((bf16[272,1024]{1,0:T(8,128)(2,1)S(1)}, bf16[272,1024]{1,0:T(8,128)(2,1)}, u32[]{:S(2)}) %copy-start.4) | copy-done | bytes 557080
  44.4 1.1 %copy-done.10 = f32[576,256]{1,0:T(8,128)S(1)} copy-done((f32[576,256]{1,0:T(8,128)S(1)}, f32[576,256]{1,0:T(8,128)}, u32[]{:S(2)}) %copy-start.10) | copy-done | bytes 589848
  45.4 1.5 %shard_map.97 = (f32[3,192,1024]{2,1,0:T(8,128)S(1)}, f32[8,128]{1,0:T(8,128)S(1)}) custom-call(s32[1]{0:T(128)} %bitcast.expert_ref, f32[8,128]{1,0:T(8,128)S(1)} %get-tuple-element.16.after_ref, f32[576,256]{1,0:T(8,128)S(1)} %copy-done.10, bf16[576,256]{1,0:T(8,128)(2,1)} %collective-permute-done.5.got, bf16[272,1024]{1,0:T(8,128)(2,1)S(1)} %shard_map.94.refs_0_, ...), custom_call_target="tpu_custom_call" | custom-call | flops 301989888 | bytes 4718592 | tf_op jit(solution)/shard_map/pallas_call | solution.py:277
  46.9 1.9 %shard_map.98 = (f32[576,256]{1,0:T(8,128)S(1)}, bf16[576,256]{1,0:T(8,128)(2,1)S(1)}, f32[8,128]{1,0:T(8,128)S(1)}) custom-call(bf16[3,192,1024]{2,1,0:T(8,128)(2,1)S(1)} %copy-done, f32[8,128]{1,0:T(8,128)S(1)} %get-tuple-element.19.after_ref, bf16[272,1024]{1,0:T(8,128)(2,1)} %collective-permute-done.6.refs_0_, ...), custom_call_target="tpu_custom_call" | custom-call | flops 301989888 | bytes 884736 | tf_op jit(solution)/shard_map/pallas_call | solution.py:218
  48.8 1.6 %collective-permute-start.8 = (bf16[576,256]{1,0:T(8,128)(2,1)S(1)}, bf16[576,256]{1,0:T(8,128)(2,1)S(1)}, u32[]{:S(2)}, u32[]{:S(2)}) collective-permute-start(bf16[576,256]{1,0:T(8,128)(2,1)S(1)} %get-tuple-element.21), channel_id=1, source_target_pairs={{0,8},{8,0},{16,24},{24,16},{1,9},{9,1},{17,25},{25,17},{2,10},{10... | collective-permute-start | bytes 884744 | tf_op jit(solution)/shard_map/ppermute | solution.py:343
  50.5 5.5 %collective-permute-done.9.got = bf16[576,512]{1,0:T(8,128)(2,1)} collective-permute-done((bf16[576,512]{1,0:T(8,128)(2,1)}, bf16[576,512]{1,0:T(8,128)(2,1)}, u32[]{:S(2)}, u32[]{:S(2)}) %collective-permute-start.9) | collective-permute-done | bytes 589856 | tf_op jit(solution)/shard_map/ppermute | solution.py:343
  56.0 2.7 %shard_map.99 = (f32[3,192,1024]{2,1,0:T(8,128)S(1)}, f32[8,128]{1,0:T(8,128)}) custom-call(s32[1]{0:T(128)} %bitcast.expert_ref, f32[8,128]{1,0:T(8,128)S(1)} %get-tuple-element.22.after_ref, f32[576,512]{1,0:T(8,128)S(1)} %copy-done.8, bf16[576,512]{1,0:T(8,128)(2,1)} %collective-permute-done.9.got, ...), custom_call_target="tpu_custom_call", output_to_operand_aliasing={{0}: (8, {})} | custom-call | flops 603979776 | bytes 4718592 | tf_op jit(solution)/shard_map/pallas_call | solution.py:277
  58.7 3.1 %collective-permute-done.8.got = bf16[576,256]{1,0:T(8,128)(2,1)S(1)} collective-permute-done((bf16[576,256]{1,0:T(8,128)(2,1)S(1)}, bf16[576,256]{1,0:T(8,128)(2,1)S(1)}, u32[]{:S(2)}, u32[]{:S(2)}) %collective-permute-start.8) | collective-permute-done | bytes 294944 | tf_op jit(solution)/shard_map/ppermute | solution.py:343
  61.8 5.9 %shard_map.100 = (bf16[3,192,1024]{2,1,0:T(8,128)(2,1)}, bf16[3,192,1024]{2,1,0:T(8,128)(2,1)}, bf16[3,192,1024]{2,1,0:T(8,128)(2,1)}) custom-call(s32[1]{0:T(128)} %bitcast.expert_ref, f32[576,256]{1,0:T(8,128)S(1)} %get-tuple-element.20.own, bf16[576,256]{1,0:T(8,128)(2,1)S(1)} %collective-permute-done.8.got, ...), custom_call_target="tpu_custom_call" | custom-call | flops 301989888 | bytes 14155776 | tf_op jit(solution)/shard_map/pallas_call | solution.py:329
  (35 shorter events, 1.8 us)
Async XLA Ops:
  0.6 1.0 %copy-start.11 = (bf16[128,2048]{1,0:T(8,128)(2,1)S(1)}, bf16[128,2048]{1,0:T(8,128)(2,1)}, u32[]{:S(2)}) copy-start(bf16[128,2048]{1,0:T(8,128)(2,1)} %tokens_ref.1) | copy-start | bytes 1572868
  1.7 1.0 %copy-start.12 = (bf16[128,2048]{1,0:T(8,128)(2,1)S(1)}, bf16[128,2048]{1,0:T(8,128)(2,1)}, u32[]{:S(2)}) copy-start(bf16[128,2048]{1,0:T(8,128)(2,1)} %cot_ref.1) | copy-start | bytes 1572868
  2.7 0.7 %copy-start.13 = (s32[128,4]{0,1:T(4,128)S(1)}, s32[128,4]{0,1:T(4,128)}, u32[]{:S(2)}) copy-start(s32[128,4]{0,1:T(4,128)} %param.9) | copy-start | bytes 6148
  4.2 26.9 %copy-start = (bf16[3,192,1024]{2,1,0:T(8,128)(2,1)S(1)}, bf16[3,192,1024]{2,1,0:T(8,128)(2,1)}, u32[]{:S(2)}) copy-start(bf16[3,192,1024]{2,1,0:T(8,128)(2,1)} %w_ref.5) | copy-start | bytes 3538948
  4.2 15.6 %collective-permute-start.1 = (bf16[272,1024]{1,0:T(8,128)(2,1)S(1)}, bf16[272,1024]{1,0:T(8,128)(2,1)S(1)}, u32[]{:S(2)}, u32[]{:S(2)}) collective-permute-start(bf16[272,1024]{1,0:T(8,128)(2,1)S(1)} %shard_map.94.refs_0_), channel_id=1, source_target_pairs={{0,2},{1,3},{2,0},{3,1},{4,6},{5,7},{6,4},{7,5},{8,10},{9,11},{10,... | collective-permute-start | bytes 1671176 | tf_op jit(solution)/shard_map/ppermute | solution.py:343
  7.2 14.1 %collective-permute-start.3 = (bf16[272,1024]{1,0:T(8,128)(2,1)S(1)}, bf16[272,1024]{1,0:T(8,128)(2,1)S(1)}, u32[]{:S(2)}, u32[]{:S(2)}) collective-permute-start(bf16[272,1024]{1,0:T(8,128)(2,1)S(1)} %shard_map.94.refs_0_), channel_id=1, source_target_pairs={{0,4},{1,5},{2,6},{3,7},{4,0},{5,1},{6,2},{7,3},{8,12},{9,13},{10,... | collective-permute-start | bytes 1671176 | tf_op jit(solution)/shard_map/ppermute | solution.py:343
  21.4 9.7 %collective-permute-start.6 = (bf16[272,1024]{1,0:T(8,128)(2,1)S(1)}, bf16[272,1024]{1,0:T(8,128)(2,1)}, u32[]{:S(2)}, u32[]{:S(2)}) collective-permute-start(bf16[272,1024]{1,0:T(8,128)(2,1)S(1)} %broadcast_select_fusion), channel_id=1, source_target_pairs={{0,4},{1,3},{2,6},{3,1},{4,0},{5,7},{6,2},{7,5},{8,12},{9,11},{10,... | collective-permute-start | bytes 1671176 | tf_op jit(solution)/shard_map/ppermute | solution.py:362
  22.9 8.1 %collective-permute-start = (bf16[272,1024]{1,0:T(8,128)(2,1)S(1)}, bf16[272,1024]{1,0:T(8,128)(2,1)S(1)}, u32[]{:S(2)}, u32[]{:S(2)}) collective-permute-start(bf16[272,1024]{1,0:T(8,128)(2,1)S(1)} %shard_map.94.refs_0_), channel_id=1, source_target_pairs={{0,1},{1,0},{2,3},{3,2},{4,5},{5,4},{6,7},{7,6},{8,9},{9,8},{10,11... | collective-permute-start | bytes 1671176 | tf_op jit(solution)/shard_map/ppermute | solution.py:343
  22.9 11.8 %collective-permute-start.2 = (bf16[272,1024]{1,0:T(8,128)(2,1)S(1)}, bf16[272,1024]{1,0:T(8,128)(2,1)S(1)}, u32[]{:S(2)}, u32[]{:S(2)}) collective-permute-start(bf16[272,1024]{1,0:T(8,128)(2,1)S(1)} %collective-permute-done.1.refs_0_), channel_id=1, source_target_pairs={{0,1},{1,0},{2,3},{3,2},{4,5},{5,4},{6,7},{7,6},{8,9},{9,8},{10,11... | collective-permute-start | bytes 1671176 | tf_op jit(solution)/shard_map/ppermute | solution.py:343
  23.4 11.3 %collective-permute-start.4 = (bf16[272,1024]{1,0:T(8,128)(2,1)S(1)}, bf16[272,1024]{1,0:T(8,128)(2,1)S(1)}, u32[]{:S(2)}, u32[]{:S(2)}) collective-permute-start(bf16[272,1024]{1,0:T(8,128)(2,1)S(1)} %collective-permute-done.3.refs_2_), channel_id=1, source_target_pairs={{0,1},{1,0},{2,3},{3,2},{4,5},{5,4},{6,7},{7,6},{8,9},{9,8},{10,11... | collective-permute-start | bytes 1671176 | tf_op jit(solution)/shard_map/ppermute | solution.py:343
  31.1 15.9 %collective-permute-start.7 = (bf16[272,1024]{1,0:T(8,128)(2,1)}, bf16[272,1024]{1,0:T(8,128)(2,1)}, u32[]{:S(2)}, u32[]{:S(2)}) collective-permute-start(bf16[272,1024]{1,0:T(8,128)(2,1)} %collective-permute-done.6.refs_0_), channel_id=1, source_target_pairs={{0,1},{1,0},{2,3},{3,2},{4,5},{5,4},{6,7},{7,6},{8,9},{9,8},{10,11... | collective-permute-start | bytes 1671176 | tf_op jit(solution)/shard_map/ppermute | solution.py:343
  31.1 5.4 %copy-start.3 = (bf16[272,1024]{1,0:T(8,128)(2,1)}, bf16[272,1024]{1,0:T(8,128)(2,1)S(1)}, u32[]{:S(2)}) copy-start(bf16[272,1024]{1,0:T(8,128)(2,1)S(1)} %collective-permute-done.refs_1_) | copy-start | bytes 1671172
  32.4 0.8 %copy-start.9 = (f32[576,256]{1,0:T(8,128)}, f32[576,256]{1,0:T(8,128)S(1)}, u32[]{:S(2)}) copy-start(f32[576,256]{1,0:T(8,128)S(1)} %get-tuple-element.17.own) | copy-start | bytes 1769476
  33.2 10.1 %collective-permute-start.5 = (bf16[576,256]{1,0:T(8,128)(2,1)}, bf16[576,256]{1,0:T(8,128)(2,1)}, u32[]{:S(2)}, u32[]{:S(2)}) collective-permute-start(bf16[576,256]{1,0:T(8,128)(2,1)} %get-tuple-element.18), channel_id=1, source_target_pairs={{0,8},{8,0},{16,24},{24,16},{1,9},{9,1},{17,25},{25,17},{2,10},{10... | collective-permute-start | bytes 884744 | tf_op jit(solution)/shard_map/ppermute | solution.py:343
  34.8 1.7 %copy-start.1 = (bf16[272,1024]{1,0:T(8,128)(2,1)}, bf16[272,1024]{1,0:T(8,128)(2,1)S(1)}, u32[]{:S(2)}) copy-start(bf16[272,1024]{1,0:T(8,128)(2,1)S(1)} %collective-permute-done.4.refs_3_) | copy-start | bytes 1671172
  36.5 1.0 %copy-start.7 = (f32[576,512]{1,0:T(8,128)}, f32[576,512]{1,0:T(8,128)S(1)}, u32[]{:S(2)}) copy-start(f32[576,512]{1,0:T(8,128)S(1)} %get-tuple-element.23.own) | copy-start | bytes 3538948
  37.5 18.4 %collective-permute-start.9 = (bf16[576,512]{1,0:T(8,128)(2,1)}, bf16[576,512]{1,0:T(8,128)(2,1)}, u32[]{:S(2)}, u32[]{:S(2)}) collective-permute-start(bf16[576,512]{1,0:T(8,128)(2,1)} %get-tuple-element.24), channel_id=1, source_target_pairs={{0,8},{8,0},{16,24},{24,16},{1,9},{9,1},{17,25},{25,17},{2,10},{10... | collective-permute-start | bytes 1769480 | tf_op jit(solution)/shard_map/ppermute | solution.py:343
  43.3 1.1 %copy-start.4 = (bf16[272,1024]{1,0:T(8,128)(2,1)S(1)}, bf16[272,1024]{1,0:T(8,128)(2,1)}, u32[]{:S(2)}) copy-start(bf16[272,1024]{1,0:T(8,128)(2,1)} %copy-done.3) | copy-start | bytes 1671172
  44.4 1.1 %copy-start.10 = (f32[576,256]{1,0:T(8,128)S(1)}, f32[576,256]{1,0:T(8,128)}, u32[]{:S(2)}) copy-start(f32[576,256]{1,0:T(8,128)} %copy-done.9) | copy-start | bytes 1769476
  46.9 9.0 %copy-start.2 = (bf16[272,1024]{1,0:T(8,128)(2,1)S(1)}, bf16[272,1024]{1,0:T(8,128)(2,1)}, u32[]{:S(2)}) copy-start(bf16[272,1024]{1,0:T(8,128)(2,1)} %copy-done.1) | copy-start | bytes 1671172
  46.9 9.0 %copy-start.8 = (f32[576,512]{1,0:T(8,128)S(1)}, f32[576,512]{1,0:T(8,128)}, u32[]{:S(2)}) copy-start(f32[576,512]{1,0:T(8,128)} %copy-done.7) | copy-start | bytes 3538948
  48.8 12.9 %collective-permute-start.8 = (bf16[576,256]{1,0:T(8,128)(2,1)S(1)}, bf16[576,256]{1,0:T(8,128)(2,1)S(1)}, u32[]{:S(2)}, u32[]{:S(2)}) collective-permute-start(bf16[576,256]{1,0:T(8,128)(2,1)S(1)} %get-tuple-element.21), channel_id=1, source_target_pairs={{0,8},{8,0},{16,24},{24,16},{1,9},{9,1},{17,25},{25,17},{2,10},{10... | collective-permute-start | bytes 884744 | tf_op jit(solution)/shard_map/ppermute | solution.py:343
  55.9 5.8 %copy-start.5 = (bf16[3,192,1024]{2,1,0:T(8,128)(2,1)S(1)}, bf16[3,192,1024]{2,1,0:T(8,128)(2,1)}, u32[]{:S(2)}) copy-start(bf16[3,192,1024]{2,1,0:T(8,128)(2,1)} %refs_3_.1) | copy-start | bytes 3538948
  55.9 5.8 %copy-start.6 = (bf16[3,192,1024]{2,1,0:T(8,128)(2,1)S(1)}, bf16[3,192,1024]{2,1,0:T(8,128)(2,1)}, u32[]{:S(2)}) copy-start(bf16[3,192,1024]{2,1,0:T(8,128)(2,1)} %refs_4_.1) | copy-start | bytes 3538948
  (1 other events, 0.7 us)

commit v3 on v2

--- a/solution.py
+++ b/solution.py
@@ -134,7 +134,7 @@
 
 
 def cost(flops, moved):
-    return pl.CostEstimate(flops=flops, bytes_accessed=moved, transcendentals=0)
+    return pl.CostEstimate(flops=flops // 1, bytes_accessed=moved // 1, transcendentals=0)
 
 
 def whole():
@@ -145,8 +145,16 @@
     return pl.BlockSpec(memory_space=pltpu.HBM)
 
 
+def unread():
+    return pl.BlockSpec(memory_space=pl.ANY)
+
+
 def smem():
     return pl.BlockSpec(memory_space=pltpu.SMEM)
+
+
+def keep_hbm(value):
+    return pltpu.with_memory_space_constraint(value, pltpu.HBM)
 
 
 def pack_kernel(
@@ -192,54 +200,80 @@
         ],
         compiler_params=params(),
         cost_estimate=cost(1000, 8 * count * width),
-    )(replica.reshape(1), ids.T, gates.T, tokens, cotangent)
-
-
-def joined(refs, first, count):
-    parts = [ref[first : first + count, :] for ref in refs]
+    )(replica.reshape(1), *[keep_hbm(value) for value in (ids.T, gates.T, tokens, cotangent)])
+
+
+def views(refs, kinds, count):
+    xs, ys = [], []
+    for ref, kind in zip(refs, kinds):
+        for part in [ref.at[0], ref.at[1]] if kind == "both" else [ref]:
+            if kind == "x":
+                xs.append(part)
+            elif kind == "y":
+                ys.append(part)
+            else:
+                xs.append(part.at[0:count, :])
+                ys.append(part.at[count:, :])
+    return xs, ys
+
+
+def joined(refs, count):
+    parts = [ref[0:count, :] for ref in refs]
     return parts[0] if len(parts) == 1 else jnp.concatenate(parts, 0)
 
 
-def partial_kernel(n, count, w_ref, after_ref, *refs):
-    blocks, (own_ref, send_ref, token_ref) = refs[:n], refs[n:]
+def kinds_of(chunk):
+    return tuple(kind for kind, value in chunk)
+
+
+def values_of(chunk):
+    return [value for kind, value in chunk]
+
+
+def tokens_in(kinds, count):
+    return count * sum({"xy": 1, "both": 2, "x": 1, "y": 0}[kind] for kind in kinds)
+
+
+def partial_kernel(kinds, count, w_ref, after_ref, *refs):
+    n = len(kinds)
+    xs, ys = views(refs[:n], kinds, count)
+    send_ref, token_ref = refs[n:]
     mats, hidden, width = w_ref.shape
-    gu = contract_last(w_ref[0:2].reshape(2 * hidden, width), joined(blocks, 0, count))
-    own_ref[0 : 2 * hidden] = gu
-    send_ref[0 : 2 * hidden] = gu.astype(jnp.bfloat16)
-    down = contract_last(w_ref[2], joined(blocks, count, count))
-    own_ref[2 * hidden :] = down
-    send_ref[2 * hidden :] = down.astype(jnp.bfloat16)
+    gu = contract_last(w_ref[0:2].reshape(2 * hidden, width), joined(xs, count))
+    send_ref[0 : 2 * hidden, :] = gu.astype(jnp.bfloat16)
+    down = contract_last(w_ref[2], joined(ys, count))
+    send_ref[2 * hidden :, :] = down.astype(jnp.bfloat16)
     token_ref[...] = jnp.zeros_like(token_ref)
 
 
-def partials(weights, after, blocks, count):
+def partials(weights, after, chunk, count):
     mats, hidden, width = weights.shape
-    shape = (mats * hidden, count * len(blocks))
-    return pl.pallas_call(
-        functools.partial(partial_kernel, len(blocks), count),
-        in_specs=[whole()] * (2 + len(blocks)),
-        out_specs=[whole()] * 3,
+    kinds = kinds_of(chunk)
+    shape = (mats * hidden, tokens_in(kinds, count))
+    return pl.pallas_call(
+        functools.partial(partial_kernel, kinds, count),
+        in_specs=[whole(), unread()] + [whole()] * len(kinds),
+        out_specs=[whole()] * 2,
         out_shape=[
-            jax.ShapeDtypeStruct(shape, jnp.float32),
             jax.ShapeDtypeStruct(shape, jnp.bfloat16),
             jax.ShapeDtypeStruct((8, 128), jnp.float32),
         ],
         compiler_params=params(),
         cost_estimate=cost(2 * shape[0] * shape[1] * width, 6 * shape[0] * shape[1]),
-    )(weights, after, *blocks)
-
-
-def gate_row(expert_ref, blocks, count):
+    )(weights, after, *values_of(chunk))
+
+
+def gate_row(expert_ref, ys, count):
     rows = []
-    for ref in blocks:
-        held = ref[2 * count :, 0:count].astype(jnp.float32)
+    for ref in ys:
+        held = ref[count:, 0:count].astype(jnp.float32)
         index = lax.broadcasted_iota(jnp.int32, held.shape, 0)
         rows.append(jnp.sum(jnp.where(index == expert_ref[0], held, 0.0), 0, keepdims=True))
     return rows[0] if len(rows) == 1 else jnp.concatenate(rows, 1)
 
 
 def hidden_grads(gate, own, got):
-    total = own[...] + got[...].astype(jnp.float32)
+    total = own[...].astype(jnp.float32) + got[...].astype(jnp.float32)
     hidden = total.shape[0] // 3
     hg, hu = total[0:hidden], total[hidden : 2 * hidden]
     dact = gate * total[2 * hidden :]
@@ -257,84 +291,169 @@
     )
 
 
-def grad_kernel(n, count, has_acc, expert_ref, after_ref, own, got, *refs):
-    blocks = refs[:n]
-    out_ref, token_ref = refs[-2:]
-    dhg, dhu, act = hidden_grads(gate_row(expert_ref, blocks, count), own, got)
-    x = joined(blocks, 0, count)
-    y = joined(blocks, count, count)
-    for m, (left, right) in enumerate(((dhg, x), (dhu, x), (act, y))):
-        value = plain(left, right)
-        out_ref[m] = value + refs[n][m] if has_acc else value
-    token_ref[...] = jnp.zeros_like(token_ref)
-
-
-def add_grads(expert, after, own, got, blocks, acc, count):
-    n = len(blocks)
-    width = blocks[0].shape[1]
-    shape = (3, own.shape[0] // 3, width)
-    operands = [expert, after, own, got, *blocks] + ([] if acc is None else [acc])
-    return pl.pallas_call(
-        functools.partial(grad_kernel, n, count, acc is not None),
-        in_specs=[smem()] + [whole()] * (len(operands) - 1),
+def onward_kernel(kinds, count, core_ref, expert_ref, own, got, x_ref, y_ref, *refs):
+    n = len(kinds)
+    both_ref, out_ref, left_ref = refs[n:]
+    both_ref[0] = x_ref[...]
+    both_ref[1] = y_ref[...]
+
+    @pl.when(core_ref[0] == 0)
+    def _():
+        out_ref[...] = x_ref[...]
+
+    @pl.when(core_ref[0] != 0)
+    def _():
+        out_ref[...] = y_ref[...]
+
+    xs, ys = views(refs[:n], kinds, count)
+    for m, value in enumerate(hidden_grads(gate_row(expert_ref, ys, count), own, got)):
+        left_ref[m] = value
+
+
+def pick_onward(core, expert, own, got, over_x, over_y, chunk, count):
+    kinds = kinds_of(chunk)
+    return pl.pallas_call(
+        functools.partial(onward_kernel, kinds, count),
+        in_specs=[smem(), smem()] + [whole()] * (4 + len(kinds)),
+        out_specs=[whole()] * 3,
+        out_shape=[
+            jax.ShapeDtypeStruct((2, *over_x.shape), over_x.dtype),
+            jax.ShapeDtypeStruct(over_x.shape, over_x.dtype),
+            jax.ShapeDtypeStruct((3, own.shape[0] // 3, own.shape[1]), jnp.bfloat16),
+        ],
+        compiler_params=params(),
+        cost_estimate=cost(1000, 4 * over_x.size),
+    )(core.reshape(1), expert, own, got, over_x, over_y, *values_of(chunk))
+
+
+def pass_kernel(count, after_ref, in_ref, x_ref, y_ref):
+    x_ref[...] = in_ref[0:count, :]
+    y_ref[...] = in_ref[count:, :]
+
+
+def passed_on(after, value, count):
+    rows, width = value.shape
+    return pl.pallas_call(
+        functools.partial(pass_kernel, count),
+        in_specs=[unread(), whole()],
         out_specs=[whole()] * 2,
         out_shape=[
-            jax.ShapeDtypeStruct(shape, jnp.float32),
+            jax.ShapeDtypeStruct((count, width), value.dtype),
+            jax.ShapeDtypeStruct((rows - count, width), value.dtype),
+        ],
+        compiler_params=params(),
+        cost_estimate=cost(1000, 2 * value.size),
+    )(after, value)
+
+
+def first_kernel(kinds, count, after_ref, left_ref, *refs):
+    n = len(kinds)
+    xs, ys = views(refs[:n], kinds, count)
+    out_ref, token_ref = refs[n:]
+    x = joined(xs, count)
+    out_ref[0] = plain(left_ref[0], x)
+    out_ref[1] = plain(left_ref[1], x)
+    out_ref[2] = plain(left_ref[2], joined(ys, count))
+    token_ref[...] = jnp.zeros_like(token_ref)
+
+
+def first_grads(after, left, chunk, count):
+    kinds = kinds_of(chunk)
+    mats, hidden, tokens = left.shape
+    width = chunk[0][1].shape[-1]
+    return pl.pallas_call(
+        functools.partial(first_kernel, kinds, count),
+        in_specs=[unread()] + [whole()] * (1 + len(kinds)),
+        out_specs=[whole()] * 2,
+        out_shape=[
+            jax.ShapeDtypeStruct((mats, hidden, width), jnp.float32),
             jax.ShapeDtypeStruct((8, 128), jnp.float32),
         ],
-        input_output_aliases={} if acc is None else {len(operands) - 1: 0},
-        compiler_params=params(),
-        cost_estimate=cost(2 * own.shape[0] * width * n * count, 8 * own.shape[0] * width),
-    )(*operands)
-
-
-def last_kernel(n, count, expert_ref, own, got, *refs):
-    blocks = refs[:n]
+        compiler_params=params(),
+        cost_estimate=cost(6 * hidden * width * tokens, 12 * hidden * width),
+    )(after, left, *values_of(chunk))
+
+
+def grad_kernel(kinds, count, expert_ref, after_ref, own, got, *refs):
+    n = len(kinds)
+    xs, ys = views(refs[:n], kinds, count)
+    acc_ref, out_ref, token_ref = refs[n:]
+    dhg, dhu, act = hidden_grads(gate_row(expert_ref, ys, count), own, got)
+    x = joined(xs, count)
+    out_ref[0] = acc_ref[0] + plain(dhg, x)
+    out_ref[1] = acc_ref[1] + plain(dhu, x)
+    out_ref[2] = acc_ref[2] + plain(act, joined(ys, count))
+    token_ref[...] = jnp.zeros_like(token_ref)
+
+
+def add_grads(expert, after, own, got, chunk, acc, count):
+    kinds = kinds_of(chunk)
+    mats, hidden, width = acc.shape
+    return pl.pallas_call(
+        functools.partial(grad_kernel, kinds, count),
+        in_specs=[smem(), unread()] + [whole()] * (3 + len(kinds)),
+        out_specs=[whole()] * 2,
+        out_shape=[
+            jax.ShapeDtypeStruct(acc.shape, jnp.float32),
+            jax.ShapeDtypeStruct((8, 128), jnp.float32),
+        ],
+        input_output_aliases={4 + len(kinds): 0},
+        compiler_params=params(),
+        cost_estimate=cost(2 * mats * hidden * width * own.shape[1], 8 * mats * hidden * width),
+    )(expert, after, own, got, *values_of(chunk), acc)
+
+
+def last_kernel(kinds, count, expert_ref, own, got, *refs):
+    n = len(kinds)
+    xs, ys = views(refs[:n], kinds, count)
     acc_ref, first_ref, second_ref, one_ref, two_ref, step_ref, left_ref = refs[n:]
     m = pl.program_id(1)
 
     @pl.when((m == 0) & (pl.program_id(0) == 0))
     def _():
-        dhg, dhu, act = hidden_grads(gate_row(expert_ref, blocks, count), own, got)
-        left_ref[0] = dhg
-        left_ref[1] = dhu
-        left_ref[2] = act
+        for k, value in enumerate(hidden_grads(gate_row(expert_ref, ys, count), own, got)):
+            left_ref[k] = value
 
     def finish(right):
         grad = acc_ref[0] + plain(left_ref[m], right)
         moment_one = beta_one * first_ref[0].astype(jnp.float32) + (1.0 - beta_one) * grad
-        moment_two = beta_two * second_ref[0].astype(jnp.float32) + (1.0 - beta_two) * grad * grad
+        moment_two = beta_two * second_ref[0].astype(jnp.float32) + (1.0 - beta_two) * (grad * grad)
         one_ref[0] = moment_one.astype(jnp.bfloat16)
         two_ref[0] = moment_two.astype(jnp.bfloat16)
         scaled = moment_two * (1.0 / (1.0 - beta_two**step_count))
         below = scaled * lax.rsqrt(scaled) + epsilon
-        step = moment_one * (1.0 / (1.0 - beta_one**step_count)) / below
+        guess = pl.reciprocal(below, approx=True)
+        inverse = guess * (2.0 - below * guess)
+        step = moment_one * (1.0 / (1.0 - beta_one**step_count)) * inverse
         step_ref[0] = step.astype(jnp.bfloat16)
 
     @pl.when(m < 2)
     def _():
-        finish(joined(blocks, 0, count))
+        finish(joined(xs, count))
 
     @pl.when(m == 2)
     def _():
-        finish(joined(blocks, count, count))
-
-
-def last_grads(expert, own, got, blocks, acc, first_moment, second_moment, count, columns):
-    n = len(blocks)
+        finish(joined(ys, count))
+
+
+def last_grads(expert, own, got, chunk, acc, first_moment, second_moment, count, columns):
+    kinds = kinds_of(chunk)
+    blocks = values_of(chunk)
     mats, hidden, width = first_moment.shape
     tile = pl.BlockSpec((1, hidden, columns), lambda j, m: (m, 0, j))
     out = jax.ShapeDtypeStruct(first_moment.shape, jnp.bfloat16)
     strip = lambda value: pl.BlockSpec((value.shape[0], columns), lambda j, m: (0, j))
     return pl.pallas_call(
-        functools.partial(last_kernel, n, count),
+        functools.partial(last_kernel, kinds, count),
         grid=(width // columns, mats),
         in_specs=[smem(), whole(), whole()] + [strip(value) for value in blocks] + [tile] * 3,
         out_specs=[tile] * 3,
         out_shape=[out] * 3,
-        scratch_shapes=[pltpu.VMEM((mats, hidden, n * count), jnp.bfloat16)],
-        compiler_params=params(),
-        cost_estimate=cost(6 * hidden * width * n * count, 24 * hidden * width * mats),
+        scratch_shapes=[pltpu.VMEM((mats, hidden, own.shape[1]), jnp.bfloat16)],
+        compiler_params=params(),
+        cost_estimate=cost(
+            2 * mats * hidden * width * own.shape[1], 8 * hidden * width * mats
+        ),
     )(expert, own, got, *blocks, acc, first_moment, second_moment)
 
 
@@ -358,26 +477,29 @@
     )
     over_x = from_masked(own, "dp", 2)
     over_y = from_masked(own, "dp", 4)
+    first = [("xy", own), ("xy", from_masked(own, "dp", 1))]
+    send, token = partials(weights, own, first, count)
+    both, picked, left = pick_onward(
+        core.astype(jnp.int32), expert, send, from_masked(send, "expert", 1), over_x, over_y, first, count
+    )
     onward = [(p, p ^ 4 if p % 2 == 0 else p ^ 2) for p in range(n_data)]
-    far = lax.ppermute(jnp.where(core == 0, over_x, over_y), "dp", onward)
-    chunks = [
-        [block for mine in group for block in (mine, from_masked(mine, "dp", 1))]
-        for group in ([own], [over_x, over_y], [far])
+    far = lax.ppermute(picked, "dp", onward)
+    near = [("both", both), ("both", from_masked(both, "dp", 1))]
+    acc, token = first_grads(picked, left, first, count)
+    near_send, token = partials(weights, token, near, count)
+    near_got = from_masked(near_send, "expert", 1)
+    far_x, far_y = passed_on(token, far, count)
+    final = [
+        ("x", far_x),
+        ("y", far_y),
+        ("x", from_masked(far_x, "dp", 1)),
+        ("y", from_masked(far_y, "dp", 1)),
     ]
-    token = jnp.zeros((8, 128), jnp.float32)
-    parts = []
-    acc = None
-    for number, blocks in enumerate(chunks):
-        mine, send, token = partials(weights, token, blocks, count)
-        parts.append((mine, from_masked(send, "expert", 1)))
-        if number > 0:
-            acc, token = add_grads(
-                expert, token, *parts[number - 1], chunks[number - 1], acc, count
-            )
+    send, token = partials(weights, token, final, count)
+    got = from_masked(send, "expert", 1)
+    acc, token = add_grads(expert, token, near_send, near_got, near, acc, count)
     return tuple(
-        last_grads(
-            expert, *parts[-1], chunks[-1], acc, first_moment, second_moment, count, width // 2
-        )
+        last_grads(expert, send, got, final, acc, first_moment, second_moment, count, width // 2)
     )
 
 

time: 68.1 us -> 51.5 us (0.76)
  local copies, waits for them, and re-layouts: 7.41 us -> 0.01 us
  waiting for transfers between devices: 34 us -> 26.8 us
  Pallas kernels: 15.1 us -> 12.1 us
  starting transfers between devices: 10.3 us -> 11.7 us
    unnamed x30 -> x6, local copies, waits for them, and re-layouts: 7.41 us -> 0.01 us
    pallas_call x6 -> x8, Pallas kernels: 15 us -> 10.9 us  [the longest x1 4.83 us: last_grads(): pl.pallas_call(functools.partial(last_kernel, kinds, count), grid=(width...]
    ppermute x9, waiting for transfers between devices: 26.4 us -> 22.5 us  [from_masked(): return lax.ppermute(value, axis, pairs)]
    ppermute x1, waiting for transfers between devices: 7.6 us -> 4.3 us  [dense_plan(): far = lax.ppermute(picked, 'dp', onward)]
    ppermute x9, starting transfers between devices: 8.7 us -> 10.1 us  [from_masked(): return lax.ppermute(value, axis, pairs)]
    pallas_call x1, Pallas kernels: 0.09 us -> 1.19 us  [pack_own(): pl.pallas_call(pack_kernel, in_specs=[smem()] + [in_hbm()] * 4, out_specs...]
  transfers between devices with their start and end apart: 10 -> 10, of which waited for: 6 -> 7; matrix products, arithmetic and copies ran while one was open for 0% -> 0% of each run, Pallas kernels for 13% -> 9%
where the time goes in v3:
time: 51.5 us; the launch traced here: 51.3 us
  waiting for transfers between devices  26.8 us (52%)
  Pallas kernels  12.1 us (23%)
  starting transfers between devices  11.7 us (23%)
  between operations  0.72 us (1%)
    ppermute x9, waiting for transfers between devices, from_masked(): return lax.ppermute(value, axis, pairs)  22.5 us
    ppermute x9, starting transfers between devices, from_masked(): return lax.ppermute(value, axis, pairs)  10.1 us
    pallas_call x1, Pallas kernels, last_grads(): pl.pallas_call(functools.partial(last_kernel, kinds, count), grid=(width...  4.83 us
    ppermute x1, waiting for transfers between devices, dense_plan(): far = lax.ppermute(picked, 'dp', onward)  4.3 us
    pallas_call x3, Pallas kernels, partials(): pl.pallas_call(functools.partial(partial_kernel, kinds, count), in_specs=...  2.72 us
    ppermute x1, starting transfers between devices, dense_plan(): far = lax.ppermute(picked, 'dp', onward)  1.58 us
    pallas_call x1, Pallas kernels, add_grads(): pl.pallas_call(functools.partial(grad_kernel, kinds, count), in_specs=[sm...  1.53 us
    pallas_call x1, Pallas kernels, pick_onward(): pl.pallas_call(functools.partial(onward_kernel, kinds, count), in_specs=[...  1.33 us
  transfers between devices with their start and end apart: 10, of which 7 were waited for; matrix products, arithmetic and copies ran while one was open for 0% of the time, Pallas kernels for 9%

profile of v3, /device:TPU:0, one launch (start us, length us, event | category | flops | bytes accessed | tf_op | source)
XLA Modules:
  0.0 51.3 jit_solution(4381711152305027338)
XLA Ops:
  0.7 1.2 %shard_map.94.after_ref.refs_0_ = bf16[272,1024]{1,0:T(8,128)(2,1)S(1)} custom-call(s32[1]{0:T(128)} %bitcast.2.replica_ref, s32[4,128]{1,0:T(4,128)} %bitcast.5, bf16[4,128]{1,0:T(4,128)(2,1)} %bitcast.6, bf16[128,2048]{1,0:T(8,128)(2,1)} %tokens_ref.1, bf16[128,2048]{1,0:T(8,128)(2,1)} %cot_ref.1), custom_call_target="tpu_custom_call" | custom-call | flops 1000 | bytes 1048576 | tf_op jit(solution)/shard_map/pallas_call | solution.py:191
  1.9 0.5 %collective-permute-start = (bf16[272,1024]{1,0:T(8,128)(2,1)S(1)}, bf16[272,1024]{1,0:T(8,128)(2,1)S(1)}, u32[]{:S(2)}, u32[]{:S(2)}) collective-permute-start(bf16[272,1024]{1,0:T(8,128)(2,1)S(1)} %shard_map.94.after_ref.refs_0_), channel_id=1, source_target_pairs={{0,1},{1,0},{2,3},{3,2},{4,5},{5,4},{6,7},{7,6},{8,9},{9,8},{10,11... | collective-permute-start | bytes 1671176 | tf_op jit(solution)/shard_map/ppermute | solution.py:462
  2.4 2.6 %collective-permute-start.2 = (bf16[272,1024]{1,0:T(8,128)(2,1)S(1)}, bf16[272,1024]{1,0:T(8,128)(2,1)S(1)}, u32[]{:S(2)}, u32[]{:S(2)}) collective-permute-start(bf16[272,1024]{1,0:T(8,128)(2,1)S(1)} %shard_map.94.after_ref.refs_0_), channel_id=1, source_target_pairs={{0,2},{1,3},{2,0},{3,1},{4,6},{5,7},{6,4},{7,5},{8,10},{9,11},{10,... | collective-permute-start | bytes 1671176 | tf_op jit(solution)/shard_map/ppermute | solution.py:462
  4.9 1.5 %collective-permute-start.3 = (bf16[272,1024]{1,0:T(8,128)(2,1)S(1)}, bf16[272,1024]{1,0:T(8,128)(2,1)S(1)}, u32[]{:S(2)}, u32[]{:S(2)}) collective-permute-start(bf16[272,1024]{1,0:T(8,128)(2,1)S(1)} %shard_map.94.after_ref.refs_0_), channel_id=1, source_target_pairs={{0,4},{1,5},{2,6},{3,7},{4,0},{5,1},{6,2},{7,3},{8,12},{9,13},{10,... | collective-permute-start | bytes 1671176 | tf_op jit(solution)/shard_map/ppermute | solution.py:462
  6.5 1.3 %shard_map.95 = (bf16[576,256]{1,0:T(8,128)(2,1)}, f32[8,128]{1,0:T(8,128)}) custom-call(bf16[3,192,1024]{2,1,0:T(8,128)(2,1)S(1)} %copy-done, bf16[272,1024]{1,0:T(8,128)(2,1)S(1)} %shard_map.94.after_ref.refs_0_, bf16[272,1024]{1,0:T(8,128)(2,1)S(1)} %shard_map.94.after_ref.refs_0_, bf16[272,1024]{1,0:T(8,128)(2,1)S(1)} %collective-permute-done.refs_1_), custom_call_target="tpu_custom_call" | custom-call | flops 301989888 | bytes 884736 | tf_op jit(solution)/shard_map/pallas_call | solution.py:253
  7.7 1.6 %collective-permute-start.1 = (bf16[576,256]{1,0:T(8,128)(2,1)}, bf16[576,256]{1,0:T(8,128)(2,1)}, u32[]{:S(2)}, u32[]{:S(2)}) collective-permute-start(bf16[576,256]{1,0:T(8,128)(2,1)} %get-tuple-element.16.own), channel_id=1, source_target_pairs={{0,8},{8,0},{16,24},{24,16},{1,9},{9,1},{17,25},{25,17},{2,10},{10... | collective-permute-start | bytes 884744 | tf_op jit(solution)/shard_map/ppermute | solution.py:462
  9.3 8.8 %collective-permute-done.2.x_ref = bf16[272,1024]{1,0:T(8,128)(2,1)S(1)} collective-permute-done((bf16[272,1024]{1,0:T(8,128)(2,1)S(1)}, bf16[272,1024]{1,0:T(8,128)(2,1)S(1)}, u32[]{:S(2)}, u32[]{:S(2)}) %collective-permute-start.2) | collective-permute-done | bytes 557088 | tf_op jit(solution)/shard_map/ppermute | solution.py:462
  18.2 1.5 %collective-permute-done.3.y_ref = bf16[272,1024]{1,0:T(8,128)(2,1)S(1)} collective-permute-done((bf16[272,1024]{1,0:T(8,128)(2,1)S(1)}, bf16[272,1024]{1,0:T(8,128)(2,1)S(1)}, u32[]{:S(2)}, u32[]{:S(2)}) %collective-permute-start.3) | collective-permute-done | bytes 557088 | tf_op jit(solution)/shard_map/ppermute | solution.py:462
  19.6 1.3 %shard_map.96 = (bf16[2,272,1024]{2,1,0:T(8,128)(2,1)S(1)}, bf16[272,1024]{1,0:T(8,128)(2,1)S(1)}, bf16[3,192,256]{2,1,0:T(8,128)(2,1)S(1)}) custom-call(s32[1]{0:T(128)} %bitcast.1.core_ref, s32[1]{0:T(128)} %bitcast.expert_ref, bf16[576,256]{1,0:T(8,128)(2,1)} %get-tuple-element.16.own, bf16[576,256]{1,0:T(8,128)(2,1)} %collective-permute-done.1.got, ...), custom_call_target="tpu_custom_call" | custom-call | flops 1000 | bytes 1114112 | tf_op jit(solution)/shard_map/pallas_call | solution.py:315
  21.1 1.6 %collective-permute-start.5 = (bf16[272,1024]{1,0:T(8,128)(2,1)S(1)}, bf16[272,1024]{1,0:T(8,128)(2,1)S(1)}, u32[]{:S(2)}, u32[]{:S(2)}) collective-permute-start(bf16[272,1024]{1,0:T(8,128)(2,1)S(1)} %get-tuple-element.17.after_ref), channel_id=1, source_target_pairs={{0,4},{1,3},{2,6},{3,1},{4,0},{5,7},{6,2},{7,5},{8,12},{9,11},{10,... | collective-permute-start | bytes 1671176 | tf_op jit(solution)/shard_map/ppermute | solution.py:486
  22.6 0.5 shard_map.97
  23.1 0.7 %collective-permute-done.4.refs_1_ = bf16[2,272,1024]{2,1,0:T(8,128)(2,1)S(1)} collective-permute-done((bf16[2,272,1024]{2,1,0:T(8,128)(2,1)S(1)}, bf16[2,272,1024]{2,1,0:T(8,128)(2,1)S(1)}, u32[]{:S(2)}, u32[]{:S(2)}) %collective-permute-start.4) | collective-permute-done | bytes 1114144 | tf_op jit(solution)/shard_map/ppermute | solution.py:462
  23.8 0.9 %shard_map.98 = (bf16[576,512]{1,0:T(8,128)(2,1)S(1)}, f32[8,128]{1,0:T(8,128)S(1)}) custom-call(bf16[3,192,1024]{2,1,0:T(8,128)(2,1)S(1)} %copy-done, f32[8,128]{1,0:T(8,128)S(1)} %get-tuple-element.19.after_ref, bf16[2,272,1024]{2,1,0:T(8,128)(2,1)S(1)} %get-tuple-element.20.refs_0_, bf16[2,272,1024]{2,1,0:T(8,128)(2,1)S(1)} %collective-permute-done.4.refs_1_), custom_call_target="tpu_custom_call" | custom-call | flops 603979776 | bytes 1769472 | tf_op jit(solution)/shard_map/pallas_call | solution.py:253
  24.7 1.6 %collective-permute-start.9 = (bf16[576,512]{1,0:T(8,128)(2,1)S(1)}, bf16[576,512]{1,0:T(8,128)(2,1)S(1)}, u32[]{:S(2)}, u32[]{:S(2)}) collective-permute-start(bf16[576,512]{1,0:T(8,128)(2,1)S(1)} %get-tuple-element.26.own), channel_id=1, source_target_pairs={{0,8},{8,0},{16,24},{24,16},{1,9},{9,1},{17,25},{25,17},{2,10},{10... | collective-permute-start | bytes 1769480 | tf_op jit(solution)/shard_map/ppermute | solution.py:462
  26.3 4.3 %collective-permute-done.5.in_ref = bf16[272,1024]{1,0:T(8,128)(2,1)S(1)} collective-permute-done((bf16[272,1024]{1,0:T(8,128)(2,1)S(1)}, bf16[272,1024]{1,0:T(8,128)(2,1)S(1)}, u32[]{:S(2)}, u32[]{:S(2)}) %collective-permute-start.5) | collective-permute-done | bytes 557088 | tf_op jit(solution)/shard_map/ppermute | solution.py:486
  30.7 0.1 collective-permute-start.7
  30.8 0.5 collective-permute-start.6
  31.3 1.4 %collective-permute-done.6.refs_2_ = bf16[128,1024]{1,0:T(8,128)(2,1)S(1)} collective-permute-done((bf16[128,1024]{1,0:T(8,128)(2,1)S(1)}, bf16[128,1024]{1,0:T(8,128)(2,1)S(1)}, u32[]{:S(2)}, u32[]{:S(2)}) %collective-permute-start.6) | collective-permute-done | bytes 262176 | tf_op jit(solution)/shard_map/ppermute | solution.py:462
  32.7 0.5 %shard_map.100 = (bf16[576,256]{1,0:T(8,128)(2,1)S(1)}, f32[8,128]{1,0:T(8,128)S(1)}) custom-call(bf16[3,192,1024]{2,1,0:T(8,128)(2,1)S(1)} %copy-done, f32[8,128]{1,0:T(8,128)S(1)} %get-tuple-element.21.after_ref, bf16[128,1024]{1,0:T(8,128)(2,1)S(1)} %get-tuple-element.22.refs_0_, bf16[144,1024]{1,0:T(8,128)(2,1)S(1)} %get-tuple-element.23.refs_1_, ...), custom_call_target="tpu_custom_call" | custom-call | flops 301989888 | bytes 884736 | tf_op jit(solution)/shard_map/pallas_call | solution.py:253
  33.3 1.6 %collective-permute-start.8 = (bf16[576,256]{1,0:T(8,128)(2,1)S(1)}, bf16[576,256]{1,0:T(8,128)(2,1)S(1)}, u32[]{:S(2)}, u32[]{:S(2)}) collective-permute-start(bf16[576,256]{1,0:T(8,128)(2,1)S(1)} %get-tuple-element.24.own), channel_id=1, source_target_pairs={{0,8},{8,0},{16,24},{24,16},{1,9},{9,1},{17,25},{25,17},{2,10},{10... | collective-permute-start | bytes 884744 | tf_op jit(solution)/shard_map/ppermute | solution.py:462
  34.9 6.0 %collective-permute-done.9.got = bf16[576,512]{1,0:T(8,128)(2,1)S(1)} collective-permute-done((bf16[576,512]{1,0:T(8,128)(2,1)S(1)}, bf16[576,512]{1,0:T(8,128)(2,1)S(1)}, u32[]{:S(2)}, u32[]{:S(2)}) %collective-permute-start.9) | collective-permute-done | bytes 589856 | tf_op jit(solution)/shard_map/ppermute | solution.py:462
  40.9 1.5 %shard_map.101 = (f32[3,192,1024]{2,1,0:T(8,128)S(1)}, f32[8,128]{1,0:T(8,128)}) custom-call(s32[1]{0:T(128)} %bitcast.expert_ref, f32[8,128]{1,0:T(8,128)S(1)} %get-tuple-element.25.after_ref, bf16[576,512]{1,0:T(8,128)(2,1)S(1)} %get-tuple-element.26.own, bf16[576,512]{1,0:T(8,128)(2,1)S(1)} %collective-permute-done.9.got, ...), custom_call_target="tpu_custom_call", output_to_operand_aliasing={{0}: (6, {})} | custom-call | flops 603979776 | bytes 4718592 | tf_op jit(solution)/shard_map/pallas_call | solution.py:392
  42.5 4.0 %collective-permute-done.8.got = bf16[576,256]{1,0:T(8,128)(2,1)S(1)} collective-permute-done((bf16[576,256]{1,0:T(8,128)(2,1)S(1)}, bf16[576,256]{1,0:T(8,128)(2,1)S(1)}, u32[]{:S(2)}, u32[]{:S(2)}) %collective-permute-start.8) | collective-permute-done | bytes 294944 | tf_op jit(solution)/shard_map/ppermute | solution.py:462
  46.5 4.8 %shard_map.102 = (bf16[3,192,1024]{2,1,0:T(8,128)(2,1)}, bf16[3,192,1024]{2,1,0:T(8,128)(2,1)}, bf16[3,192,1024]{2,1,0:T(8,128)(2,1)}) custom-call(s32[1]{0:T(128)} %bitcast.expert_ref, bf16[576,256]{1,0:T(8,128)(2,1)S(1)} %get-tuple-element.24.own, bf16[576,256]{1,0:T(8,128)(2,1)S(1)} %collective-permute-done.8.got, ...), custom_call_target="tpu_custom_call" | custom-call | flops 301989888 | bytes 4718592 | tf_op jit(solution)/shard_map/pallas_call | solution.py:446
  (11 shorter events, 0.1 us)
Async XLA Ops:
  0.6 5.8 %copy-start = (bf16[3,192,1024]{2,1,0:T(8,128)(2,1)S(1)}, bf16[3,192,1024]{2,1,0:T(8,128)(2,1)}, u32[]{:S(2)}) copy-start(bf16[3,192,1024]{2,1,0:T(8,128)(2,1)} %w_ref.5) | copy-start | bytes 3538948
  1.9 4.6 %collective-permute-start = (bf16[272,1024]{1,0:T(8,128)(2,1)S(1)}, bf16[272,1024]{1,0:T(8,128)(2,1)S(1)}, u32[]{:S(2)}, u32[]{:S(2)}) collective-permute-start(bf16[272,1024]{1,0:T(8,128)(2,1)S(1)} %shard_map.94.after_ref.refs_0_), channel_id=1, source_target_pairs={{0,1},{1,0},{2,3},{3,2},{4,5},{5,4},{6,7},{7,6},{8,9},{9,8},{10,11... | collective-permute-start | bytes 1671176 | tf_op jit(solution)/shard_map/ppermute | solution.py:462
  2.4 15.8 %collective-permute-start.2 = (bf16[272,1024]{1,0:T(8,128)(2,1)S(1)}, bf16[272,1024]{1,0:T(8,128)(2,1)S(1)}, u32[]{:S(2)}, u32[]{:S(2)}) collective-permute-start(bf16[272,1024]{1,0:T(8,128)(2,1)S(1)} %shard_map.94.after_ref.refs_0_), channel_id=1, source_target_pairs={{0,2},{1,3},{2,0},{3,1},{4,6},{5,7},{6,4},{7,5},{8,10},{9,11},{10,... | collective-permute-start | bytes 1671176 | tf_op jit(solution)/shard_map/ppermute | solution.py:462
  4.9 14.7 %collective-permute-start.3 = (bf16[272,1024]{1,0:T(8,128)(2,1)S(1)}, bf16[272,1024]{1,0:T(8,128)(2,1)S(1)}, u32[]{:S(2)}, u32[]{:S(2)}) collective-permute-start(bf16[272,1024]{1,0:T(8,128)(2,1)S(1)} %shard_map.94.after_ref.refs_0_), channel_id=1, source_target_pairs={{0,4},{1,5},{2,6},{3,7},{4,0},{5,1},{6,2},{7,3},{8,12},{9,13},{10,... | collective-permute-start | bytes 1671176 | tf_op jit(solution)/shard_map/ppermute | solution.py:462
  7.7 11.9 %collective-permute-start.1 = (bf16[576,256]{1,0:T(8,128)(2,1)}, bf16[576,256]{1,0:T(8,128)(2,1)}, u32[]{:S(2)}, u32[]{:S(2)}) collective-permute-start(bf16[576,256]{1,0:T(8,128)(2,1)} %get-tuple-element.16.own), channel_id=1, source_target_pairs={{0,8},{8,0},{16,24},{24,16},{1,9},{9,1},{17,25},{25,17},{2,10},{10... | collective-permute-start | bytes 884744 | tf_op jit(solution)/shard_map/ppermute | solution.py:462
  21.0 2.8 %collective-permute-start.4 = (bf16[2,272,1024]{2,1,0:T(8,128)(2,1)S(1)}, bf16[2,272,1024]{2,1,0:T(8,128)(2,1)S(1)}, u32[]{:S(2)}, u32[]{:S(2)}) collective-permute-start(bf16[2,272,1024]{2,1,0:T(8,128)(2,1)S(1)} %get-tuple-element.20.refs_0_), channel_id=1, source_target_pairs={{0,1},{1,0},{2,3},{3,2},{4,5},{5,4},{6,7},{7,6},{8,9},{9,8},{10,11... | collective-permute-start | bytes 3342344 | tf_op jit(solution)/shard_map/ppermute | solution.py:462
  21.1 9.6 %collective-permute-start.5 = (bf16[272,1024]{1,0:T(8,128)(2,1)S(1)}, bf16[272,1024]{1,0:T(8,128)(2,1)S(1)}, u32[]{:S(2)}, u32[]{:S(2)}) collective-permute-start(bf16[272,1024]{1,0:T(8,128)(2,1)S(1)} %get-tuple-element.17.after_ref), channel_id=1, source_target_pairs={{0,4},{1,3},{2,6},{3,1},{4,0},{5,7},{6,2},{7,5},{8,12},{9,11},{10,... | collective-permute-start | bytes 1671176 | tf_op jit(solution)/shard_map/ppermute | solution.py:486
  24.7 16.2 %collective-permute-start.9 = (bf16[576,512]{1,0:T(8,128)(2,1)S(1)}, bf16[576,512]{1,0:T(8,128)(2,1)S(1)}, u32[]{:S(2)}, u32[]{:S(2)}) collective-permute-start(bf16[576,512]{1,0:T(8,128)(2,1)S(1)} %get-tuple-element.26.own), channel_id=1, source_target_pairs={{0,8},{8,0},{16,24},{24,16},{1,9},{9,1},{17,25},{25,17},{2,10},{10... | collective-permute-start | bytes 1769480 | tf_op jit(solution)/shard_map/ppermute | solution.py:462
  30.7 2.0 %collective-permute-start.7 = (bf16[144,1024]{1,0:T(8,128)(2,1)S(1)}, bf16[144,1024]{1,0:T(8,128)(2,1)S(1)}, u32[]{:S(2)}, u32[]{:S(2)}) collective-permute-start(bf16[144,1024]{1,0:T(8,128)(2,1)S(1)} %get-tuple-element.23.refs_1_), channel_id=1, source_target_pairs={{0,1},{1,0},{2,3},{3,2},{4,5},{5,4},{6,7},{7,6},{8,9},{9,8},{10,11... | collective-permute-start | bytes 884744 | tf_op jit(solution)/shard_map/ppermute | solution.py:462
  30.8 1.9 %collective-permute-start.6 = (bf16[128,1024]{1,0:T(8,128)(2,1)S(1)}, bf16[128,1024]{1,0:T(8,128)(2,1)S(1)}, u32[]{:S(2)}, u32[]{:S(2)}) collective-permute-start(bf16[128,1024]{1,0:T(8,128)(2,1)S(1)} %get-tuple-element.22.refs_0_), channel_id=1, source_target_pairs={{0,1},{1,0},{2,3},{3,2},{4,5},{5,4},{6,7},{7,6},{8,9},{9,8},{10,11... | collective-permute-start | bytes 786440 | tf_op jit(solution)/shard_map/ppermute | solution.py:462
  33.3 13.2 %collective-permute-start.8 = (bf16[576,256]{1,0:T(8,128)(2,1)S(1)}, bf16[576,256]{1,0:T(8,128)(2,1)S(1)}, u32[]{:S(2)}, u32[]{:S(2)}) collective-permute-start(bf16[576,256]{1,0:T(8,128)(2,1)S(1)} %get-tuple-element.24.own), channel_id=1, source_target_pairs={{0,8},{8,0},{16,24},{24,16},{1,9},{9,1},{17,25},{25,17},{2,10},{10... | collective-permute-start | bytes 884744 | tf_op jit(solution)/shard_map/ppermute | solution.py:462
  40.9 5.5 %copy-start.1 = (bf16[3,192,1024]{2,1,0:T(8,128)(2,1)S(1)}, bf16[3,192,1024]{2,1,0:T(8,128)(2,1)}, u32[]{:S(2)}) copy-start(bf16[3,192,1024]{2,1,0:T(8,128)(2,1)} %refs_5_.1) | copy-start | bytes 3538948
  40.9 5.5 %copy-start.2 = (bf16[3,192,1024]{2,1,0:T(8,128)(2,1)S(1)}, bf16[3,192,1024]{2,1,0:T(8,128)(2,1)}, u32[]{:S(2)}) copy-start(bf16[3,192,1024]{2,1,0:T(8,128)(2,1)} %refs_6_.1) | copy-start | bytes 3538948

commit v4 on v3

--- a/solution.py
+++ b/solution.py
@@ -134,7 +134,7 @@
 
 
 def cost(flops, moved):
-    return pl.CostEstimate(flops=flops // 1, bytes_accessed=moved // 1, transcendentals=0)
+    return pl.CostEstimate(flops=flops, bytes_accessed=moved, transcendentals=0)
 
 
 def whole():
@@ -158,16 +158,29 @@
 
 
 def pack_kernel(
-    replica_ref, ids_hbm, gates_hbm, tokens_ref, cot_ref, out_ref, ids_ref, gates_ref, sems
+    replica_ref,
+    ids_hbm,
+    gates_hbm,
+    tokens_ref,
+    cot_ref,
+    w_hbm,
+    x_ref,
+    y_ref,
+    own_ref,
+    w_ref,
+    ids_ref,
+    gates_ref,
+    sems,
 ):
     count = tokens_ref.shape[0]
-    width = out_ref.shape[1]
+    width = x_ref.shape[1]
     columns = pl.ds(pl.multiple_of(replica_ref[0] * width, width), width)
     copies = [
         pltpu.make_async_copy(ids_hbm, ids_ref, sems.at[0]),
         pltpu.make_async_copy(gates_hbm, gates_ref, sems.at[1]),
-        pltpu.make_async_copy(tokens_ref.at[:, columns], out_ref.at[0:count, :], sems.at[2]),
-        pltpu.make_async_copy(cot_ref.at[:, columns], out_ref.at[count : 2 * count, :], sems.at[3]),
+        pltpu.make_async_copy(tokens_ref.at[:, columns], x_ref, sems.at[2]),
+        pltpu.make_async_copy(cot_ref.at[:, columns], y_ref.at[0:count, :], sems.at[3]),
+        pltpu.make_async_copy(w_hbm, w_ref, sems.at[4]),
     ]
     for copy in copies:
         copy.start()
@@ -175,50 +188,64 @@
     copies[1].wait()
     ids = ids_ref[...]
     gates = gates_ref[...].astype(jnp.float32)
-    slots = out_ref.shape[0] - 2 * count
+    slots = y_ref.shape[0] - count
     row = lax.broadcasted_iota(jnp.int32, (slots, count), 0)
     gate = jnp.zeros((slots, count), jnp.float32)
     for k in range(ids.shape[0]):
         gate = gate + jnp.where(row == ids[k : k + 1, :], gates[k : k + 1, :], 0.0)
-    out_ref[2 * count :, 0:count] = gate.astype(jnp.bfloat16)
-    out_ref[2 * count :, count:] = jnp.zeros((slots, width - count), jnp.bfloat16)
+    y_ref[count:, 0:count] = gate.astype(jnp.bfloat16)
+    y_ref[count:, count:] = jnp.zeros((slots, width - count), jnp.bfloat16)
+    own_ref[2 * count :, :] = y_ref[count:, :]
     copies[2].wait()
+    own_ref[0:count, :] = x_ref[...]
     copies[3].wait()
-
-
-def pack_own(replica, ids, gates, tokens, cotangent, width, slots):
+    own_ref[count : 2 * count, :] = y_ref[0:count, :]
+    copies[4].wait()
+
+
+def pack_own(replica, ids, gates, tokens, cotangent, weights, slots):
     count, top = ids.shape
+    width = weights.shape[2]
     return pl.pallas_call(
         pack_kernel,
-        in_specs=[smem()] + [in_hbm()] * 4,
-        out_specs=whole(),
-        out_shape=jax.ShapeDtypeStruct((2 * count + slots, width), jnp.bfloat16),
+        in_specs=[smem()] + [in_hbm()] * 5,
+        out_specs=[whole()] * 4,
+        out_shape=[
+            jax.ShapeDtypeStruct((rows, width), jnp.bfloat16)
+            for rows in (count, count + slots, 2 * count + slots)
+        ]
+        + [jax.ShapeDtypeStruct(weights.shape, weights.dtype)],
         scratch_shapes=[
             pltpu.VMEM((top, count), ids.dtype),
             pltpu.VMEM((top, count), gates.dtype),
-            pltpu.SemaphoreType.DMA((4,)),
+            pltpu.SemaphoreType.DMA((5,)),
         ],
         compiler_params=params(),
         cost_estimate=cost(1000, 8 * count * width),
-    )(replica.reshape(1), *[keep_hbm(value) for value in (ids.T, gates.T, tokens, cotangent)])
+    )(replica.reshape(1), *[keep_hbm(value) for value in (ids.T, gates.T, tokens, cotangent, weights)])
 
 
 def views(refs, kinds, count):
-    xs, ys = [], []
+    xs, ys, gates = [], [], []
     for ref, kind in zip(refs, kinds):
-        for part in [ref.at[0], ref.at[1]] if kind == "both" else [ref]:
+        for part in [ref.at[0], ref.at[1]] if ref.ndim == 3 else [ref]:
+            rows = part.shape[0]
+            if kind == "xy":
+                xs.append(part[0:count, :])
             if kind == "x":
-                xs.append(part)
-            elif kind == "y":
-                ys.append(part)
-            else:
-                xs.append(part.at[0:count, :])
-                ys.append(part.at[count:, :])
-    return xs, ys
-
-
-def joined(refs, count):
-    parts = [ref[0:count, :] for ref in refs]
+                xs.append(part[...])
+            if kind in ("xy", "y of xy"):
+                ys.append(part[count : 2 * count, :])
+                gates.append(part[2 * count :, 0:count])
+            if kind == "y":
+                ys.append(part[...])
+            if kind == "y, gates":
+                ys.append(part[0 : count // 2, :])
+                gates.append(part[count // 2 :, 0:count])
+    return xs, ys, gates
+
+
+def joined(parts):
     return parts[0] if len(parts) == 1 else jnp.concatenate(parts, 0)
 
 
@@ -230,53 +257,65 @@
     return [value for kind, value in chunk]
 
 
-def tokens_in(kinds, count):
-    return count * sum({"xy": 1, "both": 2, "x": 1, "y": 0}[kind] for kind in kinds)
-
-
 def partial_kernel(kinds, count, w_ref, after_ref, *refs):
     n = len(kinds)
-    xs, ys = views(refs[:n], kinds, count)
-    send_ref, token_ref = refs[n:]
+    xs, ys, gates = views(refs[:n], kinds, count)
+    outs, token_ref = list(refs[n:-1]), refs[-1]
     mats, hidden, width = w_ref.shape
-    gu = contract_last(w_ref[0:2].reshape(2 * hidden, width), joined(xs, count))
-    send_ref[0 : 2 * hidden, :] = gu.astype(jnp.bfloat16)
-    down = contract_last(w_ref[2], joined(ys, count))
-    send_ref[2 * hidden :, :] = down.astype(jnp.bfloat16)
+    if xs:
+        gu = contract_last(w_ref[0:2].reshape(2 * hidden, width), joined(xs))
+    if ys:
+        down = contract_last(w_ref[2], joined(ys))
+    parts = ([gu] if xs else []) + ([down] if ys else [])
+    out_ref = outs[0]
+    row = 0
+    for part in parts:
+        for first in range(0, part.shape[1], count):
+            piece = part[:, first : first + count]
+            out_ref[row : row + piece.shape[0], :] = piece.astype(jnp.bfloat16)
+            row = row + piece.shape[0]
     token_ref[...] = jnp.zeros_like(token_ref)
 
 
-def partials(weights, after, chunk, count):
-    mats, hidden, width = weights.shape
+def partials(weights, after, chunk, rows, count):
+    hidden, width = weights.shape[1:]
     kinds = kinds_of(chunk)
-    shape = (mats * hidden, tokens_in(kinds, count))
     return pl.pallas_call(
         functools.partial(partial_kernel, kinds, count),
         in_specs=[whole(), unread()] + [whole()] * len(kinds),
         out_specs=[whole()] * 2,
         out_shape=[
-            jax.ShapeDtypeStruct(shape, jnp.bfloat16),
+            jax.ShapeDtypeStruct((rows * hidden, count), jnp.bfloat16),
             jax.ShapeDtypeStruct((8, 128), jnp.float32),
         ],
         compiler_params=params(),
-        cost_estimate=cost(2 * shape[0] * shape[1] * width, 6 * shape[0] * shape[1]),
+        cost_estimate=cost(2 * rows * hidden * count * width, 6 * rows * hidden * count),
     )(weights, after, *values_of(chunk))
 
 
-def gate_row(expert_ref, ys, count):
+def gate_row(expert_ref, gates):
     rows = []
-    for ref in ys:
-        held = ref[count:, 0:count].astype(jnp.float32)
+    for held in gates:
+        held = held.astype(jnp.float32)
         index = lax.broadcasted_iota(jnp.int32, held.shape, 0)
         rows.append(jnp.sum(jnp.where(index == expert_ref[0], held, 0.0), 0, keepdims=True))
     return rows[0] if len(rows) == 1 else jnp.concatenate(rows, 1)
 
 
-def hidden_grads(gate, own, got):
-    total = own[...].astype(jnp.float32) + got[...].astype(jnp.float32)
-    hidden = total.shape[0] // 3
-    hg, hu = total[0:hidden], total[hidden : 2 * hidden]
-    dact = gate * total[2 * hidden :]
+def hidden_grads(gate, pairs):
+    parts = []
+    for own, *got in pairs:
+        part = own[...].astype(jnp.float32)
+        parts.append(part + got[0][...].astype(jnp.float32) if got else part)
+    total = parts[0] if len(parts) == 1 else jnp.concatenate(parts, 0)
+    blocks = gate.shape[1] // total.shape[1]
+    hidden = total.shape[0] // (3 * blocks)
+    row = lambda first: total[first * hidden : (first + 1) * hidden]
+    side = lambda firsts: jnp.concatenate([row(first) for first in firsts], 1)
+    hg = side(range(0, 2 * blocks, 2))
+    hu = side(range(1, 2 * blocks, 2))
+    down = side(range(2 * blocks, 3 * blocks))
+    dact = gate * down
     sig = jax.nn.sigmoid(hg)
     silu = hg * sig
     act = (gate * (silu * hu)).astype(jnp.bfloat16)
@@ -291,56 +330,66 @@
     )
 
 
-def onward_kernel(kinds, count, core_ref, expert_ref, own, got, x_ref, y_ref, *refs):
-    n = len(kinds)
-    both_ref, out_ref, left_ref = refs[n:]
-    both_ref[0] = x_ref[...]
-    both_ref[1] = y_ref[...]
+def onward_kernel(kinds, count, core_ref, expert_ref, after_ref, *refs):
+    own, got, near_own, near_got, x0_ref, x1_ref, y0_ref, y1_ref = refs[:8]
+    blocks = refs[8 : 8 + len(kinds)]
+    both_ref, out_ref, left_ref, sum_ref = refs[8 + len(kinds) :]
+    both_ref[0, 0:count, :] = x0_ref[...]
+    both_ref[1, 0:count, :] = x1_ref[...]
+    both_ref[0, count:, :] = y0_ref[...]
+    both_ref[1, count:, :] = y1_ref[...]
+
+    def pick(near, more):
+        out_ref[0:count, :] = near[...]
+        out_ref[count:, :] = more[...]
 
     @pl.when(core_ref[0] == 0)
     def _():
-        out_ref[...] = x_ref[...]
+        pick(x0_ref, y0_ref)
 
     @pl.when(core_ref[0] != 0)
     def _():
-        out_ref[...] = y_ref[...]
-
-    xs, ys = views(refs[:n], kinds, count)
-    for m, value in enumerate(hidden_grads(gate_row(expert_ref, ys, count), own, got)):
+        pick(x1_ref, y1_ref)
+
+    sum_ref[...] = near_own[...].astype(jnp.float32) + near_got[...].astype(jnp.float32)
+    xs, ys, gates = views(blocks, kinds, count)
+    for m, value in enumerate(hidden_grads(gate_row(expert_ref, gates), [(own, got)])):
         left_ref[m] = value
 
 
-def pick_onward(core, expert, own, got, over_x, over_y, chunk, count):
+def pick_onward(core, expert, after, pair, near_pair, near_x, near_y, chunk, count):
     kinds = kinds_of(chunk)
+    rows, width = near_x[0].shape[0] + near_y[0].shape[0], near_x[0].shape[1]
+    operands = [*pair, *near_pair, *near_x, *near_y, *values_of(chunk)]
     return pl.pallas_call(
         functools.partial(onward_kernel, kinds, count),
-        in_specs=[smem(), smem()] + [whole()] * (4 + len(kinds)),
-        out_specs=[whole()] * 3,
+        in_specs=[smem(), smem(), unread()] + [whole()] * len(operands),
+        out_specs=[whole()] * 4,
         out_shape=[
-            jax.ShapeDtypeStruct((2, *over_x.shape), over_x.dtype),
-            jax.ShapeDtypeStruct(over_x.shape, over_x.dtype),
-            jax.ShapeDtypeStruct((3, own.shape[0] // 3, own.shape[1]), jnp.bfloat16),
+            jax.ShapeDtypeStruct((2, rows, width), jnp.bfloat16),
+            jax.ShapeDtypeStruct((rows, width), jnp.bfloat16),
+            jax.ShapeDtypeStruct((3, pair[0].shape[0] // 6, 2 * count), jnp.bfloat16),
+            jax.ShapeDtypeStruct(near_pair[0].shape, jnp.float32),
         ],
         compiler_params=params(),
-        cost_estimate=cost(1000, 4 * over_x.size),
-    )(core.reshape(1), expert, own, got, over_x, over_y, *values_of(chunk))
-
-
-def pass_kernel(count, after_ref, in_ref, x_ref, y_ref):
-    x_ref[...] = in_ref[0:count, :]
-    y_ref[...] = in_ref[count:, :]
-
-
-def passed_on(after, value, count):
-    rows, width = value.shape
-    return pl.pallas_call(
-        functools.partial(pass_kernel, count),
+        cost_estimate=cost(1000, 8 * near_x[0].size),
+    )(core.reshape(1), expert, after, *operands)
+
+
+def pass_kernel(after_ref, in_ref, *outs):
+    row = 0
+    for out_ref in outs:
+        out_ref[...] = in_ref[row : row + out_ref.shape[0], :]
+        row = row + out_ref.shape[0]
+
+
+def passed_on(after, value, cuts):
+    width = value.shape[1]
+    return pl.pallas_call(
+        pass_kernel,
         in_specs=[unread(), whole()],
-        out_specs=[whole()] * 2,
-        out_shape=[
-            jax.ShapeDtypeStruct((count, width), value.dtype),
-            jax.ShapeDtypeStruct((rows - count, width), value.dtype),
-        ],
+        out_specs=[whole()] * len(cuts),
+        out_shape=[jax.ShapeDtypeStruct((rows, width), value.dtype) for rows in cuts],
         compiler_params=params(),
         cost_estimate=cost(1000, 2 * value.size),
     )(after, value)
@@ -348,12 +397,12 @@
 
 def first_kernel(kinds, count, after_ref, left_ref, *refs):
     n = len(kinds)
-    xs, ys = views(refs[:n], kinds, count)
+    xs, ys, gates = views(refs[:n], kinds, count)
     out_ref, token_ref = refs[n:]
-    x = joined(xs, count)
+    x = joined(xs)
     out_ref[0] = plain(left_ref[0], x)
     out_ref[1] = plain(left_ref[1], x)
-    out_ref[2] = plain(left_ref[2], joined(ys, count))
+    out_ref[2] = plain(left_ref[2], joined(ys))
     token_ref[...] = jnp.zeros_like(token_ref)
 
 
@@ -374,44 +423,42 @@
     )(after, left, *values_of(chunk))
 
 
-def grad_kernel(kinds, count, expert_ref, after_ref, own, got, *refs):
+def grad_kernel(kinds, count, expert_ref, sum_ref, own, got, *refs):
     n = len(kinds)
-    xs, ys = views(refs[:n], kinds, count)
-    acc_ref, out_ref, token_ref = refs[n:]
-    dhg, dhu, act = hidden_grads(gate_row(expert_ref, ys, count), own, got)
-    x = joined(xs, count)
-    out_ref[0] = acc_ref[0] + plain(dhg, x)
-    out_ref[1] = acc_ref[1] + plain(dhu, x)
-    out_ref[2] = acc_ref[2] + plain(act, joined(ys, count))
-    token_ref[...] = jnp.zeros_like(token_ref)
-
-
-def add_grads(expert, after, own, got, chunk, acc, count):
+    xs, ys, gates = views(refs[:n], kinds, count)
+    acc_ref, out_ref = refs[n:]
+    lefts = hidden_grads(gate_row(expert_ref, gates), [(sum_ref,), (own, got)])
+    x = joined(xs)
+    for m, right in enumerate((x, x, joined(ys))):
+        out_ref[m] = acc_ref[m] + plain(lefts[m], right)
+
+
+def add_grads(expert, near_sum, pair, chunk, acc, count):
     kinds = kinds_of(chunk)
     mats, hidden, width = acc.shape
+    operands = [near_sum, *pair, *values_of(chunk), acc]
     return pl.pallas_call(
         functools.partial(grad_kernel, kinds, count),
-        in_specs=[smem(), unread()] + [whole()] * (3 + len(kinds)),
-        out_specs=[whole()] * 2,
-        out_shape=[
-            jax.ShapeDtypeStruct(acc.shape, jnp.float32),
-            jax.ShapeDtypeStruct((8, 128), jnp.float32),
-        ],
-        input_output_aliases={4 + len(kinds): 0},
-        compiler_params=params(),
-        cost_estimate=cost(2 * mats * hidden * width * own.shape[1], 8 * mats * hidden * width),
-    )(expert, after, own, got, *values_of(chunk), acc)
+        in_specs=[smem()] + [whole()] * len(operands),
+        out_specs=whole(),
+        out_shape=jax.ShapeDtypeStruct(acc.shape, jnp.float32),
+        input_output_aliases={len(operands): 0},
+        compiler_params=params(),
+        cost_estimate=cost(
+            2 * mats * hidden * width * 4 * count, 8 * mats * hidden * width
+        ),
+    )(expert, *operands)
 
 
 def last_kernel(kinds, count, expert_ref, own, got, *refs):
     n = len(kinds)
-    xs, ys = views(refs[:n], kinds, count)
+    xs, ys, gates = views(refs[:n], kinds, count)
     acc_ref, first_ref, second_ref, one_ref, two_ref, step_ref, left_ref = refs[n:]
     m = pl.program_id(1)
 
     @pl.when((m == 0) & (pl.program_id(0) == 0))
     def _():
-        for k, value in enumerate(hidden_grads(gate_row(expert_ref, ys, count), own, got)):
+        for k, value in enumerate(hidden_grads(gate_row(expert_ref, gates), [(own, got)])):
             left_ref[k] = value
 
     def finish(right):
@@ -429,11 +476,11 @@
 
     @pl.when(m < 2)
     def _():
-        finish(joined(xs, count))
+        finish(joined(xs))
 
     @pl.when(m == 2)
     def _():
-        finish(joined(ys, count))
+        finish(joined(ys))
 
 
 def last_grads(expert, own, got, chunk, acc, first_moment, second_moment, count, columns):
@@ -449,10 +496,10 @@
         in_specs=[smem(), whole(), whole()] + [strip(value) for value in blocks] + [tile] * 3,
         out_specs=[tile] * 3,
         out_shape=[out] * 3,
-        scratch_shapes=[pltpu.VMEM((mats, hidden, own.shape[1]), jnp.bfloat16)],
+        scratch_shapes=[pltpu.VMEM((mats, hidden, 2 * count), jnp.bfloat16)],
         compiler_params=params(),
         cost_estimate=cost(
-            2 * mats * hidden * width * own.shape[1], 8 * hidden * width * mats
+            4 * mats * hidden * width * count, 8 * hidden * width * mats
         ),
     )(expert, own, got, *blocks, acc, first_moment, second_moment)
 
@@ -472,32 +519,35 @@
     count = tokens.shape[0]
     width = weights.shape[2]
     slots = -(-experts_total // 16) * 16
-    own = pack_own(
-        (place % 2).astype(jnp.int32), expert_ids, gate_probs, tokens, cotangent, width, slots
-    )
-    over_x = from_masked(own, "dp", 2)
-    over_y = from_masked(own, "dp", 4)
-    first = [("xy", own), ("xy", from_masked(own, "dp", 1))]
-    send, token = partials(weights, own, first, count)
-    both, picked, left = pick_onward(
-        core.astype(jnp.int32), expert, send, from_masked(send, "expert", 1), over_x, over_y, first, count
+    x_own, y_own, own, weights = pack_own(
+        (place % 2).astype(jnp.int32), expert_ids, gate_probs, tokens, cotangent, weights, slots
+    )
+    other = lambda value: from_masked(value, "dp", 1)
+    partner = lambda value: from_masked(value, "expert", 1)
+    first = [("xy", own), ("xy", other(own))]
+    send, token = partials(weights, own, first, 6, count)
+    first_pair = (send, partner(send))
+    near_x = [from_masked(x_own, "dp", mask) for mask in (2, 4)]
+    near_y = [from_masked(y_own, "dp", mask) for mask in (2, 4)]
+    send, token = partials(weights, token, [("x", near_x[0])], 2, count)
+    near_pair = (send, partner(send))
+    both, picked, left, near_sum = pick_onward(
+        core.astype(jnp.int32), expert, token, first_pair, near_pair, near_x, near_y, first, count
     )
     onward = [(p, p ^ 4 if p % 2 == 0 else p ^ 2) for p in range(n_data)]
     far = lax.ppermute(picked, "dp", onward)
-    near = [("both", both), ("both", from_masked(both, "dp", 1))]
     acc, token = first_grads(picked, left, first, count)
-    near_send, token = partials(weights, token, near, count)
-    near_got = from_masked(near_send, "expert", 1)
-    far_x, far_y = passed_on(token, far, count)
-    final = [
-        ("x", far_x),
-        ("y", far_y),
-        ("x", from_masked(far_x, "dp", 1)),
-        ("y", from_masked(far_y, "dp", 1)),
-    ]
-    send, token = partials(weights, token, final, count)
-    got = from_masked(send, "expert", 1)
-    acc, token = add_grads(expert, token, near_send, near_got, near, acc, count)
+    swapped = other(both)
+    more = [("x", near_x[1]), ("y of xy", both), ("xy", swapped)]
+    send, token = partials(weights, token, more, 10, count)
+    more_pair = (send, partner(send))
+    pieces = passed_on(token, far, (count // 2, count // 2, count // 2, count // 2 + slots))
+    pieces = [*pieces, *[other(value) for value in pieces]]
+    final = list(zip(("x", "x", "y", "y, gates") * 2, pieces))
+    send, token = partials(weights, token, final, 6, count)
+    got = partner(send)
+    near = [("xy", both), ("xy", swapped)]
+    acc = add_grads(expert, near_sum, more_pair, near, acc, count)
     return tuple(
         last_grads(expert, send, got, final, acc, first_moment, second_moment, count, width // 2)
     )

time: 51.5 us -> 51 us (level)
  waiting for transfers between devices: 26.8 us -> 20.9 us
  starting transfers between devices: 11.7 us -> 15.3 us
  Pallas kernels: 12.1 us -> 13.8 us
    ppermute x9 -> x14, waiting for transfers between devices: 22.5 us -> 16.6 us  [from_masked(): return lax.ppermute(value, axis, pairs)]
    ppermute x9 -> x14, starting transfers between devices: 10.1 us -> 13.7 us  [from_masked(): return lax.ppermute(value, axis, pairs)]
    pallas_call x2, Pallas kernels: 1.23 us -> 2.35 us  [the longest x1 2.31 us: pack_own(): pl.pallas_call(pack_kernel, in_specs=[smem()] + [in_hbm()] * 5, out_specs...]
    pallas_call x3 -> x4, Pallas kernels: 2.72 us -> 3.55 us  [partials(): pl.pallas_call(functools.partial(partial_kernel, kinds, count), in_specs=...]
  transfers between devices with their start and end apart: 10 -> 15, of which waited for: 7 -> 9; matrix products, arithmetic and copies ran while one was open for 0% -> 0% of each run, Pallas kernels for 9% -> 10%
where the time goes in v4:
time: 51 us; the launch traced here: 50.8 us
  waiting for transfers between devices  20.9 us (41%)
  starting transfers between devices  15.3 us (30%)
  Pallas kernels  13.8 us (27%)
  between operations  0.73 us (1%)
    ppermute x14, waiting for transfers between devices, from_masked(): return lax.ppermute(value, axis, pairs)  16.6 us
    ppermute x14, starting transfers between devices, from_masked(): return lax.ppermute(value, axis, pairs)  13.7 us
    pallas_call x1, Pallas kernels, last_grads(): pl.pallas_call(functools.partial(last_kernel, kinds, count), grid=(width...  5.07 us
    ppermute x1, waiting for transfers between devices, dense_plan(): far = lax.ppermute(picked, 'dp', onward)  4.34 us
    pallas_call x4, Pallas kernels, partials(): pl.pallas_call(functools.partial(partial_kernel, kinds, count), in_specs=...  3.55 us
    pallas_call x1, Pallas kernels, pack_own(): pl.pallas_call(pack_kernel, in_specs=[smem()] + [in_hbm()] * 5, out_specs...  2.31 us
    ppermute x1, starting transfers between devices, dense_plan(): far = lax.ppermute(picked, 'dp', onward)  1.58 us
    pallas_call x1, Pallas kernels, pick_onward(): pl.pallas_call(functools.partial(onward_kernel, kinds, count), in_specs=[...  1.38 us
  transfers between devices with their start and end apart: 15, of which 9 were waited for; matrix products, arithmetic and copies ran while one was open for 0% of the time, Pallas kernels for 10%

profile of v4, /device:TPU:0, one launch (start us, length us, event | category | flops | bytes accessed | tf_op | source)
XLA Modules:
  0.0 50.8 jit_solution(17710742460639773510)
XLA Ops:
  0.6 2.3 %shard_map.94 = (bf16[128,1024]{1,0:T(8,128)(2,1)}, bf16[144,1024]{1,0:T(8,128)(2,1)}, bf16[272,1024]{1,0:T(8,128)(2,1)S(1)}, bf16[3,192,1024]{2,1,0:T(8,128)(2,1)S(1)}) custom-call(s32[1]{0:T(128)} %bitcast.1.replica_ref, s32[4,128]{1,0:T(4,128)} %bitcast.5, bf16[4,128]{1,0:T(4,128)(2,1)} %bitcast.6, bf16[128,2048]{1,0:T(8,128)(2,1)} %tokens_ref.1, ...), custom_call_target="tpu_custom_call" | custom-call | flops 1000 | bytes 1048576 | tf_op jit(solution)/shard_map/pallas_call | solution.py:209
  3.0 0.5 %collective-permute-start = (bf16[272,1024]{1,0:T(8,128)(2,1)S(1)}, bf16[272,1024]{1,0:T(8,128)(2,1)S(1)}, u32[]{:S(2)}, u32[]{:S(2)}) collective-permute-start(bf16[272,1024]{1,0:T(8,128)(2,1)S(1)} %get-tuple-element.25.after_ref.refs_0_.refs_8_), channel_id=1, source_target_pairs={{0,1},{1,0},{2,3},{3,2},{4,5},{5,4},{6,7},{7,6},{8,9},{9,8},{10,11... | collective-permute-start | bytes 1671176 | tf_op jit(solution)/shard_map/ppermute | solution.py:509
  3.5 2.6 %collective-permute-start.1 = (bf16[128,1024]{1,0:T(8,128)(2,1)}, bf16[128,1024]{1,0:T(8,128)(2,1)S(1)}, u32[]{:S(2)}, u32[]{:S(2)}) collective-permute-start(bf16[128,1024]{1,0:T(8,128)(2,1)} %get-tuple-element.27), channel_id=1, source_target_pairs={{0,2},{1,3},{2,0},{3,1},{4,6},{5,7},{6,4},{7,5},{8,10},{9,11},{10,... | collective-permute-start | bytes 786440 | tf_op jit(solution)/shard_map/ppermute | solution.py:509
  6.0 1.5 %collective-permute-start.6 = (bf16[144,1024]{1,0:T(8,128)(2,1)}, bf16[144,1024]{1,0:T(8,128)(2,1)S(1)}, u32[]{:S(2)}, u32[]{:S(2)}) collective-permute-start(bf16[144,1024]{1,0:T(8,128)(2,1)} %get-tuple-element.31), channel_id=1, source_target_pairs={{0,4},{1,5},{2,6},{3,7},{4,0},{5,1},{6,2},{7,3},{8,12},{9,13},{10,... | collective-permute-start | bytes 884744 | tf_op jit(solution)/shard_map/ppermute | solution.py:509
  7.6 0.5 %collective-permute-start.5 = (bf16[144,1024]{1,0:T(8,128)(2,1)}, bf16[144,1024]{1,0:T(8,128)(2,1)S(1)}, u32[]{:S(2)}, u32[]{:S(2)}) collective-permute-start(bf16[144,1024]{1,0:T(8,128)(2,1)} %get-tuple-element.31), channel_id=1, source_target_pairs={{0,2},{1,3},{2,0},{3,1},{4,6},{5,7},{6,4},{7,5},{8,10},{9,11},{10,... | collective-permute-start | bytes 884744 | tf_op jit(solution)/shard_map/ppermute | solution.py:509
  8.1 1.3 %shard_map.95 = (bf16[1152,128]{1,0:T(8,128)(2,1)}, f32[8,128]{1,0:T(8,128)S(1)}) custom-call(bf16[3,192,1024]{2,1,0:T(8,128)(2,1)S(1)} %get-tuple-element.24.w_ref, bf16[272,1024]{1,0:T(8,128)(2,1)S(1)} %get-tuple-element.25.after_ref.refs_0_.refs_8_, bf16[272,1024]{1,0:T(8,128)(2,1)S(1)} %get-tuple-element.25.after_ref.refs_0_.refs_8_, ...), custom_call_target="tpu_custom_call" | custom-call | flops 301989888 | bytes 884736 | tf_op jit(solution)/shard_map/pallas_call | solution.py:283
  9.4 1.6 %collective-permute-start.2 = (bf16[1152,128]{1,0:T(8,128)(2,1)}, bf16[1152,128]{1,0:T(8,128)(2,1)}, u32[]{:S(2)}, u32[]{:S(2)}) collective-permute-start(bf16[1152,128]{1,0:T(8,128)(2,1)} %get-tuple-element.29.refs_0_), channel_id=1, source_target_pairs={{0,8},{8,0},{16,24},{24,16},{1,9},{9,1},{17,25},{25,17},{2,10},{10... | collective-permute-start | bytes 884744 | tf_op jit(solution)/shard_map/ppermute | solution.py:509
  10.9 0.5 collective-permute-start.4
  11.4 2.0 %collective-permute-done.1.refs_0_.refs_4_ = bf16[128,1024]{1,0:T(8,128)(2,1)S(1)} collective-permute-done((bf16[128,1024]{1,0:T(8,128)(2,1)}, bf16[128,1024]{1,0:T(8,128)(2,1)S(1)}, u32[]{:S(2)}, u32[]{:S(2)}) %collective-permute-start.1) | collective-permute-done | bytes 262176 | tf_op jit(solution)/shard_map/ppermute | solution.py:509
  13.8 2.1 %collective-permute-start.3 = (bf16[384,128]{1,0:T(8,128)(2,1)S(1)}, bf16[384,128]{1,0:T(8,128)(2,1)}, u32[]{:S(2)}, u32[]{:S(2)}) collective-permute-start(bf16[384,128]{1,0:T(8,128)(2,1)S(1)} %get-tuple-element.30.refs_2_), channel_id=1, source_target_pairs={{0,8},{8,0},{16,24},{24,16},{1,9},{9,1},{17,25},{25,17},{2,10},{10... | collective-permute-start | bytes 294920 | tf_op jit(solution)/shard_map/ppermute | solution.py:509
  15.9 5.1 %collective-permute-done.4.refs_5_.refs_0_ = bf16[128,1024]{1,0:T(8,128)(2,1)S(1)} collective-permute-done((bf16[128,1024]{1,0:T(8,128)(2,1)}, bf16[128,1024]{1,0:T(8,128)(2,1)S(1)}, u32[]{:S(2)}, u32[]{:S(2)}) %collective-permute-start.4) | collective-permute-done | bytes 262176 | tf_op jit(solution)/shard_map/ppermute | solution.py:509
  21.0 1.4 %shard_map.97 = (bf16[2,272,1024]{2,1,0:T(8,128)(2,1)S(1)}, bf16[272,1024]{1,0:T(8,128)(2,1)S(1)}, bf16[3,192,256]{2,1,0:T(8,128)(2,1)S(1)}, f32[384,128]{1,0:T(8,128)S(1)}) custom-call(s32[1]{0:T(128)} %bitcast.4.core_ref, s32[1]{0:T(128)} %bitcast.expert_ref, f32[8,128]{1,0:T(8,128)S(1)} %get-tuple-element.28.after_ref, ...), custom_call_target="tpu_custom_call" | custom-call | flops 1000 | bytes 1048576 | tf_op jit(solution)/shard_map/pallas_call | solution.py:364
  22.4 1.6 %collective-permute-start.8 = (bf16[272,1024]{1,0:T(8,128)(2,1)S(1)}, bf16[272,1024]{1,0:T(8,128)(2,1)S(1)}, u32[]{:S(2)}, u32[]{:S(2)}) collective-permute-start(bf16[272,1024]{1,0:T(8,128)(2,1)S(1)} %get-tuple-element.32.after_ref), channel_id=1, source_target_pairs={{0,4},{1,3},{2,6},{3,1},{4,0},{5,7},{6,2},{7,5},{8,12},{9,11},{10,... | collective-permute-start | bytes 1671176 | tf_op jit(solution)/shard_map/ppermute | solution.py:538
  24.5 0.7 %collective-permute-done.7.refs_2_.refs_1_ = bf16[2,272,1024]{2,1,0:T(8,128)(2,1)S(1)} collective-permute-done((bf16[2,272,1024]{2,1,0:T(8,128)(2,1)S(1)}, bf16[2,272,1024]{2,1,0:T(8,128)(2,1)S(1)}, u32[]{:S(2)}, u32[]{:S(2)}) %collective-permute-start.7) | collective-permute-done | bytes 1114144 | tf_op jit(solution)/shard_map/ppermute | solution.py:509
  25.2 0.9 %shard_map.99 = (bf16[1920,128]{1,0:T(8,128)(2,1)S(1)}, f32[8,128]{1,0:T(8,128)S(1)}) custom-call(bf16[3,192,1024]{2,1,0:T(8,128)(2,1)S(1)} %get-tuple-element.24.w_ref, f32[8,128]{1,0:T(8,128)S(1)} %get-tuple-element.34.after_ref, bf16[128,1024]{1,0:T(8,128)(2,1)S(1)} %collective-permute-done.4.refs_5_.refs_0_, ...), custom_call_target="tpu_custom_call" | custom-call | flops 503316480 | bytes 1474560 | tf_op jit(solution)/shard_map/pallas_call | solution.py:283
  26.1 1.6 %collective-permute-start.14 = (bf16[1920,128]{1,0:T(8,128)(2,1)S(1)}, bf16[1920,128]{1,0:T(8,128)(2,1)S(1)}, u32[]{:S(2)}, u32[]{:S(2)}) collective-permute-start(bf16[1920,128]{1,0:T(8,128)(2,1)S(1)} %get-tuple-element.43.own), channel_id=1, source_target_pairs={{0,8},{8,0},{16,24},{24,16},{1,9},{9,1},{17,25},{25,17},{2,10},{10... | collective-permute-start | bytes 1474568 | tf_op jit(solution)/shard_map/ppermute | solution.py:509
  27.7 4.3 %collective-permute-done.8.in_ref = bf16[272,1024]{1,0:T(8,128)(2,1)S(1)} collective-permute-done((bf16[272,1024]{1,0:T(8,128)(2,1)S(1)}, bf16[272,1024]{1,0:T(8,128)(2,1)S(1)}, u32[]{:S(2)}, u32[]{:S(2)}) %collective-permute-start.8) | collective-permute-done | bytes 557088 | tf_op jit(solution)/shard_map/ppermute | solution.py:538
  33.2 0.6 %collective-permute-done.9.refs_4_ = bf16[64,1024]{1,0:T(8,128)(2,1)S(1)} collective-permute-done((bf16[64,1024]{1,0:T(8,128)(2,1)S(1)}, bf16[64,1024]{1,0:T(8,128)(2,1)S(1)}, u32[]{:S(2)}, u32[]{:S(2)}) %collective-permute-start.9) | collective-permute-done | bytes 131104 | tf_op jit(solution)/shard_map/ppermute | solution.py:509
  34.2 1.0 %shard_map.101 = (bf16[1152,128]{1,0:T(8,128)(2,1)S(1)}, f32[8,128]{1,0:T(8,128)}) custom-call(bf16[3,192,1024]{2,1,0:T(8,128)(2,1)S(1)} %get-tuple-element.24.w_ref, f32[8,128]{1,0:T(8,128)S(1)} %get-tuple-element.36.after_ref, bf16[64,1024]{1,0:T(8,128)(2,1)S(1)} %get-tuple-element.37.refs_0_, bf16[64,1024]{1,0:T(8,128)(2,1)S(1)} %get-tuple-element.38.refs_1_, ...), custom_call_target="tpu_custom_call" | custom-call | flops 301989888 | bytes 884736 | tf_op jit(solution)/shard_map/pallas_call | solution.py:283
  35.2 1.6 %collective-permute-start.13 = (bf16[1152,128]{1,0:T(8,128)(2,1)S(1)}, bf16[1152,128]{1,0:T(8,128)(2,1)S(1)}, u32[]{:S(2)}, u32[]{:S(2)}) collective-permute-start(bf16[1152,128]{1,0:T(8,128)(2,1)S(1)} %get-tuple-element.41.own), channel_id=1, source_target_pairs={{0,8},{8,0},{16,24},{24,16},{1,9},{9,1},{17,25},{25,17},{2,10},{10... | collective-permute-start | bytes 884744 | tf_op jit(solution)/shard_map/ppermute | solution.py:509
  36.8 3.4 %collective-permute-done.14.got = bf16[1920,128]{1,0:T(8,128)(2,1)S(1)} collective-permute-done((bf16[1920,128]{1,0:T(8,128)(2,1)S(1)}, bf16[1920,128]{1,0:T(8,128)(2,1)S(1)}, u32[]{:S(2)}, u32[]{:S(2)}) %collective-permute-start.14) | collective-permute-done | bytes 491552 | tf_op jit(solution)/shard_map/ppermute | solution.py:509
  40.2 1.0 %shard_map.102.refs_8_ = f32[3,192,1024]{2,1,0:T(8,128)S(1)} custom-call(s32[1]{0:T(128)} %bitcast.expert_ref, f32[384,128]{1,0:T(8,128)S(1)} %get-tuple-element.42.sum_ref, bf16[1920,128]{1,0:T(8,128)(2,1)S(1)} %get-tuple-element.43.own, bf16[1920,128]{1,0:T(8,128)(2,1)S(1)} %collective-permute-done.14.got, ...), custom_call_target="tpu_custom_call", output_to_operand_aliasing={{}: (6, {})} | custom-call | flops 603979776 | bytes 4718592 | tf_op jit(solution)/shard_map/pallas_call | solution.py:440
  41.2 4.5 %collective-permute-done.13.got = bf16[1152,128]{1,0:T(8,128)(2,1)S(1)} collective-permute-done((bf16[1152,128]{1,0:T(8,128)(2,1)S(1)}, bf16[1152,128]{1,0:T(8,128)(2,1)S(1)}, u32[]{:S(2)}, u32[]{:S(2)}) %collective-permute-start.13) | collective-permute-done | bytes 294944 | tf_op jit(solution)/shard_map/ppermute | solution.py:509
  45.7 5.1 %shard_map.103 = (bf16[3,192,1024]{2,1,0:T(8,128)(2,1)}, bf16[3,192,1024]{2,1,0:T(8,128)(2,1)}, bf16[3,192,1024]{2,1,0:T(8,128)(2,1)}) custom-call(s32[1]{0:T(128)} %bitcast.expert_ref, bf16[1152,128]{1,0:T(8,128)(2,1)S(1)} %get-tuple-element.41.own, bf16[1152,128]{1,0:T(8,128)(2,1)S(1)} %collective-permute-done.13.got, ...), custom_call_target="tpu_custom_call" | custom-call | flops 301989888 | bytes 4718592 | tf_op jit(solution)/shard_map/pallas_call | solution.py:493
  (20 shorter events, 2.5 us)
Async XLA Ops:
  3.0 5.1 %collective-permute-start = (bf16[272,1024]{1,0:T(8,128)(2,1)S(1)}, bf16[272,1024]{1,0:T(8,128)(2,1)S(1)}, u32[]{:S(2)}, u32[]{:S(2)}) collective-permute-start(bf16[272,1024]{1,0:T(8,128)(2,1)S(1)} %get-tuple-element.25.after_ref.refs_0_.refs_8_), channel_id=1, source_target_pairs={{0,1},{1,0},{2,3},{3,2},{4,5},{5,4},{6,7},{7,6},{8,9},{9,8},{10,11... | collective-permute-start | bytes 1671176 | tf_op jit(solution)/shard_map/ppermute | solution.py:509
  3.5 9.9 %collective-permute-start.1 = (bf16[128,1024]{1,0:T(8,128)(2,1)}, bf16[128,1024]{1,0:T(8,128)(2,1)S(1)}, u32[]{:S(2)}, u32[]{:S(2)}) collective-permute-start(bf16[128,1024]{1,0:T(8,128)(2,1)} %get-tuple-element.27), channel_id=1, source_target_pairs={{0,2},{1,3},{2,0},{3,1},{4,6},{5,7},{6,4},{7,5},{8,10},{9,11},{10,... | collective-permute-start | bytes 786440 | tf_op jit(solution)/shard_map/ppermute | solution.py:509
  6.0 14.9 %collective-permute-start.6 = (bf16[144,1024]{1,0:T(8,128)(2,1)}, bf16[144,1024]{1,0:T(8,128)(2,1)S(1)}, u32[]{:S(2)}, u32[]{:S(2)}) collective-permute-start(bf16[144,1024]{1,0:T(8,128)(2,1)} %get-tuple-element.31), channel_id=1, source_target_pairs={{0,4},{1,5},{2,6},{3,7},{4,0},{5,1},{6,2},{7,3},{8,12},{9,13},{10,... | collective-permute-start | bytes 884744 | tf_op jit(solution)/shard_map/ppermute | solution.py:509
  7.6 13.4 %collective-permute-start.5 = (bf16[144,1024]{1,0:T(8,128)(2,1)}, bf16[144,1024]{1,0:T(8,128)(2,1)S(1)}, u32[]{:S(2)}, u32[]{:S(2)}) collective-permute-start(bf16[144,1024]{1,0:T(8,128)(2,1)} %get-tuple-element.31), channel_id=1, source_target_pairs={{0,2},{1,3},{2,0},{3,1},{4,6},{5,7},{6,4},{7,5},{8,10},{9,11},{10,... | collective-permute-start | bytes 884744 | tf_op jit(solution)/shard_map/ppermute | solution.py:509
  9.4 11.6 %collective-permute-start.2 = (bf16[1152,128]{1,0:T(8,128)(2,1)}, bf16[1152,128]{1,0:T(8,128)(2,1)}, u32[]{:S(2)}, u32[]{:S(2)}) collective-permute-start(bf16[1152,128]{1,0:T(8,128)(2,1)} %get-tuple-element.29.refs_0_), channel_id=1, source_target_pairs={{0,8},{8,0},{16,24},{24,16},{1,9},{9,1},{17,25},{25,17},{2,10},{10... | collective-permute-start | bytes 884744 | tf_op jit(solution)/shard_map/ppermute | solution.py:509
  10.9 10.0 %collective-permute-start.4 = (bf16[128,1024]{1,0:T(8,128)(2,1)}, bf16[128,1024]{1,0:T(8,128)(2,1)S(1)}, u32[]{:S(2)}, u32[]{:S(2)}) collective-permute-start(bf16[128,1024]{1,0:T(8,128)(2,1)} %get-tuple-element.27), channel_id=1, source_target_pairs={{0,4},{1,5},{2,6},{3,7},{4,0},{5,1},{6,2},{7,3},{8,12},{9,13},{10,... | collective-permute-start | bytes 786440 | tf_op jit(solution)/shard_map/ppermute | solution.py:509
  13.8 7.2 %collective-permute-start.3 = (bf16[384,128]{1,0:T(8,128)(2,1)S(1)}, bf16[384,128]{1,0:T(8,128)(2,1)}, u32[]{:S(2)}, u32[]{:S(2)}) collective-permute-start(bf16[384,128]{1,0:T(8,128)(2,1)S(1)} %get-tuple-element.30.refs_2_), channel_id=1, source_target_pairs={{0,8},{8,0},{16,24},{24,16},{1,9},{9,1},{17,25},{25,17},{2,10},{10... | collective-permute-start | bytes 294920 | tf_op jit(solution)/shard_map/ppermute | solution.py:509
  22.4 2.8 %collective-permute-start.7 = (bf16[2,272,1024]{2,1,0:T(8,128)(2,1)S(1)}, bf16[2,272,1024]{2,1,0:T(8,128)(2,1)S(1)}, u32[]{:S(2)}, u32[]{:S(2)}) collective-permute-start(bf16[2,272,1024]{2,1,0:T(8,128)(2,1)S(1)} %get-tuple-element.35.refs_1_.refs_0_), channel_id=1, source_target_pairs={{0,1},{1,0},{2,3},{3,2},{4,5},{5,4},{6,7},{7,6},{8,9},{9,8},{10,11... | collective-permute-start | bytes 3342344 | tf_op jit(solution)/shard_map/ppermute | solution.py:509
  22.4 9.6 %collective-permute-start.8 = (bf16[272,1024]{1,0:T(8,128)(2,1)S(1)}, bf16[272,1024]{1,0:T(8,128)(2,1)S(1)}, u32[]{:S(2)}, u32[]{:S(2)}) collective-permute-start(bf16[272,1024]{1,0:T(8,128)(2,1)S(1)} %get-tuple-element.32.after_ref), channel_id=1, source_target_pairs={{0,4},{1,3},{2,6},{3,1},{4,0},{5,7},{6,2},{7,5},{8,12},{9,11},{10,... | collective-permute-start | bytes 1671176 | tf_op jit(solution)/shard_map/ppermute | solution.py:538
  26.1 14.1 %collective-permute-start.14 = (bf16[1920,128]{1,0:T(8,128)(2,1)S(1)}, bf16[1920,128]{1,0:T(8,128)(2,1)S(1)}, u32[]{:S(2)}, u32[]{:S(2)}) collective-permute-start(bf16[1920,128]{1,0:T(8,128)(2,1)S(1)} %get-tuple-element.43.own), channel_id=1, source_target_pairs={{0,8},{8,0},{16,24},{24,16},{1,9},{9,1},{17,25},{25,17},{2,10},{10... | collective-permute-start | bytes 1474568 | tf_op jit(solution)/shard_map/ppermute | solution.py:509
  32.1 2.1 %collective-permute-start.12 = (bf16[80,1024]{1,0:T(8,128)(2,1)S(1)}, bf16[80,1024]{1,0:T(8,128)(2,1)S(1)}, u32[]{:S(2)}, u32[]{:S(2)}) collective-permute-start(bf16[80,1024]{1,0:T(8,128)(2,1)S(1)} %get-tuple-element.40.refs_3_), channel_id=1, source_target_pairs={{0,1},{1,0},{2,3},{3,2},{4,5},{5,4},{6,7},{7,6},{8,9},{9,8},{10,11... | collective-permute-start | bytes 491528 | tf_op jit(solution)/shard_map/ppermute | solution.py:509
  32.2 1.6 %collective-permute-start.9 = (bf16[64,1024]{1,0:T(8,128)(2,1)S(1)}, bf16[64,1024]{1,0:T(8,128)(2,1)S(1)}, u32[]{:S(2)}, u32[]{:S(2)}) collective-permute-start(bf16[64,1024]{1,0:T(8,128)(2,1)S(1)} %get-tuple-element.37.refs_0_), channel_id=1, source_target_pairs={{0,1},{1,0},{2,3},{3,2},{4,5},{5,4},{6,7},{7,6},{8,9},{9,8},{10,11... | collective-permute-start | bytes 393224 | tf_op jit(solution)/shard_map/ppermute | solution.py:509
  32.7 1.3 %collective-permute-start.10 = (bf16[64,1024]{1,0:T(8,128)(2,1)S(1)}, bf16[64,1024]{1,0:T(8,128)(2,1)S(1)}, u32[]{:S(2)}, u32[]{:S(2)}) collective-permute-start(bf16[64,1024]{1,0:T(8,128)(2,1)S(1)} %get-tuple-element.38.refs_1_), channel_id=1, source_target_pairs={{0,1},{1,0},{2,3},{3,2},{4,5},{5,4},{6,7},{7,6},{8,9},{9,8},{10,11... | collective-permute-start | bytes 393224 | tf_op jit(solution)/shard_map/ppermute | solution.py:509
  32.7 1.5 %collective-permute-start.11 = (bf16[64,1024]{1,0:T(8,128)(2,1)S(1)}, bf16[64,1024]{1,0:T(8,128)(2,1)S(1)}, u32[]{:S(2)}, u32[]{:S(2)}) collective-permute-start(bf16[64,1024]{1,0:T(8,128)(2,1)S(1)} %get-tuple-element.39.refs_2_), channel_id=1, source_target_pairs={{0,1},{1,0},{2,3},{3,2},{4,5},{5,4},{6,7},{7,6},{8,9},{9,8},{10,11... | collective-permute-start | bytes 393224 | tf_op jit(solution)/shard_map/ppermute | solution.py:509
  35.2 10.5 %collective-permute-start.13 = (bf16[1152,128]{1,0:T(8,128)(2,1)S(1)}, bf16[1152,128]{1,0:T(8,128)(2,1)S(1)}, u32[]{:S(2)}, u32[]{:S(2)}) collective-permute-start(bf16[1152,128]{1,0:T(8,128)(2,1)S(1)} %get-tuple-element.41.own), channel_id=1, source_target_pairs={{0,8},{8,0},{16,24},{24,16},{1,9},{9,1},{17,25},{25,17},{2,10},{10... | collective-permute-start | bytes 884744 | tf_op jit(solution)/shard_map/ppermute | solution.py:509
  40.2 5.5 %copy-start = (bf16[3,192,1024]{2,1,0:T(8,128)(2,1)S(1)}, bf16[3,192,1024]{2,1,0:T(8,128)(2,1)}, u32[]{:S(2)}) copy-start(bf16[3,192,1024]{2,1,0:T(8,128)(2,1)} %refs_9_.1) | copy-start | bytes 3538948
  40.2 5.5 %copy-start.1 = (bf16[3,192,1024]{2,1,0:T(8,128)(2,1)S(1)}, bf16[3,192,1024]{2,1,0:T(8,128)(2,1)}, u32[]{:S(2)}) copy-start(bf16[3,192,1024]{2,1,0:T(8,128)(2,1)} %refs_10_.1) | copy-start | bytes 3538948

commit v5 on v4

--- a/solution.py
+++ b/solution.py
@@ -163,11 +163,9 @@
     gates_hbm,
     tokens_ref,
     cot_ref,
-    w_hbm,
     x_ref,
     y_ref,
     own_ref,
-    w_ref,
     ids_ref,
     gates_ref,
     sems,
@@ -180,7 +178,6 @@
         pltpu.make_async_copy(gates_hbm, gates_ref, sems.at[1]),
         pltpu.make_async_copy(tokens_ref.at[:, columns], x_ref, sems.at[2]),
         pltpu.make_async_copy(cot_ref.at[:, columns], y_ref.at[0:count, :], sems.at[3]),
-        pltpu.make_async_copy(w_hbm, w_ref, sems.at[4]),
     ]
     for copy in copies:
         copy.start()
@@ -200,29 +197,26 @@
     own_ref[0:count, :] = x_ref[...]
     copies[3].wait()
     own_ref[count : 2 * count, :] = y_ref[0:count, :]
-    copies[4].wait()
-
-
-def pack_own(replica, ids, gates, tokens, cotangent, weights, slots):
+
+
+def pack_own(replica, ids, gates, tokens, cotangent, width, slots):
     count, top = ids.shape
-    width = weights.shape[2]
     return pl.pallas_call(
         pack_kernel,
-        in_specs=[smem()] + [in_hbm()] * 5,
-        out_specs=[whole()] * 4,
+        in_specs=[smem()] + [in_hbm()] * 4,
+        out_specs=[whole()] * 3,
         out_shape=[
             jax.ShapeDtypeStruct((rows, width), jnp.bfloat16)
             for rows in (count, count + slots, 2 * count + slots)
-        ]
-        + [jax.ShapeDtypeStruct(weights.shape, weights.dtype)],
+        ],
         scratch_shapes=[
             pltpu.VMEM((top, count), ids.dtype),
             pltpu.VMEM((top, count), gates.dtype),
-            pltpu.SemaphoreType.DMA((5,)),
+            pltpu.SemaphoreType.DMA((4,)),
         ],
         compiler_params=params(),
         cost_estimate=cost(1000, 8 * count * width),
-    )(replica.reshape(1), *[keep_hbm(value) for value in (ids.T, gates.T, tokens, cotangent, weights)])
+    )(replica.reshape(1), *[keep_hbm(value) for value in (ids.T, gates.T, tokens, cotangent)])
 
 
 def views(refs, kinds, count):
@@ -257,40 +251,85 @@
     return [value for kind, value in chunk]
 
 
-def partial_kernel(kinds, count, w_ref, after_ref, *refs):
-    n = len(kinds)
-    xs, ys, gates = views(refs[:n], kinds, count)
-    outs, token_ref = list(refs[n:-1]), refs[-1]
-    mats, hidden, width = w_ref.shape
-    if xs:
-        gu = contract_last(w_ref[0:2].reshape(2 * hidden, width), joined(xs))
-    if ys:
-        down = contract_last(w_ref[2], joined(ys))
-    parts = ([gu] if xs else []) + ([down] if ys else [])
-    out_ref = outs[0]
+def store_partials(parts, count, out_ref):
     row = 0
     for part in parts:
         for first in range(0, part.shape[1], count):
             piece = part[:, first : first + count]
             out_ref[row : row + piece.shape[0], :] = piece.astype(jnp.bfloat16)
             row = row + piece.shape[0]
-    token_ref[...] = jnp.zeros_like(token_ref)
+
+
+def partial_kernel(kinds, count, w_ref, after_ref, *refs):
+    n = len(kinds)
+    xs, ys, gates = views(refs[:n], kinds, count)
+    outs = refs[n:-1]
+    mats, hidden, width = w_ref.shape
+    parts = []
+    if xs:
+        parts.append(contract_last(w_ref[0:2].reshape(2 * hidden, width), joined(xs)))
+    if ys:
+        parts.append(contract_last(w_ref[2], joined(ys)))
+    if len(outs) == 1:
+        store_partials(parts, count, outs[0])
+    else:
+        for part, out_ref in zip(parts, outs):
+            store_partials([part], count, out_ref)
+    refs[-1][...] = jnp.zeros_like(refs[-1])
 
 
 def partials(weights, after, chunk, rows, count):
     hidden, width = weights.shape[1:]
     kinds = kinds_of(chunk)
+    total = sum(rows) * hidden * count
     return pl.pallas_call(
         functools.partial(partial_kernel, kinds, count),
         in_specs=[whole(), unread()] + [whole()] * len(kinds),
-        out_specs=[whole()] * 2,
+        out_specs=[whole()] * (len(rows) + 1),
+        out_shape=[jax.ShapeDtypeStruct((k * hidden, count), jnp.bfloat16) for k in rows]
+        + [jax.ShapeDtypeStruct((8, 128), jnp.float32)],
+        compiler_params=params(),
+        cost_estimate=cost(2 * total * width, 6 * total),
+    )(weights, after, *values_of(chunk))
+
+
+def start_kernel(kinds, count, w_hbm, *refs):
+    n = len(kinds)
+    out_ref, token_ref, w_ref, sems = refs[n:]
+    mats, hidden, width = w_ref.shape
+    copies = [pltpu.make_async_copy(w_hbm.at[m], w_ref.at[m], sems.at[m]) for m in range(mats)]
+    for copy in copies:
+        copy.start()
+    xs, ys, gates = views(refs[:n], kinds, count)
+    token_ref[...] = jnp.zeros_like(token_ref)
+    parts = []
+    for k, right in enumerate((joined(xs), joined(xs), joined(ys))):
+        copies[k].wait()
+        parts.append(contract_last(w_ref[k], right))
+    gate, up, down = parts
+    for k in range(gate.shape[1] // count):
+        side = slice(k * count, (k + 1) * count)
+        for m, part in ((2 * k, gate), (2 * k + 1, up), (gate.shape[1] // count * 2 + k, down)):
+            out_ref[m * hidden : (m + 1) * hidden, :] = part[:, side].astype(jnp.bfloat16)
+
+
+def start_partials(weights, chunk, rows, count):
+    mats, hidden, width = weights.shape
+    kinds = kinds_of(chunk)
+    total = rows * hidden * count
+    return pl.pallas_call(
+        functools.partial(start_kernel, kinds, count),
+        in_specs=[in_hbm()] + [whole()] * len(kinds),
+        out_specs=[whole()] * 3,
         out_shape=[
             jax.ShapeDtypeStruct((rows * hidden, count), jnp.bfloat16),
             jax.ShapeDtypeStruct((8, 128), jnp.float32),
+            jax.ShapeDtypeStruct(weights.shape, weights.dtype),
         ],
-        compiler_params=params(),
-        cost_estimate=cost(2 * rows * hidden * count * width, 6 * rows * hidden * count),
-    )(weights, after, *values_of(chunk))
+        scratch_shapes=[pltpu.SemaphoreType.DMA((mats,))],
+        compiler_params=params(),
+        cost_estimate=cost(2 * total * width, 6 * total),
+    )(keep_hbm(weights), *values_of(chunk))
 
 
 def gate_row(expert_ref, gates):
@@ -302,26 +341,40 @@
     return rows[0] if len(rows) == 1 else jnp.concatenate(rows, 1)
 
 
-def hidden_grads(gate, pairs):
+def summed(pairs):
     parts = []
     for own, *got in pairs:
         part = own[...].astype(jnp.float32)
         parts.append(part + got[0][...].astype(jnp.float32) if got else part)
-    total = parts[0] if len(parts) == 1 else jnp.concatenate(parts, 0)
+    return parts[0] if len(parts) == 1 else jnp.concatenate(parts, 0)
+
+
+def beside(total, hidden, firsts):
+    parts = [total[first * hidden : (first + 1) * hidden] for first in firsts]
+    return jnp.concatenate(parts, 1)
+
+
+def activation(hg, hu, gate):
+    sig = jax.nn.sigmoid(hg)
+    silu = hg * sig
+    return sig, silu, (gate * (silu * hu)).astype(jnp.bfloat16)
+
+
+def hidden_slopes(hg, hu, sig, silu, dact):
+    dhg = (dact * hu * sig * (1.0 + hg * (1.0 - sig))).astype(jnp.bfloat16)
+    dhu = (dact * silu).astype(jnp.bfloat16)
+    return dhg, dhu
+
+
+def hidden_grads(gate, pairs):
+    total = summed(pairs)
     blocks = gate.shape[1] // total.shape[1]
     hidden = total.shape[0] // (3 * blocks)
-    row = lambda first: total[first * hidden : (first + 1) * hidden]
-    side = lambda firsts: jnp.concatenate([row(first) for first in firsts], 1)
-    hg = side(range(0, 2 * blocks, 2))
-    hu = side(range(1, 2 * blocks, 2))
-    down = side(range(2 * blocks, 3 * blocks))
-    dact = gate * down
-    sig = jax.nn.sigmoid(hg)
-    silu = hg * sig
-    act = (gate * (silu * hu)).astype(jnp.bfloat16)
-    dhg = (dact * hu * sig * (1.0 + hg * (1.0 - sig))).astype(jnp.bfloat16)
-    dhu = (dact * silu).astype(jnp.bfloat16)
-    return dhg, dhu, act
+    hg = beside(total, hidden, range(0, 2 * blocks, 2))
+    hu = beside(total, hidden, range(1, 2 * blocks, 2))
+    dact = gate * beside(total, hidden, range(2 * blocks, 3 * blocks))
+    sig, silu, act = activation(hg, hu, gate)
+    return (*hidden_slopes(hg, hu, sig, silu, dact), act)
 
 
 def plain(left, right):
@@ -330,10 +383,12 @@
     )
 
 
-def onward_kernel(kinds, count, core_ref, expert_ref, after_ref, *refs):
+def onward_kernel(kinds, core_ref, expert_ref, after_ref, *refs):
     own, got, near_own, near_got, x0_ref, x1_ref, y0_ref, y1_ref = refs[:8]
-    blocks = refs[8 : 8 + len(kinds)]
-    both_ref, out_ref, left_ref, sum_ref = refs[8 + len(kinds) :]
+    both_ref, out_ref, first_ref, sum_ref, gate_ref = refs[8 + len(kinds) :]
+    count = x0_ref.shape[0]
+    gates = views(refs[8 : 8 + len(kinds)], kinds, count)[2]
+    gate_ref[...] = jnp.broadcast_to(gate_row(expert_ref, gates), gate_ref.shape)
     both_ref[0, 0:count, :] = x0_ref[...]
     both_ref[1, 0:count, :] = x1_ref[...]
     both_ref[0, count:, :] = y0_ref[...]
@@ -351,25 +406,23 @@
     def _():
         pick(x1_ref, y1_ref)
 
+    first_ref[...] = own[...].astype(jnp.float32) + got[...].astype(jnp.float32)
     sum_ref[...] = near_own[...].astype(jnp.float32) + near_got[...].astype(jnp.float32)
-    xs, ys, gates = views(blocks, kinds, count)
-    for m, value in enumerate(hidden_grads(gate_row(expert_ref, gates), [(own, got)])):
-        left_ref[m] = value
-
-
-def pick_onward(core, expert, after, pair, near_pair, near_x, near_y, chunk, count):
-    kinds = kinds_of(chunk)
+
+
+def pick_onward(core, expert, after, pair, near_pair, near_x, near_y, chunk):
     rows, width = near_x[0].shape[0] + near_y[0].shape[0], near_x[0].shape[1]
     operands = [*pair, *near_pair, *near_x, *near_y, *values_of(chunk)]
     return pl.pallas_call(
-        functools.partial(onward_kernel, kinds, count),
+        functools.partial(onward_kernel, kinds_of(chunk)),
         in_specs=[smem(), smem(), unread()] + [whole()] * len(operands),
-        out_specs=[whole()] * 4,
+        out_specs=[whole()] * 5,
         out_shape=[
             jax.ShapeDtypeStruct((2, rows, width), jnp.bfloat16),
             jax.ShapeDtypeStruct((rows, width), jnp.bfloat16),
-            jax.ShapeDtypeStruct((3, pair[0].shape[0] // 6, 2 * count), jnp.bfloat16),
+            jax.ShapeDtypeStruct(pair[0].shape, jnp.float32),
             jax.ShapeDtypeStruct(near_pair[0].shape, jnp.float32),
+            jax.ShapeDtypeStruct((8, 2 * near_x[0].shape[0]), jnp.float32),
         ],
         compiler_params=params(),
         cost_estimate=cost(1000, 8 * near_x[0].size),
@@ -395,32 +448,31 @@
     )(after, value)
 
 
-def first_kernel(kinds, count, after_ref, left_ref, *refs):
+def first_kernel(kinds, count, gate_ref, after_ref, sum_ref, *refs):
     n = len(kinds)
     xs, ys, gates = views(refs[:n], kinds, count)
     out_ref, token_ref = refs[n:]
+    lefts = hidden_grads(gate_ref[0:1, :], [(sum_ref,)])
     x = joined(xs)
-    out_ref[0] = plain(left_ref[0], x)
-    out_ref[1] = plain(left_ref[1], x)
-    out_ref[2] = plain(left_ref[2], joined(ys))
+    for m, right in enumerate((x, x, joined(ys))):
+        out_ref[m] = plain(lefts[m], right)
     token_ref[...] = jnp.zeros_like(token_ref)
 
 
-def first_grads(after, left, chunk, count):
+def first_grads(gate, after, total, chunk, hidden, count):
     kinds = kinds_of(chunk)
-    mats, hidden, tokens = left.shape
     width = chunk[0][1].shape[-1]
     return pl.pallas_call(
         functools.partial(first_kernel, kinds, count),
-        in_specs=[unread()] + [whole()] * (1 + len(kinds)),
+        in_specs=[whole(), unread()] + [whole()] * (1 + len(kinds)),
         out_specs=[whole()] * 2,
         out_shape=[
-            jax.ShapeDtypeStruct((mats, hidden, width), jnp.float32),
+            jax.ShapeDtypeStruct((3, hidden, width), jnp.float32),
             jax.ShapeDtypeStruct((8, 128), jnp.float32),
         ],
         compiler_params=params(),
-        cost_estimate=cost(6 * hidden * width * tokens, 12 * hidden * width),
-    )(after, left, *values_of(chunk))
+        cost_estimate=cost(2 * total.size * width, 12 * hidden * width),
+    )(gate, after, total, *values_of(chunk))
 
 
 def grad_kernel(kinds, count, expert_ref, sum_ref, own, got, *refs):
@@ -450,58 +502,98 @@
     )(expert, *operands)
 
 
-def last_kernel(kinds, count, expert_ref, own, got, *refs):
+def adam(grad, first_ref, second_ref, one_ref, two_ref, step_ref):
+    moment_one = beta_one * first_ref[0].astype(jnp.float32) + (1.0 - beta_one) * grad
+    moment_two = beta_two * second_ref[0].astype(jnp.float32) + (1.0 - beta_two) * (grad * grad)
+    one_ref[0] = moment_one.astype(jnp.bfloat16)
+    two_ref[0] = moment_two.astype(jnp.bfloat16)
+    scaled = moment_two * (1.0 / (1.0 - beta_two**step_count))
+    below = scaled * lax.rsqrt(scaled) + epsilon
+    guess = pl.reciprocal(below, approx=True)
+    inverse = guess * (2.0 - below * guess)
+    step = moment_one * (1.0 / (1.0 - beta_one**step_count)) * inverse
+    step_ref[0] = step.astype(jnp.bfloat16)
+
+
+def gate_up(own, got):
+    total = summed([(own, got)])
+    hidden = total.shape[0] // 4
+    return beside(total, hidden, (0, 2)), beside(total, hidden, (1, 3))
+
+
+def down_kernel(kinds, count, expert_ref, own, got, *refs):
     n = len(kinds)
+    acc_ref, first_ref, second_ref, one_ref, two_ref, step_ref, act_ref = refs[n:]
     xs, ys, gates = views(refs[:n], kinds, count)
-    acc_ref, first_ref, second_ref, one_ref, two_ref, step_ref, left_ref = refs[n:]
+
+    @pl.when(pl.program_id(0) == 0)
+    def _():
+        act_ref[...] = activation(*gate_up(own, got), gate_row(expert_ref, gates))[2]
+
+    grad = acc_ref[0] + plain(act_ref[...], joined(ys))
+    adam(grad, first_ref, second_ref, one_ref, two_ref, step_ref)
+
+
+def down_update(expert, pair, chunk, acc, first_moment, second_moment, count, columns):
+    kinds = kinds_of(chunk)
+    mats, hidden, width = first_moment.shape
+    tile = pl.BlockSpec((1, hidden, columns), lambda j: (2, 0, j))
+    strip = lambda value: pl.BlockSpec((value.shape[0], columns), lambda j: (0, j))
+    return pl.pallas_call(
+        functools.partial(down_kernel, kinds, count),
+        grid=(width // columns,),
+        in_specs=[smem(), whole(), whole()]
+        + [strip(value) for value in values_of(chunk)]
+        + [tile] * 3,
+        out_specs=[tile] * 3,
+        out_shape=[jax.ShapeDtypeStruct(first_moment.shape, jnp.bfloat16)] * 3,
+        scratch_shapes=[pltpu.VMEM((hidden, 2 * count), jnp.bfloat16)],
+        compiler_params=params(),
+        cost_estimate=cost(4 * hidden * width * count, 14 * hidden * width),
+    )(expert, *pair, *values_of(chunk), acc, first_moment, second_moment)
+
+
+def slopes_kernel(kinds, count, expert_ref, own, got, own_d, got_d, *refs):
+    n = len(kinds)
+    acc_ref, first_ref, second_ref = refs[n : n + 3]
+    one_ref, two_ref, step_ref, left_ref = refs[n + 6 :]
+    xs, ys, gates = views(refs[:n], kinds, count)
     m = pl.program_id(1)
 
-    @pl.when((m == 0) & (pl.program_id(0) == 0))
+    @pl.when((pl.program_id(0) == 0) & (m == 0))
     def _():
-        for k, value in enumerate(hidden_grads(gate_row(expert_ref, gates), [(own, got)])):
-            left_ref[k] = value
-
-    def finish(right):
-        grad = acc_ref[0] + plain(left_ref[m], right)
-        moment_one = beta_one * first_ref[0].astype(jnp.float32) + (1.0 - beta_one) * grad
-        moment_two = beta_two * second_ref[0].astype(jnp.float32) + (1.0 - beta_two) * (grad * grad)
-        one_ref[0] = moment_one.astype(jnp.bfloat16)
-        two_ref[0] = moment_two.astype(jnp.bfloat16)
-        scaled = moment_two * (1.0 / (1.0 - beta_two**step_count))
-        below = scaled * lax.rsqrt(scaled) + epsilon
-        guess = pl.reciprocal(below, approx=True)
-        inverse = guess * (2.0 - below * guess)
-        step = moment_one * (1.0 / (1.0 - beta_one**step_count)) * inverse
-        step_ref[0] = step.astype(jnp.bfloat16)
-
-    @pl.when(m < 2)
-    def _():
-        finish(joined(xs))
-
-    @pl.when(m == 2)
-    def _():
-        finish(joined(ys))
-
-
-def last_grads(expert, own, got, chunk, acc, first_moment, second_moment, count, columns):
+        gate = gate_row(expert_ref, gates)
+        hg, hu = gate_up(own, got)
+        down = summed([(own_d, got_d)])
+        dact = gate * beside(down, down.shape[0] // 2, (0, 1))
+        sig, silu, act = activation(hg, hu, gate)
+        left_ref[0], left_ref[1] = hidden_slopes(hg, hu, sig, silu, dact)
+
+    grad = acc_ref[0] + plain(left_ref[m], joined(xs))
+    adam(grad, first_ref, second_ref, one_ref, two_ref, step_ref)
+
+
+def slopes_update(expert, pair, down_pair, chunk, acc, moments, done, count, columns):
     kinds = kinds_of(chunk)
-    blocks = values_of(chunk)
-    mats, hidden, width = first_moment.shape
+    mats, hidden, width = acc.shape
     tile = pl.BlockSpec((1, hidden, columns), lambda j, m: (m, 0, j))
-    out = jax.ShapeDtypeStruct(first_moment.shape, jnp.bfloat16)
     strip = lambda value: pl.BlockSpec((value.shape[0], columns), lambda j, m: (0, j))
-    return pl.pallas_call(
-        functools.partial(last_kernel, kinds, count),
-        grid=(width // columns, mats),
-        in_specs=[smem(), whole(), whole()] + [strip(value) for value in blocks] + [tile] * 3,
+    operands = [expert, *pair, *down_pair, *values_of(chunk), acc, *moments, *done]
+    return pl.pallas_call(
+        functools.partial(slopes_kernel, kinds, count),
+        grid=(width // columns, 2),
+        in_specs=[smem()]
+        + [whole()] * 4
+        + [strip(value) for value in values_of(chunk)]
+        + [tile] * 3
+        + [unread()] * 3,
         out_specs=[tile] * 3,
-        out_shape=[out] * 3,
-        scratch_shapes=[pltpu.VMEM((mats, hidden, 2 * count), jnp.bfloat16)],
-        compiler_params=params(),
-        cost_estimate=cost(
-            4 * mats * hidden * width * count, 8 * hidden * width * mats
-        ),
-    )(expert, own, got, *blocks, acc, first_moment, second_moment)
+        out_shape=[jax.ShapeDtypeStruct(acc.shape, jnp.bfloat16)] * 3,
+        input_output_aliases={len(operands) - 3 + k: k for k in range(3)},
+        scratch_shapes=[pltpu.VMEM((2, hidden, 2 * count), jnp.bfloat16)],
+        compiler_params=params(),
+        cost_estimate=cost(8 * hidden * width * count, 28 * hidden * width),
+    )(*operands)
 
 
 def from_masked(value, axis, mask):
@@ -519,37 +611,41 @@
     count = tokens.shape[0]
     width = weights.shape[2]
     slots = -(-experts_total // 16) * 16
-    x_own, y_own, own, weights = pack_own(
-        (place % 2).astype(jnp.int32), expert_ids, gate_probs, tokens, cotangent, weights, slots
+    x_own, y_own, own = pack_own(
+        (place % 2).astype(jnp.int32), expert_ids, gate_probs, tokens, cotangent, width, slots
     )
     other = lambda value: from_masked(value, "dp", 1)
     partner = lambda value: from_masked(value, "expert", 1)
     first = [("xy", own), ("xy", other(own))]
-    send, token = partials(weights, own, first, 6, count)
+    send, token, weights = start_partials(weights, first, 6, count)
     first_pair = (send, partner(send))
     near_x = [from_masked(x_own, "dp", mask) for mask in (2, 4)]
     near_y = [from_masked(y_own, "dp", mask) for mask in (2, 4)]
-    send, token = partials(weights, token, [("x", near_x[0])], 2, count)
+    send, token = partials(weights, token, [("x", near_x[0])], (2,), count)
     near_pair = (send, partner(send))
-    both, picked, left, near_sum = pick_onward(
-        core.astype(jnp.int32), expert, token, first_pair, near_pair, near_x, near_y, first, count
+    both, picked, first_sum, near_sum, gate = pick_onward(
+        core.astype(jnp.int32), expert, token, first_pair, near_pair, near_x, near_y, first
     )
     onward = [(p, p ^ 4 if p % 2 == 0 else p ^ 2) for p in range(n_data)]
     far = lax.ppermute(picked, "dp", onward)
-    acc, token = first_grads(picked, left, first, count)
+    acc, token = first_grads(gate, picked, first_sum, first, weights.shape[1], count)
     swapped = other(both)
     more = [("x", near_x[1]), ("y of xy", both), ("xy", swapped)]
-    send, token = partials(weights, token, more, 10, count)
+    send, token = partials(weights, token, more, (10,), count)
     more_pair = (send, partner(send))
     pieces = passed_on(token, far, (count // 2, count // 2, count // 2, count // 2 + slots))
     pieces = [*pieces, *[other(value) for value in pieces]]
     final = list(zip(("x", "x", "y", "y, gates") * 2, pieces))
-    send, token = partials(weights, token, final, 6, count)
-    got = partner(send)
+    send, send_d, token = partials(weights, token, final, (4, 2), count)
+    pair, down_pair = (send, partner(send)), (send_d, partner(send_d))
     near = [("xy", both), ("xy", swapped)]
     acc = add_grads(expert, near_sum, more_pair, near, acc, count)
+    moments = (first_moment, second_moment)
+    final_y = [block for block in final if block[0] != "x"]
+    final_x = [block for block in final if block[0] != "y"]
+    done = down_update(expert, pair, final_y, acc, *moments, count, width // 2)
     return tuple(
-        last_grads(expert, send, got, final, acc, first_moment, second_moment, count, width // 2)
+        slopes_update(expert, pair, down_pair, final_x, acc, moments, done, count, width // 2)
     )
 
 

time: 51 us -> 50.7 us (level)
  Pallas kernels: 13.8 us -> 15.5 us
  waiting for transfers between devices: 20.9 us -> 19.5 us
  starting transfers between devices: 15.3 us -> 14.7 us
    pallas_call x4 -> x6, Pallas kernels: 9.23 us -> 12.1 us  [the longest x1 3.47 us: slopes_update(): pl.pallas_call(functools.partial(slopes_kernel, kinds, count), grid=(widt...]
    ppermute x14 -> x15, waiting for transfers between devices: 16.6 us -> 15.2 us  [from_masked(): return lax.ppermute(value, axis, pairs)]
    pallas_call x4 -> x3, Pallas kernels: 3.55 us -> 2.29 us  [partials(): pl.pallas_call(functools.partial(partial_kernel, kinds, count), in_specs=...]
    ppermute x1, starting transfers between devices: 1.58 us -> 0.51 us  [dense_plan(): far = lax.ppermute(picked, 'dp', onward)]
    ppermute x14 -> x15, starting transfers between devices: 13.7 us -> 14.2 us  [from_masked(): return lax.ppermute(value, axis, pairs)]
  transfers between devices with their start and end apart: 15 -> 16, of which waited for: 9 -> 10; matrix products, arithmetic and copies ran while one was open for 0% -> 0% of each run, Pallas kernels for 10% -> 18%
where the time goes in v5:
time: 50.7 us; the launch traced here: 50.5 us
  waiting for transfers between devices  19.5 us (38%)
  Pallas kernels  15.5 us (31%)
  starting transfers between devices  14.7 us (29%)
  between operations  0.74 us (1%)
    ppermute x15, waiting for transfers between devices, from_masked(): return lax.ppermute(value, axis, pairs)  15.2 us
    ppermute x15, starting transfers between devices, from_masked(): return lax.ppermute(value, axis, pairs)  14.2 us
    ppermute x1, waiting for transfers between devices, dense_plan(): far = lax.ppermute(picked, 'dp', onward)  4.33 us
    pallas_call x1, Pallas kernels, slopes_update(): pl.pallas_call(functools.partial(slopes_kernel, kinds, count), grid=(widt...  3.47 us
    pallas_call x1, Pallas kernels, start_partials(): pl.pallas_call(functools.partial(start_kernel, kinds, count), in_specs=[i...  2.95 us
    pallas_call x3, Pallas kernels, partials(): pl.pallas_call(functools.partial(partial_kernel, kinds, count), in_specs=...  2.29 us
    pallas_call x1, Pallas kernels, down_update(): pl.pallas_call(functools.partial(down_kernel, kinds, count), grid=(width...  2.04 us
    pallas_call x1, Pallas kernels, pack_own(): pl.pallas_call(pack_kernel, in_specs=[smem()] + [in_hbm()] * 4, out_specs...  1.9 us
  transfers between devices with their start and end apart: 16, of which 10 were waited for; matrix products, arithmetic and copies ran while one was open for 0% of the time, Pallas kernels for 18%

profile of v5, /device:TPU:0, one launch (start us, length us, event | category | flops | bytes accessed | tf_op | source)
XLA Modules:
  0.0 50.5 jit_solution(2513906228944592006)
XLA Ops:
  0.6 1.9 %shard_map.94 = (bf16[128,1024]{1,0:T(8,128)(2,1)}, bf16[144,1024]{1,0:T(8,128)(2,1)}, bf16[272,1024]{1,0:T(8,128)(2,1)S(1)}) custom-call(s32[1]{0:T(128)} %bitcast.1.replica_ref, s32[4,128]{1,0:T(4,128)} %bitcast.5, bf16[4,128]{1,0:T(4,128)(2,1)} %bitcast.6, bf16[128,2048]{1,0:T(8,128)(2,1)} %tokens_ref.1, bf16[128,2048]{1,0:T(8,128)(2,1)} %cot_ref.1), custom_call_target="tpu_custom_call" | custom-call | flops 1000 | bytes 1048576 | tf_op jit(solution)/shard_map/pallas_call | solution.py:204
  2.5 0.5 %collective-permute-start = (bf16[272,1024]{1,0:T(8,128)(2,1)S(1)}, bf16[272,1024]{1,0:T(8,128)(2,1)S(1)}, u32[]{:S(2)}, u32[]{:S(2)}) collective-permute-start(bf16[272,1024]{1,0:T(8,128)(2,1)S(1)} %get-tuple-element.29.refs_0_.refs_8_), channel_id=1, source_target_pairs={{0,1},{1,0},{2,3},{3,2},{4,5},{5,4},{6,7},{7,6},{8,9},{9,8},{10,11... | collective-permute-start | bytes 1671176 | tf_op jit(solution)/shard_map/ppermute | solution.py:601
  3.1 2.6 %collective-permute-start.1 = (bf16[128,1024]{1,0:T(8,128)(2,1)}, bf16[128,1024]{1,0:T(8,128)(2,1)S(1)}, u32[]{:S(2)}, u32[]{:S(2)}) collective-permute-start(bf16[128,1024]{1,0:T(8,128)(2,1)} %get-tuple-element.32), channel_id=1, source_target_pairs={{0,2},{1,3},{2,0},{3,1},{4,6},{5,7},{6,4},{7,5},{8,10},{9,11},{10,... | collective-permute-start | bytes 786440 | tf_op jit(solution)/shard_map/ppermute | solution.py:601
  5.6 1.5 %collective-permute-start.6 = (bf16[144,1024]{1,0:T(8,128)(2,1)}, bf16[144,1024]{1,0:T(8,128)(2,1)S(1)}, u32[]{:S(2)}, u32[]{:S(2)}) collective-permute-start(bf16[144,1024]{1,0:T(8,128)(2,1)} %get-tuple-element.36), channel_id=1, source_target_pairs={{0,4},{1,5},{2,6},{3,7},{4,0},{5,1},{6,2},{7,3},{8,12},{9,13},{10,... | collective-permute-start | bytes 884744 | tf_op jit(solution)/shard_map/ppermute | solution.py:601
  7.2 0.5 %collective-permute-start.5 = (bf16[144,1024]{1,0:T(8,128)(2,1)}, bf16[144,1024]{1,0:T(8,128)(2,1)S(1)}, u32[]{:S(2)}, u32[]{:S(2)}) collective-permute-start(bf16[144,1024]{1,0:T(8,128)(2,1)} %get-tuple-element.36), channel_id=1, source_target_pairs={{0,2},{1,3},{2,0},{3,1},{4,6},{5,7},{6,4},{7,5},{8,10},{9,11},{10,... | collective-permute-start | bytes 884744 | tf_op jit(solution)/shard_map/ppermute | solution.py:601
  7.7 2.9 %shard_map.95 = (bf16[1152,128]{1,0:T(8,128)(2,1)}, f32[8,128]{1,0:T(8,128)S(1)}, bf16[3,192,1024]{2,1,0:T(8,128)(2,1)S(1)}) custom-call(bf16[3,192,1024]{2,1,0:T(8,128)(2,1)} %w_hbm.1, bf16[272,1024]{1,0:T(8,128)(2,1)S(1)} %get-tuple-element.29.refs_0_.refs_8_, bf16[272,1024]{1,0:T(8,128)(2,1)S(1)} %collective-permute-done.refs_1_.refs_9_), custom_call_target="tpu_custom_call" | custom-call | flops 301989888 | bytes 884736 | tf_op jit(solution)/shard_map/pallas_call | solution.py:320
  10.6 1.6 %collective-permute-start.2 = (bf16[1152,128]{1,0:T(8,128)(2,1)}, bf16[1152,128]{1,0:T(8,128)(2,1)}, u32[]{:S(2)}, u32[]{:S(2)}) collective-permute-start(bf16[1152,128]{1,0:T(8,128)(2,1)} %get-tuple-element.34.refs_0_), channel_id=1, source_target_pairs={{0,8},{8,0},{16,24},{24,16},{1,9},{9,1},{17,25},{25,17},{2,10},{10... | collective-permute-start | bytes 884744 | tf_op jit(solution)/shard_map/ppermute | solution.py:601
  13.4 2.1 %collective-permute-start.3 = (bf16[384,128]{1,0:T(8,128)(2,1)S(1)}, bf16[384,128]{1,0:T(8,128)(2,1)}, u32[]{:S(2)}, u32[]{:S(2)}) collective-permute-start(bf16[384,128]{1,0:T(8,128)(2,1)S(1)} %get-tuple-element.35.refs_2_), channel_id=1, source_target_pairs={{0,8},{8,0},{16,24},{24,16},{1,9},{9,1},{17,25},{25,17},{2,10},{10... | collective-permute-start | bytes 294920 | tf_op jit(solution)/shard_map/ppermute | solution.py:601
  15.5 5.1 %collective-permute-done.4.refs_5_.refs_0_ = bf16[128,1024]{1,0:T(8,128)(2,1)S(1)} collective-permute-done((bf16[128,1024]{1,0:T(8,128)(2,1)}, bf16[128,1024]{1,0:T(8,128)(2,1)S(1)}, u32[]{:S(2)}, u32[]{:S(2)}) %collective-permute-start.4) | collective-permute-done | bytes 262176 | tf_op jit(solution)/shard_map/ppermute | solution.py:601
  20.5 1.1 %collective-permute-done.3.refs_3_ = bf16[384,128]{1,0:T(8,128)(2,1)} collective-permute-done((bf16[384,128]{1,0:T(8,128)(2,1)S(1)}, bf16[384,128]{1,0:T(8,128)(2,1)}, u32[]{:S(2)}, u32[]{:S(2)}) %collective-permute-start.3) | collective-permute-done | bytes 98336 | tf_op jit(solution)/shard_map/ppermute | solution.py:601
  21.7 1.3 %shard_map.97 = (bf16[2,272,1024]{2,1,0:T(8,128)(2,1)S(1)}, bf16[272,1024]{1,0:T(8,128)(2,1)S(1)}, f32[1152,128]{1,0:T(8,128)S(1)}, f32[384,128]{1,0:T(8,128)S(1)}, f32[8,256]{1,0:T(8,128)S(1)}) custom-call(s32[1]{0:T(128)} %bitcast.4.core_ref, s32[1]{0:T(128)} %bitcast.expert_ref, f32[8,128]{1,0:T(8,128)S(1)} %get-tuple-element.33.after_ref, ...), custom_call_target="tpu_custom_call" | custom-call | flops 1000 | bytes 1048576 | tf_op jit(solution)/shard_map/pallas_call | solution.py:416
  23.5 0.5 %shard_map.98 = (f32[3,192,1024]{2,1,0:T(8,128)S(1)}, f32[8,128]{1,0:T(8,128)S(1)}) custom-call(f32[8,256]{1,0:T(8,128)S(1)} %get-tuple-element.37.gate_ref, bf16[272,1024]{1,0:T(8,128)(2,1)S(1)} %get-tuple-element.38.after_ref, f32[1152,128]{1,0:T(8,128)S(1)} %get-tuple-element.39.sum_ref, bf16[272,1024]{1,0:T(8,128)(2,1)S(1)} %get-tuple-element.29.refs_0_.refs_8_, ...), custom_call_target="tpu_custom_call" | custom-call | flops 301989888 | bytes 2359296 | tf_op jit(solution)/shard_map/pallas_call | solution.py:465
  24.0 1.7 %collective-permute-done.7.refs_2_.refs_1_ = bf16[2,272,1024]{2,1,0:T(8,128)(2,1)S(1)} collective-permute-done((bf16[2,272,1024]{2,1,0:T(8,128)(2,1)S(1)}, bf16[2,272,1024]{2,1,0:T(8,128)(2,1)S(1)}, u32[]{:S(2)}, u32[]{:S(2)}) %collective-permute-start.7) | collective-permute-done | bytes 1114144 | tf_op jit(solution)/shard_map/ppermute | solution.py:601
  25.7 0.9 %shard_map.99 = (bf16[1920,128]{1,0:T(8,128)(2,1)S(1)}, f32[8,128]{1,0:T(8,128)S(1)}) custom-call(bf16[3,192,1024]{2,1,0:T(8,128)(2,1)S(1)} %get-tuple-element.30.w_ref, f32[8,128]{1,0:T(8,128)S(1)} %get-tuple-element.40.after_ref, bf16[128,1024]{1,0:T(8,128)(2,1)S(1)} %collective-permute-done.4.refs_5_.refs_0_, ...), custom_call_target="tpu_custom_call" | custom-call | flops 503316480 | bytes 1474560 | tf_op jit(solution)/shard_map/pallas_call | solution.py:285
  26.6 1.6 %collective-permute-start.15 = (bf16[1920,128]{1,0:T(8,128)(2,1)S(1)}, bf16[1920,128]{1,0:T(8,128)(2,1)S(1)}, u32[]{:S(2)}, u32[]{:S(2)}) collective-permute-start(bf16[1920,128]{1,0:T(8,128)(2,1)S(1)} %get-tuple-element.50.own), channel_id=1, source_target_pairs={{0,8},{8,0},{16,24},{24,16},{1,9},{9,1},{17,25},{25,17},{2,10},{10... | collective-permute-start | bytes 1474568 | tf_op jit(solution)/shard_map/ppermute | solution.py:601
  28.3 4.3 %collective-permute-done.8.in_ref = bf16[272,1024]{1,0:T(8,128)(2,1)S(1)} collective-permute-done((bf16[272,1024]{1,0:T(8,128)(2,1)S(1)}, bf16[272,1024]{1,0:T(8,128)(2,1)S(1)}, u32[]{:S(2)}, u32[]{:S(2)}) %collective-permute-start.8) | collective-permute-done | bytes 557088 | tf_op jit(solution)/shard_map/ppermute | solution.py:630
  33.7 0.6 %collective-permute-done.9.refs_4_.refs_3_ = bf16[64,1024]{1,0:T(8,128)(2,1)S(1)} collective-permute-done((bf16[64,1024]{1,0:T(8,128)(2,1)S(1)}, bf16[64,1024]{1,0:T(8,128)(2,1)S(1)}, u32[]{:S(2)}, u32[]{:S(2)}) %collective-permute-start.9) | collective-permute-done | bytes 131104 | tf_op jit(solution)/shard_map/ppermute | solution.py:601
  34.8 1.1 %shard_map.101 = (bf16[768,128]{1,0:T(8,128)(2,1)S(1)}, bf16[384,128]{1,0:T(8,128)(2,1)S(1)}, f32[8,128]{1,0:T(8,128)}) custom-call(bf16[3,192,1024]{2,1,0:T(8,128)(2,1)S(1)} %get-tuple-element.30.w_ref, f32[8,128]{1,0:T(8,128)S(1)} %get-tuple-element.42.after_ref, bf16[64,1024]{1,0:T(8,128)(2,1)S(1)} %get-tuple-element.43.refs_0_, ...), custom_call_target="tpu_custom_call" | custom-call | flops 301989888 | bytes 884736 | tf_op jit(solution)/shard_map/pallas_call | solution.py:285
  35.8 1.6 %collective-permute-start.13 = (bf16[768,128]{1,0:T(8,128)(2,1)S(1)}, bf16[768,128]{1,0:T(8,128)(2,1)S(1)}, u32[]{:S(2)}, u32[]{:S(2)}) collective-permute-start(bf16[768,128]{1,0:T(8,128)(2,1)S(1)} %get-tuple-element.47.own), channel_id=1, source_target_pairs={{0,8},{8,0},{16,24},{24,16},{1,9},{9,1},{17,25},{25,17},{2,10},{10... | collective-permute-start | bytes 589832 | tf_op jit(solution)/shard_map/ppermute | solution.py:601
  37.8 2.9 %collective-permute-done.15.got = bf16[1920,128]{1,0:T(8,128)(2,1)S(1)} collective-permute-done((bf16[1920,128]{1,0:T(8,128)(2,1)S(1)}, bf16[1920,128]{1,0:T(8,128)(2,1)S(1)}, u32[]{:S(2)}, u32[]{:S(2)}) %collective-permute-start.15) | collective-permute-done | bytes 491552 | tf_op jit(solution)/shard_map/ppermute | solution.py:601
  40.8 1.0 %shard_map.102.refs_4_.refs_6_ = f32[3,192,1024]{2,1,0:T(8,128)S(1)} custom-call(s32[1]{0:T(128)} %bitcast.expert_ref, f32[384,128]{1,0:T(8,128)S(1)} %get-tuple-element.49.sum_ref, bf16[1920,128]{1,0:T(8,128)(2,1)S(1)} %get-tuple-element.50.own, bf16[1920,128]{1,0:T(8,128)(2,1)S(1)} %collective-permute-done.15.got, ...), custom_call_target="tpu_custom_call", output_to_operand_aliasing={{}: (6, {})} | custom-call | flops 603979776 | bytes 4718592 | tf_op jit(solution)/shard_map/pallas_call | solution.py:492
  41.8 3.2 %collective-permute-done.13.got = bf16[768,128]{1,0:T(8,128)(2,1)S(1)} collective-permute-done((bf16[768,128]{1,0:T(8,128)(2,1)S(1)}, bf16[768,128]{1,0:T(8,128)(2,1)S(1)}, u32[]{:S(2)}, u32[]{:S(2)}) %collective-permute-start.13) | collective-permute-done | bytes 196640 | tf_op jit(solution)/shard_map/ppermute | solution.py:601
  45.0 2.0 %shard_map.103 = (bf16[3,192,1024]{2,1,0:T(8,128)(2,1)}, bf16[3,192,1024]{2,1,0:T(8,128)(2,1)}, bf16[3,192,1024]{2,1,0:T(8,128)(2,1)}) custom-call(s32[1]{0:T(128)} %bitcast.expert_ref, bf16[768,128]{1,0:T(8,128)(2,1)S(1)} %get-tuple-element.47.own, bf16[768,128]{1,0:T(8,128)(2,1)S(1)} %collective-permute-done.13.got, ...), custom_call_target="tpu_custom_call" | custom-call | flops 100663296 | bytes 2752512 | tf_op jit(solution)/shard_map/pallas_call | solution.py:542
  47.0 3.5 %shard_map.104 = (bf16[3,192,1024]{2,1,0:T(8,128)(2,1)}, bf16[3,192,1024]{2,1,0:T(8,128)(2,1)}, bf16[3,192,1024]{2,1,0:T(8,128)(2,1)}) custom-call(s32[1]{0:T(128)} %bitcast.expert_ref, bf16[768,128]{1,0:T(8,128)(2,1)S(1)} %get-tuple-element.47.own, ...), custom_call_target="tpu_custom_call", output_to_operand_aliasing={{0}: (14, {}), {1}: (15, {}), {2}: (16, {})} | custom-call | flops 201326592 | bytes 5505024 | tf_op jit(solution)/shard_map/pallas_call | solution.py:582
  (23 shorter events, 3.7 us)
Async XLA Ops:
  2.5 5.1 %collective-permute-start = (bf16[272,1024]{1,0:T(8,128)(2,1)S(1)}, bf16[272,1024]{1,0:T(8,128)(2,1)S(1)}, u32[]{:S(2)}, u32[]{:S(2)}) collective-permute-start(bf16[272,1024]{1,0:T(8,128)(2,1)S(1)} %get-tuple-element.29.refs_0_.refs_8_), channel_id=1, source_target_pairs={{0,1},{1,0},{2,3},{3,2},{4,5},{5,4},{6,7},{7,6},{8,9},{9,8},{10,11... | collective-permute-start | bytes 1671176 | tf_op jit(solution)/shard_map/ppermute | solution.py:601
  3.1 9.9 %collective-permute-start.1 = (bf16[128,1024]{1,0:T(8,128)(2,1)}, bf16[128,1024]{1,0:T(8,128)(2,1)S(1)}, u32[]{:S(2)}, u32[]{:S(2)}) collective-permute-start(bf16[128,1024]{1,0:T(8,128)(2,1)} %get-tuple-element.32), channel_id=1, source_target_pairs={{0,2},{1,3},{2,0},{3,1},{4,6},{5,7},{6,4},{7,5},{8,10},{9,11},{10,... | collective-permute-start | bytes 786440 | tf_op jit(solution)/shard_map/ppermute | solution.py:601
  5.6 14.9 %collective-permute-start.6 = (bf16[144,1024]{1,0:T(8,128)(2,1)}, bf16[144,1024]{1,0:T(8,128)(2,1)S(1)}, u32[]{:S(2)}, u32[]{:S(2)}) collective-permute-start(bf16[144,1024]{1,0:T(8,128)(2,1)} %get-tuple-element.36), channel_id=1, source_target_pairs={{0,4},{1,5},{2,6},{3,7},{4,0},{5,1},{6,2},{7,3},{8,12},{9,13},{10,... | collective-permute-start | bytes 884744 | tf_op jit(solution)/shard_map/ppermute | solution.py:601
  7.2 13.4 %collective-permute-start.5 = (bf16[144,1024]{1,0:T(8,128)(2,1)}, bf16[144,1024]{1,0:T(8,128)(2,1)S(1)}, u32[]{:S(2)}, u32[]{:S(2)}) collective-permute-start(bf16[144,1024]{1,0:T(8,128)(2,1)} %get-tuple-element.36), channel_id=1, source_target_pairs={{0,2},{1,3},{2,0},{3,1},{4,6},{5,7},{6,4},{7,5},{8,10},{9,11},{10,... | collective-permute-start | bytes 884744 | tf_op jit(solution)/shard_map/ppermute | solution.py:601
  10.6 11.0 %collective-permute-start.2 = (bf16[1152,128]{1,0:T(8,128)(2,1)}, bf16[1152,128]{1,0:T(8,128)(2,1)}, u32[]{:S(2)}, u32[]{:S(2)}) collective-permute-start(bf16[1152,128]{1,0:T(8,128)(2,1)} %get-tuple-element.34.refs_0_), channel_id=1, source_target_pairs={{0,8},{8,0},{16,24},{24,16},{1,9},{9,1},{17,25},{25,17},{2,10},{10... | collective-permute-start | bytes 884744 | tf_op jit(solution)/shard_map/ppermute | solution.py:601
  12.3 8.3 %collective-permute-start.4 = (bf16[128,1024]{1,0:T(8,128)(2,1)}, bf16[128,1024]{1,0:T(8,128)(2,1)S(1)}, u32[]{:S(2)}, u32[]{:S(2)}) collective-permute-start(bf16[128,1024]{1,0:T(8,128)(2,1)} %get-tuple-element.32), channel_id=1, source_target_pairs={{0,4},{1,5},{2,6},{3,7},{4,0},{5,1},{6,2},{7,3},{8,12},{9,13},{10,... | collective-permute-start | bytes 786440 | tf_op jit(solution)/shard_map/ppermute | solution.py:601
  13.4 8.3 %collective-permute-start.3 = (bf16[384,128]{1,0:T(8,128)(2,1)S(1)}, bf16[384,128]{1,0:T(8,128)(2,1)}, u32[]{:S(2)}, u32[]{:S(2)}) collective-permute-start(bf16[384,128]{1,0:T(8,128)(2,1)S(1)} %get-tuple-element.35.refs_2_), channel_id=1, source_target_pairs={{0,8},{8,0},{16,24},{24,16},{1,9},{9,1},{17,25},{25,17},{2,10},{10... | collective-permute-start | bytes 294920 | tf_op jit(solution)/shard_map/ppermute | solution.py:601
  22.9 2.8 %collective-permute-start.7 = (bf16[2,272,1024]{2,1,0:T(8,128)(2,1)S(1)}, bf16[2,272,1024]{2,1,0:T(8,128)(2,1)S(1)}, u32[]{:S(2)}, u32[]{:S(2)}) collective-permute-start(bf16[2,272,1024]{2,1,0:T(8,128)(2,1)S(1)} %get-tuple-element.41.refs_1_.refs_0_), channel_id=1, source_target_pairs={{0,1},{1,0},{2,3},{3,2},{4,5},{5,4},{6,7},{7,6},{8,9},{9,8},{10,11... | collective-permute-start | bytes 3342344 | tf_op jit(solution)/shard_map/ppermute | solution.py:601
  23.0 9.6 %collective-permute-start.8 = (bf16[272,1024]{1,0:T(8,128)(2,1)S(1)}, bf16[272,1024]{1,0:T(8,128)(2,1)S(1)}, u32[]{:S(2)}, u32[]{:S(2)}) collective-permute-start(bf16[272,1024]{1,0:T(8,128)(2,1)S(1)} %get-tuple-element.38.after_ref), channel_id=1, source_target_pairs={{0,4},{1,3},{2,6},{3,1},{4,0},{5,7},{6,2},{7,5},{8,12},{9,11},{10,... | collective-permute-start | bytes 1671176 | tf_op jit(solution)/shard_map/ppermute | solution.py:630
  26.6 14.1 %collective-permute-start.15 = (bf16[1920,128]{1,0:T(8,128)(2,1)S(1)}, bf16[1920,128]{1,0:T(8,128)(2,1)S(1)}, u32[]{:S(2)}, u32[]{:S(2)}) collective-permute-start(bf16[1920,128]{1,0:T(8,128)(2,1)S(1)} %get-tuple-element.50.own), channel_id=1, source_target_pairs={{0,8},{8,0},{16,24},{24,16},{1,9},{9,1},{17,25},{25,17},{2,10},{10... | collective-permute-start | bytes 1474568 | tf_op jit(solution)/shard_map/ppermute | solution.py:601
  32.6 2.1 %collective-permute-start.12 = (bf16[80,1024]{1,0:T(8,128)(2,1)S(1)}, bf16[80,1024]{1,0:T(8,128)(2,1)S(1)}, u32[]{:S(2)}, u32[]{:S(2)}) collective-permute-start(bf16[80,1024]{1,0:T(8,128)(2,1)S(1)} %get-tuple-element.46.refs_3_.refs_1_.refs_2_), channel_id=1, source_target_pairs={{0,1},{1,0},{2,3},{3,2},{4,5},{5,4},{6,7},{7,6},{8,9},{9,8},{10,11... | collective-permute-start | bytes 491528 | tf_op jit(solution)/shard_map/ppermute | solution.py:601
  32.7 1.6 %collective-permute-start.9 = (bf16[64,1024]{1,0:T(8,128)(2,1)S(1)}, bf16[64,1024]{1,0:T(8,128)(2,1)S(1)}, u32[]{:S(2)}, u32[]{:S(2)}) collective-permute-start(bf16[64,1024]{1,0:T(8,128)(2,1)S(1)} %get-tuple-element.43.refs_0_), channel_id=1, source_target_pairs={{0,1},{1,0},{2,3},{3,2},{4,5},{5,4},{6,7},{7,6},{8,9},{9,8},{10,11... | collective-permute-start | bytes 393224 | tf_op jit(solution)/shard_map/ppermute | solution.py:601
  33.2 1.3 %collective-permute-start.10 = (bf16[64,1024]{1,0:T(8,128)(2,1)S(1)}, bf16[64,1024]{1,0:T(8,128)(2,1)S(1)}, u32[]{:S(2)}, u32[]{:S(2)}) collective-permute-start(bf16[64,1024]{1,0:T(8,128)(2,1)S(1)} %get-tuple-element.44.refs_1_), channel_id=1, source_target_pairs={{0,1},{1,0},{2,3},{3,2},{4,5},{5,4},{6,7},{7,6},{8,9},{9,8},{10,11... | collective-permute-start | bytes 393224 | tf_op jit(solution)/shard_map/ppermute | solution.py:601
  33.3 1.5 %collective-permute-start.11 = (bf16[64,1024]{1,0:T(8,128)(2,1)S(1)}, bf16[64,1024]{1,0:T(8,128)(2,1)S(1)}, u32[]{:S(2)}, u32[]{:S(2)}) collective-permute-start(bf16[64,1024]{1,0:T(8,128)(2,1)S(1)} %get-tuple-element.45.refs_2_.refs_0_), channel_id=1, source_target_pairs={{0,1},{1,0},{2,3},{3,2},{4,5},{5,4},{6,7},{7,6},{8,9},{9,8},{10,11... | collective-permute-start | bytes 393224 | tf_op jit(solution)/shard_map/ppermute | solution.py:601
  35.8 9.2 %collective-permute-start.13 = (bf16[768,128]{1,0:T(8,128)(2,1)S(1)}, bf16[768,128]{1,0:T(8,128)(2,1)S(1)}, u32[]{:S(2)}, u32[]{:S(2)}) collective-permute-start(bf16[768,128]{1,0:T(8,128)(2,1)S(1)} %get-tuple-element.47.own), channel_id=1, source_target_pairs={{0,8},{8,0},{16,24},{24,16},{1,9},{9,1},{17,25},{25,17},{2,10},{10... | collective-permute-start | bytes 589832 | tf_op jit(solution)/shard_map/ppermute | solution.py:601
  37.4 9.6 %collective-permute-start.14 = (bf16[384,128]{1,0:T(8,128)(2,1)S(1)}, bf16[384,128]{1,0:T(8,128)(2,1)S(1)}, u32[]{:S(2)}, u32[]{:S(2)}) collective-permute-start(bf16[384,128]{1,0:T(8,128)(2,1)S(1)} %get-tuple-element.48.own_d), channel_id=1, source_target_pairs={{0,8},{8,0},{16,24},{24,16},{1,9},{9,1},{17,25},{25,17},{2,10},{10... | collective-permute-start | bytes 294920 | tf_op jit(solution)/shard_map/ppermute | solution.py:601
  40.8 4.2 %copy-start = (bf16[3,192,1024]{2,1,0:T(8,128)(2,1)S(1)}, bf16[3,192,1024]{2,1,0:T(8,128)(2,1)}, u32[]{:S(2)}) copy-start(bf16[3,192,1024]{2,1,0:T(8,128)(2,1)} %refs_7_.1) | copy-start | bytes 3538948
  40.8 4.2 %copy-start.1 = (bf16[3,192,1024]{2,1,0:T(8,128)(2,1)S(1)}, bf16[3,192,1024]{2,1,0:T(8,128)(2,1)}, u32[]{:S(2)}) copy-start(bf16[3,192,1024]{2,1,0:T(8,128)(2,1)} %refs_8_.1) | copy-start | bytes 3538948

commit v6 on v5

--- a/solution.py
+++ b/solution.py
@@ -149,8 +149,10 @@
     return pl.BlockSpec(memory_space=pl.ANY)
 
 
-def smem():
-    return pl.BlockSpec(memory_space=pltpu.SMEM)
+def expert_here():
+    slices = min(4, lax.axis_size("expert") // 2)
+    group = lax.axis_index("expert") // (2 * slices)
+    return group * lax.axis_size("dp") + lax.axis_index("dp")
 
 
 def keep_hbm(value):
@@ -158,26 +160,30 @@
 
 
 def pack_kernel(
-    replica_ref,
     ids_hbm,
     gates_hbm,
     tokens_ref,
     cot_ref,
+    w_hbm,
     x_ref,
     y_ref,
     own_ref,
+    w_ref,
     ids_ref,
     gates_ref,
     sems,
 ):
     count = tokens_ref.shape[0]
     width = x_ref.shape[1]
-    columns = pl.ds(pl.multiple_of(replica_ref[0] * width, width), width)
+    columns = pl.ds(pl.multiple_of(lax.axis_index("expert") % 2 * width, width), width)
     copies = [
         pltpu.make_async_copy(ids_hbm, ids_ref, sems.at[0]),
         pltpu.make_async_copy(gates_hbm, gates_ref, sems.at[1]),
         pltpu.make_async_copy(tokens_ref.at[:, columns], x_ref, sems.at[2]),
         pltpu.make_async_copy(cot_ref.at[:, columns], y_ref.at[0:count, :], sems.at[3]),
+        pltpu.make_async_copy(tokens_ref.at[:, columns], own_ref.at[0:count, :], sems.at[4]),
+        pltpu.make_async_copy(cot_ref.at[:, columns], own_ref.at[count : 2 * count, :], sems.at[5]),
+        pltpu.make_async_copy(w_hbm, w_ref, sems.at[6]),
     ]
     for copy in copies:
         copy.start()
@@ -193,47 +199,58 @@
     y_ref[count:, 0:count] = gate.astype(jnp.bfloat16)
     y_ref[count:, count:] = jnp.zeros((slots, width - count), jnp.bfloat16)
     own_ref[2 * count :, :] = y_ref[count:, :]
-    copies[2].wait()
-    own_ref[0:count, :] = x_ref[...]
-    copies[3].wait()
-    own_ref[count : 2 * count, :] = y_ref[0:count, :]
-
-
-def pack_own(replica, ids, gates, tokens, cotangent, width, slots):
+    for copy in copies[2:]:
+        copy.wait()
+
+
+def pack_own(ids, gates, tokens, cotangent, weights, slots):
     count, top = ids.shape
+    width = weights.shape[2]
     return pl.pallas_call(
         pack_kernel,
-        in_specs=[smem()] + [in_hbm()] * 4,
-        out_specs=[whole()] * 3,
+        in_specs=[in_hbm()] * 5,
+        out_specs=[whole()] * 4,
         out_shape=[
             jax.ShapeDtypeStruct((rows, width), jnp.bfloat16)
             for rows in (count, count + slots, 2 * count + slots)
-        ],
+        ]
+        + [jax.ShapeDtypeStruct(weights.shape, weights.dtype)],
         scratch_shapes=[
             pltpu.VMEM((top, count), ids.dtype),
             pltpu.VMEM((top, count), gates.dtype),
-            pltpu.SemaphoreType.DMA((4,)),
+            pltpu.SemaphoreType.DMA((7,)),
         ],
         compiler_params=params(),
         cost_estimate=cost(1000, 8 * count * width),
-    )(replica.reshape(1), *[keep_hbm(value) for value in (ids.T, gates.T, tokens, cotangent)])
+    )(*[keep_hbm(value) for value in (ids.T, gates.T, tokens, cotangent, weights)])
 
 
 def views(refs, kinds, count):
     xs, ys, gates = [], [], []
     for ref, kind in zip(refs, kinds):
+        if kind in ("first x", "second x"):
+            xs.append(ref[0 if kind == "first x" else 1])
+            continue
+        if kind == "x, y, y":
+            rows = (ref.shape[0] - count) // 2
+            xs.append(ref[0:count, :])
+            for row in (count, count + rows):
+                ys.append(ref[row : row + count, :])
+                gates.append(ref[row + count : row + rows, 0:count])
+            continue
         for part in [ref.at[0], ref.at[1]] if ref.ndim == 3 else [ref]:
-            rows = part.shape[0]
+            if kind == "x":
+                xs.append(part[...])
             if kind == "xy":
                 xs.append(part[0:count, :])
-            if kind == "x":
-                xs.append(part[...])
-            if kind in ("xy", "y of xy"):
                 ys.append(part[count : 2 * count, :])
                 gates.append(part[2 * count :, 0:count])
             if kind == "y":
                 ys.append(part[...])
             if kind == "y, gates":
+                ys.append(part[0:count, :])
+                gates.append(part[count:, 0:count])
+            if kind == "half y, gates":
                 ys.append(part[0 : count // 2, :])
                 gates.append(part[count // 2 :, 0:count])
     return xs, ys, gates
@@ -332,12 +349,13 @@
     )(keep_hbm(weights), *values_of(chunk))
 
 
-def gate_row(expert_ref, gates):
+def gate_row(gates):
     rows = []
+    expert = expert_here()
     for held in gates:
         held = held.astype(jnp.float32)
         index = lax.broadcasted_iota(jnp.int32, held.shape, 0)
-        rows.append(jnp.sum(jnp.where(index == expert_ref[0], held, 0.0), 0, keepdims=True))
+        rows.append(jnp.sum(jnp.where(index == expert, held, 0.0), 0, keepdims=True))
     return rows[0] if len(rows) == 1 else jnp.concatenate(rows, 1)
 
 
@@ -383,50 +401,52 @@
     )
 
 
-def onward_kernel(kinds, core_ref, expert_ref, after_ref, *refs):
-    own, got, near_own, near_got, x0_ref, x1_ref, y0_ref, y1_ref = refs[:8]
-    both_ref, out_ref, first_ref, sum_ref, gate_ref = refs[8 + len(kinds) :]
-    count = x0_ref.shape[0]
-    gates = views(refs[8 : 8 + len(kinds)], kinds, count)[2]
-    gate_ref[...] = jnp.broadcast_to(gate_row(expert_ref, gates), gate_ref.shape)
-    both_ref[0, 0:count, :] = x0_ref[...]
-    both_ref[1, 0:count, :] = x1_ref[...]
-    both_ref[0, count:, :] = y0_ref[...]
-    both_ref[1, count:, :] = y1_ref[...]
-
-    def pick(near, more):
-        out_ref[0:count, :] = near[...]
-        out_ref[count:, :] = more[...]
-
-    @pl.when(core_ref[0] == 0)
+def onward_kernel(kinds, after_ref, own, got, near_own, near_got, *refs):
+    x0_ref, x1_ref, s0_ref, y0_ref, y1_ref = refs[:5]
+    pair_ref, rest_ref, out_ref, first_ref, sum_ref, gate_ref = refs[5 + len(kinds) :]
+    count, rows = x0_ref.shape[0], y0_ref.shape[0]
+    gates = views(refs[5 : 5 + len(kinds)], kinds, count)[2]
+    gate_ref[...] = jnp.broadcast_to(gate_row(gates), gate_ref.shape)
+    pair_ref[0] = x0_ref[...]
+    pair_ref[1] = s0_ref[...]
+    rest_ref[0:count, :] = x1_ref[...]
+    rest_ref[count : count + rows, :] = y0_ref[...]
+    rest_ref[count + rows :, :] = y1_ref[...]
+    core = lax.axis_index("dp") % 2
+
+    @pl.when(core == 0)
     def _():
-        pick(x0_ref, y0_ref)
-
-    @pl.when(core_ref[0] != 0)
+        out_ref[0:count, :] = x0_ref[...]
+        out_ref[count:, :] = y0_ref[...]
+
+    @pl.when(core != 0)
     def _():
-        pick(x1_ref, y1_ref)
+        out_ref[0:count, :] = x1_ref[...]
+        out_ref[count:, :] = y1_ref[...]
 
     first_ref[...] = own[...].astype(jnp.float32) + got[...].astype(jnp.float32)
     sum_ref[...] = near_own[...].astype(jnp.float32) + near_got[...].astype(jnp.float32)
 
 
-def pick_onward(core, expert, after, pair, near_pair, near_x, near_y, chunk):
-    rows, width = near_x[0].shape[0] + near_y[0].shape[0], near_x[0].shape[1]
-    operands = [*pair, *near_pair, *near_x, *near_y, *values_of(chunk)]
+def pick_onward(after, pair, near_pair, near_x, other_x, near_y, chunk):
+    count, width = other_x.shape
+    rows = near_y[0].shape[0]
+    operands = [*pair, *near_pair, *near_x, other_x, *near_y, *values_of(chunk)]
     return pl.pallas_call(
         functools.partial(onward_kernel, kinds_of(chunk)),
-        in_specs=[smem(), smem(), unread()] + [whole()] * len(operands),
-        out_specs=[whole()] * 5,
+        in_specs=[unread()] + [whole()] * len(operands),
+        out_specs=[whole()] * 6,
         out_shape=[
-            jax.ShapeDtypeStruct((2, rows, width), jnp.bfloat16),
-            jax.ShapeDtypeStruct((rows, width), jnp.bfloat16),
+            jax.ShapeDtypeStruct((2, count, width), jnp.bfloat16),
+            jax.ShapeDtypeStruct((count + 2 * rows, width), jnp.bfloat16),
+            jax.ShapeDtypeStruct((count + rows, width), jnp.bfloat16),
             jax.ShapeDtypeStruct(pair[0].shape, jnp.float32),
             jax.ShapeDtypeStruct(near_pair[0].shape, jnp.float32),
-            jax.ShapeDtypeStruct((8, 2 * near_x[0].shape[0]), jnp.float32),
+            jax.ShapeDtypeStruct((8, 2 * count), jnp.float32),
         ],
         compiler_params=params(),
-        cost_estimate=cost(1000, 8 * near_x[0].size),
-    )(core.reshape(1), expert, after, *operands)
+        cost_estimate=cost(1000, 8 * other_x.size),
+    )(after, *operands)
 
 
 def pass_kernel(after_ref, in_ref, *outs):
@@ -475,44 +495,41 @@
     )(gate, after, total, *values_of(chunk))
 
 
-def grad_kernel(kinds, count, expert_ref, sum_ref, own, got, *refs):
+def grad_kernel(kinds, count, sum_ref, own, got, *refs):
     n = len(kinds)
     xs, ys, gates = views(refs[:n], kinds, count)
     acc_ref, out_ref = refs[n:]
-    lefts = hidden_grads(gate_row(expert_ref, gates), [(sum_ref,), (own, got)])
+    lefts = hidden_grads(gate_row(gates), [(sum_ref,), (own, got)])
     x = joined(xs)
     for m, right in enumerate((x, x, joined(ys))):
         out_ref[m] = acc_ref[m] + plain(lefts[m], right)
 
 
-def add_grads(expert, near_sum, pair, chunk, acc, count):
+def add_grads(near_sum, pair, chunk, acc, count):
     kinds = kinds_of(chunk)
     mats, hidden, width = acc.shape
     operands = [near_sum, *pair, *values_of(chunk), acc]
     return pl.pallas_call(
         functools.partial(grad_kernel, kinds, count),
-        in_specs=[smem()] + [whole()] * len(operands),
+        in_specs=[whole()] * len(operands),
         out_specs=whole(),
         out_shape=jax.ShapeDtypeStruct(acc.shape, jnp.float32),
-        input_output_aliases={len(operands): 0},
+        input_output_aliases={len(operands) - 1: 0},
         compiler_params=params(),
         cost_estimate=cost(
             2 * mats * hidden * width * 4 * count, 8 * mats * hidden * width
         ),
-    )(expert, *operands)
-
-
-def adam(grad, first_ref, second_ref, one_ref, two_ref, step_ref):
-    moment_one = beta_one * first_ref[0].astype(jnp.float32) + (1.0 - beta_one) * grad
-    moment_two = beta_two * second_ref[0].astype(jnp.float32) + (1.0 - beta_two) * (grad * grad)
-    one_ref[0] = moment_one.astype(jnp.bfloat16)
-    two_ref[0] = moment_two.astype(jnp.bfloat16)
-    scaled = moment_two * (1.0 / (1.0 - beta_two**step_count))
-    below = scaled * lax.rsqrt(scaled) + epsilon
-    guess = pl.reciprocal(below, approx=True)
-    inverse = guess * (2.0 - below * guess)
-    step = moment_one * (1.0 / (1.0 - beta_one**step_count)) * inverse
-    step_ref[0] = step.astype(jnp.bfloat16)
+    )(*operands)
+
+
+def adam(grad, first, second):
+    moment_one = beta_one * first.astype(jnp.float32) + (1.0 - beta_one) * grad
+    moment_two = beta_two * second.astype(jnp.float32) + (1.0 - beta_two) * (grad * grad)
+    root = (1.0 / (1.0 - beta_two**step_count)) ** 0.5
+    below = moment_two * lax.rsqrt(moment_two) + epsilon / root
+    scaled = moment_one * (1.0 / (1.0 - beta_one**step_count) / root)
+    step = scaled * pl.reciprocal(below, approx=True)
+    return [value.astype(jnp.bfloat16) for value in (moment_one, moment_two, step)]
 
 
 def gate_up(own, got):
@@ -521,76 +538,67 @@
     return beside(total, hidden, (0, 2)), beside(total, hidden, (1, 3))
 
 
-def down_kernel(kinds, count, expert_ref, own, got, *refs):
+def down_kernel(kinds, count, own, got, *refs):
     n = len(kinds)
-    acc_ref, first_ref, second_ref, one_ref, two_ref, step_ref, act_ref = refs[n:]
+    acc_ref, first_ref, second_ref, *outs = refs[n:]
     xs, ys, gates = views(refs[:n], kinds, count)
-
-    @pl.when(pl.program_id(0) == 0)
-    def _():
-        act_ref[...] = activation(*gate_up(own, got), gate_row(expert_ref, gates))[2]
-
-    grad = acc_ref[0] + plain(act_ref[...], joined(ys))
-    adam(grad, first_ref, second_ref, one_ref, two_ref, step_ref)
-
-
-def down_update(expert, pair, chunk, acc, first_moment, second_moment, count, columns):
+    act = activation(*gate_up(own, got), gate_row(gates))[2]
+    grad = acc_ref[2] + plain(act, joined(ys))
+    for out_ref, value in zip(outs, adam(grad, first_ref[2], second_ref[2])):
+        out_ref[...] = value
+
+
+def down_update(pair, chunk, acc, moments, count):
     kinds = kinds_of(chunk)
-    mats, hidden, width = first_moment.shape
-    tile = pl.BlockSpec((1, hidden, columns), lambda j: (2, 0, j))
-    strip = lambda value: pl.BlockSpec((value.shape[0], columns), lambda j: (0, j))
+    mats, hidden, width = acc.shape
+    operands = [*pair, *values_of(chunk), acc, *moments]
     return pl.pallas_call(
         functools.partial(down_kernel, kinds, count),
-        grid=(width // columns,),
-        in_specs=[smem(), whole(), whole()]
-        + [strip(value) for value in values_of(chunk)]
-        + [tile] * 3,
-        out_specs=[tile] * 3,
-        out_shape=[jax.ShapeDtypeStruct(first_moment.shape, jnp.bfloat16)] * 3,
-        scratch_shapes=[pltpu.VMEM((hidden, 2 * count), jnp.bfloat16)],
+        in_specs=[whole()] * len(operands),
+        out_specs=[whole()] * 3,
+        out_shape=[jax.ShapeDtypeStruct((hidden, width), jnp.bfloat16)] * 3,
         compiler_params=params(),
         cost_estimate=cost(4 * hidden * width * count, 14 * hidden * width),
-    )(expert, *pair, *values_of(chunk), acc, first_moment, second_moment)
-
-
-def slopes_kernel(kinds, count, expert_ref, own, got, own_d, got_d, *refs):
+    )(*operands)
+
+
+def slopes_kernel(kinds, count, own, got, own_d, got_d, *refs):
     n = len(kinds)
     acc_ref, first_ref, second_ref = refs[n : n + 3]
-    one_ref, two_ref, step_ref, left_ref = refs[n + 6 :]
+    done, outs = refs[n + 3 : n + 6], refs[n + 6 : n + 9]
+    held, sems = refs[n + 9 : n + 12], refs[n + 12]
+    copies = [
+        pltpu.make_async_copy(done[k], outs[k].at[2], sems.at[2, k]) for k in range(3)
+    ]
+    for copy in copies:
+        copy.start()
     xs, ys, gates = views(refs[:n], kinds, count)
-    m = pl.program_id(1)
-
-    @pl.when((pl.program_id(0) == 0) & (m == 0))
-    def _():
-        gate = gate_row(expert_ref, gates)
-        hg, hu = gate_up(own, got)
-        down = summed([(own_d, got_d)])
-        dact = gate * beside(down, down.shape[0] // 2, (0, 1))
-        sig, silu, act = activation(hg, hu, gate)
-        left_ref[0], left_ref[1] = hidden_slopes(hg, hu, sig, silu, dact)
-
-    grad = acc_ref[0] + plain(left_ref[m], joined(xs))
-    adam(grad, first_ref, second_ref, one_ref, two_ref, step_ref)
-
-
-def slopes_update(expert, pair, down_pair, chunk, acc, moments, done, count, columns):
+    hg, hu = gate_up(own, got)
+    down = summed([(own_d, got_d)])
+    dact = gate_row(gates) * beside(down, down.shape[0] // 2, (0, 1))
+    sig, silu, act = activation(hg, hu, 1.0)
+    right = joined(xs)
+    for m, left in enumerate(hidden_slopes(hg, hu, sig, silu, dact)):
+        grad = acc_ref[m] + plain(left, right)
+        for k, value in enumerate(adam(grad, first_ref[m], second_ref[m])):
+            held[k][m] = value
+            copies.append(pltpu.make_async_copy(held[k].at[m], outs[k].at[m], sems.at[m, k]))
+            copies[-1].start()
+    for copy in copies:
+        copy.wait()
+
+
+def slopes_update(pair, down_pair, chunk, acc, moments, done, count):
     kinds = kinds_of(chunk)
     mats, hidden, width = acc.shape
-    tile = pl.BlockSpec((1, hidden, columns), lambda j, m: (m, 0, j))
-    strip = lambda value: pl.BlockSpec((value.shape[0], columns), lambda j, m: (0, j))
-    operands = [expert, *pair, *down_pair, *values_of(chunk), acc, *moments, *done]
+    operands = [*pair, *down_pair, *values_of(chunk), acc, *moments, *done]
     return pl.pallas_call(
         functools.partial(slopes_kernel, kinds, count),
-        grid=(width // columns, 2),
-        in_specs=[smem()]
-        + [whole()] * 4
-        + [strip(value) for value in values_of(chunk)]
-        + [tile] * 3
-        + [unread()] * 3,
-        out_specs=[tile] * 3,
+        in_specs=[whole()] * len(operands),
+        out_specs=[in_hbm()] * 3,
         out_shape=[jax.ShapeDtypeStruct(acc.shape, jnp.bfloat16)] * 3,
-        input_output_aliases={len(operands) - 3 + k: k for k in range(3)},
-        scratch_shapes=[pltpu.VMEM((2, hidden, 2 * count), jnp.bfloat16)],
+        scratch_shapes=[pltpu.VMEM((2, hidden, width), jnp.bfloat16)] * 3
+        + [pltpu.SemaphoreType.DMA((3, 3))],
         compiler_params=params(),
         cost_estimate=cost(8 * hidden * width * count, 28 * hidden * width),
     )(*operands)
@@ -603,50 +611,44 @@
 
 def dense_plan(tokens, cotangent, expert_ids, gate_probs, weights, first_moment, second_moment):
     n_data = lax.axis_size("dp")
-    place = lax.axis_index("expert")
-    core = lax.axis_index("dp") % 2
     slices = min(4, lax.axis_size("expert") // 2)
-    expert = (place // (2 * slices) * n_data + lax.axis_index("dp")).astype(jnp.int32).reshape(1)
     experts_total = lax.axis_size("expert") // (2 * slices) * n_data
     count = tokens.shape[0]
-    width = weights.shape[2]
+    hidden, width = weights.shape[1:]
     slots = -(-experts_total // 16) * 16
-    x_own, y_own, own = pack_own(
-        (place % 2).astype(jnp.int32), expert_ids, gate_probs, tokens, cotangent, width, slots
-    )
     other = lambda value: from_masked(value, "dp", 1)
     partner = lambda value: from_masked(value, "expert", 1)
+    x_own, y_own, own, weights = pack_own(
+        expert_ids, gate_probs, tokens, cotangent, weights, slots
+    )
     first = [("xy", own), ("xy", other(own))]
-    send, token, weights = start_partials(weights, first, 6, count)
+    send, token = partials(weights, own, first, (6,), count)
     first_pair = (send, partner(send))
     near_x = [from_masked(x_own, "dp", mask) for mask in (2, 4)]
     near_y = [from_masked(y_own, "dp", mask) for mask in (2, 4)]
-    send, token = partials(weights, token, [("x", near_x[0])], (2,), count)
+    send, token = partials(weights, token, [("x", near_x[0]), ("", near_x[1])], (2,), count)
     near_pair = (send, partner(send))
-    both, picked, first_sum, near_sum, gate = pick_onward(
-        core.astype(jnp.int32), expert, token, first_pair, near_pair, near_x, near_y, first
+    x_pair, rest, picked, first_sum, near_sum, gate = pick_onward(
+        token, first_pair, near_pair, near_x, other(near_x[0]), near_y, first
     )
     onward = [(p, p ^ 4 if p % 2 == 0 else p ^ 2) for p in range(n_data)]
     far = lax.ppermute(picked, "dp", onward)
-    acc, token = first_grads(gate, picked, first_sum, first, weights.shape[1], count)
-    swapped = other(both)
-    more = [("x", near_x[1]), ("y of xy", both), ("xy", swapped)]
-    send, token = partials(weights, token, more, (10,), count)
+    acc, token = first_grads(gate, picked, first_sum, first, hidden, count)
+    ends = [("x, y, y", rest), ("second x", x_pair), ("x, y, y", other(rest))]
+    send, token = partials(weights, token, ends, (10,), count)
     more_pair = (send, partner(send))
     pieces = passed_on(token, far, (count // 2, count // 2, count // 2, count // 2 + slots))
     pieces = [*pieces, *[other(value) for value in pieces]]
-    final = list(zip(("x", "x", "y", "y, gates") * 2, pieces))
+    final = list(zip(("x", "x", "y", "half y, gates") * 2, pieces))
     send, send_d, token = partials(weights, token, final, (4, 2), count)
     pair, down_pair = (send, partner(send)), (send_d, partner(send_d))
-    near = [("xy", both), ("xy", swapped)]
-    acc = add_grads(expert, near_sum, more_pair, near, acc, count)
+    near = [("first x", x_pair), *ends]
+    acc = add_grads(near_sum, more_pair, near, acc, count)
     moments = (first_moment, second_moment)
     final_y = [block for block in final if block[0] != "x"]
     final_x = [block for block in final if block[0] != "y"]
-    done = down_update(expert, pair, final_y, acc, *moments, count, width // 2)
-    return tuple(
-        slopes_update(expert, pair, down_pair, final_x, acc, moments, done, count, width // 2)
-    )
+    done = down_update(pair, final_y, acc, moments, count)
+    return tuple(slopes_update(pair, down_pair, final_x, acc, moments, done, count))
 
 
 def per_device(tokens, cotangent, expert_ids, gate_probs, weights, first_moment, second_moment):

time: 50.7 us -> 45.7 us (0.901)
  Pallas kernels: 15.5 us -> 9.12 us
  waiting for transfers between devices: 19.5 us -> 20.3 us
  starting transfers between devices: 14.7 us -> 15.3 us
    pallas_call x5 -> x4, Pallas kernels: 11.4 us -> 5.52 us  [the longest x1 2.2 us: slopes_update(): pl.pallas_call(functools.partial(slopes_kernel, kinds, count), in_specs=[...]
    ppermute x1, starting transfers between devices: 0.51 us -> 1.58 us  [dense_plan(): far = lax.ppermute(picked, 'dp', onward)]
    pallas_call x1, Pallas kernels: 1.26 us -> 0.22 us  [pick_onward(): pl.pallas_call(functools.partial(onward_kernel, kinds_of(chunk)), in_spec...]
    pallas_call x3 -> x4, Pallas kernels: 2.29 us -> 2.84 us  [partials(): pl.pallas_call(functools.partial(partial_kernel, kinds, count), in_specs=...]
    ppermute x15 -> x16, starting transfers between devices: 14.2 us -> 13.7 us  [from_masked(): return lax.ppermute(value, axis, pairs)]
    ppermute x15 -> x16, waiting for transfers between devices: 15.2 us -> 15.6 us  [from_masked(): return lax.ppermute(value, axis, pairs)]
  transfers between devices with their start and end apart: 16 -> 17, of which waited for: 10 -> 11; matrix products, arithmetic and copies ran while one was open for 0% -> 0% of each run, Pallas kernels for 18% -> 11%
where the time goes in v6:
time: 45.7 us; the launch traced here: 45.5 us
  waiting for transfers between devices  20.3 us (44%)
  starting transfers between devices  15.3 us (33%)
  Pallas kernels  9.12 us (20%)
  between operations  0.74 us (2%)
    ppermute x16, waiting for transfers between devices, from_masked(): return lax.ppermute(value, axis, pairs)  15.6 us
    ppermute x16, starting transfers between devices, from_masked(): return lax.ppermute(value, axis, pairs)  13.7 us
    ppermute x1, waiting for transfers between devices, dense_plan(): far = lax.ppermute(picked, 'dp', onward)  4.71 us
    pallas_call x4, Pallas kernels, partials(): pl.pallas_call(functools.partial(partial_kernel, kinds, count), in_specs=...  2.84 us
    pallas_call x1, Pallas kernels, slopes_update(): pl.pallas_call(functools.partial(slopes_kernel, kinds, count), in_specs=[...  2.2 us
    pallas_call x1, Pallas kernels, pack_own(): pl.pallas_call(pack_kernel, in_specs=[in_hbm()] * 5, out_specs=[whole()]...  1.69 us
    ppermute x1, starting transfers between devices, dense_plan(): far = lax.ppermute(picked, 'dp', onward)  1.58 us
    pallas_call x1, Pallas kernels, add_grads(): pl.pallas_call(functools.partial(grad_kernel, kinds, count), in_specs=[wh...  1.01 us
  transfers between devices with their start and end apart: 17, of which 11 were waited for; matrix products, arithmetic and copies ran while one was open for 0% of the time, Pallas kernels for 11%

profile of v6, /device:TPU:0, one launch (start us, length us, event | category | flops | bytes accessed | tf_op | source)
XLA Modules:
  0.0 45.5 jit_solution(5576418248888278025)
XLA Ops:
  0.6 1.7 %shard_map.94 = (bf16[128,1024]{1,0:T(8,128)(2,1)S(1)}, bf16[144,1024]{1,0:T(8,128)(2,1)S(1)}, bf16[272,1024]{1,0:T(8,128)(2,1)S(1)}, bf16[3,192,1024]{2,1,0:T(8,128)(2,1)S(1)}) custom-call(s32[4,128]{1,0:T(4,128)} %bitcast.2, bf16[4,128]{1,0:T(4,128)(2,1)} %bitcast.3, bf16[128,2048]{1,0:T(8,128)(2,1)} %tokens_ref.1, bf16[128,2048]{1,0:T(8,128)(2,1)} %cot_ref.1, ...), custom_call_target="tpu_custom_call" | custom-call | flops 1000 | bytes 1048576 | tf_op jit(solution)/shard_map/pallas_call | solution.py:209
  2.3 0.5 %collective-permute-start = (bf16[272,1024]{1,0:T(8,128)(2,1)S(1)}, bf16[272,1024]{1,0:T(8,128)(2,1)S(1)}, u32[]{:S(2)}, u32[]{:S(2)}) collective-permute-start(bf16[272,1024]{1,0:T(8,128)(2,1)S(1)} %get-tuple-element.31.after_ref.refs_0_.refs_5_), channel_id=1, source_target_pairs={{0,1},{1,0},{2,3},{3,2},{4,5},{5,4},{6,7},{7,6},{8,9},{9,8},{10,11... | collective-permute-start | bytes 1671176 | tf_op jit(solution)/shard_map/ppermute | solution.py:609
  2.8 2.6 %collective-permute-start.1 = (bf16[128,1024]{1,0:T(8,128)(2,1)S(1)}, bf16[128,1024]{1,0:T(8,128)(2,1)S(1)}, u32[]{:S(2)}, u32[]{:S(2)}) collective-permute-start(bf16[128,1024]{1,0:T(8,128)(2,1)S(1)} %get-tuple-element.33), channel_id=1, source_target_pairs={{0,2},{1,3},{2,0},{3,1},{4,6},{5,7},{6,4},{7,5},{8,10},{9,11},{10,... | collective-permute-start | bytes 786440 | tf_op jit(solution)/shard_map/ppermute | solution.py:609
  5.4 1.6 %collective-permute-start.2 = (bf16[128,1024]{1,0:T(8,128)(2,1)S(1)}, bf16[128,1024]{1,0:T(8,128)(2,1)S(1)}, u32[]{:S(2)}, u32[]{:S(2)}) collective-permute-start(bf16[128,1024]{1,0:T(8,128)(2,1)S(1)} %get-tuple-element.33), channel_id=1, source_target_pairs={{0,4},{1,5},{2,6},{3,7},{4,0},{5,1},{6,2},{7,3},{8,12},{9,13},{10,... | collective-permute-start | bytes 786440 | tf_op jit(solution)/shard_map/ppermute | solution.py:609
  7.5 0.5 %shard_map.95 = (bf16[1152,128]{1,0:T(8,128)(2,1)S(1)}, f32[8,128]{1,0:T(8,128)S(1)}) custom-call(bf16[3,192,1024]{2,1,0:T(8,128)(2,1)S(1)} %get-tuple-element.30.w_ref, bf16[272,1024]{1,0:T(8,128)(2,1)S(1)} %get-tuple-element.31.after_ref.refs_0_.refs_5_, bf16[272,1024]{1,0:T(8,128)(2,1)S(1)} %get-tuple-element.31.after_ref.refs_0_.refs_5_, ...), custom_call_target="tpu_custom_call" | custom-call | flops 301989888 | bytes 884736 | tf_op jit(solution)/shard_map/pallas_call | solution.py:302
  8.1 2.1 %collective-permute-start.3 = (bf16[1152,128]{1,0:T(8,128)(2,1)S(1)}, bf16[1152,128]{1,0:T(8,128)(2,1)S(1)}, u32[]{:S(2)}, u32[]{:S(2)}) collective-permute-start(bf16[1152,128]{1,0:T(8,128)(2,1)S(1)} %get-tuple-element.35.own), channel_id=1, source_target_pairs={{0,8},{8,0},{16,24},{24,16},{1,9},{9,1},{17,25},{25,17},{2,10},{10... | collective-permute-start | bytes 884744 | tf_op jit(solution)/shard_map/ppermute | solution.py:609
  10.2 2.4 %collective-permute-done.1.refs_0_ = bf16[128,1024]{1,0:T(8,128)(2,1)S(1)} collective-permute-done((bf16[128,1024]{1,0:T(8,128)(2,1)S(1)}, bf16[128,1024]{1,0:T(8,128)(2,1)S(1)}, u32[]{:S(2)}, u32[]{:S(2)}) %collective-permute-start.1) | collective-permute-done | bytes 262176 | tf_op jit(solution)/shard_map/ppermute | solution.py:609
  12.6 2.0 %collective-permute-done.2.refs_1_ = bf16[128,1024]{1,0:T(8,128)(2,1)S(1)} collective-permute-done((bf16[128,1024]{1,0:T(8,128)(2,1)S(1)}, bf16[128,1024]{1,0:T(8,128)(2,1)S(1)}, u32[]{:S(2)}, u32[]{:S(2)}) %collective-permute-start.2) | collective-permute-done | bytes 262176 | tf_op jit(solution)/shard_map/ppermute | solution.py:609
  14.9 1.6 %collective-permute-start.4 = (bf16[384,128]{1,0:T(8,128)(2,1)S(1)}, bf16[384,128]{1,0:T(8,128)(2,1)S(1)}, u32[]{:S(2)}, u32[]{:S(2)}) collective-permute-start(bf16[384,128]{1,0:T(8,128)(2,1)S(1)} %get-tuple-element.36.near_own), channel_id=1, source_target_pairs={{0,8},{8,0},{16,24},{24,16},{1,9},{9,1},{17,25},{25,17},{2,10},{10... | collective-permute-start | bytes 294920 | tf_op jit(solution)/shard_map/ppermute | solution.py:609
  16.6 3.5 %collective-permute-done.7.refs_4_ = bf16[144,1024]{1,0:T(8,128)(2,1)S(1)} collective-permute-done((bf16[144,1024]{1,0:T(8,128)(2,1)S(1)}, bf16[144,1024]{1,0:T(8,128)(2,1)S(1)}, u32[]{:S(2)}, u32[]{:S(2)}) %collective-permute-start.7) | collective-permute-done | bytes 294944 | tf_op jit(solution)/shard_map/ppermute | solution.py:609
  20.4 1.6 %collective-permute-start.9 = (bf16[272,1024]{1,0:T(8,128)(2,1)S(1)}, bf16[272,1024]{1,0:T(8,128)(2,1)S(1)}, u32[]{:S(2)}, u32[]{:S(2)}) collective-permute-start(bf16[272,1024]{1,0:T(8,128)(2,1)S(1)} %get-tuple-element.39.after_ref), channel_id=1, source_target_pairs={{0,4},{1,3},{2,6},{3,1},{4,0},{5,7},{6,2},{7,5},{8,12},{9,11},{10,... | collective-permute-start | bytes 1671176 | tf_op jit(solution)/shard_map/ppermute | solution.py:635
  22.0 0.5 %shard_map.98 = (f32[3,192,1024]{2,1,0:T(8,128)S(1)}, f32[8,128]{1,0:T(8,128)S(1)}) custom-call(f32[8,256]{1,0:T(8,128)S(1)} %get-tuple-element.38.gate_ref, bf16[272,1024]{1,0:T(8,128)(2,1)S(1)} %get-tuple-element.39.after_ref, f32[1152,128]{1,0:T(8,128)S(1)} %get-tuple-element.40.sum_ref, ...), custom_call_target="tpu_custom_call" | custom-call | flops 301989888 | bytes 2359296 | tf_op jit(solution)/shard_map/pallas_call | solution.py:485
  22.8 0.9 %shard_map.99 = (bf16[1920,128]{1,0:T(8,128)(2,1)S(1)}, f32[8,128]{1,0:T(8,128)S(1)}) custom-call(bf16[3,192,1024]{2,1,0:T(8,128)(2,1)S(1)} %get-tuple-element.30.w_ref, f32[8,128]{1,0:T(8,128)S(1)} %get-tuple-element.41.after_ref, bf16[416,1024]{1,0:T(8,128)(2,1)S(1)} %get-tuple-element.42.refs_0_.refs_1_, ...), custom_call_target="tpu_custom_call" | custom-call | flops 503316480 | bytes 1474560 | tf_op jit(solution)/shard_map/pallas_call | solution.py:302
  23.7 1.6 %collective-permute-start.16 = (bf16[1920,128]{1,0:T(8,128)(2,1)S(1)}, bf16[1920,128]{1,0:T(8,128)(2,1)S(1)}, u32[]{:S(2)}, u32[]{:S(2)}) collective-permute-start(bf16[1920,128]{1,0:T(8,128)(2,1)S(1)} %get-tuple-element.52.own), channel_id=1, source_target_pairs={{0,8},{8,0},{16,24},{24,16},{1,9},{9,1},{17,25},{25,17},{2,10},{10... | collective-permute-start | bytes 1474568 | tf_op jit(solution)/shard_map/ppermute | solution.py:609
  25.3 4.7 %collective-permute-done.9.in_ref = bf16[272,1024]{1,0:T(8,128)(2,1)S(1)} collective-permute-done((bf16[272,1024]{1,0:T(8,128)(2,1)S(1)}, bf16[272,1024]{1,0:T(8,128)(2,1)S(1)}, u32[]{:S(2)}, u32[]{:S(2)}) %collective-permute-start.9) | collective-permute-done | bytes 557088 | tf_op jit(solution)/shard_map/ppermute | solution.py:635
  31.2 0.6 %collective-permute-done.10.refs_4_.refs_3_ = bf16[64,1024]{1,0:T(8,128)(2,1)S(1)} collective-permute-done((bf16[64,1024]{1,0:T(8,128)(2,1)S(1)}, bf16[64,1024]{1,0:T(8,128)(2,1)S(1)}, u32[]{:S(2)}, u32[]{:S(2)}) %collective-permute-start.10) | collective-permute-done | bytes 131104 | tf_op jit(solution)/shard_map/ppermute | solution.py:609
  32.2 1.1 %shard_map.101 = (bf16[768,128]{1,0:T(8,128)(2,1)S(1)}, bf16[384,128]{1,0:T(8,128)(2,1)S(1)}, f32[8,128]{1,0:T(8,128)}) custom-call(bf16[3,192,1024]{2,1,0:T(8,128)(2,1)S(1)} %get-tuple-element.30.w_ref, f32[8,128]{1,0:T(8,128)S(1)} %get-tuple-element.44.after_ref, bf16[64,1024]{1,0:T(8,128)(2,1)S(1)} %get-tuple-element.45.refs_0_, ...), custom_call_target="tpu_custom_call" | custom-call | flops 301989888 | bytes 884736 | tf_op jit(solution)/shard_map/pallas_call | solution.py:302
  33.2 1.6 %collective-permute-start.14 = (bf16[768,128]{1,0:T(8,128)(2,1)S(1)}, bf16[768,128]{1,0:T(8,128)(2,1)S(1)}, u32[]{:S(2)}, u32[]{:S(2)}) collective-permute-start(bf16[768,128]{1,0:T(8,128)(2,1)S(1)} %get-tuple-element.49.own), channel_id=1, source_target_pairs={{0,8},{8,0},{16,24},{24,16},{1,9},{9,1},{17,25},{25,17},{2,10},{10... | collective-permute-start | bytes 589832 | tf_op jit(solution)/shard_map/ppermute | solution.py:609
  35.3 2.5 %collective-permute-done.16.got = bf16[1920,128]{1,0:T(8,128)(2,1)S(1)} collective-permute-done((bf16[1920,128]{1,0:T(8,128)(2,1)S(1)}, bf16[1920,128]{1,0:T(8,128)(2,1)S(1)}, u32[]{:S(2)}, u32[]{:S(2)}) %collective-permute-start.16) | collective-permute-done | bytes 491552 | tf_op jit(solution)/shard_map/ppermute | solution.py:609
  37.8 1.0 %shard_map.102.refs_4_.refs_6_ = f32[3,192,1024]{2,1,0:T(8,128)S(1)} custom-call(f32[384,128]{1,0:T(8,128)S(1)} %get-tuple-element.51.sum_ref, bf16[1920,128]{1,0:T(8,128)(2,1)S(1)} %get-tuple-element.52.own, bf16[1920,128]{1,0:T(8,128)(2,1)S(1)} %collective-permute-done.16.got, ...), custom_call_target="tpu_custom_call", output_to_operand_aliasing={{}: (7, {})} | custom-call | flops 603979776 | bytes 4718592 | tf_op jit(solution)/shard_map/pallas_call | solution.py:512
  38.8 3.2 %collective-permute-done.14.got = bf16[768,128]{1,0:T(8,128)(2,1)S(1)} collective-permute-done((bf16[768,128]{1,0:T(8,128)(2,1)S(1)}, bf16[768,128]{1,0:T(8,128)(2,1)S(1)}, u32[]{:S(2)}, u32[]{:S(2)}) %collective-permute-start.14) | collective-permute-done | bytes 196640 | tf_op jit(solution)/shard_map/ppermute | solution.py:609
  42.0 0.6 %shard_map.103 = (bf16[192,1024]{1,0:T(8,128)(2,1)S(1)}, bf16[192,1024]{1,0:T(8,128)(2,1)S(1)}, bf16[192,1024]{1,0:T(8,128)(2,1)S(1)}) custom-call(bf16[768,128]{1,0:T(8,128)(2,1)S(1)} %get-tuple-element.49.own, bf16[768,128]{1,0:T(8,128)(2,1)S(1)} %collective-permute-done.14.got, bf16[64,1024]{1,0:T(8,128)(2,1)S(1)} %get-tuple-element.47.refs_2_.refs_0_, ...), custom_call_target="tpu_custom_call" | custom-call | flops 100663296 | bytes 2752512 | tf_op jit(solution)/shard_map/pallas_call | solution.py:555
  42.7 0.7 %collective-permute-done.15.got_d = bf16[384,128]{1,0:T(8,128)(2,1)S(1)} collective-permute-done((bf16[384,128]{1,0:T(8,128)(2,1)S(1)}, bf16[384,128]{1,0:T(8,128)(2,1)S(1)}, u32[]{:S(2)}, u32[]{:S(2)}) %collective-permute-start.15) | collective-permute-done | bytes 98336 | tf_op jit(solution)/shard_map/ppermute | solution.py:609
  43.3 2.2 %shard_map.104 = (bf16[3,192,1024]{2,1,0:T(8,128)(2,1)}, bf16[3,192,1024]{2,1,0:T(8,128)(2,1)}, bf16[3,192,1024]{2,1,0:T(8,128)(2,1)}) custom-call(bf16[768,128]{1,0:T(8,128)(2,1)S(1)} %get-tuple-element.49.own, bf16[768,128]{1,0:T(8,128)(2,1)S(1)} %collective-permute-done.14.got, bf16[384,128]{1,0:T(8,128)(2,1)S(1)} %get-tuple-element.50.own_d, ...), custom_call_target="tpu_custom_call" | custom-call | flops 201326592 | bytes 5505024 | tf_op jit(solution)/shard_map/pallas_call | solution.py:595
  (25 shorter events, 3.5 us)
Async XLA Ops:
  2.3 5.2 %collective-permute-start = (bf16[272,1024]{1,0:T(8,128)(2,1)S(1)}, bf16[272,1024]{1,0:T(8,128)(2,1)S(1)}, u32[]{:S(2)}, u32[]{:S(2)}) collective-permute-start(bf16[272,1024]{1,0:T(8,128)(2,1)S(1)} %get-tuple-element.31.after_ref.refs_0_.refs_5_), channel_id=1, source_target_pairs={{0,1},{1,0},{2,3},{3,2},{4,5},{5,4},{6,7},{7,6},{8,9},{9,8},{10,11... | collective-permute-start | bytes 1671176 | tf_op jit(solution)/shard_map/ppermute | solution.py:609
  2.8 9.7 %collective-permute-start.1 = (bf16[128,1024]{1,0:T(8,128)(2,1)S(1)}, bf16[128,1024]{1,0:T(8,128)(2,1)S(1)}, u32[]{:S(2)}, u32[]{:S(2)}) collective-permute-start(bf16[128,1024]{1,0:T(8,128)(2,1)S(1)} %get-tuple-element.33), channel_id=1, source_target_pairs={{0,2},{1,3},{2,0},{3,1},{4,6},{5,7},{6,4},{7,5},{8,10},{9,11},{10,... | collective-permute-start | bytes 786440 | tf_op jit(solution)/shard_map/ppermute | solution.py:609
  5.4 9.2 %collective-permute-start.2 = (bf16[128,1024]{1,0:T(8,128)(2,1)S(1)}, bf16[128,1024]{1,0:T(8,128)(2,1)S(1)}, u32[]{:S(2)}, u32[]{:S(2)}) collective-permute-start(bf16[128,1024]{1,0:T(8,128)(2,1)S(1)} %get-tuple-element.33), channel_id=1, source_target_pairs={{0,4},{1,5},{2,6},{3,7},{4,0},{5,1},{6,2},{7,3},{8,12},{9,13},{10,... | collective-permute-start | bytes 786440 | tf_op jit(solution)/shard_map/ppermute | solution.py:609
  7.0 13.1 %collective-permute-start.7 = (bf16[144,1024]{1,0:T(8,128)(2,1)S(1)}, bf16[144,1024]{1,0:T(8,128)(2,1)S(1)}, u32[]{:S(2)}, u32[]{:S(2)}) collective-permute-start(bf16[144,1024]{1,0:T(8,128)(2,1)S(1)} %get-tuple-element.37), channel_id=1, source_target_pairs={{0,4},{1,5},{2,6},{3,7},{4,0},{5,1},{6,2},{7,3},{8,12},{9,13},{10,... | collective-permute-start | bytes 884744 | tf_op jit(solution)/shard_map/ppermute | solution.py:609
  7.4 12.7 %collective-permute-start.6 = (bf16[144,1024]{1,0:T(8,128)(2,1)S(1)}, bf16[144,1024]{1,0:T(8,128)(2,1)S(1)}, u32[]{:S(2)}, u32[]{:S(2)}) collective-permute-start(bf16[144,1024]{1,0:T(8,128)(2,1)S(1)} %get-tuple-element.37), channel_id=1, source_target_pairs={{0,2},{1,3},{2,0},{3,1},{4,6},{5,7},{6,4},{7,5},{8,10},{9,11},{10,... | collective-permute-start | bytes 884744 | tf_op jit(solution)/shard_map/ppermute | solution.py:609
  8.1 12.0 %collective-permute-start.3 = (bf16[1152,128]{1,0:T(8,128)(2,1)S(1)}, bf16[1152,128]{1,0:T(8,128)(2,1)S(1)}, u32[]{:S(2)}, u32[]{:S(2)}) collective-permute-start(bf16[1152,128]{1,0:T(8,128)(2,1)S(1)} %get-tuple-element.35.own), channel_id=1, source_target_pairs={{0,8},{8,0},{16,24},{24,16},{1,9},{9,1},{17,25},{25,17},{2,10},{10... | collective-permute-start | bytes 884744 | tf_op jit(solution)/shard_map/ppermute | solution.py:609
  12.6 7.5 %collective-permute-start.5 = (bf16[128,1024]{1,0:T(8,128)(2,1)S(1)}, bf16[128,1024]{1,0:T(8,128)(2,1)S(1)}, u32[]{:S(2)}, u32[]{:S(2)}) collective-permute-start(bf16[128,1024]{1,0:T(8,128)(2,1)S(1)} %collective-permute-done.1.refs_0_), channel_id=1, source_target_pairs={{0,1},{1,0},{2,3},{3,2},{4,5},{5,4},{6,7},{7,6},{8,9},{9,8},{10,11... | collective-permute-start | bytes 786440 | tf_op jit(solution)/shard_map/ppermute | solution.py:609
  14.9 5.2 %collective-permute-start.4 = (bf16[384,128]{1,0:T(8,128)(2,1)S(1)}, bf16[384,128]{1,0:T(8,128)(2,1)S(1)}, u32[]{:S(2)}, u32[]{:S(2)}) collective-permute-start(bf16[384,128]{1,0:T(8,128)(2,1)S(1)} %get-tuple-element.36.near_own), channel_id=1, source_target_pairs={{0,8},{8,0},{16,24},{24,16},{1,9},{9,1},{17,25},{25,17},{2,10},{10... | collective-permute-start | bytes 294920 | tf_op jit(solution)/shard_map/ppermute | solution.py:609
  20.4 2.4 %collective-permute-start.8 = (bf16[416,1024]{1,0:T(8,128)(2,1)S(1)}, bf16[416,1024]{1,0:T(8,128)(2,1)S(1)}, u32[]{:S(2)}, u32[]{:S(2)}) collective-permute-start(bf16[416,1024]{1,0:T(8,128)(2,1)S(1)} %get-tuple-element.42.refs_0_.refs_1_), channel_id=1, source_target_pairs={{0,1},{1,0},{2,3},{3,2},{4,5},{5,4},{6,7},{7,6},{8,9},{9,8},{10,11... | collective-permute-start | bytes 2555912 | tf_op jit(solution)/shard_map/ppermute | solution.py:609
  20.4 9.6 %collective-permute-start.9 = (bf16[272,1024]{1,0:T(8,128)(2,1)S(1)}, bf16[272,1024]{1,0:T(8,128)(2,1)S(1)}, u32[]{:S(2)}, u32[]{:S(2)}) collective-permute-start(bf16[272,1024]{1,0:T(8,128)(2,1)S(1)} %get-tuple-element.39.after_ref), channel_id=1, source_target_pairs={{0,4},{1,3},{2,6},{3,1},{4,0},{5,7},{6,2},{7,5},{8,12},{9,11},{10,... | collective-permute-start | bytes 1671176 | tf_op jit(solution)/shard_map/ppermute | solution.py:635
  23.7 14.1 %collective-permute-start.16 = (bf16[1920,128]{1,0:T(8,128)(2,1)S(1)}, bf16[1920,128]{1,0:T(8,128)(2,1)S(1)}, u32[]{:S(2)}, u32[]{:S(2)}) collective-permute-start(bf16[1920,128]{1,0:T(8,128)(2,1)S(1)} %get-tuple-element.52.own), channel_id=1, source_target_pairs={{0,8},{8,0},{16,24},{24,16},{1,9},{9,1},{17,25},{25,17},{2,10},{10... | collective-permute-start | bytes 1474568 | tf_op jit(solution)/shard_map/ppermute | solution.py:609
  30.1 2.1 %collective-permute-start.13 = (bf16[80,1024]{1,0:T(8,128)(2,1)S(1)}, bf16[80,1024]{1,0:T(8,128)(2,1)S(1)}, u32[]{:S(2)}, u32[]{:S(2)}) collective-permute-start(bf16[80,1024]{1,0:T(8,128)(2,1)S(1)} %get-tuple-element.48.refs_3_.refs_1_.refs_2_), channel_id=1, source_target_pairs={{0,1},{1,0},{2,3},{3,2},{4,5},{5,4},{6,7},{7,6},{8,9},{9,8},{10,11... | collective-permute-start | bytes 491528 | tf_op jit(solution)/shard_map/ppermute | solution.py:609
  30.1 1.6 %collective-permute-start.10 = (bf16[64,1024]{1,0:T(8,128)(2,1)S(1)}, bf16[64,1024]{1,0:T(8,128)(2,1)S(1)}, u32[]{:S(2)}, u32[]{:S(2)}) collective-permute-start(bf16[64,1024]{1,0:T(8,128)(2,1)S(1)} %get-tuple-element.45.refs_0_), channel_id=1, source_target_pairs={{0,1},{1,0},{2,3},{3,2},{4,5},{5,4},{6,7},{7,6},{8,9},{9,8},{10,11... | collective-permute-start | bytes 393224 | tf_op jit(solution)/shard_map/ppermute | solution.py:609
  30.6 1.3 %collective-permute-start.11 = (bf16[64,1024]{1,0:T(8,128)(2,1)S(1)}, bf16[64,1024]{1,0:T(8,128)(2,1)S(1)}, u32[]{:S(2)}, u32[]{:S(2)}) collective-permute-start(bf16[64,1024]{1,0:T(8,128)(2,1)S(1)} %get-tuple-element.46.refs_1_), channel_id=1, source_target_pairs={{0,1},{1,0},{2,3},{3,2},{4,5},{5,4},{6,7},{7,6},{8,9},{9,8},{10,11... | collective-permute-start | bytes 393224 | tf_op jit(solution)/shard_map/ppermute | solution.py:609
  30.7 1.5 %collective-permute-start.12 = (bf16[64,1024]{1,0:T(8,128)(2,1)S(1)}, bf16[64,1024]{1,0:T(8,128)(2,1)S(1)}, u32[]{:S(2)}, u32[]{:S(2)}) collective-permute-start(bf16[64,1024]{1,0:T(8,128)(2,1)S(1)} %get-tuple-element.47.refs_2_.refs_0_), channel_id=1, source_target_pairs={{0,1},{1,0},{2,3},{3,2},{4,5},{5,4},{6,7},{7,6},{8,9},{9,8},{10,11... | collective-permute-start | bytes 393224 | tf_op jit(solution)/shard_map/ppermute | solution.py:609
  33.2 8.8 %collective-permute-start.14 = (bf16[768,128]{1,0:T(8,128)(2,1)S(1)}, bf16[768,128]{1,0:T(8,128)(2,1)S(1)}, u32[]{:S(2)}, u32[]{:S(2)}) collective-permute-start(bf16[768,128]{1,0:T(8,128)(2,1)S(1)} %get-tuple-element.49.own), channel_id=1, source_target_pairs={{0,8},{8,0},{16,24},{24,16},{1,9},{9,1},{17,25},{25,17},{2,10},{10... | collective-permute-start | bytes 589832 | tf_op jit(solution)/shard_map/ppermute | solution.py:609
  34.8 8.5 %collective-permute-start.15 = (bf16[384,128]{1,0:T(8,128)(2,1)S(1)}, bf16[384,128]{1,0:T(8,128)(2,1)S(1)}, u32[]{:S(2)}, u32[]{:S(2)}) collective-permute-start(bf16[384,128]{1,0:T(8,128)(2,1)S(1)} %get-tuple-element.50.own_d), channel_id=1, source_target_pairs={{0,8},{8,0},{16,24},{24,16},{1,9},{9,1},{17,25},{25,17},{2,10},{10... | collective-permute-start | bytes 294920 | tf_op jit(solution)/shard_map/ppermute | solution.py:609
  37.8 4.2 %copy-start = (bf16[3,192,1024]{2,1,0:T(8,128)(2,1)S(1)}, bf16[3,192,1024]{2,1,0:T(8,128)(2,1)}, u32[]{:S(2)}) copy-start(bf16[3,192,1024]{2,1,0:T(8,128)(2,1)} %refs_7_.1) | copy-start | bytes 3538948
  37.8 4.2 %copy-start.1 = (bf16[3,192,1024]{2,1,0:T(8,128)(2,1)S(1)}, bf16[3,192,1024]{2,1,0:T(8,128)(2,1)}, u32[]{:S(2)}) copy-start(bf16[3,192,1024]{2,1,0:T(8,128)(2,1)} %refs_8_.1) | copy-start | bytes 3538948

commit v7 on v6

--- a/solution.py
+++ b/solution.py
@@ -277,10 +277,10 @@
             row = row + piece.shape[0]
 
 
-def partial_kernel(kinds, count, w_ref, after_ref, *refs):
+def partial_kernel(kinds, count, tokened, w_ref, after_ref, *refs):
     n = len(kinds)
     xs, ys, gates = views(refs[:n], kinds, count)
-    outs = refs[n:-1]
+    outs = refs[n : n + len(refs[n:]) - tokened]
     mats, hidden, width = w_ref.shape
     parts = []
     if xs:
@@ -292,22 +292,57 @@
     else:
         for part, out_ref in zip(parts, outs):
             store_partials([part], count, out_ref)
-    refs[-1][...] = jnp.zeros_like(refs[-1])
-
-
-def partials(weights, after, chunk, rows, count):
+    if tokened:
+        refs[-1][...] = jnp.zeros_like(refs[-1])
+
+
+def partials(weights, after, chunk, rows, count, tokened=1):
     hidden, width = weights.shape[1:]
     kinds = kinds_of(chunk)
     total = sum(rows) * hidden * count
     return pl.pallas_call(
-        functools.partial(partial_kernel, kinds, count),
+        functools.partial(partial_kernel, kinds, count, tokened),
         in_specs=[whole(), unread()] + [whole()] * len(kinds),
-        out_specs=[whole()] * (len(rows) + 1),
+        out_specs=[whole()] * (len(rows) + tokened),
         out_shape=[jax.ShapeDtypeStruct((k * hidden, count), jnp.bfloat16) for k in rows]
-        + [jax.ShapeDtypeStruct((8, 128), jnp.float32)],
+        + [jax.ShapeDtypeStruct((8, 128), jnp.float32)] * tokened,
         compiler_params=params(),
         cost_estimate=cost(2 * total * width, 6 * total),
     )(weights, after, *values_of(chunk))
+
+
+def side_kernel(kinds, count, gu_row, down_row, has_send, w_ref, *refs):
+    n = len(kinds)
+    xs, ys, gates = views(refs[:n], kinds, count)
+    send_ref, token_ref = refs[n + has_send :]
+    mats, hidden, width = w_ref.shape
+    gu = contract_last(w_ref[0:2].reshape(2 * hidden, width), joined(xs))
+    down = contract_last(w_ref[2], joined(ys))
+    for row, part in ((gu_row, gu), (down_row, down)):
+        rows = part.shape[1] // count * part.shape[0]
+        store_partials([part], count, send_ref.at[row : row + rows, :])
+    token_ref[...] = jnp.zeros_like(token_ref)
+
+
+def side_partials(weights, chunk, send, blocks, first_gu, first_down, count):
+    hidden, width = weights.shape[1:]
+    kinds = kinds_of(chunk)
+    operands = [weights, *values_of(chunk)] + ([] if send is None else [send])
+    gu_row = first_gu * 2 * hidden
+    down_row = (2 * blocks[0] + first_down) * hidden
+    shape = ((2 * blocks[0] + blocks[1]) * hidden, count)
+    return pl.pallas_call(
+        functools.partial(side_kernel, kinds, count, gu_row, down_row, send is not None),
+        in_specs=[whole()] * len(operands),
+        out_specs=[whole()] * 2,
+        out_shape=[
+            jax.ShapeDtypeStruct(shape, jnp.bfloat16),
+            jax.ShapeDtypeStruct((8, 128), jnp.float32),
+        ],
+        input_output_aliases={} if send is None else {len(operands) - 1: 0},
+        compiler_params=params(),
+        cost_estimate=cost(shape[0] * count * width, 3 * shape[0] * count),
+    )(*operands)
 
 
 def start_kernel(kinds, count, w_hbm, *refs):
@@ -412,18 +447,8 @@
     rest_ref[0:count, :] = x1_ref[...]
     rest_ref[count : count + rows, :] = y0_ref[...]
     rest_ref[count + rows :, :] = y1_ref[...]
-    core = lax.axis_index("dp") % 2
-
-    @pl.when(core == 0)
-    def _():
-        out_ref[0:count, :] = x0_ref[...]
-        out_ref[count:, :] = y0_ref[...]
-
-    @pl.when(core != 0)
-    def _():
-        out_ref[0:count, :] = x1_ref[...]
-        out_ref[count:, :] = y1_ref[...]
-
+    out_ref[0:count, :] = x0_ref[...]
+    out_ref[count:, :] = y0_ref[...]
     first_ref[...] = own[...].astype(jnp.float32) + got[...].astype(jnp.float32)
     sum_ref[...] = near_own[...].astype(jnp.float32) + near_got[...].astype(jnp.float32)
 
@@ -624,23 +649,24 @@
     first = [("xy", own), ("xy", other(own))]
     send, token = partials(weights, own, first, (6,), count)
     first_pair = (send, partner(send))
-    near_x = [from_masked(x_own, "dp", mask) for mask in (2, 4)]
-    near_y = [from_masked(y_own, "dp", mask) for mask in (2, 4)]
+    along = [[(p, p ^ (2 if p % 2 == k else 4)) for p in range(n_data)] for k in (0, 1)]
+    near_x = [lax.ppermute(x_own, "dp", pairs) for pairs in along]
+    near_y = [lax.ppermute(y_own, "dp", pairs) for pairs in along]
     send, token = partials(weights, token, [("x", near_x[0]), ("", near_x[1])], (2,), count)
     near_pair = (send, partner(send))
     x_pair, rest, picked, first_sum, near_sum, gate = pick_onward(
         token, first_pair, near_pair, near_x, other(near_x[0]), near_y, first
     )
-    onward = [(p, p ^ 4 if p % 2 == 0 else p ^ 2) for p in range(n_data)]
-    far = lax.ppermute(picked, "dp", onward)
-    acc, token = first_grads(gate, picked, first_sum, first, hidden, count)
+    far = lax.ppermute(picked, "dp", along[1])
     ends = [("x, y, y", rest), ("second x", x_pair), ("x, y, y", other(rest))]
-    send, token = partials(weights, token, ends, (10,), count)
+    send, token = side_partials(weights, ends[:2], None, (3, 4), 0, 0, count)
+    send, token = side_partials(weights, ends[2:], send, (3, 4), 2, 2, count)
     more_pair = (send, partner(send))
+    acc, token = first_grads(gate, token, first_sum, first, hidden, count)
     pieces = passed_on(token, far, (count // 2, count // 2, count // 2, count // 2 + slots))
     pieces = [*pieces, *[other(value) for value in pieces]]
     final = list(zip(("x", "x", "y", "half y, gates") * 2, pieces))
-    send, send_d, token = partials(weights, token, final, (4, 2), count)
+    send, send_d = partials(weights, token, final, (4, 2), count, 0)
     pair, down_pair = (send, partner(send)), (send_d, partner(send_d))
     near = [("first x", x_pair), *ends]
     acc = add_grads(near_sum, more_pair, near, acc, count)

time: 45.7 us -> 44.9 us (0.982)
  waiting for transfers between devices: 20.3 us -> 19.3 us
    ppermute x16 -> x12, waiting for transfers between devices: 15.6 us -> 8.54 us  [from_masked(): return lax.ppermute(value, axis, pairs)]
    ppermute x1 -> x5, waiting for transfers between devices: 4.71 us -> 10.7 us  [the longest x2 4.48 us: dense_plan(): near_x = [lax.ppermute(x_own, 'dp', pairs) for pairs in along]]
    ppermute x1 -> x5, starting transfers between devices: 1.58 us -> 6.28 us  [the longest x2 4.1 us: dense_plan(): near_x = [lax.ppermute(x_own, 'dp', pairs) for pairs in along]]
    ppermute x16 -> x12, starting transfers between devices: 13.7 us -> 9.16 us  [from_masked(): return lax.ppermute(value, axis, pairs)]
    pallas_call x4 -> x5, Pallas kernels: 2.84 us -> 3.01 us  [the longest x2 1.55 us: side_partials(): pl.pallas_call(functools.partial(side_kernel, kinds, count, gu_row, down_...]
  transfers between devices with their start and end apart: 17 -> 17, of which waited for: 11 -> 12; matrix products, arithmetic and copies ran while one was open for 0% -> 0% of each run, Pallas kernels for 11% -> 12%
where the time goes in v7:
time: 44.9 us; the launch traced here: 44.7 us
  waiting for transfers between devices  19.3 us (43%)
  starting transfers between devices  15.4 us (34%)
  Pallas kernels  9.27 us (21%)
  between operations  0.74 us (2%)
    ppermute x12, starting transfers between devices, from_masked(): return lax.ppermute(value, axis, pairs)  9.16 us
    ppermute x12, waiting for transfers between devices, from_masked(): return lax.ppermute(value, axis, pairs)  8.54 us
    ppermute x2, waiting for transfers between devices, dense_plan(): near_x = [lax.ppermute(x_own, 'dp', pairs) for pairs in along]  4.48 us
    ppermute x1, waiting for transfers between devices, dense_plan(): far = lax.ppermute(picked, 'dp', along[1])  4.26 us
    ppermute x2, starting transfers between devices, dense_plan(): near_x = [lax.ppermute(x_own, 'dp', pairs) for pairs in along]  4.1 us
    pallas_call x1, Pallas kernels, slopes_update(): pl.pallas_call(functools.partial(slopes_kernel, kinds, count), in_specs=[...  2.19 us
    ppermute x2, waiting for transfers between devices, dense_plan(): near_y = [lax.ppermute(y_own, 'dp', pairs) for pairs in along]  1.98 us
    pallas_call x1, Pallas kernels, pack_own(): pl.pallas_call(pack_kernel, in_specs=[in_hbm()] * 5, out_specs=[whole()]...  1.69 us
  transfers between devices with their start and end apart: 17, of which 12 were waited for; matrix products, arithmetic and copies ran while one was open for 0% of the time, Pallas kernels for 12%

profile of v7, /device:TPU:0, one launch (start us, length us, event | category | flops | bytes accessed | tf_op | source)
XLA Modules:
  0.0 44.7 jit_solution(14828571001866881520)
XLA Ops:
  0.6 1.7 %shard_map.94 = (bf16[128,1024]{1,0:T(8,128)(2,1)S(1)}, bf16[144,1024]{1,0:T(8,128)(2,1)S(1)}, bf16[272,1024]{1,0:T(8,128)(2,1)S(1)}, bf16[3,192,1024]{2,1,0:T(8,128)(2,1)S(1)}) custom-call(s32[4,128]{1,0:T(4,128)} %bitcast.2, bf16[4,128]{1,0:T(4,128)(2,1)} %bitcast.3, bf16[128,2048]{1,0:T(8,128)(2,1)} %tokens_ref.1, bf16[128,2048]{1,0:T(8,128)(2,1)} %cot_ref.1, ...), custom_call_target="tpu_custom_call" | custom-call | flops 1000 | bytes 1048576 | tf_op jit(solution)/shard_map/pallas_call | solution.py:209
  2.8 2.6 %collective-permute-start.1 = (bf16[128,1024]{1,0:T(8,128)(2,1)S(1)}, bf16[128,1024]{1,0:T(8,128)(2,1)S(1)}, u32[]{:S(2)}, u32[]{:S(2)}) collective-permute-start(bf16[128,1024]{1,0:T(8,128)(2,1)S(1)} %get-tuple-element.34), channel_id=1, source_target_pairs={{0,2},{1,5},{2,0},{3,7},{4,6},{5,1},{6,4},{7,3},{8,10},{9,13},{10,... | collective-permute-start | bytes 786440 | tf_op jit(solution)/shard_map/ppermute | solution.py:653
  5.4 1.5 %collective-permute-start.2 = (bf16[128,1024]{1,0:T(8,128)(2,1)S(1)}, bf16[128,1024]{1,0:T(8,128)(2,1)S(1)}, u32[]{:S(2)}, u32[]{:S(2)}) collective-permute-start(bf16[128,1024]{1,0:T(8,128)(2,1)S(1)} %get-tuple-element.34), channel_id=1, source_target_pairs={{0,4},{1,3},{2,6},{3,1},{4,0},{5,7},{6,2},{7,5},{8,12},{9,11},{10,... | collective-permute-start | bytes 786440 | tf_op jit(solution)/shard_map/ppermute | solution.py:653
  7.5 0.5 %shard_map.95 = (bf16[1152,128]{1,0:T(8,128)(2,1)S(1)}, f32[8,128]{1,0:T(8,128)S(1)}) custom-call(bf16[3,192,1024]{2,1,0:T(8,128)(2,1)S(1)} %get-tuple-element.31.w_ref, bf16[272,1024]{1,0:T(8,128)(2,1)S(1)} %get-tuple-element.32.after_ref.refs_0_.refs_5_, bf16[272,1024]{1,0:T(8,128)(2,1)S(1)} %get-tuple-element.32.after_ref.refs_0_.refs_5_, ...), custom_call_target="tpu_custom_call" | custom-call | flops 301989888 | bytes 884736 | tf_op jit(solution)/shard_map/pallas_call | solution.py:303
  8.1 2.1 %collective-permute-start.3 = (bf16[1152,128]{1,0:T(8,128)(2,1)S(1)}, bf16[1152,128]{1,0:T(8,128)(2,1)S(1)}, u32[]{:S(2)}, u32[]{:S(2)}) collective-permute-start(bf16[1152,128]{1,0:T(8,128)(2,1)S(1)} %get-tuple-element.36.own), channel_id=1, source_target_pairs={{0,8},{8,0},{16,24},{24,16},{1,9},{9,1},{17,25},{25,17},{2,10},{10... | collective-permute-start | bytes 884744 | tf_op jit(solution)/shard_map/ppermute | solution.py:634
  10.2 1.3 %collective-permute-done.1.refs_0_ = bf16[128,1024]{1,0:T(8,128)(2,1)S(1)} collective-permute-done((bf16[128,1024]{1,0:T(8,128)(2,1)S(1)}, bf16[128,1024]{1,0:T(8,128)(2,1)S(1)}, u32[]{:S(2)}, u32[]{:S(2)}) %collective-permute-start.1) | collective-permute-done | bytes 262176 | tf_op jit(solution)/shard_map/ppermute | solution.py:653
  11.5 3.2 %collective-permute-done.2.refs_1_ = bf16[128,1024]{1,0:T(8,128)(2,1)S(1)} collective-permute-done((bf16[128,1024]{1,0:T(8,128)(2,1)S(1)}, bf16[128,1024]{1,0:T(8,128)(2,1)S(1)}, u32[]{:S(2)}, u32[]{:S(2)}) %collective-permute-start.2) | collective-permute-done | bytes 262176 | tf_op jit(solution)/shard_map/ppermute | solution.py:653
  15.0 1.7 %collective-permute-start.4 = (bf16[384,128]{1,0:T(8,128)(2,1)S(1)}, bf16[384,128]{1,0:T(8,128)(2,1)S(1)}, u32[]{:S(2)}, u32[]{:S(2)}) collective-permute-start(bf16[384,128]{1,0:T(8,128)(2,1)S(1)} %get-tuple-element.37.near_own), channel_id=1, source_target_pairs={{0,8},{8,0},{16,24},{24,16},{1,9},{9,1},{17,25},{25,17},{2,10},{10... | collective-permute-start | bytes 294920 | tf_op jit(solution)/shard_map/ppermute | solution.py:634
  16.7 1.1 %collective-permute-done.6.refs_3_ = bf16[144,1024]{1,0:T(8,128)(2,1)S(1)} collective-permute-done((bf16[144,1024]{1,0:T(8,128)(2,1)S(1)}, bf16[144,1024]{1,0:T(8,128)(2,1)S(1)}, u32[]{:S(2)}, u32[]{:S(2)}) %collective-permute-start.6) | collective-permute-done | bytes 294944 | tf_op jit(solution)/shard_map/ppermute | solution.py:654
  17.8 0.9 %collective-permute-done.7.refs_4_ = bf16[144,1024]{1,0:T(8,128)(2,1)S(1)} collective-permute-done((bf16[144,1024]{1,0:T(8,128)(2,1)S(1)}, bf16[144,1024]{1,0:T(8,128)(2,1)S(1)}, u32[]{:S(2)}, u32[]{:S(2)}) %collective-permute-start.7) | collective-permute-done | bytes 294944 | tf_op jit(solution)/shard_map/ppermute | solution.py:654
  18.7 1.0 %collective-permute-done.4.near_got = bf16[384,128]{1,0:T(8,128)(2,1)S(1)} collective-permute-done((bf16[384,128]{1,0:T(8,128)(2,1)S(1)}, bf16[384,128]{1,0:T(8,128)(2,1)S(1)}, u32[]{:S(2)}, u32[]{:S(2)}) %collective-permute-start.4) | collective-permute-done | bytes 98336 | tf_op jit(solution)/shard_map/ppermute | solution.py:634
  20.0 1.6 %collective-permute-start.9 = (bf16[272,1024]{1,0:T(8,128)(2,1)S(1)}, bf16[272,1024]{1,0:T(8,128)(2,1)S(1)}, u32[]{:S(2)}, u32[]{:S(2)}) collective-permute-start(bf16[272,1024]{1,0:T(8,128)(2,1)S(1)} %get-tuple-element.46), channel_id=1, source_target_pairs={{0,4},{1,3},{2,6},{3,1},{4,0},{5,7},{6,2},{7,5},{8,12},{9,11},{10,... | collective-permute-start | bytes 1671176 | tf_op jit(solution)/shard_map/ppermute | solution.py:660
  21.6 1.0 %shard_map.98 = (bf16[1920,128]{1,0:T(8,128)(2,1)S(1)}, f32[8,128]{1,0:T(8,128)}) custom-call(bf16[3,192,1024]{2,1,0:T(8,128)(2,1)S(1)} %get-tuple-element.31.w_ref, bf16[416,1024]{1,0:T(8,128)(2,1)S(1)} %get-tuple-element.40.refs_0_.refs_1_, bf16[2,128,1024]{2,1,0:T(8,128)(2,1)S(1)} %get-tuple-element.41.refs_1_.refs_0_.refs_2_), custom_call_target="tpu_custom_call" | custom-call | flops 251658240 | bytes 737280 | tf_op jit(solution)/shard_map/pallas_call | solution.py:334
  23.2 1.6 %collective-permute-start.16 = (bf16[1920,128]{1,0:T(8,128)(2,1)S(1)}, bf16[1920,128]{1,0:T(8,128)(2,1)S(1)}, u32[]{:S(2)}, u32[]{:S(2)}) collective-permute-start(bf16[1920,128]{1,0:T(8,128)(2,1)S(1)} %get-tuple-element.54.own), channel_id=1, source_target_pairs={{0,8},{8,0},{16,24},{24,16},{1,9},{9,1},{17,25},{25,17},{2,10},{10... | collective-permute-start | bytes 1474568 | tf_op jit(solution)/shard_map/ppermute | solution.py:634
  25.3 4.3 %collective-permute-done.9.in_ref = bf16[272,1024]{1,0:T(8,128)(2,1)S(1)} collective-permute-done((bf16[272,1024]{1,0:T(8,128)(2,1)S(1)}, bf16[272,1024]{1,0:T(8,128)(2,1)S(1)}, u32[]{:S(2)}, u32[]{:S(2)}) %collective-permute-start.9) | collective-permute-done | bytes 557088 | tf_op jit(solution)/shard_map/ppermute | solution.py:660
  30.7 0.6 %collective-permute-done.10.refs_4_.refs_3_ = bf16[64,1024]{1,0:T(8,128)(2,1)S(1)} collective-permute-done((bf16[64,1024]{1,0:T(8,128)(2,1)S(1)}, bf16[64,1024]{1,0:T(8,128)(2,1)S(1)}, u32[]{:S(2)}, u32[]{:S(2)}) %collective-permute-start.10) | collective-permute-done | bytes 131104 | tf_op jit(solution)/shard_map/ppermute | solution.py:634
  31.7 0.6 %shard_map.102 = (bf16[768,128]{1,0:T(8,128)(2,1)S(1)}, bf16[384,128]{1,0:T(8,128)(2,1)S(1)}) custom-call(bf16[3,192,1024]{2,1,0:T(8,128)(2,1)S(1)} %get-tuple-element.31.w_ref, f32[8,128]{1,0:T(8,128)S(1)} %get-tuple-element.45.after_ref, bf16[64,1024]{1,0:T(8,128)(2,1)S(1)} %get-tuple-element.47.refs_0_, bf16[64,1024]{1,0:T(8,128)(2,1)S(1)} %get-tuple-element.48.refs_1_, ...), custom_call_target="tpu_custom_call" | custom-call | flops 301989888 | bytes 884736 | tf_op jit(solution)/shard_map/pallas_call | solution.py:303
  32.3 1.6 %collective-permute-start.14 = (bf16[768,128]{1,0:T(8,128)(2,1)S(1)}, bf16[768,128]{1,0:T(8,128)(2,1)S(1)}, u32[]{:S(2)}, u32[]{:S(2)}) collective-permute-start(bf16[768,128]{1,0:T(8,128)(2,1)S(1)} %get-tuple-element.51.own), channel_id=1, source_target_pairs={{0,8},{8,0},{16,24},{24,16},{1,9},{9,1},{17,25},{25,17},{2,10},{10... | collective-permute-start | bytes 589832 | tf_op jit(solution)/shard_map/ppermute | solution.py:634
  34.4 2.6 %collective-permute-done.16.got = bf16[1920,128]{1,0:T(8,128)(2,1)S(1)} collective-permute-done((bf16[1920,128]{1,0:T(8,128)(2,1)S(1)}, bf16[1920,128]{1,0:T(8,128)(2,1)S(1)}, u32[]{:S(2)}, u32[]{:S(2)}) %collective-permute-start.16) | collective-permute-done | bytes 491552 | tf_op jit(solution)/shard_map/ppermute | solution.py:634
  37.0 1.0 %shard_map.103.refs_4_.refs_6_ = f32[3,192,1024]{2,1,0:T(8,128)S(1)} custom-call(f32[384,128]{1,0:T(8,128)S(1)} %get-tuple-element.53.sum_ref, bf16[1920,128]{1,0:T(8,128)(2,1)S(1)} %get-tuple-element.54.own, bf16[1920,128]{1,0:T(8,128)(2,1)S(1)} %collective-permute-done.16.got, ...), custom_call_target="tpu_custom_call", output_to_operand_aliasing={{}: (7, {})} | custom-call | flops 603979776 | bytes 4718592 | tf_op jit(solution)/shard_map/pallas_call | solution.py:537
  38.1 3.2 %collective-permute-done.14.got = bf16[768,128]{1,0:T(8,128)(2,1)S(1)} collective-permute-done((bf16[768,128]{1,0:T(8,128)(2,1)S(1)}, bf16[768,128]{1,0:T(8,128)(2,1)S(1)}, u32[]{:S(2)}, u32[]{:S(2)}) %collective-permute-start.14) | collective-permute-done | bytes 196640 | tf_op jit(solution)/shard_map/ppermute | solution.py:634
  41.3 0.6 %shard_map.104 = (bf16[192,1024]{1,0:T(8,128)(2,1)S(1)}, bf16[192,1024]{1,0:T(8,128)(2,1)S(1)}, bf16[192,1024]{1,0:T(8,128)(2,1)S(1)}) custom-call(bf16[768,128]{1,0:T(8,128)(2,1)S(1)} %get-tuple-element.51.own, bf16[768,128]{1,0:T(8,128)(2,1)S(1)} %collective-permute-done.14.got, bf16[64,1024]{1,0:T(8,128)(2,1)S(1)} %get-tuple-element.49.refs_2_.refs_0_, ...), custom_call_target="tpu_custom_call" | custom-call | flops 100663296 | bytes 2752512 | tf_op jit(solution)/shard_map/pallas_call | solution.py:580
  41.9 0.6 %collective-permute-done.15.got_d = bf16[384,128]{1,0:T(8,128)(2,1)S(1)} collective-permute-done((bf16[384,128]{1,0:T(8,128)(2,1)S(1)}, bf16[384,128]{1,0:T(8,128)(2,1)S(1)}, u32[]{:S(2)}, u32[]{:S(2)}) %collective-permute-start.15) | collective-permute-done | bytes 98336 | tf_op jit(solution)/shard_map/ppermute | solution.py:634
  42.5 2.2 %shard_map.105 = (bf16[3,192,1024]{2,1,0:T(8,128)(2,1)}, bf16[3,192,1024]{2,1,0:T(8,128)(2,1)}, bf16[3,192,1024]{2,1,0:T(8,128)(2,1)}) custom-call(bf16[768,128]{1,0:T(8,128)(2,1)S(1)} %get-tuple-element.51.own, bf16[768,128]{1,0:T(8,128)(2,1)S(1)} %collective-permute-done.14.got, bf16[384,128]{1,0:T(8,128)(2,1)S(1)} %get-tuple-element.52.own_d, ...), custom_call_target="tpu_custom_call" | custom-call | flops 201326592 | bytes 5505024 | tf_op jit(solution)/shard_map/pallas_call | solution.py:620
  (26 shorter events, 4.8 us)
Async XLA Ops:
  2.3 5.2 %collective-permute-start = (bf16[272,1024]{1,0:T(8,128)(2,1)S(1)}, bf16[272,1024]{1,0:T(8,128)(2,1)S(1)}, u32[]{:S(2)}, u32[]{:S(2)}) collective-permute-start(bf16[272,1024]{1,0:T(8,128)(2,1)S(1)} %get-tuple-element.32.after_ref.refs_0_.refs_5_), channel_id=1, source_target_pairs={{0,1},{1,0},{2,3},{3,2},{4,5},{5,4},{6,7},{7,6},{8,9},{9,8},{10,11... | collective-permute-start | bytes 1671176 | tf_op jit(solution)/shard_map/ppermute | solution.py:634
  2.8 8.6 %collective-permute-start.1 = (bf16[128,1024]{1,0:T(8,128)(2,1)S(1)}, bf16[128,1024]{1,0:T(8,128)(2,1)S(1)}, u32[]{:S(2)}, u32[]{:S(2)}) collective-permute-start(bf16[128,1024]{1,0:T(8,128)(2,1)S(1)} %get-tuple-element.34), channel_id=1, source_target_pairs={{0,2},{1,5},{2,0},{3,7},{4,6},{5,1},{6,4},{7,3},{8,10},{9,13},{10,... | collective-permute-start | bytes 786440 | tf_op jit(solution)/shard_map/ppermute | solution.py:653
  5.4 9.2 %collective-permute-start.2 = (bf16[128,1024]{1,0:T(8,128)(2,1)S(1)}, bf16[128,1024]{1,0:T(8,128)(2,1)S(1)}, u32[]{:S(2)}, u32[]{:S(2)}) collective-permute-start(bf16[128,1024]{1,0:T(8,128)(2,1)S(1)} %get-tuple-element.34), channel_id=1, source_target_pairs={{0,4},{1,3},{2,6},{3,1},{4,0},{5,7},{6,2},{7,5},{8,12},{9,11},{10,... | collective-permute-start | bytes 786440 | tf_op jit(solution)/shard_map/ppermute | solution.py:653
  6.9 10.8 %collective-permute-start.6 = (bf16[144,1024]{1,0:T(8,128)(2,1)S(1)}, bf16[144,1024]{1,0:T(8,128)(2,1)S(1)}, u32[]{:S(2)}, u32[]{:S(2)}) collective-permute-start(bf16[144,1024]{1,0:T(8,128)(2,1)S(1)} %get-tuple-element.38), channel_id=1, source_target_pairs={{0,2},{1,5},{2,0},{3,7},{4,6},{5,1},{6,4},{7,3},{8,10},{9,13},{10,... | collective-permute-start | bytes 884744 | tf_op jit(solution)/shard_map/ppermute | solution.py:654
  7.5 11.2 %collective-permute-start.7 = (bf16[144,1024]{1,0:T(8,128)(2,1)S(1)}, bf16[144,1024]{1,0:T(8,128)(2,1)S(1)}, u32[]{:S(2)}, u32[]{:S(2)}) collective-permute-start(bf16[144,1024]{1,0:T(8,128)(2,1)S(1)} %get-tuple-element.38), channel_id=1, source_target_pairs={{0,4},{1,3},{2,6},{3,1},{4,0},{5,7},{6,2},{7,5},{8,12},{9,11},{10,... | collective-permute-start | bytes 884744 | tf_op jit(solution)/shard_map/ppermute | solution.py:654
  8.1 11.6 %collective-permute-start.3 = (bf16[1152,128]{1,0:T(8,128)(2,1)S(1)}, bf16[1152,128]{1,0:T(8,128)(2,1)S(1)}, u32[]{:S(2)}, u32[]{:S(2)}) collective-permute-start(bf16[1152,128]{1,0:T(8,128)(2,1)S(1)} %get-tuple-element.36.own), channel_id=1, source_target_pairs={{0,8},{8,0},{16,24},{24,16},{1,9},{9,1},{17,25},{25,17},{2,10},{10... | collective-permute-start | bytes 884744 | tf_op jit(solution)/shard_map/ppermute | solution.py:634
  11.5 7.2 %collective-permute-start.5 = (bf16[128,1024]{1,0:T(8,128)(2,1)S(1)}, bf16[128,1024]{1,0:T(8,128)(2,1)S(1)}, u32[]{:S(2)}, u32[]{:S(2)}) collective-permute-start(bf16[128,1024]{1,0:T(8,128)(2,1)S(1)} %collective-permute-done.1.refs_0_), channel_id=1, source_target_pairs={{0,1},{1,0},{2,3},{3,2},{4,5},{5,4},{6,7},{7,6},{8,9},{9,8},{10,11... | collective-permute-start | bytes 786440 | tf_op jit(solution)/shard_map/ppermute | solution.py:634
  15.0 4.7 %collective-permute-start.4 = (bf16[384,128]{1,0:T(8,128)(2,1)S(1)}, bf16[384,128]{1,0:T(8,128)(2,1)S(1)}, u32[]{:S(2)}, u32[]{:S(2)}) collective-permute-start(bf16[384,128]{1,0:T(8,128)(2,1)S(1)} %get-tuple-element.37.near_own), channel_id=1, source_target_pairs={{0,8},{8,0},{16,24},{24,16},{1,9},{9,1},{17,25},{25,17},{2,10},{10... | collective-permute-start | bytes 294920 | tf_op jit(solution)/shard_map/ppermute | solution.py:634
  19.9 2.7 %collective-permute-start.8 = (bf16[416,1024]{1,0:T(8,128)(2,1)S(1)}, bf16[416,1024]{1,0:T(8,128)(2,1)S(1)}, u32[]{:S(2)}, u32[]{:S(2)}) collective-permute-start(bf16[416,1024]{1,0:T(8,128)(2,1)S(1)} %get-tuple-element.40.refs_0_.refs_1_), channel_id=1, source_target_pairs={{0,1},{1,0},{2,3},{3,2},{4,5},{5,4},{6,7},{7,6},{8,9},{9,8},{10,11... | collective-permute-start | bytes 2555912 | tf_op jit(solution)/shard_map/ppermute | solution.py:634
  20.0 9.6 %collective-permute-start.9 = (bf16[272,1024]{1,0:T(8,128)(2,1)S(1)}, bf16[272,1024]{1,0:T(8,128)(2,1)S(1)}, u32[]{:S(2)}, u32[]{:S(2)}) collective-permute-start(bf16[272,1024]{1,0:T(8,128)(2,1)S(1)} %get-tuple-element.46), channel_id=1, source_target_pairs={{0,4},{1,3},{2,6},{3,1},{4,0},{5,7},{6,2},{7,5},{8,12},{9,11},{10,... | collective-permute-start | bytes 1671176 | tf_op jit(solution)/shard_map/ppermute | solution.py:660
  23.2 13.9 %collective-permute-start.16 = (bf16[1920,128]{1,0:T(8,128)(2,1)S(1)}, bf16[1920,128]{1,0:T(8,128)(2,1)S(1)}, u32[]{:S(2)}, u32[]{:S(2)}) collective-permute-start(bf16[1920,128]{1,0:T(8,128)(2,1)S(1)} %get-tuple-element.54.own), channel_id=1, source_target_pairs={{0,8},{8,0},{16,24},{24,16},{1,9},{9,1},{17,25},{25,17},{2,10},{10... | collective-permute-start | bytes 1474568 | tf_op jit(solution)/shard_map/ppermute | solution.py:634
  29.6 2.1 %collective-permute-start.13 = (bf16[80,1024]{1,0:T(8,128)(2,1)S(1)}, bf16[80,1024]{1,0:T(8,128)(2,1)S(1)}, u32[]{:S(2)}, u32[]{:S(2)}) collective-permute-start(bf16[80,1024]{1,0:T(8,128)(2,1)S(1)} %get-tuple-element.50.refs_3_.refs_1_.refs_2_), channel_id=1, source_target_pairs={{0,1},{1,0},{2,3},{3,2},{4,5},{5,4},{6,7},{7,6},{8,9},{9,8},{10,11... | collective-permute-start | bytes 491528 | tf_op jit(solution)/shard_map/ppermute | solution.py:634
  29.7 1.6 %collective-permute-start.10 = (bf16[64,1024]{1,0:T(8,128)(2,1)S(1)}, bf16[64,1024]{1,0:T(8,128)(2,1)S(1)}, u32[]{:S(2)}, u32[]{:S(2)}) collective-permute-start(bf16[64,1024]{1,0:T(8,128)(2,1)S(1)} %get-tuple-element.47.refs_0_), channel_id=1, source_target_pairs={{0,1},{1,0},{2,3},{3,2},{4,5},{5,4},{6,7},{7,6},{8,9},{9,8},{10,11... | collective-permute-start | bytes 393224 | tf_op jit(solution)/shard_map/ppermute | solution.py:634
  30.2 1.3 %collective-permute-start.11 = (bf16[64,1024]{1,0:T(8,128)(2,1)S(1)}, bf16[64,1024]{1,0:T(8,128)(2,1)S(1)}, u32[]{:S(2)}, u32[]{:S(2)}) collective-permute-start(bf16[64,1024]{1,0:T(8,128)(2,1)S(1)} %get-tuple-element.48.refs_1_), channel_id=1, source_target_pairs={{0,1},{1,0},{2,3},{3,2},{4,5},{5,4},{6,7},{7,6},{8,9},{9,8},{10,11... | collective-permute-start | bytes 393224 | tf_op jit(solution)/shard_map/ppermute | solution.py:634
  30.3 1.5 %collective-permute-start.12 = (bf16[64,1024]{1,0:T(8,128)(2,1)S(1)}, bf16[64,1024]{1,0:T(8,128)(2,1)S(1)}, u32[]{:S(2)}, u32[]{:S(2)}) collective-permute-start(bf16[64,1024]{1,0:T(8,128)(2,1)S(1)} %get-tuple-element.49.refs_2_.refs_0_), channel_id=1, source_target_pairs={{0,1},{1,0},{2,3},{3,2},{4,5},{5,4},{6,7},{7,6},{8,9},{9,8},{10,11... | collective-permute-start | bytes 393224 | tf_op jit(solution)/shard_map/ppermute | solution.py:634
  32.3 9.0 %collective-permute-start.14 = (bf16[768,128]{1,0:T(8,128)(2,1)S(1)}, bf16[768,128]{1,0:T(8,128)(2,1)S(1)}, u32[]{:S(2)}, u32[]{:S(2)}) collective-permute-start(bf16[768,128]{1,0:T(8,128)(2,1)S(1)} %get-tuple-element.51.own), channel_id=1, source_target_pairs={{0,8},{8,0},{16,24},{24,16},{1,9},{9,1},{17,25},{25,17},{2,10},{10... | collective-permute-start | bytes 589832 | tf_op jit(solution)/shard_map/ppermute | solution.py:634
  33.9 8.6 %collective-permute-start.15 = (bf16[384,128]{1,0:T(8,128)(2,1)S(1)}, bf16[384,128]{1,0:T(8,128)(2,1)S(1)}, u32[]{:S(2)}, u32[]{:S(2)}) collective-permute-start(bf16[384,128]{1,0:T(8,128)(2,1)S(1)} %get-tuple-element.52.own_d), channel_id=1, source_target_pairs={{0,8},{8,0},{16,24},{24,16},{1,9},{9,1},{17,25},{25,17},{2,10},{10... | collective-permute-start | bytes 294920 | tf_op jit(solution)/shard_map/ppermute | solution.py:634
  37.0 4.2 %copy-start = (bf16[3,192,1024]{2,1,0:T(8,128)(2,1)S(1)}, bf16[3,192,1024]{2,1,0:T(8,128)(2,1)}, u32[]{:S(2)}) copy-start(bf16[3,192,1024]{2,1,0:T(8,128)(2,1)} %refs_7_.1) | copy-start | bytes 3538948
  37.0 4.2 %copy-start.1 = (bf16[3,192,1024]{2,1,0:T(8,128)(2,1)S(1)}, bf16[3,192,1024]{2,1,0:T(8,128)(2,1)}, u32[]{:S(2)}) copy-start(bf16[3,192,1024]{2,1,0:T(8,128)(2,1)} %refs_8_.1) | copy-start | bytes 3538948

commit v8 on v7

--- a/solution.py
+++ b/solution.py
@@ -231,9 +231,13 @@
         if kind in ("first x", "second x"):
             xs.append(ref[0 if kind == "first x" else 1])
             continue
-        if kind == "x, y, y":
+        if kind == "x of xyy":
+            xs.append(ref[0:count, :])
+            continue
+        if kind in ("x, y, y", "y, y of xyy"):
             rows = (ref.shape[0] - count) // 2
-            xs.append(ref[0:count, :])
+            if kind == "x, y, y":
+                xs.append(ref[0:count, :])
             for row in (count, count + rows):
                 ys.append(ref[row : row + count, :])
                 gates.append(ref[row + count : row + rows, 0:count])
@@ -280,10 +284,12 @@
 def partial_kernel(kinds, count, tokened, w_ref, after_ref, *refs):
     n = len(kinds)
     xs, ys, gates = views(refs[:n], kinds, count)
-    outs = refs[n : n + len(refs[n:]) - tokened]
+    outs = refs[n : len(refs) - tokened]
     mats, hidden, width = w_ref.shape
     parts = []
-    if xs:
+    if xs and len(outs) == mats:
+        parts.extend(contract_last(w_ref[m], joined(xs)) for m in (0, 1))
+    elif xs:
         parts.append(contract_last(w_ref[0:2].reshape(2 * hidden, width), joined(xs)))
     if ys:
         parts.append(contract_last(w_ref[2], joined(ys)))
@@ -309,79 +315,6 @@
         compiler_params=params(),
         cost_estimate=cost(2 * total * width, 6 * total),
     )(weights, after, *values_of(chunk))
-
-
-def side_kernel(kinds, count, gu_row, down_row, has_send, w_ref, *refs):
-    n = len(kinds)
-    xs, ys, gates = views(refs[:n], kinds, count)
-    send_ref, token_ref = refs[n + has_send :]
-    mats, hidden, width = w_ref.shape
-    gu = contract_last(w_ref[0:2].reshape(2 * hidden, width), joined(xs))
-    down = contract_last(w_ref[2], joined(ys))
-    for row, part in ((gu_row, gu), (down_row, down)):
-        rows = part.shape[1] // count * part.shape[0]
-        store_partials([part], count, send_ref.at[row : row + rows, :])
-    token_ref[...] = jnp.zeros_like(token_ref)
-
-
-def side_partials(weights, chunk, send, blocks, first_gu, first_down, count):
-    hidden, width = weights.shape[1:]
-    kinds = kinds_of(chunk)
-    operands = [weights, *values_of(chunk)] + ([] if send is None else [send])
-    gu_row = first_gu * 2 * hidden
-    down_row = (2 * blocks[0] + first_down) * hidden
-    shape = ((2 * blocks[0] + blocks[1]) * hidden, count)
-    return pl.pallas_call(
-        functools.partial(side_kernel, kinds, count, gu_row, down_row, send is not None),
-        in_specs=[whole()] * len(operands),
-        out_specs=[whole()] * 2,
-        out_shape=[
-            jax.ShapeDtypeStruct(shape, jnp.bfloat16),
-            jax.ShapeDtypeStruct((8, 128), jnp.float32),
-        ],
-        input_output_aliases={} if send is None else {len(operands) - 1: 0},
-        compiler_params=params(),
-        cost_estimate=cost(shape[0] * count * width, 3 * shape[0] * count),
-    )(*operands)
-
-
-def start_kernel(kinds, count, w_hbm, *refs):
-    n = len(kinds)
-    out_ref, token_ref, w_ref, sems = refs[n:]
-    mats, hidden, width = w_ref.shape
-    copies = [pltpu.make_async_copy(w_hbm.at[m], w_ref.at[m], sems.at[m]) for m in range(mats)]
-    for copy in copies:
-        copy.start()
-    xs, ys, gates = views(refs[:n], kinds, count)
-    token_ref[...] = jnp.zeros_like(token_ref)
-    parts = []
-    for k, right in enumerate((joined(xs), joined(xs), joined(ys))):
-        copies[k].wait()
-        parts.append(contract_last(w_ref[k], right))
-    gate, up, down = parts
-    for k in range(gate.shape[1] // count):
-        side = slice(k * count, (k + 1) * count)
-        for m, part in ((2 * k, gate), (2 * k + 1, up), (gate.shape[1] // count * 2 + k, down)):
-            out_ref[m * hidden : (m + 1) * hidden, :] = part[:, side].astype(jnp.bfloat16)
-
-
-def start_partials(weights, chunk, rows, count):
-    mats, hidden, width = weights.shape
-    kinds = kinds_of(chunk)
-    total = rows * hidden * count
-    return pl.pallas_call(
-        functools.partial(start_kernel, kinds, count),
-        in_specs=[in_hbm()] + [whole()] * len(kinds),
-        out_specs=[whole()] * 3,
-        out_shape=[
-            jax.ShapeDtypeStruct((rows * hidden, count), jnp.bfloat16),
-            jax.ShapeDtypeStruct((8, 128), jnp.float32),
-            jax.ShapeDtypeStruct(weights.shape, weights.dtype),
-        ],
-        scratch_shapes=[pltpu.SemaphoreType.DMA((mats,))],
-        compiler_params=params(),
-        cost_estimate=cost(2 * total * width, 6 * total),
-    )(keep_hbm(weights), *values_of(chunk))
 
 
 def gate_row(gates):
@@ -493,10 +426,11 @@
     )(after, value)
 
 
-def first_kernel(kinds, count, gate_ref, after_ref, sum_ref, *refs):
+def first_kernel(kinds, count, gate_ref, after_ref, sum_ref, own, got, *refs):
     n = len(kinds)
     xs, ys, gates = views(refs[:n], kinds, count)
-    out_ref, token_ref = refs[n:]
+    out_ref, more_ref, token_ref = refs[n:]
+    more_ref[...] = summed([(own, got)])
     lefts = hidden_grads(gate_ref[0:1, :], [(sum_ref,)])
     x = joined(xs)
     for m, right in enumerate((x, x, joined(ys))):
@@ -504,36 +438,37 @@
     token_ref[...] = jnp.zeros_like(token_ref)
 
 
-def first_grads(gate, after, total, chunk, hidden, count):
+def first_grads(gate, after, total, pair, chunk, hidden, count):
     kinds = kinds_of(chunk)
     width = chunk[0][1].shape[-1]
     return pl.pallas_call(
         functools.partial(first_kernel, kinds, count),
-        in_specs=[whole(), unread()] + [whole()] * (1 + len(kinds)),
-        out_specs=[whole()] * 2,
+        in_specs=[whole(), unread()] + [whole()] * (3 + len(kinds)),
+        out_specs=[whole()] * 3,
         out_shape=[
             jax.ShapeDtypeStruct((3, hidden, width), jnp.float32),
+            jax.ShapeDtypeStruct(pair[0].shape, jnp.float32),
             jax.ShapeDtypeStruct((8, 128), jnp.float32),
         ],
         compiler_params=params(),
         cost_estimate=cost(2 * total.size * width, 12 * hidden * width),
-    )(gate, after, total, *values_of(chunk))
-
-
-def grad_kernel(kinds, count, sum_ref, own, got, *refs):
+    )(gate, after, total, *pair, *values_of(chunk))
+
+
+def grad_kernel(kinds, count, sum_ref, more_ref, own, got, *refs):
     n = len(kinds)
     xs, ys, gates = views(refs[:n], kinds, count)
     acc_ref, out_ref = refs[n:]
-    lefts = hidden_grads(gate_row(gates), [(sum_ref,), (own, got)])
+    lefts = hidden_grads(gate_row(gates), [(sum_ref,), (more_ref,), (own, got)])
     x = joined(xs)
     for m, right in enumerate((x, x, joined(ys))):
         out_ref[m] = acc_ref[m] + plain(lefts[m], right)
 
 
-def add_grads(near_sum, pair, chunk, acc, count):
+def add_grads(near_sum, more_sum, pair, chunk, acc, count):
     kinds = kinds_of(chunk)
     mats, hidden, width = acc.shape
-    operands = [near_sum, *pair, *values_of(chunk), acc]
+    operands = [near_sum, more_sum, *pair, *values_of(chunk), acc]
     return pl.pallas_call(
         functools.partial(grad_kernel, kinds, count),
         in_specs=[whole()] * len(operands),
@@ -557,26 +492,26 @@
     return [value.astype(jnp.bfloat16) for value in (moment_one, moment_two, step)]
 
 
-def gate_up(own, got):
+def pair_of_blocks(own, got):
     total = summed([(own, got)])
-    hidden = total.shape[0] // 4
-    return beside(total, hidden, (0, 2)), beside(total, hidden, (1, 3))
-
-
-def down_kernel(kinds, count, own, got, *refs):
+    return beside(total, total.shape[0] // 2, (0, 1))
+
+
+def down_kernel(kinds, count, own_g, got_g, own_u, got_u, *refs):
     n = len(kinds)
     acc_ref, first_ref, second_ref, *outs = refs[n:]
     xs, ys, gates = views(refs[:n], kinds, count)
-    act = activation(*gate_up(own, got), gate_row(gates))[2]
+    hg, hu = pair_of_blocks(own_g, got_g), pair_of_blocks(own_u, got_u)
+    act = activation(hg, hu, gate_row(gates))[2]
     grad = acc_ref[2] + plain(act, joined(ys))
     for out_ref, value in zip(outs, adam(grad, first_ref[2], second_ref[2])):
         out_ref[...] = value
 
 
-def down_update(pair, chunk, acc, moments, count):
+def down_update(pairs, chunk, acc, moments, count):
     kinds = kinds_of(chunk)
     mats, hidden, width = acc.shape
-    operands = [*pair, *values_of(chunk), acc, *moments]
+    operands = [*pairs, *values_of(chunk), acc, *moments]
     return pl.pallas_call(
         functools.partial(down_kernel, kinds, count),
         in_specs=[whole()] * len(operands),
@@ -587,7 +522,7 @@
     )(*operands)
 
 
-def slopes_kernel(kinds, count, own, got, own_d, got_d, *refs):
+def slopes_kernel(kinds, count, own_g, got_g, own_u, got_u, own_d, got_d, *refs):
     n = len(kinds)
     acc_ref, first_ref, second_ref = refs[n : n + 3]
     done, outs = refs[n + 3 : n + 6], refs[n + 6 : n + 9]
@@ -598,9 +533,8 @@
     for copy in copies:
         copy.start()
     xs, ys, gates = views(refs[:n], kinds, count)
-    hg, hu = gate_up(own, got)
-    down = summed([(own_d, got_d)])
-    dact = gate_row(gates) * beside(down, down.shape[0] // 2, (0, 1))
+    hg, hu = pair_of_blocks(own_g, got_g), pair_of_blocks(own_u, got_u)
+    dact = gate_row(gates) * pair_of_blocks(own_d, got_d)
     sig, silu, act = activation(hg, hu, 1.0)
     right = joined(xs)
     for m, left in enumerate(hidden_slopes(hg, hu, sig, silu, dact)):
@@ -613,10 +547,10 @@
         copy.wait()
 
 
-def slopes_update(pair, down_pair, chunk, acc, moments, done, count):
+def slopes_update(pairs, chunk, acc, moments, done, count):
     kinds = kinds_of(chunk)
     mats, hidden, width = acc.shape
-    operands = [*pair, *down_pair, *values_of(chunk), acc, *moments, *done]
+    operands = [*pairs, *values_of(chunk), acc, *moments, *done]
     return pl.pallas_call(
         functools.partial(slopes_kernel, kinds, count),
         in_specs=[whole()] * len(operands),
@@ -658,23 +592,28 @@
         token, first_pair, near_pair, near_x, other(near_x[0]), near_y, first
     )
     far = lax.ppermute(picked, "dp", along[1])
-    ends = [("x, y, y", rest), ("second x", x_pair), ("x, y, y", other(rest))]
-    send, token = side_partials(weights, ends[:2], None, (3, 4), 0, 0, count)
-    send, token = side_partials(weights, ends[2:], send, (3, 4), 2, 2, count)
-    more_pair = (send, partner(send))
-    acc, token = first_grads(gate, token, first_sum, first, hidden, count)
+    rest_other = other(rest)
+    early = [("x of xyy", rest), ("second x", x_pair)]
+    late = [("y, y of xyy", rest), ("x, y, y", rest_other)]
+    send, token = partials(weights, picked, early, (4,), count)
+    early_pair = (send, partner(send))
+    send, token = partials(weights, token, late, (6,), count)
+    late_pair = (send, partner(send))
+    acc, early_sum, token = first_grads(
+        gate, token, first_sum, early_pair, first, hidden, count
+    )
     pieces = passed_on(token, far, (count // 2, count // 2, count // 2, count // 2 + slots))
     pieces = [*pieces, *[other(value) for value in pieces]]
     final = list(zip(("x", "x", "y", "half y, gates") * 2, pieces))
-    send, send_d = partials(weights, token, final, (4, 2), count, 0)
-    pair, down_pair = (send, partner(send)), (send_d, partner(send_d))
-    near = [("first x", x_pair), *ends]
-    acc = add_grads(near_sum, more_pair, near, acc, count)
+    sends = partials(weights, token, final, (2, 2, 2), count, 0)
+    pairs = [value for send in sends for value in (send, partner(send))]
+    near = [("first x", x_pair), ("x, y, y", rest), ("second x", x_pair), ("x, y, y", rest_other)]
+    acc = add_grads(near_sum, early_sum, late_pair, near, acc, count)
     moments = (first_moment, second_moment)
     final_y = [block for block in final if block[0] != "x"]
     final_x = [block for block in final if block[0] != "y"]
-    done = down_update(pair, final_y, acc, moments, count)
-    return tuple(slopes_update(pair, down_pair, final_x, acc, moments, done, count))
+    done = down_update(pairs[:4], final_y, acc, moments, count)
+    return tuple(slopes_update(pairs, final_x, acc, moments, done, count))
 
 
 def per_device(tokens, cotangent, expert_ids, gate_probs, weights, first_moment, second_moment):

time: 44.9 us -> 45 us (level)
  starting transfers between devices: 15.4 us -> 17.5 us
  waiting for transfers between devices: 19.3 us -> 17.6 us
    ppermute x1, waiting for transfers between devices: 4.26 us -> 0.01 us  [dense_plan(): far = lax.ppermute(picked, 'dp', along[1])]
    ppermute x12 -> x14, waiting for transfers between devices: 8.54 us -> 11.2 us  [from_masked(): return lax.ppermute(value, axis, pairs)]
    ppermute x12 -> x14, starting transfers between devices: 9.16 us -> 11.2 us  [from_masked(): return lax.ppermute(value, axis, pairs)]
    pallas_call x2 -> x0, Pallas kernels: 1.55 us -> none  [side_partials(): pl.pallas_call(functools.partial(side_kernel, kinds, count, gu_row, down_...]
    pallas_call x3 -> x5, Pallas kernels: 1.46 us -> 2.63 us  [partials(): pl.pallas_call(functools.partial(partial_kernel, kinds, count, tokened),...]
  transfers between devices with their start and end apart: 17 -> 19, of which waited for: 12 -> 12; matrix products, arithmetic and copies ran while one was open for 0% -> 0% of each run, Pallas kernels for 12% -> 11%
where the time goes in v8:
time: 45 us; the launch traced here: 44.8 us
  waiting for transfers between devices  17.6 us (39%)
  starting transfers between devices  17.5 us (39%)
  Pallas kernels  8.93 us (20%)
  between operations  0.75 us (2%)
    ppermute x14, starting transfers between devices, from_masked(): return lax.ppermute(value, axis, pairs)  11.2 us
    ppermute x14, waiting for transfers between devices, from_masked(): return lax.ppermute(value, axis, pairs)  11.2 us
    ppermute x2, waiting for transfers between devices, dense_plan(): near_x = [lax.ppermute(x_own, 'dp', pairs) for pairs in along]  4.48 us
    ppermute x2, starting transfers between devices, dense_plan(): near_x = [lax.ppermute(x_own, 'dp', pairs) for pairs in along]  4.1 us
    pallas_call x5, Pallas kernels, partials(): pl.pallas_call(functools.partial(partial_kernel, kinds, count, tokened),...  2.63 us
    pallas_call x1, Pallas kernels, slopes_update(): pl.pallas_call(functools.partial(slopes_kernel, kinds, count), in_specs=[...  2.2 us
    ppermute x2, waiting for transfers between devices, dense_plan(): near_y = [lax.ppermute(y_own, 'dp', pairs) for pairs in along]  1.98 us
    pallas_call x1, Pallas kernels, pack_own(): pl.pallas_call(pack_kernel, in_specs=[in_hbm()] * 5, out_specs=[whole()]...  1.69 us
  transfers between devices with their start and end apart: 19, of which 12 were waited for; matrix products, arithmetic and copies ran while one was open for 0% of the time, Pallas kernels for 11%

profile of v8, /device:TPU:0, one launch (start us, length us, event | category | flops | bytes accessed | tf_op | source)
XLA Modules:
  0.0 44.8 jit_solution(11036094514711163049)
XLA Ops:
  0.6 1.7 %shard_map.94 = (bf16[128,1024]{1,0:T(8,128)(2,1)S(1)}, bf16[144,1024]{1,0:T(8,128)(2,1)S(1)}, bf16[272,1024]{1,0:T(8,128)(2,1)S(1)}, bf16[3,192,1024]{2,1,0:T(8,128)(2,1)S(1)}) custom-call(s32[4,128]{1,0:T(4,128)} %bitcast.2, bf16[4,128]{1,0:T(4,128)(2,1)} %bitcast.3, bf16[128,2048]{1,0:T(8,128)(2,1)} %tokens_ref.1, bf16[128,2048]{1,0:T(8,128)(2,1)} %cot_ref.1, ...), custom_call_target="tpu_custom_call" | custom-call | flops 1000 | bytes 1048576 | tf_op jit(solution)/shard_map/pallas_call | solution.py:209
  2.8 2.6 %collective-permute-start.1 = (bf16[128,1024]{1,0:T(8,128)(2,1)S(1)}, bf16[128,1024]{1,0:T(8,128)(2,1)S(1)}, u32[]{:S(2)}, u32[]{:S(2)}) collective-permute-start(bf16[128,1024]{1,0:T(8,128)(2,1)S(1)} %get-tuple-element.37), channel_id=1, source_target_pairs={{0,2},{1,5},{2,0},{3,7},{4,6},{5,1},{6,4},{7,3},{8,10},{9,13},{10,... | collective-permute-start | bytes 786440 | tf_op jit(solution)/shard_map/ppermute | solution.py:587
  5.4 1.5 %collective-permute-start.2 = (bf16[128,1024]{1,0:T(8,128)(2,1)S(1)}, bf16[128,1024]{1,0:T(8,128)(2,1)S(1)}, u32[]{:S(2)}, u32[]{:S(2)}) collective-permute-start(bf16[128,1024]{1,0:T(8,128)(2,1)S(1)} %get-tuple-element.37), channel_id=1, source_target_pairs={{0,4},{1,3},{2,6},{3,1},{4,0},{5,7},{6,2},{7,5},{8,12},{9,11},{10,... | collective-permute-start | bytes 786440 | tf_op jit(solution)/shard_map/ppermute | solution.py:587
  8.1 2.1 %collective-permute-start.3 = (bf16[1152,128]{1,0:T(8,128)(2,1)S(1)}, bf16[1152,128]{1,0:T(8,128)(2,1)S(1)}, u32[]{:S(2)}, u32[]{:S(2)}) collective-permute-start(bf16[1152,128]{1,0:T(8,128)(2,1)S(1)} %get-tuple-element.39.own), channel_id=1, source_target_pairs={{0,8},{8,0},{16,24},{24,16},{1,9},{9,1},{17,25},{25,17},{2,10},{10... | collective-permute-start | bytes 884744 | tf_op jit(solution)/shard_map/ppermute | solution.py:568
  10.2 1.3 %collective-permute-done.1.refs_0_ = bf16[128,1024]{1,0:T(8,128)(2,1)S(1)} collective-permute-done((bf16[128,1024]{1,0:T(8,128)(2,1)S(1)}, bf16[128,1024]{1,0:T(8,128)(2,1)S(1)}, u32[]{:S(2)}, u32[]{:S(2)}) %collective-permute-start.1) | collective-permute-done | bytes 262176 | tf_op jit(solution)/shard_map/ppermute | solution.py:587
  11.5 3.2 %collective-permute-done.2.refs_1_ = bf16[128,1024]{1,0:T(8,128)(2,1)S(1)} collective-permute-done((bf16[128,1024]{1,0:T(8,128)(2,1)S(1)}, bf16[128,1024]{1,0:T(8,128)(2,1)S(1)}, u32[]{:S(2)}, u32[]{:S(2)}) %collective-permute-start.2) | collective-permute-done | bytes 262176 | tf_op jit(solution)/shard_map/ppermute | solution.py:587
  15.0 1.7 %collective-permute-start.4 = (bf16[384,128]{1,0:T(8,128)(2,1)S(1)}, bf16[384,128]{1,0:T(8,128)(2,1)S(1)}, u32[]{:S(2)}, u32[]{:S(2)}) collective-permute-start(bf16[384,128]{1,0:T(8,128)(2,1)S(1)} %get-tuple-element.40.near_own), channel_id=1, source_target_pairs={{0,8},{8,0},{16,24},{24,16},{1,9},{9,1},{17,25},{25,17},{2,10},{10... | collective-permute-start | bytes 294920 | tf_op jit(solution)/shard_map/ppermute | solution.py:568
  16.7 1.1 %collective-permute-done.6.refs_3_ = bf16[144,1024]{1,0:T(8,128)(2,1)S(1)} collective-permute-done((bf16[144,1024]{1,0:T(8,128)(2,1)S(1)}, bf16[144,1024]{1,0:T(8,128)(2,1)S(1)}, u32[]{:S(2)}, u32[]{:S(2)}) %collective-permute-start.6) | collective-permute-done | bytes 294944 | tf_op jit(solution)/shard_map/ppermute | solution.py:588
  17.8 0.9 %collective-permute-done.7.refs_4_ = bf16[144,1024]{1,0:T(8,128)(2,1)S(1)} collective-permute-done((bf16[144,1024]{1,0:T(8,128)(2,1)S(1)}, bf16[144,1024]{1,0:T(8,128)(2,1)S(1)}, u32[]{:S(2)}, u32[]{:S(2)}) %collective-permute-start.7) | collective-permute-done | bytes 294944 | tf_op jit(solution)/shard_map/ppermute | solution.py:588
  18.7 1.0 %collective-permute-done.4.near_got = bf16[384,128]{1,0:T(8,128)(2,1)S(1)} collective-permute-done((bf16[384,128]{1,0:T(8,128)(2,1)S(1)}, bf16[384,128]{1,0:T(8,128)(2,1)S(1)}, u32[]{:S(2)}, u32[]{:S(2)}) %collective-permute-start.4) | collective-permute-done | bytes 98336 | tf_op jit(solution)/shard_map/ppermute | solution.py:568
  20.0 1.6 %collective-permute-start.10 = (bf16[272,1024]{1,0:T(8,128)(2,1)S(1)}, bf16[272,1024]{1,0:T(8,128)(2,1)S(1)}, u32[]{:S(2)}, u32[]{:S(2)}) collective-permute-start(bf16[272,1024]{1,0:T(8,128)(2,1)S(1)} %get-tuple-element.43.after_ref), channel_id=1, source_target_pairs={{0,4},{1,3},{2,6},{3,1},{4,0},{5,7},{6,2},{7,5},{8,12},{9,11},{10,... | collective-permute-start | bytes 1671176 | tf_op jit(solution)/shard_map/ppermute | solution.py:594
  22.0 1.6 %collective-permute-start.9 = (bf16[768,128]{1,0:T(8,128)(2,1)S(1)}, bf16[768,128]{1,0:T(8,128)(2,1)S(1)}, u32[]{:S(2)}, u32[]{:S(2)}) collective-permute-start(bf16[768,128]{1,0:T(8,128)(2,1)S(1)} %get-tuple-element.49.own), channel_id=1, source_target_pairs={{0,8},{8,0},{16,24},{24,16},{1,9},{9,1},{17,25},{25,17},{2,10},{10... | collective-permute-start | bytes 589832 | tf_op jit(solution)/shard_map/ppermute | solution.py:568
  23.7 0.7 %shard_map.99 = (bf16[1152,128]{1,0:T(8,128)(2,1)S(1)}, f32[8,128]{1,0:T(8,128)S(1)}) custom-call(bf16[3,192,1024]{2,1,0:T(8,128)(2,1)S(1)} %get-tuple-element.34.w_ref, f32[8,128]{1,0:T(8,128)S(1)} %get-tuple-element.46.after_ref, bf16[416,1024]{1,0:T(8,128)(2,1)S(1)} %get-tuple-element.44.refs_0_.refs_1_, ...), custom_call_target="tpu_custom_call" | custom-call | flops 301989888 | bytes 884736 | tf_op jit(solution)/shard_map/pallas_call | solution.py:309
  24.8 5.1 %collective-permute-done.9.got = bf16[768,128]{1,0:T(8,128)(2,1)S(1)} collective-permute-done((bf16[768,128]{1,0:T(8,128)(2,1)S(1)}, bf16[768,128]{1,0:T(8,128)(2,1)S(1)}, u32[]{:S(2)}, u32[]{:S(2)}) %collective-permute-start.9) | collective-permute-done | bytes 196640 | tf_op jit(solution)/shard_map/ppermute | solution.py:568
  31.6 0.6 %collective-permute-done.11.refs_4_.refs_3_ = bf16[64,1024]{1,0:T(8,128)(2,1)S(1)} collective-permute-done((bf16[64,1024]{1,0:T(8,128)(2,1)S(1)}, bf16[64,1024]{1,0:T(8,128)(2,1)S(1)}, u32[]{:S(2)}, u32[]{:S(2)}) %collective-permute-start.11) | collective-permute-done | bytes 131104 | tf_op jit(solution)/shard_map/ppermute | solution.py:568
  32.7 0.7 %shard_map.102 = (bf16[384,128]{1,0:T(8,128)(2,1)S(1)}, bf16[384,128]{1,0:T(8,128)(2,1)S(1)}, bf16[384,128]{1,0:T(8,128)(2,1)S(1)}) custom-call(bf16[3,192,1024]{2,1,0:T(8,128)(2,1)S(1)} %get-tuple-element.34.w_ref, f32[8,128]{1,0:T(8,128)S(1)} %get-tuple-element.50.after_ref, bf16[64,1024]{1,0:T(8,128)(2,1)S(1)} %get-tuple-element.51.refs_0_, ...), custom_call_target="tpu_custom_call" | custom-call | flops 301989888 | bytes 884736 | tf_op jit(solution)/shard_map/pallas_call | solution.py:309
  33.3 1.6 %collective-permute-start.15 = (bf16[384,128]{1,0:T(8,128)(2,1)S(1)}, bf16[384,128]{1,0:T(8,128)(2,1)S(1)}, u32[]{:S(2)}, u32[]{:S(2)}) collective-permute-start(bf16[384,128]{1,0:T(8,128)(2,1)S(1)} %get-tuple-element.55.own_g), channel_id=1, source_target_pairs={{0,8},{8,0},{16,24},{24,16},{1,9},{9,1},{17,25},{25,17},{2,10},{10... | collective-permute-start | bytes 294920 | tf_op jit(solution)/shard_map/ppermute | solution.py:568
  35.4 1.6 %collective-permute-start.17 = (bf16[384,128]{1,0:T(8,128)(2,1)S(1)}, bf16[384,128]{1,0:T(8,128)(2,1)S(1)}, u32[]{:S(2)}, u32[]{:S(2)}) collective-permute-start(bf16[384,128]{1,0:T(8,128)(2,1)S(1)} %get-tuple-element.57.own_d), channel_id=1, source_target_pairs={{0,8},{8,0},{16,24},{24,16},{1,9},{9,1},{17,25},{25,17},{2,10},{10... | collective-permute-start | bytes 294920 | tf_op jit(solution)/shard_map/ppermute | solution.py:568
  37.0 1.0 %shard_map.103.refs_4_.refs_6_ = f32[3,192,1024]{2,1,0:T(8,128)S(1)} custom-call(f32[384,128]{1,0:T(8,128)S(1)} %get-tuple-element.58.sum_ref, f32[768,128]{1,0:T(8,128)S(1)} %get-tuple-element.59.more_ref, bf16[1152,128]{1,0:T(8,128)(2,1)S(1)} %get-tuple-element.60.own, ...), custom_call_target="tpu_custom_call", output_to_operand_aliasing={{}: (8, {})} | custom-call | flops 603979776 | bytes 4718592 | tf_op jit(solution)/shard_map/pallas_call | solution.py:472
  38.0 1.0 %collective-permute-done.15.got_g = bf16[384,128]{1,0:T(8,128)(2,1)S(1)} collective-permute-done((bf16[384,128]{1,0:T(8,128)(2,1)S(1)}, bf16[384,128]{1,0:T(8,128)(2,1)S(1)}, u32[]{:S(2)}, u32[]{:S(2)}) %collective-permute-start.15) | collective-permute-done | bytes 98336 | tf_op jit(solution)/shard_map/ppermute | solution.py:568
  39.0 2.1 %collective-permute-done.16.got_u = bf16[384,128]{1,0:T(8,128)(2,1)S(1)} collective-permute-done((bf16[384,128]{1,0:T(8,128)(2,1)S(1)}, bf16[384,128]{1,0:T(8,128)(2,1)S(1)}, u32[]{:S(2)}, u32[]{:S(2)}) %collective-permute-start.16) | collective-permute-done | bytes 98336 | tf_op jit(solution)/shard_map/ppermute | solution.py:568
  41.1 0.6 %shard_map.104 = (bf16[192,1024]{1,0:T(8,128)(2,1)S(1)}, bf16[192,1024]{1,0:T(8,128)(2,1)S(1)}, bf16[192,1024]{1,0:T(8,128)(2,1)S(1)}) custom-call(bf16[384,128]{1,0:T(8,128)(2,1)S(1)} %get-tuple-element.55.own_g, bf16[384,128]{1,0:T(8,128)(2,1)S(1)} %collective-permute-done.15.got_g, bf16[384,128]{1,0:T(8,128)(2,1)S(1)} %get-tuple-element.56.own_u, ...), custom_call_target="tpu_custom_call" | custom-call | flops 100663296 | bytes 2752512 | tf_op jit(solution)/shard_map/pallas_call | solution.py:515
  41.8 0.9 %collective-permute-done.17.got_d = bf16[384,128]{1,0:T(8,128)(2,1)S(1)} collective-permute-done((bf16[384,128]{1,0:T(8,128)(2,1)S(1)}, bf16[384,128]{1,0:T(8,128)(2,1)S(1)}, u32[]{:S(2)}, u32[]{:S(2)}) %collective-permute-start.17) | collective-permute-done | bytes 98336 | tf_op jit(solution)/shard_map/ppermute | solution.py:568
  42.6 2.2 %shard_map.105 = (bf16[3,192,1024]{2,1,0:T(8,128)(2,1)}, bf16[3,192,1024]{2,1,0:T(8,128)(2,1)}, bf16[3,192,1024]{2,1,0:T(8,128)(2,1)}) custom-call(bf16[384,128]{1,0:T(8,128)(2,1)S(1)} %get-tuple-element.55.own_g, bf16[384,128]{1,0:T(8,128)(2,1)S(1)} %collective-permute-done.15.got_g, bf16[384,128]{1,0:T(8,128)(2,1)S(1)} %get-tuple-element.56.own_u, ...), custom_call_target="tpu_custom_call" | custom-call | flops 201326592 | bytes 5505024 | tf_op jit(solution)/shard_map/pallas_call | solution.py:554
  (30 shorter events, 5.8 us)
Async XLA Ops:
  2.3 5.2 %collective-permute-start = (bf16[272,1024]{1,0:T(8,128)(2,1)S(1)}, bf16[272,1024]{1,0:T(8,128)(2,1)S(1)}, u32[]{:S(2)}, u32[]{:S(2)}) collective-permute-start(bf16[272,1024]{1,0:T(8,128)(2,1)S(1)} %get-tuple-element.35.after_ref.refs_0_.refs_5_), channel_id=1, source_target_pairs={{0,1},{1,0},{2,3},{3,2},{4,5},{5,4},{6,7},{7,6},{8,9},{9,8},{10,11... | collective-permute-start | bytes 1671176 | tf_op jit(solution)/shard_map/ppermute | solution.py:568
  2.8 8.6 %collective-permute-start.1 = (bf16[128,1024]{1,0:T(8,128)(2,1)S(1)}, bf16[128,1024]{1,0:T(8,128)(2,1)S(1)}, u32[]{:S(2)}, u32[]{:S(2)}) collective-permute-start(bf16[128,1024]{1,0:T(8,128)(2,1)S(1)} %get-tuple-element.37), channel_id=1, source_target_pairs={{0,2},{1,5},{2,0},{3,7},{4,6},{5,1},{6,4},{7,3},{8,10},{9,13},{10,... | collective-permute-start | bytes 786440 | tf_op jit(solution)/shard_map/ppermute | solution.py:587
  5.4 9.2 %collective-permute-start.2 = (bf16[128,1024]{1,0:T(8,128)(2,1)S(1)}, bf16[128,1024]{1,0:T(8,128)(2,1)S(1)}, u32[]{:S(2)}, u32[]{:S(2)}) collective-permute-start(bf16[128,1024]{1,0:T(8,128)(2,1)S(1)} %get-tuple-element.37), channel_id=1, source_target_pairs={{0,4},{1,3},{2,6},{3,1},{4,0},{5,7},{6,2},{7,5},{8,12},{9,11},{10,... | collective-permute-start | bytes 786440 | tf_op jit(solution)/shard_map/ppermute | solution.py:587
  6.9 10.8 %collective-permute-start.6 = (bf16[144,1024]{1,0:T(8,128)(2,1)S(1)}, bf16[144,1024]{1,0:T(8,128)(2,1)S(1)}, u32[]{:S(2)}, u32[]{:S(2)}) collective-permute-start(bf16[144,1024]{1,0:T(8,128)(2,1)S(1)} %get-tuple-element.41), channel_id=1, source_target_pairs={{0,2},{1,5},{2,0},{3,7},{4,6},{5,1},{6,4},{7,3},{8,10},{9,13},{10,... | collective-permute-start | bytes 884744 | tf_op jit(solution)/shard_map/ppermute | solution.py:588
  7.5 11.2 %collective-permute-start.7 = (bf16[144,1024]{1,0:T(8,128)(2,1)S(1)}, bf16[144,1024]{1,0:T(8,128)(2,1)S(1)}, u32[]{:S(2)}, u32[]{:S(2)}) collective-permute-start(bf16[144,1024]{1,0:T(8,128)(2,1)S(1)} %get-tuple-element.41), channel_id=1, source_target_pairs={{0,4},{1,3},{2,6},{3,1},{4,0},{5,7},{6,2},{7,5},{8,12},{9,11},{10,... | collective-permute-start | bytes 884744 | tf_op jit(solution)/shard_map/ppermute | solution.py:588
  8.1 11.6 %collective-permute-start.3 = (bf16[1152,128]{1,0:T(8,128)(2,1)S(1)}, bf16[1152,128]{1,0:T(8,128)(2,1)S(1)}, u32[]{:S(2)}, u32[]{:S(2)}) collective-permute-start(bf16[1152,128]{1,0:T(8,128)(2,1)S(1)} %get-tuple-element.39.own), channel_id=1, source_target_pairs={{0,8},{8,0},{16,24},{24,16},{1,9},{9,1},{17,25},{25,17},{2,10},{10... | collective-permute-start | bytes 884744 | tf_op jit(solution)/shard_map/ppermute | solution.py:568
  11.5 7.2 %collective-permute-start.5 = (bf16[128,1024]{1,0:T(8,128)(2,1)S(1)}, bf16[128,1024]{1,0:T(8,128)(2,1)S(1)}, u32[]{:S(2)}, u32[]{:S(2)}) collective-permute-start(bf16[128,1024]{1,0:T(8,128)(2,1)S(1)} %collective-permute-done.1.refs_0_), channel_id=1, source_target_pairs={{0,1},{1,0},{2,3},{3,2},{4,5},{5,4},{6,7},{7,6},{8,9},{9,8},{10,11... | collective-permute-start | bytes 786440 | tf_op jit(solution)/shard_map/ppermute | solution.py:568
  15.0 4.7 %collective-permute-start.4 = (bf16[384,128]{1,0:T(8,128)(2,1)S(1)}, bf16[384,128]{1,0:T(8,128)(2,1)S(1)}, u32[]{:S(2)}, u32[]{:S(2)}) collective-permute-start(bf16[384,128]{1,0:T(8,128)(2,1)S(1)} %get-tuple-element.40.near_own), channel_id=1, source_target_pairs={{0,8},{8,0},{16,24},{24,16},{1,9},{9,1},{17,25},{25,17},{2,10},{10... | collective-permute-start | bytes 294920 | tf_op jit(solution)/shard_map/ppermute | solution.py:568
  19.9 3.7 %collective-permute-start.8 = (bf16[416,1024]{1,0:T(8,128)(2,1)S(1)}, bf16[416,1024]{1,0:T(8,128)(2,1)S(1)}, u32[]{:S(2)}, u32[]{:S(2)}) collective-permute-start(bf16[416,1024]{1,0:T(8,128)(2,1)S(1)} %get-tuple-element.44.refs_0_.refs_1_), channel_id=1, source_target_pairs={{0,1},{1,0},{2,3},{3,2},{4,5},{5,4},{6,7},{7,6},{8,9},{9,8},{10,11... | collective-permute-start | bytes 2555912 | tf_op jit(solution)/shard_map/ppermute | solution.py:568
  20.0 10.5 %collective-permute-start.10 = (bf16[272,1024]{1,0:T(8,128)(2,1)S(1)}, bf16[272,1024]{1,0:T(8,128)(2,1)S(1)}, u32[]{:S(2)}, u32[]{:S(2)}) collective-permute-start(bf16[272,1024]{1,0:T(8,128)(2,1)S(1)} %get-tuple-element.43.after_ref), channel_id=1, source_target_pairs={{0,4},{1,3},{2,6},{3,1},{4,0},{5,7},{6,2},{7,5},{8,12},{9,11},{10,... | collective-permute-start | bytes 1671176 | tf_op jit(solution)/shard_map/ppermute | solution.py:594
  22.0 7.9 %collective-permute-start.9 = (bf16[768,128]{1,0:T(8,128)(2,1)S(1)}, bf16[768,128]{1,0:T(8,128)(2,1)S(1)}, u32[]{:S(2)}, u32[]{:S(2)}) collective-permute-start(bf16[768,128]{1,0:T(8,128)(2,1)S(1)} %get-tuple-element.49.own), channel_id=1, source_target_pairs={{0,8},{8,0},{16,24},{24,16},{1,9},{9,1},{17,25},{25,17},{2,10},{10... | collective-permute-start | bytes 589832 | tf_op jit(solution)/shard_map/ppermute | solution.py:568
  24.3 12.7 %collective-permute-start.18 = (bf16[1152,128]{1,0:T(8,128)(2,1)S(1)}, bf16[1152,128]{1,0:T(8,128)(2,1)S(1)}, u32[]{:S(2)}, u32[]{:S(2)}) collective-permute-start(bf16[1152,128]{1,0:T(8,128)(2,1)S(1)} %get-tuple-element.60.own), channel_id=1, source_target_pairs={{0,8},{8,0},{16,24},{24,16},{1,9},{9,1},{17,25},{25,17},{2,10},{10... | collective-permute-start | bytes 884744 | tf_op jit(solution)/shard_map/ppermute | solution.py:568
  30.5 2.1 %collective-permute-start.14 = (bf16[80,1024]{1,0:T(8,128)(2,1)S(1)}, bf16[80,1024]{1,0:T(8,128)(2,1)S(1)}, u32[]{:S(2)}, u32[]{:S(2)}) collective-permute-start(bf16[80,1024]{1,0:T(8,128)(2,1)S(1)} %get-tuple-element.54.refs_3_.refs_1_.refs_2_), channel_id=1, source_target_pairs={{0,1},{1,0},{2,3},{3,2},{4,5},{5,4},{6,7},{7,6},{8,9},{9,8},{10,11... | collective-permute-start | bytes 491528 | tf_op jit(solution)/shard_map/ppermute | solution.py:568
  30.6 1.6 %collective-permute-start.11 = (bf16[64,1024]{1,0:T(8,128)(2,1)S(1)}, bf16[64,1024]{1,0:T(8,128)(2,1)S(1)}, u32[]{:S(2)}, u32[]{:S(2)}) collective-permute-start(bf16[64,1024]{1,0:T(8,128)(2,1)S(1)} %get-tuple-element.51.refs_0_), channel_id=1, source_target_pairs={{0,1},{1,0},{2,3},{3,2},{4,5},{5,4},{6,7},{7,6},{8,9},{9,8},{10,11... | collective-permute-start | bytes 393224 | tf_op jit(solution)/shard_map/ppermute | solution.py:568
  31.1 1.3 %collective-permute-start.12 = (bf16[64,1024]{1,0:T(8,128)(2,1)S(1)}, bf16[64,1024]{1,0:T(8,128)(2,1)S(1)}, u32[]{:S(2)}, u32[]{:S(2)}) collective-permute-start(bf16[64,1024]{1,0:T(8,128)(2,1)S(1)} %get-tuple-element.52.refs_1_), channel_id=1, source_target_pairs={{0,1},{1,0},{2,3},{3,2},{4,5},{5,4},{6,7},{7,6},{8,9},{9,8},{10,11... | collective-permute-start | bytes 393224 | tf_op jit(solution)/shard_map/ppermute | solution.py:568
  31.2 1.5 %collective-permute-start.13 = (bf16[64,1024]{1,0:T(8,128)(2,1)S(1)}, bf16[64,1024]{1,0:T(8,128)(2,1)S(1)}, u32[]{:S(2)}, u32[]{:S(2)}) collective-permute-start(bf16[64,1024]{1,0:T(8,128)(2,1)S(1)} %get-tuple-element.53.refs_2_.refs_0_), channel_id=1, source_target_pairs={{0,1},{1,0},{2,3},{3,2},{4,5},{5,4},{6,7},{7,6},{8,9},{9,8},{10,11... | collective-permute-start | bytes 393224 | tf_op jit(solution)/shard_map/ppermute | solution.py:568
  33.3 5.7 %collective-permute-start.15 = (bf16[384,128]{1,0:T(8,128)(2,1)S(1)}, bf16[384,128]{1,0:T(8,128)(2,1)S(1)}, u32[]{:S(2)}, u32[]{:S(2)}) collective-permute-start(bf16[384,128]{1,0:T(8,128)(2,1)S(1)} %get-tuple-element.55.own_g), channel_id=1, source_target_pairs={{0,8},{8,0},{16,24},{24,16},{1,9},{9,1},{17,25},{25,17},{2,10},{10... | collective-permute-start | bytes 294920 | tf_op jit(solution)/shard_map/ppermute | solution.py:568
  35.0 6.2 %collective-permute-start.16 = (bf16[384,128]{1,0:T(8,128)(2,1)S(1)}, bf16[384,128]{1,0:T(8,128)(2,1)S(1)}, u32[]{:S(2)}, u32[]{:S(2)}) collective-permute-start(bf16[384,128]{1,0:T(8,128)(2,1)S(1)} %get-tuple-element.56.own_u), channel_id=1, source_target_pairs={{0,8},{8,0},{16,24},{24,16},{1,9},{9,1},{17,25},{25,17},{2,10},{10... | collective-permute-start | bytes 294920 | tf_op jit(solution)/shard_map/ppermute | solution.py:568
  35.4 7.2 %collective-permute-start.17 = (bf16[384,128]{1,0:T(8,128)(2,1)S(1)}, bf16[384,128]{1,0:T(8,128)(2,1)S(1)}, u32[]{:S(2)}, u32[]{:S(2)}) collective-permute-start(bf16[384,128]{1,0:T(8,128)(2,1)S(1)} %get-tuple-element.57.own_d), channel_id=1, source_target_pairs={{0,8},{8,0},{16,24},{24,16},{1,9},{9,1},{17,25},{25,17},{2,10},{10... | collective-permute-start | bytes 294920 | tf_op jit(solution)/shard_map/ppermute | solution.py:568
  37.0 4.1 %copy-start = (bf16[3,192,1024]{2,1,0:T(8,128)(2,1)S(1)}, bf16[3,192,1024]{2,1,0:T(8,128)(2,1)}, u32[]{:S(2)}) copy-start(bf16[3,192,1024]{2,1,0:T(8,128)(2,1)} %refs_7_.1) | copy-start | bytes 3538948
  37.0 4.1 %copy-start.1 = (bf16[3,192,1024]{2,1,0:T(8,128)(2,1)S(1)}, bf16[3,192,1024]{2,1,0:T(8,128)(2,1)}, u32[]{:S(2)}) copy-start(bf16[3,192,1024]{2,1,0:T(8,128)(2,1)} %refs_8_.1) | copy-start | bytes 3538948

commit v9 on v8

--- a/solution.py
+++ b/solution.py
@@ -599,10 +599,10 @@
     early_pair = (send, partner(send))
     send, token = partials(weights, token, late, (6,), count)
     late_pair = (send, partner(send))
+    pieces = passed_on(token, far, (count // 2, count // 2, count // 2, count // 2 + slots))
     acc, early_sum, token = first_grads(
-        gate, token, first_sum, early_pair, first, hidden, count
-    )
-    pieces = passed_on(token, far, (count // 2, count // 2, count // 2, count // 2 + slots))
+        gate, pieces[0], first_sum, early_pair, first, hidden, count
+    )
     pieces = [*pieces, *[other(value) for value in pieces]]
     final = list(zip(("x", "x", "y", "half y, gates") * 2, pieces))
     sends = partials(weights, token, final, (2, 2, 2), count, 0)

time: 45 us -> 44.1 us (0.980)
  waiting for transfers between devices: 17.6 us -> 16.7 us
    ppermute x14, waiting for transfers between devices: 11.2 us -> 5.48 us  [from_masked(): return lax.ppermute(value, axis, pairs)]
    ppermute x1, waiting for transfers between devices: 0.01 us -> 4.76 us  [dense_plan(): far = lax.ppermute(picked, 'dp', along[1])]
  transfers between devices with their start and end apart: 19 -> 19, of which waited for: 12 -> 11; matrix products, arithmetic and copies ran while one was open for 0% -> 0% of each run, Pallas kernels for 11% -> 11%
where the time goes in v9:
time: 44.1 us; the launch traced here: 43.9 us
  starting transfers between devices  17.5 us (40%)
  waiting for transfers between devices  16.7 us (38%)
  Pallas kernels  8.94 us (20%)
  between operations  0.75 us (2%)
    ppermute x14, starting transfers between devices, from_masked(): return lax.ppermute(value, axis, pairs)  11.2 us
    ppermute x14, waiting for transfers between devices, from_masked(): return lax.ppermute(value, axis, pairs)  5.48 us
    ppermute x1, waiting for transfers between devices, dense_plan(): far = lax.ppermute(picked, 'dp', along[1])  4.76 us
    ppermute x2, waiting for transfers between devices, dense_plan(): near_x = [lax.ppermute(x_own, 'dp', pairs) for pairs in along]  4.47 us
    ppermute x2, starting transfers between devices, dense_plan(): near_x = [lax.ppermute(x_own, 'dp', pairs) for pairs in along]  4.1 us
    pallas_call x5, Pallas kernels, partials(): pl.pallas_call(functools.partial(partial_kernel, kinds, count, tokened),...  2.64 us
    pallas_call x1, Pallas kernels, slopes_update(): pl.pallas_call(functools.partial(slopes_kernel, kinds, count), in_specs=[...  2.19 us
    ppermute x2, waiting for transfers between devices, dense_plan(): near_y = [lax.ppermute(y_own, 'dp', pairs) for pairs in along]  1.99 us
  transfers between devices with their start and end apart: 19, of which 11 were waited for; matrix products, arithmetic and copies ran while one was open for 0% of the time, Pallas kernels for 11%

profile of v9, /device:TPU:0, one launch (start us, length us, event | category | flops | bytes accessed | tf_op | source)
XLA Modules:
  0.0 43.9 jit_solution(4449214202003048411)
XLA Ops:
  0.6 1.7 %shard_map.94 = (bf16[128,1024]{1,0:T(8,128)(2,1)S(1)}, bf16[144,1024]{1,0:T(8,128)(2,1)S(1)}, bf16[272,1024]{1,0:T(8,128)(2,1)S(1)}, bf16[3,192,1024]{2,1,0:T(8,128)(2,1)S(1)}) custom-call(s32[4,128]{1,0:T(4,128)} %bitcast.2, bf16[4,128]{1,0:T(4,128)(2,1)} %bitcast.3, bf16[128,2048]{1,0:T(8,128)(2,1)} %tokens_ref.1, bf16[128,2048]{1,0:T(8,128)(2,1)} %cot_ref.1, ...), custom_call_target="tpu_custom_call" | custom-call | flops 1000 | bytes 1048576 | tf_op jit(solution)/shard_map/pallas_call | solution.py:209
  2.8 2.6 %collective-permute-start.1 = (bf16[128,1024]{1,0:T(8,128)(2,1)S(1)}, bf16[128,1024]{1,0:T(8,128)(2,1)S(1)}, u32[]{:S(2)}, u32[]{:S(2)}) collective-permute-start(bf16[128,1024]{1,0:T(8,128)(2,1)S(1)} %get-tuple-element.37), channel_id=1, source_target_pairs={{0,2},{1,5},{2,0},{3,7},{4,6},{5,1},{6,4},{7,3},{8,10},{9,13},{10,... | collective-permute-start | bytes 786440 | tf_op jit(solution)/shard_map/ppermute | solution.py:587
  5.4 1.5 %collective-permute-start.2 = (bf16[128,1024]{1,0:T(8,128)(2,1)S(1)}, bf16[128,1024]{1,0:T(8,128)(2,1)S(1)}, u32[]{:S(2)}, u32[]{:S(2)}) collective-permute-start(bf16[128,1024]{1,0:T(8,128)(2,1)S(1)} %get-tuple-element.37), channel_id=1, source_target_pairs={{0,4},{1,3},{2,6},{3,1},{4,0},{5,7},{6,2},{7,5},{8,12},{9,11},{10,... | collective-permute-start | bytes 786440 | tf_op jit(solution)/shard_map/ppermute | solution.py:587
  8.1 2.1 %collective-permute-start.3 = (bf16[1152,128]{1,0:T(8,128)(2,1)S(1)}, bf16[1152,128]{1,0:T(8,128)(2,1)S(1)}, u32[]{:S(2)}, u32[]{:S(2)}) collective-permute-start(bf16[1152,128]{1,0:T(8,128)(2,1)S(1)} %get-tuple-element.39.own), channel_id=1, source_target_pairs={{0,8},{8,0},{16,24},{24,16},{1,9},{9,1},{17,25},{25,17},{2,10},{10... | collective-permute-start | bytes 884744 | tf_op jit(solution)/shard_map/ppermute | solution.py:568
  10.2 1.3 %collective-permute-done.1.refs_0_ = bf16[128,1024]{1,0:T(8,128)(2,1)S(1)} collective-permute-done((bf16[128,1024]{1,0:T(8,128)(2,1)S(1)}, bf16[128,1024]{1,0:T(8,128)(2,1)S(1)}, u32[]{:S(2)}, u32[]{:S(2)}) %collective-permute-start.1) | collective-permute-done | bytes 262176 | tf_op jit(solution)/shard_map/ppermute | solution.py:587
  11.5 3.2 %collective-permute-done.2.refs_1_ = bf16[128,1024]{1,0:T(8,128)(2,1)S(1)} collective-permute-done((bf16[128,1024]{1,0:T(8,128)(2,1)S(1)}, bf16[128,1024]{1,0:T(8,128)(2,1)S(1)}, u32[]{:S(2)}, u32[]{:S(2)}) %collective-permute-start.2) | collective-permute-done | bytes 262176 | tf_op jit(solution)/shard_map/ppermute | solution.py:587
  15.0 1.6 %collective-permute-start.4 = (bf16[384,128]{1,0:T(8,128)(2,1)S(1)}, bf16[384,128]{1,0:T(8,128)(2,1)S(1)}, u32[]{:S(2)}, u32[]{:S(2)}) collective-permute-start(bf16[384,128]{1,0:T(8,128)(2,1)S(1)} %get-tuple-element.40.near_own), channel_id=1, source_target_pairs={{0,8},{8,0},{16,24},{24,16},{1,9},{9,1},{17,25},{25,17},{2,10},{10... | collective-permute-start | bytes 294920 | tf_op jit(solution)/shard_map/ppermute | solution.py:568
  16.7 1.1 %collective-permute-done.6.refs_3_ = bf16[144,1024]{1,0:T(8,128)(2,1)S(1)} collective-permute-done((bf16[144,1024]{1,0:T(8,128)(2,1)S(1)}, bf16[144,1024]{1,0:T(8,128)(2,1)S(1)}, u32[]{:S(2)}, u32[]{:S(2)}) %collective-permute-start.6) | collective-permute-done | bytes 294944 | tf_op jit(solution)/shard_map/ppermute | solution.py:588
  17.8 0.9 %collective-permute-done.7.refs_4_ = bf16[144,1024]{1,0:T(8,128)(2,1)S(1)} collective-permute-done((bf16[144,1024]{1,0:T(8,128)(2,1)S(1)}, bf16[144,1024]{1,0:T(8,128)(2,1)S(1)}, u32[]{:S(2)}, u32[]{:S(2)}) %collective-permute-start.7) | collective-permute-done | bytes 294944 | tf_op jit(solution)/shard_map/ppermute | solution.py:588
  18.7 1.0 %collective-permute-done.4.near_got = bf16[384,128]{1,0:T(8,128)(2,1)S(1)} collective-permute-done((bf16[384,128]{1,0:T(8,128)(2,1)S(1)}, bf16[384,128]{1,0:T(8,128)(2,1)S(1)}, u32[]{:S(2)}, u32[]{:S(2)}) %collective-permute-start.4) | collective-permute-done | bytes 98336 | tf_op jit(solution)/shard_map/ppermute | solution.py:568
  20.0 1.6 %collective-permute-start.9 = (bf16[272,1024]{1,0:T(8,128)(2,1)S(1)}, bf16[272,1024]{1,0:T(8,128)(2,1)S(1)}, u32[]{:S(2)}, u32[]{:S(2)}) collective-permute-start(bf16[272,1024]{1,0:T(8,128)(2,1)S(1)} %get-tuple-element.43.after_ref), channel_id=1, source_target_pairs={{0,4},{1,3},{2,6},{3,1},{4,0},{5,7},{6,2},{7,5},{8,12},{9,11},{10,... | collective-permute-start | bytes 1671176 | tf_op jit(solution)/shard_map/ppermute | solution.py:594
  22.0 1.6 %collective-permute-start.10 = (bf16[768,128]{1,0:T(8,128)(2,1)S(1)}, bf16[768,128]{1,0:T(8,128)(2,1)S(1)}, u32[]{:S(2)}, u32[]{:S(2)}) collective-permute-start(bf16[768,128]{1,0:T(8,128)(2,1)S(1)} %get-tuple-element.50.own), channel_id=1, source_target_pairs={{0,8},{8,0},{16,24},{24,16},{1,9},{9,1},{17,25},{25,17},{2,10},{10... | collective-permute-start | bytes 589832 | tf_op jit(solution)/shard_map/ppermute | solution.py:568
  23.7 0.7 %shard_map.99 = (bf16[1152,128]{1,0:T(8,128)(2,1)S(1)}, f32[8,128]{1,0:T(8,128)S(1)}) custom-call(bf16[3,192,1024]{2,1,0:T(8,128)(2,1)S(1)} %get-tuple-element.34.w_ref, f32[8,128]{1,0:T(8,128)S(1)} %get-tuple-element.46.after_ref, bf16[416,1024]{1,0:T(8,128)(2,1)S(1)} %get-tuple-element.44.refs_0_.refs_1_, ...), custom_call_target="tpu_custom_call" | custom-call | flops 301989888 | bytes 884736 | tf_op jit(solution)/shard_map/pallas_call | solution.py:309
  24.8 4.8 %collective-permute-done.9.in_ref = bf16[272,1024]{1,0:T(8,128)(2,1)S(1)} collective-permute-done((bf16[272,1024]{1,0:T(8,128)(2,1)S(1)}, bf16[272,1024]{1,0:T(8,128)(2,1)S(1)}, u32[]{:S(2)}, u32[]{:S(2)}) %collective-permute-start.9) | collective-permute-done | bytes 557088 | tf_op jit(solution)/shard_map/ppermute | solution.py:594
  30.7 0.6 %shard_map.101 = (f32[3,192,1024]{2,1,0:T(8,128)S(1)}, f32[768,128]{1,0:T(8,128)S(1)}, f32[8,128]{1,0:T(8,128)S(1)}) custom-call(f32[8,256]{1,0:T(8,128)S(1)} %get-tuple-element.42.gate_ref, bf16[64,1024]{1,0:T(8,128)(2,1)S(1)} %get-tuple-element.48.after_ref.refs_0_, f32[1152,128]{1,0:T(8,128)S(1)} %get-tuple-element.49.sum_ref, ...), custom_call_target="tpu_custom_call" | custom-call | flops 301989888 | bytes 2359296 | tf_op jit(solution)/shard_map/pallas_call | solution.py:444
  31.7 0.7 %shard_map.102 = (bf16[384,128]{1,0:T(8,128)(2,1)S(1)}, bf16[384,128]{1,0:T(8,128)(2,1)S(1)}, bf16[384,128]{1,0:T(8,128)(2,1)S(1)}) custom-call(bf16[3,192,1024]{2,1,0:T(8,128)(2,1)S(1)} %get-tuple-element.34.w_ref, f32[8,128]{1,0:T(8,128)S(1)} %get-tuple-element.51.after_ref, bf16[64,1024]{1,0:T(8,128)(2,1)S(1)} %get-tuple-element.48.after_ref.refs_0_, ...), custom_call_target="tpu_custom_call" | custom-call | flops 301989888 | bytes 884736 | tf_op jit(solution)/shard_map/pallas_call | solution.py:309
  32.4 1.6 %collective-permute-start.15 = (bf16[384,128]{1,0:T(8,128)(2,1)S(1)}, bf16[384,128]{1,0:T(8,128)(2,1)S(1)}, u32[]{:S(2)}, u32[]{:S(2)}) collective-permute-start(bf16[384,128]{1,0:T(8,128)(2,1)S(1)} %get-tuple-element.55.own_g), channel_id=1, source_target_pairs={{0,8},{8,0},{16,24},{24,16},{1,9},{9,1},{17,25},{25,17},{2,10},{10... | collective-permute-start | bytes 294920 | tf_op jit(solution)/shard_map/ppermute | solution.py:568
  34.5 1.6 %collective-permute-start.17 = (bf16[384,128]{1,0:T(8,128)(2,1)S(1)}, bf16[384,128]{1,0:T(8,128)(2,1)S(1)}, u32[]{:S(2)}, u32[]{:S(2)}) collective-permute-start(bf16[384,128]{1,0:T(8,128)(2,1)S(1)} %get-tuple-element.57.own_d), channel_id=1, source_target_pairs={{0,8},{8,0},{16,24},{24,16},{1,9},{9,1},{17,25},{25,17},{2,10},{10... | collective-permute-start | bytes 294920 | tf_op jit(solution)/shard_map/ppermute | solution.py:568
  36.1 1.0 %shard_map.103.refs_4_.refs_6_ = f32[3,192,1024]{2,1,0:T(8,128)S(1)} custom-call(f32[384,128]{1,0:T(8,128)S(1)} %get-tuple-element.58.sum_ref, f32[768,128]{1,0:T(8,128)S(1)} %get-tuple-element.59.more_ref, bf16[1152,128]{1,0:T(8,128)(2,1)S(1)} %get-tuple-element.60.own, ...), custom_call_target="tpu_custom_call", output_to_operand_aliasing={{}: (8, {})} | custom-call | flops 603979776 | bytes 4718592 | tf_op jit(solution)/shard_map/pallas_call | solution.py:472
  37.1 1.0 %collective-permute-done.15.got_g = bf16[384,128]{1,0:T(8,128)(2,1)S(1)} collective-permute-done((bf16[384,128]{1,0:T(8,128)(2,1)S(1)}, bf16[384,128]{1,0:T(8,128)(2,1)S(1)}, u32[]{:S(2)}, u32[]{:S(2)}) %collective-permute-start.15) | collective-permute-done | bytes 98336 | tf_op jit(solution)/shard_map/ppermute | solution.py:568
  38.1 2.1 %collective-permute-done.16.got_u = bf16[384,128]{1,0:T(8,128)(2,1)S(1)} collective-permute-done((bf16[384,128]{1,0:T(8,128)(2,1)S(1)}, bf16[384,128]{1,0:T(8,128)(2,1)S(1)}, u32[]{:S(2)}, u32[]{:S(2)}) %collective-permute-start.16) | collective-permute-done | bytes 98336 | tf_op jit(solution)/shard_map/ppermute | solution.py:568
  40.2 0.6 %shard_map.104 = (bf16[192,1024]{1,0:T(8,128)(2,1)S(1)}, bf16[192,1024]{1,0:T(8,128)(2,1)S(1)}, bf16[192,1024]{1,0:T(8,128)(2,1)S(1)}) custom-call(bf16[384,128]{1,0:T(8,128)(2,1)S(1)} %get-tuple-element.55.own_g, bf16[384,128]{1,0:T(8,128)(2,1)S(1)} %collective-permute-done.15.got_g, bf16[384,128]{1,0:T(8,128)(2,1)S(1)} %get-tuple-element.56.own_u, ...), custom_call_target="tpu_custom_call" | custom-call | flops 100663296 | bytes 2752512 | tf_op jit(solution)/shard_map/pallas_call | solution.py:515
  40.8 0.9 %collective-permute-done.17.got_d = bf16[384,128]{1,0:T(8,128)(2,1)S(1)} collective-permute-done((bf16[384,128]{1,0:T(8,128)(2,1)S(1)}, bf16[384,128]{1,0:T(8,128)(2,1)S(1)}, u32[]{:S(2)}, u32[]{:S(2)}) %collective-permute-start.17) | collective-permute-done | bytes 98336 | tf_op jit(solution)/shard_map/ppermute | solution.py:568
  41.7 2.2 %shard_map.105 = (bf16[3,192,1024]{2,1,0:T(8,128)(2,1)}, bf16[3,192,1024]{2,1,0:T(8,128)(2,1)}, bf16[3,192,1024]{2,1,0:T(8,128)(2,1)}) custom-call(bf16[384,128]{1,0:T(8,128)(2,1)S(1)} %get-tuple-element.55.own_g, bf16[384,128]{1,0:T(8,128)(2,1)S(1)} %collective-permute-done.15.got_g, bf16[384,128]{1,0:T(8,128)(2,1)S(1)} %get-tuple-element.56.own_u, ...), custom_call_target="tpu_custom_call" | custom-call | flops 201326592 | bytes 5505024 | tf_op jit(solution)/shard_map/pallas_call | solution.py:554
  (30 shorter events, 5.2 us)
Async XLA Ops:
  2.3 5.2 %collective-permute-start = (bf16[272,1024]{1,0:T(8,128)(2,1)S(1)}, bf16[272,1024]{1,0:T(8,128)(2,1)S(1)}, u32[]{:S(2)}, u32[]{:S(2)}) collective-permute-start(bf16[272,1024]{1,0:T(8,128)(2,1)S(1)} %get-tuple-element.35.after_ref.refs_0_.refs_5_), channel_id=1, source_target_pairs={{0,1},{1,0},{2,3},{3,2},{4,5},{5,4},{6,7},{7,6},{8,9},{9,8},{10,11... | collective-permute-start | bytes 1671176 | tf_op jit(solution)/shard_map/ppermute | solution.py:568
  2.8 8.6 %collective-permute-start.1 = (bf16[128,1024]{1,0:T(8,128)(2,1)S(1)}, bf16[128,1024]{1,0:T(8,128)(2,1)S(1)}, u32[]{:S(2)}, u32[]{:S(2)}) collective-permute-start(bf16[128,1024]{1,0:T(8,128)(2,1)S(1)} %get-tuple-element.37), channel_id=1, source_target_pairs={{0,2},{1,5},{2,0},{3,7},{4,6},{5,1},{6,4},{7,3},{8,10},{9,13},{10,... | collective-permute-start | bytes 786440 | tf_op jit(solution)/shard_map/ppermute | solution.py:587
  5.4 9.2 %collective-permute-start.2 = (bf16[128,1024]{1,0:T(8,128)(2,1)S(1)}, bf16[128,1024]{1,0:T(8,128)(2,1)S(1)}, u32[]{:S(2)}, u32[]{:S(2)}) collective-permute-start(bf16[128,1024]{1,0:T(8,128)(2,1)S(1)} %get-tuple-element.37), channel_id=1, source_target_pairs={{0,4},{1,3},{2,6},{3,1},{4,0},{5,7},{6,2},{7,5},{8,12},{9,11},{10,... | collective-permute-start | bytes 786440 | tf_op jit(solution)/shard_map/ppermute | solution.py:587
  6.9 10.8 %collective-permute-start.6 = (bf16[144,1024]{1,0:T(8,128)(2,1)S(1)}, bf16[144,1024]{1,0:T(8,128)(2,1)S(1)}, u32[]{:S(2)}, u32[]{:S(2)}) collective-permute-start(bf16[144,1024]{1,0:T(8,128)(2,1)S(1)} %get-tuple-element.41), channel_id=1, source_target_pairs={{0,2},{1,5},{2,0},{3,7},{4,6},{5,1},{6,4},{7,3},{8,10},{9,13},{10,... | collective-permute-start | bytes 884744 | tf_op jit(solution)/shard_map/ppermute | solution.py:588
  7.5 11.2 %collective-permute-start.7 = (bf16[144,1024]{1,0:T(8,128)(2,1)S(1)}, bf16[144,1024]{1,0:T(8,128)(2,1)S(1)}, u32[]{:S(2)}, u32[]{:S(2)}) collective-permute-start(bf16[144,1024]{1,0:T(8,128)(2,1)S(1)} %get-tuple-element.41), channel_id=1, source_target_pairs={{0,4},{1,3},{2,6},{3,1},{4,0},{5,7},{6,2},{7,5},{8,12},{9,11},{10,... | collective-permute-start | bytes 884744 | tf_op jit(solution)/shard_map/ppermute | solution.py:588
  8.1 11.6 %collective-permute-start.3 = (bf16[1152,128]{1,0:T(8,128)(2,1)S(1)}, bf16[1152,128]{1,0:T(8,128)(2,1)S(1)}, u32[]{:S(2)}, u32[]{:S(2)}) collective-permute-start(bf16[1152,128]{1,0:T(8,128)(2,1)S(1)} %get-tuple-element.39.own), channel_id=1, source_target_pairs={{0,8},{8,0},{16,24},{24,16},{1,9},{9,1},{17,25},{25,17},{2,10},{10... | collective-permute-start | bytes 884744 | tf_op jit(solution)/shard_map/ppermute | solution.py:568
  11.5 7.2 %collective-permute-start.5 = (bf16[128,1024]{1,0:T(8,128)(2,1)S(1)}, bf16[128,1024]{1,0:T(8,128)(2,1)S(1)}, u32[]{:S(2)}, u32[]{:S(2)}) collective-permute-start(bf16[128,1024]{1,0:T(8,128)(2,1)S(1)} %collective-permute-done.1.refs_0_), channel_id=1, source_target_pairs={{0,1},{1,0},{2,3},{3,2},{4,5},{5,4},{6,7},{7,6},{8,9},{9,8},{10,11... | collective-permute-start | bytes 786440 | tf_op jit(solution)/shard_map/ppermute | solution.py:568
  15.0 4.7 %collective-permute-start.4 = (bf16[384,128]{1,0:T(8,128)(2,1)S(1)}, bf16[384,128]{1,0:T(8,128)(2,1)S(1)}, u32[]{:S(2)}, u32[]{:S(2)}) collective-permute-start(bf16[384,128]{1,0:T(8,128)(2,1)S(1)} %get-tuple-element.40.near_own), channel_id=1, source_target_pairs={{0,8},{8,0},{16,24},{24,16},{1,9},{9,1},{17,25},{25,17},{2,10},{10... | collective-permute-start | bytes 294920 | tf_op jit(solution)/shard_map/ppermute | solution.py:568
  19.9 3.7 %collective-permute-start.8 = (bf16[416,1024]{1,0:T(8,128)(2,1)S(1)}, bf16[416,1024]{1,0:T(8,128)(2,1)S(1)}, u32[]{:S(2)}, u32[]{:S(2)}) collective-permute-start(bf16[416,1024]{1,0:T(8,128)(2,1)S(1)} %get-tuple-element.44.refs_0_.refs_1_), channel_id=1, source_target_pairs={{0,1},{1,0},{2,3},{3,2},{4,5},{5,4},{6,7},{7,6},{8,9},{9,8},{10,11... | collective-permute-start | bytes 2555912 | tf_op jit(solution)/shard_map/ppermute | solution.py:568
  20.0 9.6 %collective-permute-start.9 = (bf16[272,1024]{1,0:T(8,128)(2,1)S(1)}, bf16[272,1024]{1,0:T(8,128)(2,1)S(1)}, u32[]{:S(2)}, u32[]{:S(2)}) collective-permute-start(bf16[272,1024]{1,0:T(8,128)(2,1)S(1)} %get-tuple-element.43.after_ref), channel_id=1, source_target_pairs={{0,4},{1,3},{2,6},{3,1},{4,0},{5,7},{6,2},{7,5},{8,12},{9,11},{10,... | collective-permute-start | bytes 1671176 | tf_op jit(solution)/shard_map/ppermute | solution.py:594
  22.0 8.3 %collective-permute-start.10 = (bf16[768,128]{1,0:T(8,128)(2,1)S(1)}, bf16[768,128]{1,0:T(8,128)(2,1)S(1)}, u32[]{:S(2)}, u32[]{:S(2)}) collective-permute-start(bf16[768,128]{1,0:T(8,128)(2,1)S(1)} %get-tuple-element.50.own), channel_id=1, source_target_pairs={{0,8},{8,0},{16,24},{24,16},{1,9},{9,1},{17,25},{25,17},{2,10},{10... | collective-permute-start | bytes 589832 | tf_op jit(solution)/shard_map/ppermute | solution.py:568
  24.3 11.8 %collective-permute-start.18 = (bf16[1152,128]{1,0:T(8,128)(2,1)S(1)}, bf16[1152,128]{1,0:T(8,128)(2,1)S(1)}, u32[]{:S(2)}, u32[]{:S(2)}) collective-permute-start(bf16[1152,128]{1,0:T(8,128)(2,1)S(1)} %get-tuple-element.60.own), channel_id=1, source_target_pairs={{0,8},{8,0},{16,24},{24,16},{1,9},{9,1},{17,25},{25,17},{2,10},{10... | collective-permute-start | bytes 884744 | tf_op jit(solution)/shard_map/ppermute | solution.py:568
  29.6 2.1 %collective-permute-start.14 = (bf16[80,1024]{1,0:T(8,128)(2,1)S(1)}, bf16[80,1024]{1,0:T(8,128)(2,1)S(1)}, u32[]{:S(2)}, u32[]{:S(2)}) collective-permute-start(bf16[80,1024]{1,0:T(8,128)(2,1)S(1)} %get-tuple-element.54.refs_3_.refs_1_.refs_2_), channel_id=1, source_target_pairs={{0,1},{1,0},{2,3},{3,2},{4,5},{5,4},{6,7},{7,6},{8,9},{9,8},{10,11... | collective-permute-start | bytes 491528 | tf_op jit(solution)/shard_map/ppermute | solution.py:568
  29.7 1.6 %collective-permute-start.11 = (bf16[64,1024]{1,0:T(8,128)(2,1)S(1)}, bf16[64,1024]{1,0:T(8,128)(2,1)S(1)}, u32[]{:S(2)}, u32[]{:S(2)}) collective-permute-start(bf16[64,1024]{1,0:T(8,128)(2,1)S(1)} %get-tuple-element.48.after_ref.refs_0_), channel_id=1, source_target_pairs={{0,1},{1,0},{2,3},{3,2},{4,5},{5,4},{6,7},{7,6},{8,9},{9,8},{10,11... | collective-permute-start | bytes 393224 | tf_op jit(solution)/shard_map/ppermute | solution.py:568
  30.2 1.3 %collective-permute-start.12 = (bf16[64,1024]{1,0:T(8,128)(2,1)S(1)}, bf16[64,1024]{1,0:T(8,128)(2,1)S(1)}, u32[]{:S(2)}, u32[]{:S(2)}) collective-permute-start(bf16[64,1024]{1,0:T(8,128)(2,1)S(1)} %get-tuple-element.52.refs_1_), channel_id=1, source_target_pairs={{0,1},{1,0},{2,3},{3,2},{4,5},{5,4},{6,7},{7,6},{8,9},{9,8},{10,11... | collective-permute-start | bytes 393224 | tf_op jit(solution)/shard_map/ppermute | solution.py:568
  30.3 1.5 %collective-permute-start.13 = (bf16[64,1024]{1,0:T(8,128)(2,1)S(1)}, bf16[64,1024]{1,0:T(8,128)(2,1)S(1)}, u32[]{:S(2)}, u32[]{:S(2)}) collective-permute-start(bf16[64,1024]{1,0:T(8,128)(2,1)S(1)} %get-tuple-element.53.refs_2_.refs_0_), channel_id=1, source_target_pairs={{0,1},{1,0},{2,3},{3,2},{4,5},{5,4},{6,7},{7,6},{8,9},{9,8},{10,11... | collective-permute-start | bytes 393224 | tf_op jit(solution)/shard_map/ppermute | solution.py:568
  32.4 5.7 %collective-permute-start.15 = (bf16[384,128]{1,0:T(8,128)(2,1)S(1)}, bf16[384,128]{1,0:T(8,128)(2,1)S(1)}, u32[]{:S(2)}, u32[]{:S(2)}) collective-permute-start(bf16[384,128]{1,0:T(8,128)(2,1)S(1)} %get-tuple-element.55.own_g), channel_id=1, source_target_pairs={{0,8},{8,0},{16,24},{24,16},{1,9},{9,1},{17,25},{25,17},{2,10},{10... | collective-permute-start | bytes 294920 | tf_op jit(solution)/shard_map/ppermute | solution.py:568
  34.1 6.1 %collective-permute-start.16 = (bf16[384,128]{1,0:T(8,128)(2,1)S(1)}, bf16[384,128]{1,0:T(8,128)(2,1)S(1)}, u32[]{:S(2)}, u32[]{:S(2)}) collective-permute-start(bf16[384,128]{1,0:T(8,128)(2,1)S(1)} %get-tuple-element.56.own_u), channel_id=1, source_target_pairs={{0,8},{8,0},{16,24},{24,16},{1,9},{9,1},{17,25},{25,17},{2,10},{10... | collective-permute-start | bytes 294920 | tf_op jit(solution)/shard_map/ppermute | solution.py:568
  34.5 7.2 %collective-permute-start.17 = (bf16[384,128]{1,0:T(8,128)(2,1)S(1)}, bf16[384,128]{1,0:T(8,128)(2,1)S(1)}, u32[]{:S(2)}, u32[]{:S(2)}) collective-permute-start(bf16[384,128]{1,0:T(8,128)(2,1)S(1)} %get-tuple-element.57.own_d), channel_id=1, source_target_pairs={{0,8},{8,0},{16,24},{24,16},{1,9},{9,1},{17,25},{25,17},{2,10},{10... | collective-permute-start | bytes 294920 | tf_op jit(solution)/shard_map/ppermute | solution.py:568
  36.1 4.1 %copy-start = (bf16[3,192,1024]{2,1,0:T(8,128)(2,1)S(1)}, bf16[3,192,1024]{2,1,0:T(8,128)(2,1)}, u32[]{:S(2)}) copy-start(bf16[3,192,1024]{2,1,0:T(8,128)(2,1)} %refs_7_.1) | copy-start | bytes 3538948
  36.1 4.1 %copy-start.1 = (bf16[3,192,1024]{2,1,0:T(8,128)(2,1)S(1)}, bf16[3,192,1024]{2,1,0:T(8,128)(2,1)}, u32[]{:S(2)}) copy-start(bf16[3,192,1024]{2,1,0:T(8,128)(2,1)} %refs_8_.1) | copy-start | bytes 3538948

commit v10 on v9

--- a/solution.py
+++ b/solution.py
@@ -499,10 +499,13 @@
 
 def down_kernel(kinds, count, own_g, got_g, own_u, got_u, *refs):
     n = len(kinds)
-    acc_ref, first_ref, second_ref, *outs = refs[n:]
+    acc_ref, first_ref, second_ref, *outs, gate_factor_ref, up_factor_ref = refs[n:]
     xs, ys, gates = views(refs[:n], kinds, count)
     hg, hu = pair_of_blocks(own_g, got_g), pair_of_blocks(own_u, got_u)
-    act = activation(hg, hu, gate_row(gates))[2]
+    gate = gate_row(gates)
+    sig, silu, act = activation(hg, hu, gate)
+    gate_factor_ref[...] = gate * (hu * sig * (1.0 + hg * (1.0 - sig)))
+    up_factor_ref[...] = gate * silu
     grad = acc_ref[2] + plain(act, joined(ys))
     for out_ref, value in zip(outs, adam(grad, first_ref[2], second_ref[2])):
         out_ref[...] = value
@@ -515,49 +518,57 @@
     return pl.pallas_call(
         functools.partial(down_kernel, kinds, count),
         in_specs=[whole()] * len(operands),
-        out_specs=[whole()] * 3,
-        out_shape=[jax.ShapeDtypeStruct((hidden, width), jnp.bfloat16)] * 3,
+        out_specs=[whole()] * 5,
+        out_shape=[jax.ShapeDtypeStruct((hidden, width), jnp.bfloat16)] * 3
+        + [jax.ShapeDtypeStruct((hidden, 2 * count), jnp.float32)] * 2,
         compiler_params=params(),
         cost_estimate=cost(4 * hidden * width * count, 14 * hidden * width),
     )(*operands)
 
 
-def slopes_kernel(kinds, count, own_g, got_g, own_u, got_u, own_d, got_d, *refs):
+def slopes_kernel(kinds, count, own_d, got_d, gate_factor_ref, up_factor_ref, *refs):
     n = len(kinds)
     acc_ref, first_ref, second_ref = refs[n : n + 3]
     done, outs = refs[n + 3 : n + 6], refs[n + 6 : n + 9]
     held, sems = refs[n + 9 : n + 12], refs[n + 12]
     copies = [
-        pltpu.make_async_copy(done[k], outs[k].at[2], sems.at[2, k]) for k in range(3)
+        pltpu.make_async_copy(done[k], outs[k].at[2], sems.at[2, 0, k]) for k in range(3)
     ]
     for copy in copies:
         copy.start()
     xs, ys, gates = views(refs[:n], kinds, count)
-    hg, hu = pair_of_blocks(own_g, got_g), pair_of_blocks(own_u, got_u)
-    dact = gate_row(gates) * pair_of_blocks(own_d, got_d)
-    sig, silu, act = activation(hg, hu, 1.0)
-    right = joined(xs)
-    for m, left in enumerate(hidden_slopes(hg, hu, sig, silu, dact)):
-        grad = acc_ref[m] + plain(left, right)
-        for k, value in enumerate(adam(grad, first_ref[m], second_ref[m])):
-            held[k][m] = value
-            copies.append(pltpu.make_async_copy(held[k].at[m], outs[k].at[m], sems.at[m, k]))
-            copies[-1].start()
+    dact = pair_of_blocks(own_d, got_d)
+    half = acc_ref.shape[2] // 2
+    for m, factor_ref in enumerate((gate_factor_ref, up_factor_ref)):
+        left = (dact * factor_ref[...]).astype(jnp.bfloat16)
+        for side in (0, 1):
+            columns = slice(side * half, (side + 1) * half)
+            right = jnp.concatenate([x[:, columns] for x in xs], 0)
+            grad = acc_ref[m, :, columns] + plain(left, right)
+            values = adam(grad, first_ref[m, :, columns], second_ref[m, :, columns])
+            for k, value in enumerate(values):
+                held[k][m, side] = value
+                copies.append(
+                    pltpu.make_async_copy(
+                        held[k].at[m, side], outs[k].at[m, :, columns], sems.at[m, side, k]
+                    )
+                )
+                copies[-1].start()
     for copy in copies:
         copy.wait()
 
 
-def slopes_update(pairs, chunk, acc, moments, done, count):
+def slopes_update(pair, factors, chunk, acc, moments, done, count):
     kinds = kinds_of(chunk)
     mats, hidden, width = acc.shape
-    operands = [*pairs, *values_of(chunk), acc, *moments, *done]
+    operands = [*pair, *factors, *values_of(chunk), acc, *moments, *done]
     return pl.pallas_call(
         functools.partial(slopes_kernel, kinds, count),
         in_specs=[whole()] * len(operands),
         out_specs=[in_hbm()] * 3,
         out_shape=[jax.ShapeDtypeStruct(acc.shape, jnp.bfloat16)] * 3,
-        scratch_shapes=[pltpu.VMEM((2, hidden, width), jnp.bfloat16)] * 3
-        + [pltpu.SemaphoreType.DMA((3, 3))],
+        scratch_shapes=[pltpu.VMEM((2, 2, hidden, width // 2), jnp.bfloat16)] * 3
+        + [pltpu.SemaphoreType.DMA((3, 2, 3))],
         compiler_params=params(),
         cost_estimate=cost(8 * hidden * width * count, 28 * hidden * width),
     )(*operands)
@@ -611,9 +622,10 @@
     acc = add_grads(near_sum, early_sum, late_pair, near, acc, count)
     moments = (first_moment, second_moment)
     final_y = [block for block in final if block[0] != "x"]
-    final_x = [block for block in final if block[0] != "y"]
-    done = down_update(pairs[:4], final_y, acc, moments, count)
-    return tuple(slopes_update(pairs, final_x, acc, moments, done, count))
+    final_x = [block for block in final if block[0] == "x"]
+    *done, gate_factor, up_factor = down_update(pairs[:4], final_y, acc, moments, count)
+    factors = (gate_factor, up_factor)
+    return tuple(slopes_update(pairs[4:], factors, final_x, acc, moments, done, count))
 
 
 def per_device(tokens, cotangent, expert_ids, gate_probs, weights, first_moment, second_moment):

time: 44.1 us -> 43.9 us (level)
  no operation moved by 1% of the time
where the time goes in v10:
time: 43.9 us; the launch traced here: 43.8 us
  starting transfers between devices  17.5 us (40%)
  waiting for transfers between devices  16.7 us (38%)
  Pallas kernels  8.8 us (20%)
  between operations  0.75 us (2%)
    ppermute x14, starting transfers between devices, from_masked(): return lax.ppermute(value, axis, pairs)  11.2 us
    ppermute x14, waiting for transfers between devices, from_masked(): return lax.ppermute(value, axis, pairs)  5.48 us
    ppermute x1, waiting for transfers between devices, dense_plan(): far = lax.ppermute(picked, 'dp', along[1])  4.76 us
    ppermute x2, waiting for transfers between devices, dense_plan(): near_x = [lax.ppermute(x_own, 'dp', pairs) for pairs in along]  4.47 us
    ppermute x2, starting transfers between devices, dense_plan(): near_x = [lax.ppermute(x_own, 'dp', pairs) for pairs in along]  4.1 us
    pallas_call x5, Pallas kernels, partials(): pl.pallas_call(functools.partial(partial_kernel, kinds, count, tokened),...  2.64 us
    pallas_call x1, Pallas kernels, slopes_update(): pl.pallas_call(functools.partial(slopes_kernel, kinds, count), in_specs=[...  2.04 us
    ppermute x2, waiting for transfers between devices, dense_plan(): near_y = [lax.ppermute(y_own, 'dp', pairs) for pairs in along]  1.99 us
  transfers between devices with their start and end apart: 19, of which 11 were waited for; matrix products, arithmetic and copies ran while one was open for 0% of the time, Pallas kernels for 11%

profile of v10, /device:TPU:0, one launch (start us, length us, event | category | flops | bytes accessed | tf_op | source)
XLA Modules:
  0.0 43.8 jit_solution(12839141625582039042)
XLA Ops:
  0.6 1.7 %shard_map.94 = (bf16[128,1024]{1,0:T(8,128)(2,1)S(1)}, bf16[144,1024]{1,0:T(8,128)(2,1)S(1)}, bf16[272,1024]{1,0:T(8,128)(2,1)S(1)}, bf16[3,192,1024]{2,1,0:T(8,128)(2,1)S(1)}) custom-call(s32[4,128]{1,0:T(4,128)} %bitcast.2, bf16[4,128]{1,0:T(4,128)(2,1)} %bitcast.3, bf16[128,2048]{1,0:T(8,128)(2,1)} %tokens_ref.1, bf16[128,2048]{1,0:T(8,128)(2,1)} %cot_ref.1, ...), custom_call_target="tpu_custom_call" | custom-call | flops 1000 | bytes 1048576 | tf_op jit(solution)/shard_map/pallas_call | solution.py:209
  2.8 2.6 %collective-permute-start.1 = (bf16[128,1024]{1,0:T(8,128)(2,1)S(1)}, bf16[128,1024]{1,0:T(8,128)(2,1)S(1)}, u32[]{:S(2)}, u32[]{:S(2)}) collective-permute-start(bf16[128,1024]{1,0:T(8,128)(2,1)S(1)} %get-tuple-element.39), channel_id=1, source_target_pairs={{0,2},{1,5},{2,0},{3,7},{4,6},{5,1},{6,4},{7,3},{8,10},{9,13},{10,... | collective-permute-start | bytes 786440 | tf_op jit(solution)/shard_map/ppermute | solution.py:598
  5.4 1.5 %collective-permute-start.2 = (bf16[128,1024]{1,0:T(8,128)(2,1)S(1)}, bf16[128,1024]{1,0:T(8,128)(2,1)S(1)}, u32[]{:S(2)}, u32[]{:S(2)}) collective-permute-start(bf16[128,1024]{1,0:T(8,128)(2,1)S(1)} %get-tuple-element.39), channel_id=1, source_target_pairs={{0,4},{1,3},{2,6},{3,1},{4,0},{5,7},{6,2},{7,5},{8,12},{9,11},{10,... | collective-permute-start | bytes 786440 | tf_op jit(solution)/shard_map/ppermute | solution.py:598
  8.1 2.1 %collective-permute-start.3 = (bf16[1152,128]{1,0:T(8,128)(2,1)S(1)}, bf16[1152,128]{1,0:T(8,128)(2,1)S(1)}, u32[]{:S(2)}, u32[]{:S(2)}) collective-permute-start(bf16[1152,128]{1,0:T(8,128)(2,1)S(1)} %get-tuple-element.41.own), channel_id=1, source_target_pairs={{0,8},{8,0},{16,24},{24,16},{1,9},{9,1},{17,25},{25,17},{2,10},{10... | collective-permute-start | bytes 884744 | tf_op jit(solution)/shard_map/ppermute | solution.py:579
  10.2 1.3 %collective-permute-done.1.refs_0_ = bf16[128,1024]{1,0:T(8,128)(2,1)S(1)} collective-permute-done((bf16[128,1024]{1,0:T(8,128)(2,1)S(1)}, bf16[128,1024]{1,0:T(8,128)(2,1)S(1)}, u32[]{:S(2)}, u32[]{:S(2)}) %collective-permute-start.1) | collective-permute-done | bytes 262176 | tf_op jit(solution)/shard_map/ppermute | solution.py:598
  11.5 3.2 %collective-permute-done.2.refs_1_ = bf16[128,1024]{1,0:T(8,128)(2,1)S(1)} collective-permute-done((bf16[128,1024]{1,0:T(8,128)(2,1)S(1)}, bf16[128,1024]{1,0:T(8,128)(2,1)S(1)}, u32[]{:S(2)}, u32[]{:S(2)}) %collective-permute-start.2) | collective-permute-done | bytes 262176 | tf_op jit(solution)/shard_map/ppermute | solution.py:598
  15.0 1.6 %collective-permute-start.4 = (bf16[384,128]{1,0:T(8,128)(2,1)S(1)}, bf16[384,128]{1,0:T(8,128)(2,1)S(1)}, u32[]{:S(2)}, u32[]{:S(2)}) collective-permute-start(bf16[384,128]{1,0:T(8,128)(2,1)S(1)} %get-tuple-element.42.near_own), channel_id=1, source_target_pairs={{0,8},{8,0},{16,24},{24,16},{1,9},{9,1},{17,25},{25,17},{2,10},{10... | collective-permute-start | bytes 294920 | tf_op jit(solution)/shard_map/ppermute | solution.py:579
  16.7 1.1 %collective-permute-done.6.refs_3_ = bf16[144,1024]{1,0:T(8,128)(2,1)S(1)} collective-permute-done((bf16[144,1024]{1,0:T(8,128)(2,1)S(1)}, bf16[144,1024]{1,0:T(8,128)(2,1)S(1)}, u32[]{:S(2)}, u32[]{:S(2)}) %collective-permute-start.6) | collective-permute-done | bytes 294944 | tf_op jit(solution)/shard_map/ppermute | solution.py:599
  17.8 0.9 %collective-permute-done.7.refs_4_ = bf16[144,1024]{1,0:T(8,128)(2,1)S(1)} collective-permute-done((bf16[144,1024]{1,0:T(8,128)(2,1)S(1)}, bf16[144,1024]{1,0:T(8,128)(2,1)S(1)}, u32[]{:S(2)}, u32[]{:S(2)}) %collective-permute-start.7) | collective-permute-done | bytes 294944 | tf_op jit(solution)/shard_map/ppermute | solution.py:599
  18.7 1.0 %collective-permute-done.4.near_got = bf16[384,128]{1,0:T(8,128)(2,1)S(1)} collective-permute-done((bf16[384,128]{1,0:T(8,128)(2,1)S(1)}, bf16[384,128]{1,0:T(8,128)(2,1)S(1)}, u32[]{:S(2)}, u32[]{:S(2)}) %collective-permute-start.4) | collective-permute-done | bytes 98336 | tf_op jit(solution)/shard_map/ppermute | solution.py:579
  20.0 1.6 %collective-permute-start.9 = (bf16[272,1024]{1,0:T(8,128)(2,1)S(1)}, bf16[272,1024]{1,0:T(8,128)(2,1)S(1)}, u32[]{:S(2)}, u32[]{:S(2)}) collective-permute-start(bf16[272,1024]{1,0:T(8,128)(2,1)S(1)} %get-tuple-element.45.after_ref), channel_id=1, source_target_pairs={{0,4},{1,3},{2,6},{3,1},{4,0},{5,7},{6,2},{7,5},{8,12},{9,11},{10,... | collective-permute-start | bytes 1671176 | tf_op jit(solution)/shard_map/ppermute | solution.py:605
  22.0 1.6 %collective-permute-start.10 = (bf16[768,128]{1,0:T(8,128)(2,1)S(1)}, bf16[768,128]{1,0:T(8,128)(2,1)S(1)}, u32[]{:S(2)}, u32[]{:S(2)}) collective-permute-start(bf16[768,128]{1,0:T(8,128)(2,1)S(1)} %get-tuple-element.52.own), channel_id=1, source_target_pairs={{0,8},{8,0},{16,24},{24,16},{1,9},{9,1},{17,25},{25,17},{2,10},{10... | collective-permute-start | bytes 589832 | tf_op jit(solution)/shard_map/ppermute | solution.py:579
  23.7 0.7 %shard_map.99 = (bf16[1152,128]{1,0:T(8,128)(2,1)S(1)}, f32[8,128]{1,0:T(8,128)S(1)}) custom-call(bf16[3,192,1024]{2,1,0:T(8,128)(2,1)S(1)} %get-tuple-element.36.w_ref, f32[8,128]{1,0:T(8,128)S(1)} %get-tuple-element.48.after_ref, bf16[416,1024]{1,0:T(8,128)(2,1)S(1)} %get-tuple-element.46.refs_0_.refs_1_, ...), custom_call_target="tpu_custom_call" | custom-call | flops 301989888 | bytes 884736 | tf_op jit(solution)/shard_map/pallas_call | solution.py:309
  24.8 4.8 %collective-permute-done.9.in_ref = bf16[272,1024]{1,0:T(8,128)(2,1)S(1)} collective-permute-done((bf16[272,1024]{1,0:T(8,128)(2,1)S(1)}, bf16[272,1024]{1,0:T(8,128)(2,1)S(1)}, u32[]{:S(2)}, u32[]{:S(2)}) %collective-permute-start.9) | collective-permute-done | bytes 557088 | tf_op jit(solution)/shard_map/ppermute | solution.py:605
  30.7 0.6 %shard_map.101 = (f32[3,192,1024]{2,1,0:T(8,128)S(1)}, f32[768,128]{1,0:T(8,128)S(1)}, f32[8,128]{1,0:T(8,128)S(1)}) custom-call(f32[8,256]{1,0:T(8,128)S(1)} %get-tuple-element.44.gate_ref, bf16[64,1024]{1,0:T(8,128)(2,1)S(1)} %get-tuple-element.50.after_ref.refs_0_, f32[1152,128]{1,0:T(8,128)S(1)} %get-tuple-element.51.sum_ref, ...), custom_call_target="tpu_custom_call" | custom-call | flops 301989888 | bytes 2359296 | tf_op jit(solution)/shard_map/pallas_call | solution.py:444
  31.7 0.7 %shard_map.102 = (bf16[384,128]{1,0:T(8,128)(2,1)S(1)}, bf16[384,128]{1,0:T(8,128)(2,1)S(1)}, bf16[384,128]{1,0:T(8,128)(2,1)S(1)}) custom-call(bf16[3,192,1024]{2,1,0:T(8,128)(2,1)S(1)} %get-tuple-element.36.w_ref, f32[8,128]{1,0:T(8,128)S(1)} %get-tuple-element.53.after_ref, bf16[64,1024]{1,0:T(8,128)(2,1)S(1)} %get-tuple-element.50.after_ref.refs_0_, ...), custom_call_target="tpu_custom_call" | custom-call | flops 301989888 | bytes 884736 | tf_op jit(solution)/shard_map/pallas_call | solution.py:309
  32.4 1.6 %collective-permute-start.16 = (bf16[384,128]{1,0:T(8,128)(2,1)S(1)}, bf16[384,128]{1,0:T(8,128)(2,1)S(1)}, u32[]{:S(2)}, u32[]{:S(2)}) collective-permute-start(bf16[384,128]{1,0:T(8,128)(2,1)S(1)} %get-tuple-element.58.own_g), channel_id=1, source_target_pairs={{0,8},{8,0},{16,24},{24,16},{1,9},{9,1},{17,25},{25,17},{2,10},{10... | collective-permute-start | bytes 294920 | tf_op jit(solution)/shard_map/ppermute | solution.py:579
  34.5 1.6 %collective-permute-start.15 = (bf16[384,128]{1,0:T(8,128)(2,1)S(1)}, bf16[384,128]{1,0:T(8,128)(2,1)S(1)}, u32[]{:S(2)}, u32[]{:S(2)}) collective-permute-start(bf16[384,128]{1,0:T(8,128)(2,1)S(1)} %get-tuple-element.57.own_d), channel_id=1, source_target_pairs={{0,8},{8,0},{16,24},{24,16},{1,9},{9,1},{17,25},{25,17},{2,10},{10... | collective-permute-start | bytes 294920 | tf_op jit(solution)/shard_map/ppermute | solution.py:579
  36.1 1.0 %shard_map.103.refs_4_ = f32[3,192,1024]{2,1,0:T(8,128)S(1)} custom-call(f32[384,128]{1,0:T(8,128)S(1)} %get-tuple-element.60.sum_ref, f32[768,128]{1,0:T(8,128)S(1)} %get-tuple-element.61.more_ref, bf16[1152,128]{1,0:T(8,128)(2,1)S(1)} %get-tuple-element.62.own, bf16[1152,128]{1,0:T(8,128)(2,1)S(1)} %collective-permute-done.18.got, ...), custom_call_target="tpu_custom_call", output_to_operand_aliasing={{}: (8, {})} | custom-call | flops 603979776 | bytes 4718592 | tf_op jit(solution)/shard_map/pallas_call | solution.py:472
  37.1 1.0 %collective-permute-done.16.got_g = bf16[384,128]{1,0:T(8,128)(2,1)S(1)} collective-permute-done((bf16[384,128]{1,0:T(8,128)(2,1)S(1)}, bf16[384,128]{1,0:T(8,128)(2,1)S(1)}, u32[]{:S(2)}, u32[]{:S(2)}) %collective-permute-start.16) | collective-permute-done | bytes 98336 | tf_op jit(solution)/shard_map/ppermute | solution.py:579
  38.1 2.1 %collective-permute-done.17.got_u = bf16[384,128]{1,0:T(8,128)(2,1)S(1)} collective-permute-done((bf16[384,128]{1,0:T(8,128)(2,1)S(1)}, bf16[384,128]{1,0:T(8,128)(2,1)S(1)}, u32[]{:S(2)}, u32[]{:S(2)}) %collective-permute-start.17) | collective-permute-done | bytes 98336 | tf_op jit(solution)/shard_map/ppermute | solution.py:579
  40.2 0.6 %shard_map.104 = (bf16[192,1024]{1,0:T(8,128)(2,1)S(1)}, bf16[192,1024]{1,0:T(8,128)(2,1)S(1)}, bf16[192,1024]{1,0:T(8,128)(2,1)S(1)}, f32[192,256]{1,0:T(8,128)S(1)}, f32[192,256]{1,0:T(8,128)S(1)}) custom-call(bf16[384,128]{1,0:T(8,128)(2,1)S(1)} %get-tuple-element.58.own_g, bf16[384,128]{1,0:T(8,128)(2,1)S(1)} %collective-permute-done.16.got_g, ...), custom_call_target="tpu_custom_call" | custom-call | flops 100663296 | bytes 2752512 | tf_op jit(solution)/shard_map/pallas_call | solution.py:518
  40.9 0.9 %collective-permute-done.15.got_d = bf16[384,128]{1,0:T(8,128)(2,1)S(1)} collective-permute-done((bf16[384,128]{1,0:T(8,128)(2,1)S(1)}, bf16[384,128]{1,0:T(8,128)(2,1)S(1)}, u32[]{:S(2)}, u32[]{:S(2)}) %collective-permute-start.15) | collective-permute-done | bytes 98336 | tf_op jit(solution)/shard_map/ppermute | solution.py:579
  41.7 2.0 %shard_map.105 = (bf16[3,192,1024]{2,1,0:T(8,128)(2,1)}, bf16[3,192,1024]{2,1,0:T(8,128)(2,1)}, bf16[3,192,1024]{2,1,0:T(8,128)(2,1)}) custom-call(bf16[384,128]{1,0:T(8,128)(2,1)S(1)} %get-tuple-element.57.own_d, bf16[384,128]{1,0:T(8,128)(2,1)S(1)} %collective-permute-done.15.got_d, f32[192,256]{1,0:T(8,128)S(1)} %get-tuple-element.64.gate_factor_ref, ...), custom_call_target="tpu_custom_call" | custom-call | flops 201326592 | bytes 5505024 | tf_op jit(solution)/shard_map/pallas_call | solution.py:565
  (30 shorter events, 5.2 us)
Async XLA Ops:
  2.3 5.2 %collective-permute-start = (bf16[272,1024]{1,0:T(8,128)(2,1)S(1)}, bf16[272,1024]{1,0:T(8,128)(2,1)S(1)}, u32[]{:S(2)}, u32[]{:S(2)}) collective-permute-start(bf16[272,1024]{1,0:T(8,128)(2,1)S(1)} %get-tuple-element.37.after_ref.refs_0_.refs_5_), channel_id=1, source_target_pairs={{0,1},{1,0},{2,3},{3,2},{4,5},{5,4},{6,7},{7,6},{8,9},{9,8},{10,11... | collective-permute-start | bytes 1671176 | tf_op jit(solution)/shard_map/ppermute | solution.py:579
  2.8 8.6 %collective-permute-start.1 = (bf16[128,1024]{1,0:T(8,128)(2,1)S(1)}, bf16[128,1024]{1,0:T(8,128)(2,1)S(1)}, u32[]{:S(2)}, u32[]{:S(2)}) collective-permute-start(bf16[128,1024]{1,0:T(8,128)(2,1)S(1)} %get-tuple-element.39), channel_id=1, source_target_pairs={{0,2},{1,5},{2,0},{3,7},{4,6},{5,1},{6,4},{7,3},{8,10},{9,13},{10,... | collective-permute-start | bytes 786440 | tf_op jit(solution)/shard_map/ppermute | solution.py:598
  5.4 9.2 %collective-permute-start.2 = (bf16[128,1024]{1,0:T(8,128)(2,1)S(1)}, bf16[128,1024]{1,0:T(8,128)(2,1)S(1)}, u32[]{:S(2)}, u32[]{:S(2)}) collective-permute-start(bf16[128,1024]{1,0:T(8,128)(2,1)S(1)} %get-tuple-element.39), channel_id=1, source_target_pairs={{0,4},{1,3},{2,6},{3,1},{4,0},{5,7},{6,2},{7,5},{8,12},{9,11},{10,... | collective-permute-start | bytes 786440 | tf_op jit(solution)/shard_map/ppermute | solution.py:598
  6.9 10.8 %collective-permute-start.6 = (bf16[144,1024]{1,0:T(8,128)(2,1)S(1)}, bf16[144,1024]{1,0:T(8,128)(2,1)S(1)}, u32[]{:S(2)}, u32[]{:S(2)}) collective-permute-start(bf16[144,1024]{1,0:T(8,128)(2,1)S(1)} %get-tuple-element.43), channel_id=1, source_target_pairs={{0,2},{1,5},{2,0},{3,7},{4,6},{5,1},{6,4},{7,3},{8,10},{9,13},{10,... | collective-permute-start | bytes 884744 | tf_op jit(solution)/shard_map/ppermute | solution.py:599
  7.5 11.2 %collective-permute-start.7 = (bf16[144,1024]{1,0:T(8,128)(2,1)S(1)}, bf16[144,1024]{1,0:T(8,128)(2,1)S(1)}, u32[]{:S(2)}, u32[]{:S(2)}) collective-permute-start(bf16[144,1024]{1,0:T(8,128)(2,1)S(1)} %get-tuple-element.43), channel_id=1, source_target_pairs={{0,4},{1,3},{2,6},{3,1},{4,0},{5,7},{6,2},{7,5},{8,12},{9,11},{10,... | collective-permute-start | bytes 884744 | tf_op jit(solution)/shard_map/ppermute | solution.py:599
  8.1 11.6 %collective-permute-start.3 = (bf16[1152,128]{1,0:T(8,128)(2,1)S(1)}, bf16[1152,128]{1,0:T(8,128)(2,1)S(1)}, u32[]{:S(2)}, u32[]{:S(2)}) collective-permute-start(bf16[1152,128]{1,0:T(8,128)(2,1)S(1)} %get-tuple-element.41.own), channel_id=1, source_target_pairs={{0,8},{8,0},{16,24},{24,16},{1,9},{9,1},{17,25},{25,17},{2,10},{10... | collective-permute-start | bytes 884744 | tf_op jit(solution)/shard_map/ppermute | solution.py:579
  11.5 7.2 %collective-permute-start.5 = (bf16[128,1024]{1,0:T(8,128)(2,1)S(1)}, bf16[128,1024]{1,0:T(8,128)(2,1)S(1)}, u32[]{:S(2)}, u32[]{:S(2)}) collective-permute-start(bf16[128,1024]{1,0:T(8,128)(2,1)S(1)} %collective-permute-done.1.refs_0_), channel_id=1, source_target_pairs={{0,1},{1,0},{2,3},{3,2},{4,5},{5,4},{6,7},{7,6},{8,9},{9,8},{10,11... | collective-permute-start | bytes 786440 | tf_op jit(solution)/shard_map/ppermute | solution.py:579
  15.0 4.7 %collective-permute-start.4 = (bf16[384,128]{1,0:T(8,128)(2,1)S(1)}, bf16[384,128]{1,0:T(8,128)(2,1)S(1)}, u32[]{:S(2)}, u32[]{:S(2)}) collective-permute-start(bf16[384,128]{1,0:T(8,128)(2,1)S(1)} %get-tuple-element.42.near_own), channel_id=1, source_target_pairs={{0,8},{8,0},{16,24},{24,16},{1,9},{9,1},{17,25},{25,17},{2,10},{10... | collective-permute-start | bytes 294920 | tf_op jit(solution)/shard_map/ppermute | solution.py:579
  19.9 3.7 %collective-permute-start.8 = (bf16[416,1024]{1,0:T(8,128)(2,1)S(1)}, bf16[416,1024]{1,0:T(8,128)(2,1)S(1)}, u32[]{:S(2)}, u32[]{:S(2)}) collective-permute-start(bf16[416,1024]{1,0:T(8,128)(2,1)S(1)} %get-tuple-element.46.refs_0_.refs_1_), channel_id=1, source_target_pairs={{0,1},{1,0},{2,3},{3,2},{4,5},{5,4},{6,7},{7,6},{8,9},{9,8},{10,11... | collective-permute-start | bytes 2555912 | tf_op jit(solution)/shard_map/ppermute | solution.py:579
  20.0 9.6 %collective-permute-start.9 = (bf16[272,1024]{1,0:T(8,128)(2,1)S(1)}, bf16[272,1024]{1,0:T(8,128)(2,1)S(1)}, u32[]{:S(2)}, u32[]{:S(2)}) collective-permute-start(bf16[272,1024]{1,0:T(8,128)(2,1)S(1)} %get-tuple-element.45.after_ref), channel_id=1, source_target_pairs={{0,4},{1,3},{2,6},{3,1},{4,0},{5,7},{6,2},{7,5},{8,12},{9,11},{10,... | collective-permute-start | bytes 1671176 | tf_op jit(solution)/shard_map/ppermute | solution.py:605
  22.0 8.3 %collective-permute-start.10 = (bf16[768,128]{1,0:T(8,128)(2,1)S(1)}, bf16[768,128]{1,0:T(8,128)(2,1)S(1)}, u32[]{:S(2)}, u32[]{:S(2)}) collective-permute-start(bf16[768,128]{1,0:T(8,128)(2,1)S(1)} %get-tuple-element.52.own), channel_id=1, source_target_pairs={{0,8},{8,0},{16,24},{24,16},{1,9},{9,1},{17,25},{25,17},{2,10},{10... | collective-permute-start | bytes 589832 | tf_op jit(solution)/shard_map/ppermute | solution.py:579
  24.3 11.8 %collective-permute-start.18 = (bf16[1152,128]{1,0:T(8,128)(2,1)S(1)}, bf16[1152,128]{1,0:T(8,128)(2,1)S(1)}, u32[]{:S(2)}, u32[]{:S(2)}) collective-permute-start(bf16[1152,128]{1,0:T(8,128)(2,1)S(1)} %get-tuple-element.62.own), channel_id=1, source_target_pairs={{0,8},{8,0},{16,24},{24,16},{1,9},{9,1},{17,25},{25,17},{2,10},{10... | collective-permute-start | bytes 884744 | tf_op jit(solution)/shard_map/ppermute | solution.py:579
  29.6 2.1 %collective-permute-start.14 = (bf16[80,1024]{1,0:T(8,128)(2,1)S(1)}, bf16[80,1024]{1,0:T(8,128)(2,1)S(1)}, u32[]{:S(2)}, u32[]{:S(2)}) collective-permute-start(bf16[80,1024]{1,0:T(8,128)(2,1)S(1)} %get-tuple-element.56.refs_3_.refs_1_), channel_id=1, source_target_pairs={{0,1},{1,0},{2,3},{3,2},{4,5},{5,4},{6,7},{7,6},{8,9},{9,8},{10,11... | collective-permute-start | bytes 491528 | tf_op jit(solution)/shard_map/ppermute | solution.py:579
  29.7 1.6 %collective-permute-start.11 = (bf16[64,1024]{1,0:T(8,128)(2,1)S(1)}, bf16[64,1024]{1,0:T(8,128)(2,1)S(1)}, u32[]{:S(2)}, u32[]{:S(2)}) collective-permute-start(bf16[64,1024]{1,0:T(8,128)(2,1)S(1)} %get-tuple-element.50.after_ref.refs_0_), channel_id=1, source_target_pairs={{0,1},{1,0},{2,3},{3,2},{4,5},{5,4},{6,7},{7,6},{8,9},{9,8},{10,11... | collective-permute-start | bytes 393224 | tf_op jit(solution)/shard_map/ppermute | solution.py:579
  30.2 1.3 %collective-permute-start.12 = (bf16[64,1024]{1,0:T(8,128)(2,1)S(1)}, bf16[64,1024]{1,0:T(8,128)(2,1)S(1)}, u32[]{:S(2)}, u32[]{:S(2)}) collective-permute-start(bf16[64,1024]{1,0:T(8,128)(2,1)S(1)} %get-tuple-element.54.refs_1_), channel_id=1, source_target_pairs={{0,1},{1,0},{2,3},{3,2},{4,5},{5,4},{6,7},{7,6},{8,9},{9,8},{10,11... | collective-permute-start | bytes 393224 | tf_op jit(solution)/shard_map/ppermute | solution.py:579
  30.3 1.5 %collective-permute-start.13 = (bf16[64,1024]{1,0:T(8,128)(2,1)S(1)}, bf16[64,1024]{1,0:T(8,128)(2,1)S(1)}, u32[]{:S(2)}, u32[]{:S(2)}) collective-permute-start(bf16[64,1024]{1,0:T(8,128)(2,1)S(1)} %get-tuple-element.55.refs_2_.refs_0_), channel_id=1, source_target_pairs={{0,1},{1,0},{2,3},{3,2},{4,5},{5,4},{6,7},{7,6},{8,9},{9,8},{10,11... | collective-permute-start | bytes 393224 | tf_op jit(solution)/shard_map/ppermute | solution.py:579
  32.4 5.7 %collective-permute-start.16 = (bf16[384,128]{1,0:T(8,128)(2,1)S(1)}, bf16[384,128]{1,0:T(8,128)(2,1)S(1)}, u32[]{:S(2)}, u32[]{:S(2)}) collective-permute-start(bf16[384,128]{1,0:T(8,128)(2,1)S(1)} %get-tuple-element.58.own_g), channel_id=1, source_target_pairs={{0,8},{8,0},{16,24},{24,16},{1,9},{9,1},{17,25},{25,17},{2,10},{10... | collective-permute-start | bytes 294920 | tf_op jit(solution)/shard_map/ppermute | solution.py:579
  34.1 6.1 %collective-permute-start.17 = (bf16[384,128]{1,0:T(8,128)(2,1)S(1)}, bf16[384,128]{1,0:T(8,128)(2,1)S(1)}, u32[]{:S(2)}, u32[]{:S(2)}) collective-permute-start(bf16[384,128]{1,0:T(8,128)(2,1)S(1)} %get-tuple-element.59.own_u), channel_id=1, source_target_pairs={{0,8},{8,0},{16,24},{24,16},{1,9},{9,1},{17,25},{25,17},{2,10},{10... | collective-permute-start | bytes 294920 | tf_op jit(solution)/shard_map/ppermute | solution.py:579
  34.5 7.2 %collective-permute-start.15 = (bf16[384,128]{1,0:T(8,128)(2,1)S(1)}, bf16[384,128]{1,0:T(8,128)(2,1)S(1)}, u32[]{:S(2)}, u32[]{:S(2)}) collective-permute-start(bf16[384,128]{1,0:T(8,128)(2,1)S(1)} %get-tuple-element.57.own_d), channel_id=1, source_target_pairs={{0,8},{8,0},{16,24},{24,16},{1,9},{9,1},{17,25},{25,17},{2,10},{10... | collective-permute-start | bytes 294920 | tf_op jit(solution)/shard_map/ppermute | solution.py:579
  36.1 4.1 %copy-start = (bf16[3,192,1024]{2,1,0:T(8,128)(2,1)S(1)}, bf16[3,192,1024]{2,1,0:T(8,128)(2,1)}, u32[]{:S(2)}) copy-start(bf16[3,192,1024]{2,1,0:T(8,128)(2,1)} %refs_5_.3) | copy-start | bytes 3538948
  36.1 4.1 %copy-start.1 = (bf16[3,192,1024]{2,1,0:T(8,128)(2,1)S(1)}, bf16[3,192,1024]{2,1,0:T(8,128)(2,1)}, u32[]{:S(2)}) copy-start(bf16[3,192,1024]{2,1,0:T(8,128)(2,1)} %refs_6_.3) | copy-start | bytes 3538948

commit v11 on v9

--- a/solution.py
+++ b/solution.py
@@ -492,75 +492,95 @@
     return [value.astype(jnp.bfloat16) for value in (moment_one, moment_two, step)]
 
 
-def pair_of_blocks(own, got):
+def far_kernel(kinds, count, w_ref, after_ref, *refs):
+    n = len(kinds)
+    xs, ys, gates = views(refs[:n], kinds, count)
+    outs = refs[n:]
+    x, y = joined(xs), joined(ys)
+    third = w_ref.shape[1] // len(outs)
+    for m, right in enumerate((x, x, y)):
+        part = contract_last(w_ref[m], right).astype(jnp.bfloat16)
+        for k, out_ref in enumerate(outs):
+            for side in (0, 1):
+                row = (2 * m + side) * third
+                out_ref[row : row + third, :] = part[
+                    k * third : (k + 1) * third, side * count : (side + 1) * count
+                ]
+
+
+def far_partials(weights, after, chunk, pieces, count):
+    mats, hidden, width = weights.shape
+    kinds = kinds_of(chunk)
+    rows = 2 * mats * hidden // pieces
+    return pl.pallas_call(
+        functools.partial(far_kernel, kinds, count),
+        in_specs=[whole(), unread()] + [whole()] * len(kinds),
+        out_specs=[whole()] * pieces,
+        out_shape=[jax.ShapeDtypeStruct((rows, count), jnp.bfloat16)] * pieces,
+        compiler_params=params(),
+        cost_estimate=cost(4 * mats * hidden * count * width, 12 * mats * hidden * count),
+    )(weights, after, *values_of(chunk))
+
+
+def update_kernel(kinds, count, piece, last, own, got, *refs):
+    n = len(kinds)
+    acc_ref, first_ref, second_ref = refs[n : n + 3]
+    rest = refs[n + 3 :]
+    third = own.shape[0] // 6
+    copies = []
+    if piece > 0:
+        done = rest[:3]
+        rest = rest[3 + 3 * last :]
+        outs, rest = rest[:3], rest[3:]
+        sems = rest[-1]
+        before = slice((piece - 1) * third, piece * third)
+        for k in range(3):
+            copies.append(
+                pltpu.make_async_copy(done[k], outs[k].at[:, before, :], sems.at[3, k])
+            )
+            copies[-1].start()
+    held = rest[:3]
+    xs, ys, gates = views(refs[:n], kinds, count)
     total = summed([(own, got)])
-    return beside(total, total.shape[0] // 2, (0, 1))
-
-
-def down_kernel(kinds, count, own_g, got_g, own_u, got_u, *refs):
-    n = len(kinds)
-    acc_ref, first_ref, second_ref, *outs = refs[n:]
-    xs, ys, gates = views(refs[:n], kinds, count)
-    hg, hu = pair_of_blocks(own_g, got_g), pair_of_blocks(own_u, got_u)
-    act = activation(hg, hu, gate_row(gates))[2]
-    grad = acc_ref[2] + plain(act, joined(ys))
-    for out_ref, value in zip(outs, adam(grad, first_ref[2], second_ref[2])):
-        out_ref[...] = value
-
-
-def down_update(pairs, chunk, acc, moments, count):
+    hg, hu, down = [beside(total, third, (2 * m, 2 * m + 1)) for m in range(3)]
+    gate = gate_row(gates)
+    sig, silu, act = activation(hg, hu, gate)
+    lefts = (*hidden_slopes(hg, hu, sig, silu, gate * down), act)
+    x = joined(xs)
+    rows = slice(piece * third, (piece + 1) * third)
+    for m, right in enumerate((x, x, joined(ys))):
+        grad = acc_ref[m, rows, :] + plain(lefts[m], right)
+        for k, value in enumerate(adam(grad, first_ref[m, rows, :], second_ref[m, rows, :])):
+            held[k][m] = value
+            if last:
+                copies.append(
+                    pltpu.make_async_copy(held[k].at[m], outs[k].at[m, rows, :], sems.at[m, k])
+                )
+                copies[-1].start()
+    for copy in copies:
+        copy.wait()
+
+
+def update_piece(piece, last, pair, chunk, acc, moments, done, whole_outs, count):
     kinds = kinds_of(chunk)
     mats, hidden, width = acc.shape
-    operands = [*pairs, *values_of(chunk), acc, *moments]
-    return pl.pallas_call(
-        functools.partial(down_kernel, kinds, count),
-        in_specs=[whole()] * len(operands),
-        out_specs=[whole()] * 3,
-        out_shape=[jax.ShapeDtypeStruct((hidden, width), jnp.bfloat16)] * 3,
-        compiler_params=params(),
-        cost_estimate=cost(4 * hidden * width * count, 14 * hidden * width),
-    )(*operands)
-
-
-def slopes_kernel(kinds, count, own_g, got_g, own_u, got_u, own_d, got_d, *refs):
-    n = len(kinds)
-    acc_ref, first_ref, second_ref = refs[n : n + 3]
-    done, outs = refs[n + 3 : n + 6], refs[n + 6 : n + 9]
-    held, sems = refs[n + 9 : n + 12], refs[n + 12]
-    copies = [
-        pltpu.make_async_copy(done[k], outs[k].at[2], sems.at[2, k]) for k in range(3)
-    ]
-    for copy in copies:
-        copy.start()
-    xs, ys, gates = views(refs[:n], kinds, count)
-    hg, hu = pair_of_blocks(own_g, got_g), pair_of_blocks(own_u, got_u)
-    dact = gate_row(gates) * pair_of_blocks(own_d, got_d)
-    sig, silu, act = activation(hg, hu, 1.0)
-    right = joined(xs)
-    for m, left in enumerate(hidden_slopes(hg, hu, sig, silu, dact)):
-        grad = acc_ref[m] + plain(left, right)
-        for k, value in enumerate(adam(grad, first_ref[m], second_ref[m])):
-            held[k][m] = value
-            copies.append(pltpu.make_async_copy(held[k].at[m], outs[k].at[m], sems.at[m, k]))
-            copies[-1].start()
-    for copy in copies:
-        copy.wait()
-
-
-def slopes_update(pairs, chunk, acc, moments, done, count):
-    kinds = kinds_of(chunk)
-    mats, hidden, width = acc.shape
-    operands = [*pairs, *values_of(chunk), acc, *moments, *done]
-    return pl.pallas_call(
-        functools.partial(slopes_kernel, kinds, count),
-        in_specs=[whole()] * len(operands),
-        out_specs=[in_hbm()] * 3,
-        out_shape=[jax.ShapeDtypeStruct(acc.shape, jnp.bfloat16)] * 3,
-        scratch_shapes=[pltpu.VMEM((2, hidden, width), jnp.bfloat16)] * 3
-        + [pltpu.SemaphoreType.DMA((3, 3))],
-        compiler_params=params(),
-        cost_estimate=cost(8 * hidden * width * count, 28 * hidden * width),
-    )(*operands)
+    third = pair[0].shape[0] // 6
+    operands = [*pair, *values_of(chunk), acc, *moments, *done]
+    in_specs = [whole()] * len(operands) + [unread()] * len(whole_outs)
+    large = [jax.ShapeDtypeStruct(acc.shape, jnp.bfloat16)] * 3
+    small = [jax.ShapeDtypeStruct((mats, third, width), jnp.bfloat16)] * 3
+    scratch = [pltpu.VMEM((mats, third, width), jnp.bfloat16)] * 3
+    return pl.pallas_call(
+        functools.partial(update_kernel, kinds, count, piece, last),
+        in_specs=in_specs,
+        out_specs=([in_hbm()] * 3 if piece else []) + ([] if last else [whole()] * 3),
+        out_shape=(large if piece else []) + ([] if last else small),
+        input_output_aliases={len(operands) + k: k for k in range(3)} if last else {},
+        scratch_shapes=(scratch if last else [])
+        + ([pltpu.SemaphoreType.DMA((mats + 1, 3))] if piece else []),
+        compiler_params=params(),
+        cost_estimate=cost(4 * mats * third * width * count, 14 * mats * third * width),
+    )(*operands, *whole_outs)
 
 
 def from_masked(value, axis, mask):
@@ -605,15 +625,15 @@
     )
     pieces = [*pieces, *[other(value) for value in pieces]]
     final = list(zip(("x", "x", "y", "half y, gates") * 2, pieces))
-    sends = partials(weights, token, final, (2, 2, 2), count, 0)
-    pairs = [value for send in sends for value in (send, partner(send))]
+    sends = far_partials(weights, token, final, 3, count)
+    pairs = [(send, partner(send)) for send in sends]
     near = [("first x", x_pair), ("x, y, y", rest), ("second x", x_pair), ("x, y, y", rest_other)]
     acc = add_grads(near_sum, early_sum, late_pair, near, acc, count)
     moments = (first_moment, second_moment)
-    final_y = [block for block in final if block[0] != "x"]
-    final_x = [block for block in final if block[0] != "y"]
-    done = down_update(pairs[:4], final_y, acc, moments, count)
-    return tuple(slopes_update(pairs, final_x, acc, moments, done, count))
+    done = update_piece(0, False, pairs[0], final, acc, moments, (), (), count)
+    outs = update_piece(1, False, pairs[1], final, acc, moments, done, (), count)
+    outs = update_piece(2, True, pairs[2], final, acc, moments, outs[3:], outs[:3], count)
+    return tuple(outs)
 
 
 def per_device(tokens, cotangent, expert_ids, gate_probs, weights, first_moment, second_moment):

time: 44.1 us -> 43.6 us (0.989)
  waiting for transfers between devices: 16.7 us -> 15.3 us
  Pallas kernels: 8.94 us -> 9.84 us
    pallas_call x2 -> x4, Pallas kernels: 2.82 us -> 4.42 us  [the longest x3 3.76 us: update_piece(): pl.pallas_call(functools.partial(update_kernel, kinds, count, piece, last...]
    ppermute x14, waiting for transfers between devices: 5.48 us -> 4.05 us  [from_masked(): return lax.ppermute(value, axis, pairs)]
    pallas_call x5 -> x4, Pallas kernels: 2.64 us -> 1.97 us  [partials(): pl.pallas_call(functools.partial(partial_kernel, kinds, count, tokened),...]
  transfers between devices with their start and end apart: 19 -> 19, of which waited for: 11 -> 10; matrix products, arithmetic and copies ran while one was open for 0% -> 0% of each run, Pallas kernels for 11% -> 14%
where the time goes in v11:
time: 43.6 us; the launch traced here: 43.4 us
  starting transfers between devices  17.5 us (40%)
  waiting for transfers between devices  15.3 us (35%)
  Pallas kernels  9.84 us (23%)
  between operations  0.76 us (2%)
    ppermute x14, starting transfers between devices, from_masked(): return lax.ppermute(value, axis, pairs)  11.2 us
    ppermute x1, waiting for transfers between devices, dense_plan(): far = lax.ppermute(picked, 'dp', along[1])  4.77 us
    ppermute x2, waiting for transfers between devices, dense_plan(): near_x = [lax.ppermute(x_own, 'dp', pairs) for pairs in along]  4.48 us
    ppermute x2, starting transfers between devices, dense_plan(): near_x = [lax.ppermute(x_own, 'dp', pairs) for pairs in along]  4.08 us
    ppermute x14, waiting for transfers between devices, from_masked(): return lax.ppermute(value, axis, pairs)  4.05 us
    pallas_call x3, Pallas kernels, update_piece(): pl.pallas_call(functools.partial(update_kernel, kinds, count, piece, last...  3.76 us
    ppermute x2, waiting for transfers between devices, dense_plan(): near_y = [lax.ppermute(y_own, 'dp', pairs) for pairs in along]  2 us
    pallas_call x4, Pallas kernels, partials(): pl.pallas_call(functools.partial(partial_kernel, kinds, count, tokened),...  1.97 us
  transfers between devices with their start and end apart: 19, of which 10 were waited for; matrix products, arithmetic and copies ran while one was open for 0% of the time, Pallas kernels for 14%

profile of v11, /device:TPU:0, one launch (start us, length us, event | category | flops | bytes accessed | tf_op | source)
XLA Modules:
  0.0 43.4 jit_solution(9954788986644465767)
XLA Ops:
  0.6 1.7 %shard_map.94 = (bf16[128,1024]{1,0:T(8,128)(2,1)S(1)}, bf16[144,1024]{1,0:T(8,128)(2,1)S(1)}, bf16[272,1024]{1,0:T(8,128)(2,1)S(1)}, bf16[3,192,1024]{2,1,0:T(8,128)(2,1)S(1)}) custom-call(s32[4,128]{1,0:T(4,128)} %bitcast.2, bf16[4,128]{1,0:T(4,128)(2,1)} %bitcast.3, bf16[128,2048]{1,0:T(8,128)(2,1)} %tokens_ref.1, bf16[128,2048]{1,0:T(8,128)(2,1)} %cot_ref.1, ...), custom_call_target="tpu_custom_call" | custom-call | flops 1000 | bytes 1048576 | tf_op jit(solution)/shard_map/pallas_call | solution.py:209
  2.8 2.6 %collective-permute-start.1 = (bf16[128,1024]{1,0:T(8,128)(2,1)S(1)}, bf16[128,1024]{1,0:T(8,128)(2,1)S(1)}, u32[]{:S(2)}, u32[]{:S(2)}) collective-permute-start(bf16[128,1024]{1,0:T(8,128)(2,1)S(1)} %get-tuple-element.43), channel_id=1, source_target_pairs={{0,2},{1,5},{2,0},{3,7},{4,6},{5,1},{6,4},{7,3},{8,10},{9,13},{10,... | collective-permute-start | bytes 786440 | tf_op jit(solution)/shard_map/ppermute | solution.py:607
  5.4 1.5 %collective-permute-start.2 = (bf16[128,1024]{1,0:T(8,128)(2,1)S(1)}, bf16[128,1024]{1,0:T(8,128)(2,1)S(1)}, u32[]{:S(2)}, u32[]{:S(2)}) collective-permute-start(bf16[128,1024]{1,0:T(8,128)(2,1)S(1)} %get-tuple-element.43), channel_id=1, source_target_pairs={{0,4},{1,3},{2,6},{3,1},{4,0},{5,7},{6,2},{7,5},{8,12},{9,11},{10,... | collective-permute-start | bytes 786440 | tf_op jit(solution)/shard_map/ppermute | solution.py:607
  7.5 0.5 %shard_map.95 = (bf16[1152,128]{1,0:T(8,128)(2,1)S(1)}, f32[8,128]{1,0:T(8,128)S(1)}) custom-call(bf16[3,192,1024]{2,1,0:T(8,128)(2,1)S(1)} %get-tuple-element.40.w_ref, bf16[272,1024]{1,0:T(8,128)(2,1)S(1)} %get-tuple-element.41.after_ref.refs_0_.refs_5_, bf16[272,1024]{1,0:T(8,128)(2,1)S(1)} %get-tuple-element.41.after_ref.refs_0_.refs_5_, ...), custom_call_target="tpu_custom_call" | custom-call | flops 301989888 | bytes 884736 | tf_op jit(solution)/shard_map/pallas_call | solution.py:309
  8.1 2.1 %collective-permute-start.3 = (bf16[1152,128]{1,0:T(8,128)(2,1)S(1)}, bf16[1152,128]{1,0:T(8,128)(2,1)S(1)}, u32[]{:S(2)}, u32[]{:S(2)}) collective-permute-start(bf16[1152,128]{1,0:T(8,128)(2,1)S(1)} %get-tuple-element.45.own), channel_id=1, source_target_pairs={{0,8},{8,0},{16,24},{24,16},{1,9},{9,1},{17,25},{25,17},{2,10},{10... | collective-permute-start | bytes 884744 | tf_op jit(solution)/shard_map/ppermute | solution.py:588
  10.2 1.3 %collective-permute-done.1.refs_0_ = bf16[128,1024]{1,0:T(8,128)(2,1)S(1)} collective-permute-done((bf16[128,1024]{1,0:T(8,128)(2,1)S(1)}, bf16[128,1024]{1,0:T(8,128)(2,1)S(1)}, u32[]{:S(2)}, u32[]{:S(2)}) %collective-permute-start.1) | collective-permute-done | bytes 262176 | tf_op jit(solution)/shard_map/ppermute | solution.py:607
  11.5 3.2 %collective-permute-done.2.refs_1_ = bf16[128,1024]{1,0:T(8,128)(2,1)S(1)} collective-permute-done((bf16[128,1024]{1,0:T(8,128)(2,1)S(1)}, bf16[128,1024]{1,0:T(8,128)(2,1)S(1)}, u32[]{:S(2)}, u32[]{:S(2)}) %collective-permute-start.2) | collective-permute-done | bytes 262176 | tf_op jit(solution)/shard_map/ppermute | solution.py:607
  15.0 1.6 %collective-permute-start.4 = (bf16[384,128]{1,0:T(8,128)(2,1)S(1)}, bf16[384,128]{1,0:T(8,128)(2,1)S(1)}, u32[]{:S(2)}, u32[]{:S(2)}) collective-permute-start(bf16[384,128]{1,0:T(8,128)(2,1)S(1)} %get-tuple-element.46.near_own), channel_id=1, source_target_pairs={{0,8},{8,0},{16,24},{24,16},{1,9},{9,1},{17,25},{25,17},{2,10},{10... | collective-permute-start | bytes 294920 | tf_op jit(solution)/shard_map/ppermute | solution.py:588
  16.7 2.0 %collective-permute-done.7.refs_4_ = bf16[144,1024]{1,0:T(8,128)(2,1)S(1)} collective-permute-done((bf16[144,1024]{1,0:T(8,128)(2,1)S(1)}, bf16[144,1024]{1,0:T(8,128)(2,1)S(1)}, u32[]{:S(2)}, u32[]{:S(2)}) %collective-permute-start.7) | collective-permute-done | bytes 294944 | tf_op jit(solution)/shard_map/ppermute | solution.py:608
  18.7 1.0 %collective-permute-done.4.near_got = bf16[384,128]{1,0:T(8,128)(2,1)S(1)} collective-permute-done((bf16[384,128]{1,0:T(8,128)(2,1)S(1)}, bf16[384,128]{1,0:T(8,128)(2,1)S(1)}, u32[]{:S(2)}, u32[]{:S(2)}) %collective-permute-start.4) | collective-permute-done | bytes 98336 | tf_op jit(solution)/shard_map/ppermute | solution.py:588
  20.0 1.6 %collective-permute-start.9 = (bf16[272,1024]{1,0:T(8,128)(2,1)S(1)}, bf16[272,1024]{1,0:T(8,128)(2,1)S(1)}, u32[]{:S(2)}, u32[]{:S(2)}) collective-permute-start(bf16[272,1024]{1,0:T(8,128)(2,1)S(1)} %get-tuple-element.49.after_ref), channel_id=1, source_target_pairs={{0,4},{1,3},{2,6},{3,1},{4,0},{5,7},{6,2},{7,5},{8,12},{9,11},{10,... | collective-permute-start | bytes 1671176 | tf_op jit(solution)/shard_map/ppermute | solution.py:614
  22.0 1.6 %collective-permute-start.10 = (bf16[768,128]{1,0:T(8,128)(2,1)S(1)}, bf16[768,128]{1,0:T(8,128)(2,1)S(1)}, u32[]{:S(2)}, u32[]{:S(2)}) collective-permute-start(bf16[768,128]{1,0:T(8,128)(2,1)S(1)} %get-tuple-element.56.own), channel_id=1, source_target_pairs={{0,8},{8,0},{16,24},{24,16},{1,9},{9,1},{17,25},{25,17},{2,10},{10... | collective-permute-start | bytes 589832 | tf_op jit(solution)/shard_map/ppermute | solution.py:588
  23.6 0.7 %shard_map.99 = (bf16[1152,128]{1,0:T(8,128)(2,1)S(1)}, f32[8,128]{1,0:T(8,128)S(1)}) custom-call(bf16[3,192,1024]{2,1,0:T(8,128)(2,1)S(1)} %get-tuple-element.40.w_ref, f32[8,128]{1,0:T(8,128)S(1)} %get-tuple-element.52.after_ref, bf16[416,1024]{1,0:T(8,128)(2,1)S(1)} %get-tuple-element.50.refs_0_.refs_1_, ...), custom_call_target="tpu_custom_call" | custom-call | flops 301989888 | bytes 884736 | tf_op jit(solution)/shard_map/pallas_call | solution.py:309
  24.8 4.8 %collective-permute-done.9.in_ref = bf16[272,1024]{1,0:T(8,128)(2,1)S(1)} collective-permute-done((bf16[272,1024]{1,0:T(8,128)(2,1)S(1)}, bf16[272,1024]{1,0:T(8,128)(2,1)S(1)}, u32[]{:S(2)}, u32[]{:S(2)}) %collective-permute-start.9) | collective-permute-done | bytes 557088 | tf_op jit(solution)/shard_map/ppermute | solution.py:614
  30.7 0.6 %shard_map.101 = (f32[3,192,1024]{2,1,0:T(8,128)S(1)}, f32[768,128]{1,0:T(8,128)S(1)}, f32[8,128]{1,0:T(8,128)S(1)}) custom-call(f32[8,256]{1,0:T(8,128)S(1)} %get-tuple-element.48.gate_ref, bf16[64,1024]{1,0:T(8,128)(2,1)S(1)} %get-tuple-element.54.after_ref.refs_0_, f32[1152,128]{1,0:T(8,128)S(1)} %get-tuple-element.55.sum_ref, ...), custom_call_target="tpu_custom_call" | custom-call | flops 301989888 | bytes 2359296 | tf_op jit(solution)/shard_map/pallas_call | solution.py:444
  31.7 0.7 %shard_map.102 = (bf16[384,128]{1,0:T(8,128)(2,1)S(1)}, bf16[384,128]{1,0:T(8,128)(2,1)S(1)}, bf16[384,128]{1,0:T(8,128)(2,1)S(1)}) custom-call(bf16[3,192,1024]{2,1,0:T(8,128)(2,1)S(1)} %get-tuple-element.40.w_ref, f32[8,128]{1,0:T(8,128)S(1)} %get-tuple-element.57.after_ref, bf16[64,1024]{1,0:T(8,128)(2,1)S(1)} %get-tuple-element.54.after_ref.refs_0_, ...), custom_call_target="tpu_custom_call" | custom-call | flops 301989888 | bytes 884736 | tf_op jit(solution)/shard_map/pallas_call | solution.py:515
  32.4 1.6 %collective-permute-start.18 = (bf16[384,128]{1,0:T(8,128)(2,1)S(1)}, bf16[384,128]{1,0:T(8,128)(2,1)S(1)}, u32[]{:S(2)}, u32[]{:S(2)}) collective-permute-start(bf16[384,128]{1,0:T(8,128)(2,1)S(1)} %get-tuple-element.67.own), channel_id=1, source_target_pairs={{0,8},{8,0},{16,24},{24,16},{1,9},{9,1},{17,25},{25,17},{2,10},{10... | collective-permute-start | bytes 294920 | tf_op jit(solution)/shard_map/ppermute | solution.py:588
  34.5 1.6 %collective-permute-start.15 = (bf16[384,128]{1,0:T(8,128)(2,1)S(1)}, bf16[384,128]{1,0:T(8,128)(2,1)S(1)}, u32[]{:S(2)}, u32[]{:S(2)}) collective-permute-start(bf16[384,128]{1,0:T(8,128)(2,1)S(1)} %get-tuple-element.61.own), channel_id=1, source_target_pairs={{0,8},{8,0},{16,24},{24,16},{1,9},{9,1},{17,25},{25,17},{2,10},{10... | collective-permute-start | bytes 294920 | tf_op jit(solution)/shard_map/ppermute | solution.py:588
  36.1 1.0 %shard_map.103.refs_8_ = f32[3,192,1024]{2,1,0:T(8,128)S(1)} custom-call(f32[384,128]{1,0:T(8,128)S(1)} %get-tuple-element.62.sum_ref, f32[768,128]{1,0:T(8,128)S(1)} %get-tuple-element.63.more_ref, bf16[1152,128]{1,0:T(8,128)(2,1)S(1)} %get-tuple-element.64.own, bf16[1152,128]{1,0:T(8,128)(2,1)S(1)} %collective-permute-done.16.got, ...), custom_call_target="tpu_custom_call", output_to_operand_aliasing={{}: (8, {})} | custom-call | flops 603979776 | bytes 4718592 | tf_op jit(solution)/shard_map/pallas_call | solution.py:472
  37.1 1.0 %collective-permute-done.18.got = bf16[384,128]{1,0:T(8,128)(2,1)S(1)} collective-permute-done((bf16[384,128]{1,0:T(8,128)(2,1)S(1)}, bf16[384,128]{1,0:T(8,128)(2,1)S(1)}, u32[]{:S(2)}, u32[]{:S(2)}) %collective-permute-start.18) | collective-permute-done | bytes 98336 | tf_op jit(solution)/shard_map/ppermute | solution.py:588
  38.1 0.7 %shard_map.104 = (bf16[3,64,1024]{2,1,0:T(8,128)(2,1)S(1)}, bf16[3,64,1024]{2,1,0:T(8,128)(2,1)S(1)}, bf16[3,64,1024]{2,1,0:T(8,128)(2,1)S(1)}) custom-call(bf16[384,128]{1,0:T(8,128)(2,1)S(1)} %get-tuple-element.67.own, bf16[384,128]{1,0:T(8,128)(2,1)S(1)} %collective-permute-done.18.got, bf16[64,1024]{1,0:T(8,128)(2,1)S(1)} %get-tuple-element.54.after_ref.refs_0_, ...), custom_call_target="tpu_custom_call" | custom-call | flops 100663296 | bytes 2752512 | tf_op jit(solution)/shard_map/pallas_call | solution.py:573
  38.8 1.4 %collective-permute-done.17.got = bf16[384,128]{1,0:T(8,128)(2,1)S(1)} collective-permute-done((bf16[384,128]{1,0:T(8,128)(2,1)S(1)}, bf16[384,128]{1,0:T(8,128)(2,1)S(1)}, u32[]{:S(2)}, u32[]{:S(2)}) %collective-permute-start.17) | collective-permute-done | bytes 98336 | tf_op jit(solution)/shard_map/ppermute | solution.py:588
  40.2 1.4 %shard_map.105 = (bf16[3,192,1024]{2,1,0:T(8,128)(2,1)}, bf16[3,192,1024]{2,1,0:T(8,128)(2,1)}, bf16[3,192,1024]{2,1,0:T(8,128)(2,1)}, bf16[3,64,1024]{2,1,0:T(8...) custom-call(bf16[384,128]{1,0:T(8,128)(2,1)S(1)} %get-tuple-element.66.own, ...), custom_call_target="tpu_custom_call" | custom-call | flops 100663296 | bytes 2752512 | tf_op jit(solution)/shard_map/pallas_call | solution.py:573
  41.7 1.7 %shard_map.106 = (bf16[3,192,1024]{2,1,0:T(8,128)(2,1)}, bf16[3,192,1024]{2,1,0:T(8,128)(2,1)}, bf16[3,192,1024]{2,1,0:T(8,128)(2,1)}) custom-call(bf16[384,128]{1,0:T(8,128)(2,1)S(1)} %get-tuple-element.61.own, bf16[384,128]{1,0:T(8,128)(2,1)S(1)} %collective-permute-done.15.got, ...), custom_call_target="tpu_custom_call", output_to_operand_aliasing={{0}: (16, {}), {1}: (17, {}), {2}: (18, {})} | custom-call | flops 100663296 | bytes 2752512 | tf_op jit(solution)/shard_map/pallas_call | solution.py:573
  (31 shorter events, 4.8 us)
Async XLA Ops:
  2.3 5.2 %collective-permute-start = (bf16[272,1024]{1,0:T(8,128)(2,1)S(1)}, bf16[272,1024]{1,0:T(8,128)(2,1)S(1)}, u32[]{:S(2)}, u32[]{:S(2)}) collective-permute-start(bf16[272,1024]{1,0:T(8,128)(2,1)S(1)} %get-tuple-element.41.after_ref.refs_0_.refs_5_), channel_id=1, source_target_pairs={{0,1},{1,0},{2,3},{3,2},{4,5},{5,4},{6,7},{7,6},{8,9},{9,8},{10,11... | collective-permute-start | bytes 1671176 | tf_op jit(solution)/shard_map/ppermute | solution.py:588
  2.8 8.6 %collective-permute-start.1 = (bf16[128,1024]{1,0:T(8,128)(2,1)S(1)}, bf16[128,1024]{1,0:T(8,128)(2,1)S(1)}, u32[]{:S(2)}, u32[]{:S(2)}) collective-permute-start(bf16[128,1024]{1,0:T(8,128)(2,1)S(1)} %get-tuple-element.43), channel_id=1, source_target_pairs={{0,2},{1,5},{2,0},{3,7},{4,6},{5,1},{6,4},{7,3},{8,10},{9,13},{10,... | collective-permute-start | bytes 786440 | tf_op jit(solution)/shard_map/ppermute | solution.py:607
  5.4 9.2 %collective-permute-start.2 = (bf16[128,1024]{1,0:T(8,128)(2,1)S(1)}, bf16[128,1024]{1,0:T(8,128)(2,1)S(1)}, u32[]{:S(2)}, u32[]{:S(2)}) collective-permute-start(bf16[128,1024]{1,0:T(8,128)(2,1)S(1)} %get-tuple-element.43), channel_id=1, source_target_pairs={{0,4},{1,3},{2,6},{3,1},{4,0},{5,7},{6,2},{7,5},{8,12},{9,11},{10,... | collective-permute-start | bytes 786440 | tf_op jit(solution)/shard_map/ppermute | solution.py:607
  6.9 11.7 %collective-permute-start.7 = (bf16[144,1024]{1,0:T(8,128)(2,1)S(1)}, bf16[144,1024]{1,0:T(8,128)(2,1)S(1)}, u32[]{:S(2)}, u32[]{:S(2)}) collective-permute-start(bf16[144,1024]{1,0:T(8,128)(2,1)S(1)} %get-tuple-element.47), channel_id=1, source_target_pairs={{0,4},{1,3},{2,6},{3,1},{4,0},{5,7},{6,2},{7,5},{8,12},{9,11},{10,... | collective-permute-start | bytes 884744 | tf_op jit(solution)/shard_map/ppermute | solution.py:608
  7.4 11.2 %collective-permute-start.6 = (bf16[144,1024]{1,0:T(8,128)(2,1)S(1)}, bf16[144,1024]{1,0:T(8,128)(2,1)S(1)}, u32[]{:S(2)}, u32[]{:S(2)}) collective-permute-start(bf16[144,1024]{1,0:T(8,128)(2,1)S(1)} %get-tuple-element.47), channel_id=1, source_target_pairs={{0,2},{1,5},{2,0},{3,7},{4,6},{5,1},{6,4},{7,3},{8,10},{9,13},{10,... | collective-permute-start | bytes 884744 | tf_op jit(solution)/shard_map/ppermute | solution.py:608
  8.1 11.6 %collective-permute-start.3 = (bf16[1152,128]{1,0:T(8,128)(2,1)S(1)}, bf16[1152,128]{1,0:T(8,128)(2,1)S(1)}, u32[]{:S(2)}, u32[]{:S(2)}) collective-permute-start(bf16[1152,128]{1,0:T(8,128)(2,1)S(1)} %get-tuple-element.45.own), channel_id=1, source_target_pairs={{0,8},{8,0},{16,24},{24,16},{1,9},{9,1},{17,25},{25,17},{2,10},{10... | collective-permute-start | bytes 884744 | tf_op jit(solution)/shard_map/ppermute | solution.py:588
  11.5 7.2 %collective-permute-start.5 = (bf16[128,1024]{1,0:T(8,128)(2,1)S(1)}, bf16[128,1024]{1,0:T(8,128)(2,1)S(1)}, u32[]{:S(2)}, u32[]{:S(2)}) collective-permute-start(bf16[128,1024]{1,0:T(8,128)(2,1)S(1)} %collective-permute-done.1.refs_0_), channel_id=1, source_target_pairs={{0,1},{1,0},{2,3},{3,2},{4,5},{5,4},{6,7},{7,6},{8,9},{9,8},{10,11... | collective-permute-start | bytes 786440 | tf_op jit(solution)/shard_map/ppermute | solution.py:588
  15.0 4.7 %collective-permute-start.4 = (bf16[384,128]{1,0:T(8,128)(2,1)S(1)}, bf16[384,128]{1,0:T(8,128)(2,1)S(1)}, u32[]{:S(2)}, u32[]{:S(2)}) collective-permute-start(bf16[384,128]{1,0:T(8,128)(2,1)S(1)} %get-tuple-element.46.near_own), channel_id=1, source_target_pairs={{0,8},{8,0},{16,24},{24,16},{1,9},{9,1},{17,25},{25,17},{2,10},{10... | collective-permute-start | bytes 294920 | tf_op jit(solution)/shard_map/ppermute | solution.py:588
  19.9 3.7 %collective-permute-start.8 = (bf16[416,1024]{1,0:T(8,128)(2,1)S(1)}, bf16[416,1024]{1,0:T(8,128)(2,1)S(1)}, u32[]{:S(2)}, u32[]{:S(2)}) collective-permute-start(bf16[416,1024]{1,0:T(8,128)(2,1)S(1)} %get-tuple-element.50.refs_0_.refs_1_), channel_id=1, source_target_pairs={{0,1},{1,0},{2,3},{3,2},{4,5},{5,4},{6,7},{7,6},{8,9},{9,8},{10,11... | collective-permute-start | bytes 2555912 | tf_op jit(solution)/shard_map/ppermute | solution.py:588
  20.0 9.6 %collective-permute-start.9 = (bf16[272,1024]{1,0:T(8,128)(2,1)S(1)}, bf16[272,1024]{1,0:T(8,128)(2,1)S(1)}, u32[]{:S(2)}, u32[]{:S(2)}) collective-permute-start(bf16[272,1024]{1,0:T(8,128)(2,1)S(1)} %get-tuple-element.49.after_ref), channel_id=1, source_target_pairs={{0,4},{1,3},{2,6},{3,1},{4,0},{5,7},{6,2},{7,5},{8,12},{9,11},{10,... | collective-permute-start | bytes 1671176 | tf_op jit(solution)/shard_map/ppermute | solution.py:614
  22.0 8.3 %collective-permute-start.10 = (bf16[768,128]{1,0:T(8,128)(2,1)S(1)}, bf16[768,128]{1,0:T(8,128)(2,1)S(1)}, u32[]{:S(2)}, u32[]{:S(2)}) collective-permute-start(bf16[768,128]{1,0:T(8,128)(2,1)S(1)} %get-tuple-element.56.own), channel_id=1, source_target_pairs={{0,8},{8,0},{16,24},{24,16},{1,9},{9,1},{17,25},{25,17},{2,10},{10... | collective-permute-start | bytes 589832 | tf_op jit(solution)/shard_map/ppermute | solution.py:588
  24.3 11.8 %collective-permute-start.16 = (bf16[1152,128]{1,0:T(8,128)(2,1)S(1)}, bf16[1152,128]{1,0:T(8,128)(2,1)S(1)}, u32[]{:S(2)}, u32[]{:S(2)}) collective-permute-start(bf16[1152,128]{1,0:T(8,128)(2,1)S(1)} %get-tuple-element.64.own), channel_id=1, source_target_pairs={{0,8},{8,0},{16,24},{24,16},{1,9},{9,1},{17,25},{25,17},{2,10},{10... | collective-permute-start | bytes 884744 | tf_op jit(solution)/shard_map/ppermute | solution.py:588
  29.6 2.1 %collective-permute-start.14 = (bf16[80,1024]{1,0:T(8,128)(2,1)S(1)}, bf16[80,1024]{1,0:T(8,128)(2,1)S(1)}, u32[]{:S(2)}, u32[]{:S(2)}) collective-permute-start(bf16[80,1024]{1,0:T(8,128)(2,1)S(1)} %get-tuple-element.60.refs_3_), channel_id=1, source_target_pairs={{0,1},{1,0},{2,3},{3,2},{4,5},{5,4},{6,7},{7,6},{8,9},{9,8},{10,11... | collective-permute-start | bytes 491528 | tf_op jit(solution)/shard_map/ppermute | solution.py:588
  29.7 1.6 %collective-permute-start.12 = (bf16[64,1024]{1,0:T(8,128)(2,1)S(1)}, bf16[64,1024]{1,0:T(8,128)(2,1)S(1)}, u32[]{:S(2)}, u32[]{:S(2)}) collective-permute-start(bf16[64,1024]{1,0:T(8,128)(2,1)S(1)} %get-tuple-element.58.refs_1_), channel_id=1, source_target_pairs={{0,1},{1,0},{2,3},{3,2},{4,5},{5,4},{6,7},{7,6},{8,9},{9,8},{10,11... | collective-permute-start | bytes 393224 | tf_op jit(solution)/shard_map/ppermute | solution.py:588
  30.2 1.3 %collective-permute-start.13 = (bf16[64,1024]{1,0:T(8,128)(2,1)S(1)}, bf16[64,1024]{1,0:T(8,128)(2,1)S(1)}, u32[]{:S(2)}, u32[]{:S(2)}) collective-permute-start(bf16[64,1024]{1,0:T(8,128)(2,1)S(1)} %get-tuple-element.59.refs_2_), channel_id=1, source_target_pairs={{0,1},{1,0},{2,3},{3,2},{4,5},{5,4},{6,7},{7,6},{8,9},{9,8},{10,11... | collective-permute-start | bytes 393224 | tf_op jit(solution)/shard_map/ppermute | solution.py:588
  30.3 1.5 %collective-permute-start.11 = (bf16[64,1024]{1,0:T(8,128)(2,1)S(1)}, bf16[64,1024]{1,0:T(8,128)(2,1)S(1)}, u32[]{:S(2)}, u32[]{:S(2)}) collective-permute-start(bf16[64,1024]{1,0:T(8,128)(2,1)S(1)} %get-tuple-element.54.after_ref.refs_0_), channel_id=1, source_target_pairs={{0,1},{1,0},{2,3},{3,2},{4,5},{5,4},{6,7},{7,6},{8,9},{9,8},{10,11... | collective-permute-start | bytes 393224 | tf_op jit(solution)/shard_map/ppermute | solution.py:588
  32.4 5.7 %collective-permute-start.18 = (bf16[384,128]{1,0:T(8,128)(2,1)S(1)}, bf16[384,128]{1,0:T(8,128)(2,1)S(1)}, u32[]{:S(2)}, u32[]{:S(2)}) collective-permute-start(bf16[384,128]{1,0:T(8,128)(2,1)S(1)} %get-tuple-element.67.own), channel_id=1, source_target_pairs={{0,8},{8,0},{16,24},{24,16},{1,9},{9,1},{17,25},{25,17},{2,10},{10... | collective-permute-start | bytes 294920 | tf_op jit(solution)/shard_map/ppermute | solution.py:588
  34.1 6.1 %collective-permute-start.17 = (bf16[384,128]{1,0:T(8,128)(2,1)S(1)}, bf16[384,128]{1,0:T(8,128)(2,1)S(1)}, u32[]{:S(2)}, u32[]{:S(2)}) collective-permute-start(bf16[384,128]{1,0:T(8,128)(2,1)S(1)} %get-tuple-element.66.own), channel_id=1, source_target_pairs={{0,8},{8,0},{16,24},{24,16},{1,9},{9,1},{17,25},{25,17},{2,10},{10... | collective-permute-start | bytes 294920 | tf_op jit(solution)/shard_map/ppermute | solution.py:588
  34.5 7.2 %collective-permute-start.15 = (bf16[384,128]{1,0:T(8,128)(2,1)S(1)}, bf16[384,128]{1,0:T(8,128)(2,1)S(1)}, u32[]{:S(2)}, u32[]{:S(2)}) collective-permute-start(bf16[384,128]{1,0:T(8,128)(2,1)S(1)} %get-tuple-element.61.own), channel_id=1, source_target_pairs={{0,8},{8,0},{16,24},{24,16},{1,9},{9,1},{17,25},{25,17},{2,10},{10... | collective-permute-start | bytes 294920 | tf_op jit(solution)/shard_map/ppermute | solution.py:588
  36.1 2.0 %copy-start = (bf16[3,192,1024]{2,1,0:T(8,128)(2,1)S(1)}, bf16[3,192,1024]{2,1,0:T(8,128)(2,1)}, u32[]{:S(2)}) copy-start(bf16[3,192,1024]{2,1,0:T(8,128)(2,1)} %refs_9_.5) | copy-start | bytes 3538948
  36.1 2.0 %copy-start.1 = (bf16[3,192,1024]{2,1,0:T(8,128)(2,1)S(1)}, bf16[3,192,1024]{2,1,0:T(8,128)(2,1)}, u32[]{:S(2)}) copy-start(bf16[3,192,1024]{2,1,0:T(8,128)(2,1)} %refs_10_.5) | copy-start | bytes 3538948

commit v12 on v11

--- a/solution.py
+++ b/solution.py
@@ -274,6 +274,9 @@
 
 def store_partials(parts, count, out_ref):
     row = 0
+    used = sum(part.size for part in parts) // count
+    if used < out_ref.shape[0]:
+        out_ref[used:, :] = jnp.zeros((out_ref.shape[0] - used, count), jnp.bfloat16)
     for part in parts:
         for first in range(0, part.shape[1], count):
             piece = part[:, first : first + count]
@@ -302,7 +305,7 @@
         refs[-1][...] = jnp.zeros_like(refs[-1])
 
 
-def partials(weights, after, chunk, rows, count, tokened=1):
+def partials(weights, after, chunk, rows, count, tokened=1, spare=0):
     hidden, width = weights.shape[1:]
     kinds = kinds_of(chunk)
     total = sum(rows) * hidden * count
@@ -310,7 +313,7 @@
         functools.partial(partial_kernel, kinds, count, tokened),
         in_specs=[whole(), unread()] + [whole()] * len(kinds),
         out_specs=[whole()] * (len(rows) + tokened),
-        out_shape=[jax.ShapeDtypeStruct((k * hidden, count), jnp.bfloat16) for k in rows]
+        out_shape=[jax.ShapeDtypeStruct((k * hidden + spare, count), jnp.bfloat16) for k in rows]
         + [jax.ShapeDtypeStruct((8, 128), jnp.float32)] * tokened,
         compiler_params=params(),
         cost_estimate=cost(2 * total * width, 6 * total),
@@ -382,7 +385,8 @@
     rest_ref[count + rows :, :] = y1_ref[...]
     out_ref[0:count, :] = x0_ref[...]
     out_ref[count:, :] = y0_ref[...]
-    first_ref[...] = own[...].astype(jnp.float32) + got[...].astype(jnp.float32)
+    used = first_ref.shape[0]
+    first_ref[...] = own[0:used, :].astype(jnp.float32) + got[0:used, :].astype(jnp.float32)
     sum_ref[...] = near_own[...].astype(jnp.float32) + near_got[...].astype(jnp.float32)
 
 
@@ -398,7 +402,7 @@
             jax.ShapeDtypeStruct((2, count, width), jnp.bfloat16),
             jax.ShapeDtypeStruct((count + 2 * rows, width), jnp.bfloat16),
             jax.ShapeDtypeStruct((count + rows, width), jnp.bfloat16),
-            jax.ShapeDtypeStruct(pair[0].shape, jnp.float32),
+            jax.ShapeDtypeStruct((3 * near_pair[0].shape[0], count), jnp.float32),
             jax.ShapeDtypeStruct(near_pair[0].shape, jnp.float32),
             jax.ShapeDtypeStruct((8, 2 * count), jnp.float32),
         ],
@@ -601,7 +605,7 @@
         expert_ids, gate_probs, tokens, cotangent, weights, slots
     )
     first = [("xy", own), ("xy", other(own))]
-    send, token = partials(weights, own, first, (6,), count)
+    send, token = partials(weights, own, first, (6,), count, 1, 16)
     first_pair = (send, partner(send))
     along = [[(p, p ^ (2 if p % 2 == k else 4)) for p in range(n_data)] for k in (0, 1)]
     near_x = [lax.ppermute(x_own, "dp", pairs) for pairs in along]

time: 43.6 us -> 43.3 us (level)
  waiting for transfers between devices: 15.3 us -> 11.8 us
  starting transfers between devices: 17.5 us -> 20.6 us
    ppermute x2, waiting for transfers between devices: 4.48 us -> 1.96 us  [dense_plan(): near_x = [lax.ppermute(x_own, 'dp', pairs) for pairs in along]]
    ppermute x14, starting transfers between devices: 11.2 us -> 13.1 us  [from_masked(): return lax.ppermute(value, axis, pairs)]
    ppermute x2, starting transfers between devices: 0.58 us -> 1.85 us  [dense_plan(): near_y = [lax.ppermute(y_own, 'dp', pairs) for pairs in along]]
    ppermute x14, waiting for transfers between devices: 4.05 us -> 2.98 us  [from_masked(): return lax.ppermute(value, axis, pairs)]
  transfers between devices with their start and end apart: 19 -> 19, of which waited for: 10 -> 11; matrix products, arithmetic and copies ran while one was open for 0% -> 0% of each run, Pallas kernels for 14% -> 15%
where the time goes in v12:
time: 43.3 us; the launch traced here: 43.1 us
  starting transfers between devices  20.6 us (48%)
  waiting for transfers between devices  11.8 us (27%)
  Pallas kernels  9.87 us (23%)
  between operations  0.75 us (2%)
    ppermute x14, starting transfers between devices, from_masked(): return lax.ppermute(value, axis, pairs)  13.1 us
    ppermute x1, waiting for transfers between devices, dense_plan(): far = lax.ppermute(picked, 'dp', along[1])  4.48 us
    ppermute x2, starting transfers between devices, dense_plan(): near_x = [lax.ppermute(x_own, 'dp', pairs) for pairs in along]  4.08 us
    pallas_call x3, Pallas kernels, update_piece(): pl.pallas_call(functools.partial(update_kernel, kinds, count, piece, last...  3.76 us
    ppermute x14, waiting for transfers between devices, from_masked(): return lax.ppermute(value, axis, pairs)  2.98 us
    ppermute x2, waiting for transfers between devices, dense_plan(): near_y = [lax.ppermute(y_own, 'dp', pairs) for pairs in along]  2.35 us
    pallas_call x4, Pallas kernels, partials(): pl.pallas_call(functools.partial(partial_kernel, kinds, count, tokened),...  1.96 us
    ppermute x2, waiting for transfers between devices, dense_plan(): near_x = [lax.ppermute(x_own, 'dp', pairs) for pairs in along]  1.96 us
  transfers between devices with their start and end apart: 19, of which 11 were waited for; matrix products, arithmetic and copies ran while one was open for 0% of the time, Pallas kernels for 15%

profile of v12, /device:TPU:0, one launch (start us, length us, event | category | flops | bytes accessed | tf_op | source)
XLA Modules:
  0.0 43.1 jit_solution(2949778711235349476)
XLA Ops:
  0.6 1.7 %shard_map.94 = (bf16[128,1024]{1,0:T(8,128)(2,1)S(1)}, bf16[144,1024]{1,0:T(8,128)(2,1)S(1)}, bf16[272,1024]{1,0:T(8,128)(2,1)S(1)}, bf16[3,192,1024]{2,1,0:T(8,128)(2,1)S(1)}) custom-call(s32[4,128]{1,0:T(4,128)} %bitcast.2, bf16[4,128]{1,0:T(4,128)(2,1)} %bitcast.3, bf16[128,2048]{1,0:T(8,128)(2,1)} %tokens_ref.1, bf16[128,2048]{1,0:T(8,128)(2,1)} %cot_ref.1, ...), custom_call_target="tpu_custom_call" | custom-call | flops 1000 | bytes 1048576 | tf_op jit(solution)/shard_map/pallas_call | solution.py:209
  2.3 0.5 %collective-permute-start = (bf16[272,1024]{1,0:T(8,128)(2,1)S(1)}, bf16[272,1024]{1,0:T(8,128)(2,1)S(1)}, u32[]{:S(2)}, u32[]{:S(2)}) collective-permute-start(bf16[272,1024]{1,0:T(8,128)(2,1)S(1)} %get-tuple-element.41.after_ref.refs_0_.refs_5_), channel_id=1, source_target_pairs={{0,1},{1,0},{2,3},{3,2},{4,5},{5,4},{6,7},{7,6},{8,9},{9,8},{10,11... | collective-permute-start | bytes 1671176 | tf_op jit(solution)/shard_map/ppermute | solution.py:592
  2.8 2.6 %collective-permute-start.1 = (bf16[128,1024]{1,0:T(8,128)(2,1)S(1)}, bf16[128,1024]{1,0:T(8,128)(2,1)S(1)}, u32[]{:S(2)}, u32[]{:S(2)}) collective-permute-start(bf16[128,1024]{1,0:T(8,128)(2,1)S(1)} %get-tuple-element.43), channel_id=1, source_target_pairs={{0,2},{1,5},{2,0},{3,7},{4,6},{5,1},{6,4},{7,3},{8,10},{9,13},{10,... | collective-permute-start | bytes 786440 | tf_op jit(solution)/shard_map/ppermute | solution.py:611
  5.4 1.5 %collective-permute-start.2 = (bf16[128,1024]{1,0:T(8,128)(2,1)S(1)}, bf16[128,1024]{1,0:T(8,128)(2,1)S(1)}, u32[]{:S(2)}, u32[]{:S(2)}) collective-permute-start(bf16[128,1024]{1,0:T(8,128)(2,1)S(1)} %get-tuple-element.43), channel_id=1, source_target_pairs={{0,4},{1,3},{2,6},{3,1},{4,0},{5,7},{6,2},{7,5},{8,12},{9,11},{10,... | collective-permute-start | bytes 786440 | tf_op jit(solution)/shard_map/ppermute | solution.py:611
  6.9 0.5 %shard_map.95 = (bf16[1168,128]{1,0:T(8,128)(2,1)S(1)}, f32[8,128]{1,0:T(8,128)S(1)}) custom-call(bf16[3,192,1024]{2,1,0:T(8,128)(2,1)S(1)} %get-tuple-element.40.w_ref, bf16[272,1024]{1,0:T(8,128)(2,1)S(1)} %get-tuple-element.41.after_ref.refs_0_.refs_5_, bf16[272,1024]{1,0:T(8,128)(2,1)S(1)} %get-tuple-element.41.after_ref.refs_0_.refs_5_, ...), custom_call_target="tpu_custom_call" | custom-call | flops 301989888 | bytes 884736 | tf_op jit(solution)/shard_map/pallas_call | solution.py:312
  7.5 1.6 %collective-permute-start.3 = (bf16[1168,128]{1,0:T(8,128)(2,1)S(1)}, bf16[1168,128]{1,0:T(8,128)(2,1)S(1)}, u32[]{:S(2)}, u32[]{:S(2)}) collective-permute-start(bf16[1168,128]{1,0:T(8,128)(2,1)S(1)} %get-tuple-element.45.own), channel_id=1, source_target_pairs={{0,8},{8,0},{16,24},{24,16},{1,9},{9,1},{17,25},{25,17},{2,10},{10... | collective-permute-start | bytes 897032 | tf_op jit(solution)/shard_map/ppermute | solution.py:592
  9.6 1.4 %collective-permute-start.6 = (bf16[144,1024]{1,0:T(8,128)(2,1)S(1)}, bf16[144,1024]{1,0:T(8,128)(2,1)S(1)}, u32[]{:S(2)}, u32[]{:S(2)}) collective-permute-start(bf16[144,1024]{1,0:T(8,128)(2,1)S(1)} %get-tuple-element.47), channel_id=1, source_target_pairs={{0,2},{1,5},{2,0},{3,7},{4,6},{5,1},{6,4},{7,3},{8,10},{9,13},{10,... | collective-permute-start | bytes 884744 | tf_op jit(solution)/shard_map/ppermute | solution.py:612
  11.5 1.5 %collective-permute-done.2.refs_1_ = bf16[128,1024]{1,0:T(8,128)(2,1)S(1)} collective-permute-done((bf16[128,1024]{1,0:T(8,128)(2,1)S(1)}, bf16[128,1024]{1,0:T(8,128)(2,1)S(1)}, u32[]{:S(2)}, u32[]{:S(2)}) %collective-permute-start.2) | collective-permute-done | bytes 262176 | tf_op jit(solution)/shard_map/ppermute | solution.py:611
  13.3 3.2 %collective-permute-start.4 = (bf16[384,128]{1,0:T(8,128)(2,1)S(1)}, bf16[384,128]{1,0:T(8,128)(2,1)S(1)}, u32[]{:S(2)}, u32[]{:S(2)}) collective-permute-start(bf16[384,128]{1,0:T(8,128)(2,1)S(1)} %get-tuple-element.46.near_own), channel_id=1, source_target_pairs={{0,8},{8,0},{16,24},{24,16},{1,9},{9,1},{17,25},{25,17},{2,10},{10... | collective-permute-start | bytes 294920 | tf_op jit(solution)/shard_map/ppermute | solution.py:592
  16.5 2.1 %collective-permute-done.7.refs_4_ = bf16[144,1024]{1,0:T(8,128)(2,1)S(1)} collective-permute-done((bf16[144,1024]{1,0:T(8,128)(2,1)S(1)}, bf16[144,1024]{1,0:T(8,128)(2,1)S(1)}, u32[]{:S(2)}, u32[]{:S(2)}) %collective-permute-start.7) | collective-permute-done | bytes 294944 | tf_op jit(solution)/shard_map/ppermute | solution.py:612
  19.4 1.6 %collective-permute-start.9 = (bf16[272,1024]{1,0:T(8,128)(2,1)S(1)}, bf16[272,1024]{1,0:T(8,128)(2,1)S(1)}, u32[]{:S(2)}, u32[]{:S(2)}) collective-permute-start(bf16[272,1024]{1,0:T(8,128)(2,1)S(1)} %get-tuple-element.49.after_ref), channel_id=1, source_target_pairs={{0,4},{1,3},{2,6},{3,1},{4,0},{5,7},{6,2},{7,5},{8,12},{9,11},{10,... | collective-permute-start | bytes 1671176 | tf_op jit(solution)/shard_map/ppermute | solution.py:618
  21.4 2.1 %collective-permute-start.10 = (bf16[768,128]{1,0:T(8,128)(2,1)S(1)}, bf16[768,128]{1,0:T(8,128)(2,1)S(1)}, u32[]{:S(2)}, u32[]{:S(2)}) collective-permute-start(bf16[768,128]{1,0:T(8,128)(2,1)S(1)} %get-tuple-element.56.own), channel_id=1, source_target_pairs={{0,8},{8,0},{16,24},{24,16},{1,9},{9,1},{17,25},{25,17},{2,10},{10... | collective-permute-start | bytes 589832 | tf_op jit(solution)/shard_map/ppermute | solution.py:592
  23.5 0.7 %shard_map.99 = (bf16[1152,128]{1,0:T(8,128)(2,1)S(1)}, f32[8,128]{1,0:T(8,128)S(1)}) custom-call(bf16[3,192,1024]{2,1,0:T(8,128)(2,1)S(1)} %get-tuple-element.40.w_ref, f32[8,128]{1,0:T(8,128)S(1)} %get-tuple-element.52.after_ref, bf16[416,1024]{1,0:T(8,128)(2,1)S(1)} %get-tuple-element.50.refs_0_.refs_1_, ...), custom_call_target="tpu_custom_call" | custom-call | flops 301989888 | bytes 884736 | tf_op jit(solution)/shard_map/pallas_call | solution.py:312
  24.6 4.5 %collective-permute-done.9.in_ref = bf16[272,1024]{1,0:T(8,128)(2,1)S(1)} collective-permute-done((bf16[272,1024]{1,0:T(8,128)(2,1)S(1)}, bf16[272,1024]{1,0:T(8,128)(2,1)S(1)}, u32[]{:S(2)}, u32[]{:S(2)}) %collective-permute-start.9) | collective-permute-done | bytes 557088 | tf_op jit(solution)/shard_map/ppermute | solution.py:618
  30.2 0.6 %shard_map.101 = (f32[3,192,1024]{2,1,0:T(8,128)S(1)}, f32[768,128]{1,0:T(8,128)S(1)}, f32[8,128]{1,0:T(8,128)S(1)}) custom-call(f32[8,256]{1,0:T(8,128)S(1)} %get-tuple-element.48.gate_ref, bf16[64,1024]{1,0:T(8,128)(2,1)S(1)} %get-tuple-element.54.after_ref.refs_0_, f32[1152,128]{1,0:T(8,128)S(1)} %get-tuple-element.55.sum_ref, ...), custom_call_target="tpu_custom_call" | custom-call | flops 301989888 | bytes 2359296 | tf_op jit(solution)/shard_map/pallas_call | solution.py:448
  31.2 0.7 %shard_map.102 = (bf16[384,128]{1,0:T(8,128)(2,1)S(1)}, bf16[384,128]{1,0:T(8,128)(2,1)S(1)}, bf16[384,128]{1,0:T(8,128)(2,1)S(1)}) custom-call(bf16[3,192,1024]{2,1,0:T(8,128)(2,1)S(1)} %get-tuple-element.40.w_ref, f32[8,128]{1,0:T(8,128)S(1)} %get-tuple-element.57.after_ref, bf16[64,1024]{1,0:T(8,128)(2,1)S(1)} %get-tuple-element.54.after_ref.refs_0_, ...), custom_call_target="tpu_custom_call" | custom-call | flops 301989888 | bytes 884736 | tf_op jit(solution)/shard_map/pallas_call | solution.py:519
  31.9 2.1 %collective-permute-start.18 = (bf16[384,128]{1,0:T(8,128)(2,1)S(1)}, bf16[384,128]{1,0:T(8,128)(2,1)S(1)}, u32[]{:S(2)}, u32[]{:S(2)}) collective-permute-start(bf16[384,128]{1,0:T(8,128)(2,1)S(1)} %get-tuple-element.67.own), channel_id=1, source_target_pairs={{0,8},{8,0},{16,24},{24,16},{1,9},{9,1},{17,25},{25,17},{2,10},{10... | collective-permute-start | bytes 294920 | tf_op jit(solution)/shard_map/ppermute | solution.py:592
  34.0 1.9 %collective-permute-start.15 = (bf16[384,128]{1,0:T(8,128)(2,1)S(1)}, bf16[384,128]{1,0:T(8,128)(2,1)S(1)}, u32[]{:S(2)}, u32[]{:S(2)}) collective-permute-start(bf16[384,128]{1,0:T(8,128)(2,1)S(1)} %get-tuple-element.61.own), channel_id=1, source_target_pairs={{0,8},{8,0},{16,24},{24,16},{1,9},{9,1},{17,25},{25,17},{2,10},{10... | collective-permute-start | bytes 294920 | tf_op jit(solution)/shard_map/ppermute | solution.py:592
  36.0 1.0 %shard_map.103.refs_8_ = f32[3,192,1024]{2,1,0:T(8,128)S(1)} custom-call(f32[384,128]{1,0:T(8,128)S(1)} %get-tuple-element.62.sum_ref, f32[768,128]{1,0:T(8,128)S(1)} %get-tuple-element.63.more_ref, bf16[1152,128]{1,0:T(8,128)(2,1)S(1)} %get-tuple-element.64.own, bf16[1152,128]{1,0:T(8,128)(2,1)S(1)} %collective-permute-done.16.got, ...), custom_call_target="tpu_custom_call", output_to_operand_aliasing={{}: (8, {})} | custom-call | flops 603979776 | bytes 4718592 | tf_op jit(solution)/shard_map/pallas_call | solution.py:476
  37.0 0.5 %collective-permute-done.18.got = bf16[384,128]{1,0:T(8,128)(2,1)S(1)} collective-permute-done((bf16[384,128]{1,0:T(8,128)(2,1)S(1)}, bf16[384,128]{1,0:T(8,128)(2,1)S(1)}, u32[]{:S(2)}, u32[]{:S(2)}) %collective-permute-start.18) | collective-permute-done | bytes 98336 | tf_op jit(solution)/shard_map/ppermute | solution.py:592
  37.6 0.7 %shard_map.104 = (bf16[3,64,1024]{2,1,0:T(8,128)(2,1)S(1)}, bf16[3,64,1024]{2,1,0:T(8,128)(2,1)S(1)}, bf16[3,64,1024]{2,1,0:T(8,128)(2,1)S(1)}) custom-call(bf16[384,128]{1,0:T(8,128)(2,1)S(1)} %get-tuple-element.67.own, bf16[384,128]{1,0:T(8,128)(2,1)S(1)} %collective-permute-done.18.got, bf16[64,1024]{1,0:T(8,128)(2,1)S(1)} %get-tuple-element.54.after_ref.refs_0_, ...), custom_call_target="tpu_custom_call" | custom-call | flops 100663296 | bytes 2752512 | tf_op jit(solution)/shard_map/pallas_call | solution.py:577
  38.3 1.4 %collective-permute-done.17.got = bf16[384,128]{1,0:T(8,128)(2,1)S(1)} collective-permute-done((bf16[384,128]{1,0:T(8,128)(2,1)S(1)}, bf16[384,128]{1,0:T(8,128)(2,1)S(1)}, u32[]{:S(2)}, u32[]{:S(2)}) %collective-permute-start.17) | collective-permute-done | bytes 98336 | tf_op jit(solution)/shard_map/ppermute | solution.py:592
  39.7 1.4 %shard_map.105 = (bf16[3,192,1024]{2,1,0:T(8,128)(2,1)}, bf16[3,192,1024]{2,1,0:T(8,128)(2,1)}, bf16[3,192,1024]{2,1,0:T(8,128)(2,1)}, bf16[3,64,1024]{2,1,0:T(8...) custom-call(bf16[384,128]{1,0:T(8,128)(2,1)S(1)} %get-tuple-element.66.own, ...), custom_call_target="tpu_custom_call" | custom-call | flops 100663296 | bytes 2752512 | tf_op jit(solution)/shard_map/pallas_call | solution.py:577
  41.5 1.7 %shard_map.106 = (bf16[3,192,1024]{2,1,0:T(8,128)(2,1)}, bf16[3,192,1024]{2,1,0:T(8,128)(2,1)}, bf16[3,192,1024]{2,1,0:T(8,128)(2,1)}) custom-call(bf16[384,128]{1,0:T(8,128)(2,1)S(1)} %get-tuple-element.61.own, bf16[384,128]{1,0:T(8,128)(2,1)S(1)} %collective-permute-done.15.got, ...), custom_call_target="tpu_custom_call", output_to_operand_aliasing={{0}: (16, {}), {1}: (17, {}), {2}: (18, {})} | custom-call | flops 100663296 | bytes 2752512 | tf_op jit(solution)/shard_map/pallas_call | solution.py:577
  (31 shorter events, 5.0 us)
Async XLA Ops:
  2.3 4.6 %collective-permute-start = (bf16[272,1024]{1,0:T(8,128)(2,1)S(1)}, bf16[272,1024]{1,0:T(8,128)(2,1)S(1)}, u32[]{:S(2)}, u32[]{:S(2)}) collective-permute-start(bf16[272,1024]{1,0:T(8,128)(2,1)S(1)} %get-tuple-element.41.after_ref.refs_0_.refs_5_), channel_id=1, source_target_pairs={{0,1},{1,0},{2,3},{3,2},{4,5},{5,4},{6,7},{7,6},{8,9},{9,8},{10,11... | collective-permute-start | bytes 1671176 | tf_op jit(solution)/shard_map/ppermute | solution.py:592
  2.8 8.6 %collective-permute-start.1 = (bf16[128,1024]{1,0:T(8,128)(2,1)S(1)}, bf16[128,1024]{1,0:T(8,128)(2,1)S(1)}, u32[]{:S(2)}, u32[]{:S(2)}) collective-permute-start(bf16[128,1024]{1,0:T(8,128)(2,1)S(1)} %get-tuple-element.43), channel_id=1, source_target_pairs={{0,2},{1,5},{2,0},{3,7},{4,6},{5,1},{6,4},{7,3},{8,10},{9,13},{10,... | collective-permute-start | bytes 786440 | tf_op jit(solution)/shard_map/ppermute | solution.py:611
  5.4 7.5 %collective-permute-start.2 = (bf16[128,1024]{1,0:T(8,128)(2,1)S(1)}, bf16[128,1024]{1,0:T(8,128)(2,1)S(1)}, u32[]{:S(2)}, u32[]{:S(2)}) collective-permute-start(bf16[128,1024]{1,0:T(8,128)(2,1)S(1)} %get-tuple-element.43), channel_id=1, source_target_pairs={{0,4},{1,3},{2,6},{3,1},{4,0},{5,7},{6,2},{7,5},{8,12},{9,11},{10,... | collective-permute-start | bytes 786440 | tf_op jit(solution)/shard_map/ppermute | solution.py:611
  7.5 11.7 %collective-permute-start.3 = (bf16[1168,128]{1,0:T(8,128)(2,1)S(1)}, bf16[1168,128]{1,0:T(8,128)(2,1)S(1)}, u32[]{:S(2)}, u32[]{:S(2)}) collective-permute-start(bf16[1168,128]{1,0:T(8,128)(2,1)S(1)} %get-tuple-element.45.own), channel_id=1, source_target_pairs={{0,8},{8,0},{16,24},{24,16},{1,9},{9,1},{17,25},{25,17},{2,10},{10... | collective-permute-start | bytes 897032 | tf_op jit(solution)/shard_map/ppermute | solution.py:592
  9.1 9.5 %collective-permute-start.7 = (bf16[144,1024]{1,0:T(8,128)(2,1)S(1)}, bf16[144,1024]{1,0:T(8,128)(2,1)S(1)}, u32[]{:S(2)}, u32[]{:S(2)}) collective-permute-start(bf16[144,1024]{1,0:T(8,128)(2,1)S(1)} %get-tuple-element.47), channel_id=1, source_target_pairs={{0,4},{1,3},{2,6},{3,1},{4,0},{5,7},{6,2},{7,5},{8,12},{9,11},{10,... | collective-permute-start | bytes 884744 | tf_op jit(solution)/shard_map/ppermute | solution.py:612
  9.6 9.3 %collective-permute-start.6 = (bf16[144,1024]{1,0:T(8,128)(2,1)S(1)}, bf16[144,1024]{1,0:T(8,128)(2,1)S(1)}, u32[]{:S(2)}, u32[]{:S(2)}) collective-permute-start(bf16[144,1024]{1,0:T(8,128)(2,1)S(1)} %get-tuple-element.47), channel_id=1, source_target_pairs={{0,2},{1,5},{2,0},{3,7},{4,6},{5,1},{6,4},{7,3},{8,10},{9,13},{10,... | collective-permute-start | bytes 884744 | tf_op jit(solution)/shard_map/ppermute | solution.py:612
  11.5 7.4 %collective-permute-start.5 = (bf16[128,1024]{1,0:T(8,128)(2,1)S(1)}, bf16[128,1024]{1,0:T(8,128)(2,1)S(1)}, u32[]{:S(2)}, u32[]{:S(2)}) collective-permute-start(bf16[128,1024]{1,0:T(8,128)(2,1)S(1)} %collective-permute-done.1.refs_0_), channel_id=1, source_target_pairs={{0,1},{1,0},{2,3},{3,2},{4,5},{5,4},{6,7},{7,6},{8,9},{9,8},{10,11... | collective-permute-start | bytes 786440 | tf_op jit(solution)/shard_map/ppermute | solution.py:592
  13.3 5.8 %collective-permute-start.4 = (bf16[384,128]{1,0:T(8,128)(2,1)S(1)}, bf16[384,128]{1,0:T(8,128)(2,1)S(1)}, u32[]{:S(2)}, u32[]{:S(2)}) collective-permute-start(bf16[384,128]{1,0:T(8,128)(2,1)S(1)} %get-tuple-element.46.near_own), channel_id=1, source_target_pairs={{0,8},{8,0},{16,24},{24,16},{1,9},{9,1},{17,25},{25,17},{2,10},{10... | collective-permute-start | bytes 294920 | tf_op jit(solution)/shard_map/ppermute | solution.py:592
  19.4 4.2 %collective-permute-start.8 = (bf16[416,1024]{1,0:T(8,128)(2,1)S(1)}, bf16[416,1024]{1,0:T(8,128)(2,1)S(1)}, u32[]{:S(2)}, u32[]{:S(2)}) collective-permute-start(bf16[416,1024]{1,0:T(8,128)(2,1)S(1)} %get-tuple-element.50.refs_0_.refs_1_), channel_id=1, source_target_pairs={{0,1},{1,0},{2,3},{3,2},{4,5},{5,4},{6,7},{7,6},{8,9},{9,8},{10,11... | collective-permute-start | bytes 2555912 | tf_op jit(solution)/shard_map/ppermute | solution.py:592
  19.4 9.6 %collective-permute-start.9 = (bf16[272,1024]{1,0:T(8,128)(2,1)S(1)}, bf16[272,1024]{1,0:T(8,128)(2,1)S(1)}, u32[]{:S(2)}, u32[]{:S(2)}) collective-permute-start(bf16[272,1024]{1,0:T(8,128)(2,1)S(1)} %get-tuple-element.49.after_ref), channel_id=1, source_target_pairs={{0,4},{1,3},{2,6},{3,1},{4,0},{5,7},{6,2},{7,5},{8,12},{9,11},{10,... | collective-permute-start | bytes 1671176 | tf_op jit(solution)/shard_map/ppermute | solution.py:618
  21.4 8.3 %collective-permute-start.10 = (bf16[768,128]{1,0:T(8,128)(2,1)S(1)}, bf16[768,128]{1,0:T(8,128)(2,1)S(1)}, u32[]{:S(2)}, u32[]{:S(2)}) collective-permute-start(bf16[768,128]{1,0:T(8,128)(2,1)S(1)} %get-tuple-element.56.own), channel_id=1, source_target_pairs={{0,8},{8,0},{16,24},{24,16},{1,9},{9,1},{17,25},{25,17},{2,10},{10... | collective-permute-start | bytes 589832 | tf_op jit(solution)/shard_map/ppermute | solution.py:592
  24.2 11.8 %collective-permute-start.16 = (bf16[1152,128]{1,0:T(8,128)(2,1)S(1)}, bf16[1152,128]{1,0:T(8,128)(2,1)S(1)}, u32[]{:S(2)}, u32[]{:S(2)}) collective-permute-start(bf16[1152,128]{1,0:T(8,128)(2,1)S(1)} %get-tuple-element.64.own), channel_id=1, source_target_pairs={{0,8},{8,0},{16,24},{24,16},{1,9},{9,1},{17,25},{25,17},{2,10},{10... | collective-permute-start | bytes 884744 | tf_op jit(solution)/shard_map/ppermute | solution.py:592
  29.1 2.1 %collective-permute-start.14 = (bf16[80,1024]{1,0:T(8,128)(2,1)S(1)}, bf16[80,1024]{1,0:T(8,128)(2,1)S(1)}, u32[]{:S(2)}, u32[]{:S(2)}) collective-permute-start(bf16[80,1024]{1,0:T(8,128)(2,1)S(1)} %get-tuple-element.60.refs_3_), channel_id=1, source_target_pairs={{0,1},{1,0},{2,3},{3,2},{4,5},{5,4},{6,7},{7,6},{8,9},{9,8},{10,11... | collective-permute-start | bytes 491528 | tf_op jit(solution)/shard_map/ppermute | solution.py:592
  29.1 1.6 %collective-permute-start.12 = (bf16[64,1024]{1,0:T(8,128)(2,1)S(1)}, bf16[64,1024]{1,0:T(8,128)(2,1)S(1)}, u32[]{:S(2)}, u32[]{:S(2)}) collective-permute-start(bf16[64,1024]{1,0:T(8,128)(2,1)S(1)} %get-tuple-element.58.refs_1_), channel_id=1, source_target_pairs={{0,1},{1,0},{2,3},{3,2},{4,5},{5,4},{6,7},{7,6},{8,9},{9,8},{10,11... | collective-permute-start | bytes 393224 | tf_op jit(solution)/shard_map/ppermute | solution.py:592
  29.6 1.3 %collective-permute-start.13 = (bf16[64,1024]{1,0:T(8,128)(2,1)S(1)}, bf16[64,1024]{1,0:T(8,128)(2,1)S(1)}, u32[]{:S(2)}, u32[]{:S(2)}) collective-permute-start(bf16[64,1024]{1,0:T(8,128)(2,1)S(1)} %get-tuple-element.59.refs_2_), channel_id=1, source_target_pairs={{0,1},{1,0},{2,3},{3,2},{4,5},{5,4},{6,7},{7,6},{8,9},{9,8},{10,11... | collective-permute-start | bytes 393224 | tf_op jit(solution)/shard_map/ppermute | solution.py:592
  29.7 1.5 %collective-permute-start.11 = (bf16[64,1024]{1,0:T(8,128)(2,1)S(1)}, bf16[64,1024]{1,0:T(8,128)(2,1)S(1)}, u32[]{:S(2)}, u32[]{:S(2)}) collective-permute-start(bf16[64,1024]{1,0:T(8,128)(2,1)S(1)} %get-tuple-element.54.after_ref.refs_0_), channel_id=1, source_target_pairs={{0,1},{1,0},{2,3},{3,2},{4,5},{5,4},{6,7},{7,6},{8,9},{9,8},{10,11... | collective-permute-start | bytes 393224 | tf_op jit(solution)/shard_map/ppermute | solution.py:592
  31.9 5.6 %collective-permute-start.18 = (bf16[384,128]{1,0:T(8,128)(2,1)S(1)}, bf16[384,128]{1,0:T(8,128)(2,1)S(1)}, u32[]{:S(2)}, u32[]{:S(2)}) collective-permute-start(bf16[384,128]{1,0:T(8,128)(2,1)S(1)} %get-tuple-element.67.own), channel_id=1, source_target_pairs={{0,8},{8,0},{16,24},{24,16},{1,9},{9,1},{17,25},{25,17},{2,10},{10... | collective-permute-start | bytes 294920 | tf_op jit(solution)/shard_map/ppermute | solution.py:592
  34.0 5.7 %collective-permute-start.17 = (bf16[384,128]{1,0:T(8,128)(2,1)S(1)}, bf16[384,128]{1,0:T(8,128)(2,1)S(1)}, u32[]{:S(2)}, u32[]{:S(2)}) collective-permute-start(bf16[384,128]{1,0:T(8,128)(2,1)S(1)} %get-tuple-element.66.own), channel_id=1, source_target_pairs={{0,8},{8,0},{16,24},{24,16},{1,9},{9,1},{17,25},{25,17},{2,10},{10... | collective-permute-start | bytes 294920 | tf_op jit(solution)/shard_map/ppermute | solution.py:592
  34.0 7.4 %collective-permute-start.15 = (bf16[384,128]{1,0:T(8,128)(2,1)S(1)}, bf16[384,128]{1,0:T(8,128)(2,1)S(1)}, u32[]{:S(2)}, u32[]{:S(2)}) collective-permute-start(bf16[384,128]{1,0:T(8,128)(2,1)S(1)} %get-tuple-element.61.own), channel_id=1, source_target_pairs={{0,8},{8,0},{16,24},{24,16},{1,9},{9,1},{17,25},{25,17},{2,10},{10... | collective-permute-start | bytes 294920 | tf_op jit(solution)/shard_map/ppermute | solution.py:592
  36.0 1.5 %copy-start = (bf16[3,192,1024]{2,1,0:T(8,128)(2,1)S(1)}, bf16[3,192,1024]{2,1,0:T(8,128)(2,1)}, u32[]{:S(2)}) copy-start(bf16[3,192,1024]{2,1,0:T(8,128)(2,1)} %refs_9_.5) | copy-start | bytes 3538948
  36.0 1.6 %copy-start.1 = (bf16[3,192,1024]{2,1,0:T(8,128)(2,1)S(1)}, bf16[3,192,1024]{2,1,0:T(8,128)(2,1)}, u32[]{:S(2)}) copy-start(bf16[3,192,1024]{2,1,0:T(8,128)(2,1)} %refs_10_.5) | copy-start | bytes 3538948

commit v13 on v12

--- a/solution.py
+++ b/solution.py
@@ -373,13 +373,14 @@
 
 
 def onward_kernel(kinds, after_ref, own, got, near_own, near_got, *refs):
-    x0_ref, x1_ref, s0_ref, y0_ref, y1_ref = refs[:5]
-    pair_ref, rest_ref, out_ref, first_ref, sum_ref, gate_ref = refs[5 + len(kinds) :]
+    x0_ref, x1_ref, s0_ref, s1_ref, y0_ref, y1_ref = refs[:6]
+    pair_ref, rest_ref, out_ref, first_ref, sum_ref, gate_ref = refs[7 + len(kinds) :]
     count, rows = x0_ref.shape[0], y0_ref.shape[0]
-    gates = views(refs[5 : 5 + len(kinds)], kinds, count)[2]
+    gates = views(refs[6 : 6 + len(kinds)], kinds, count)[2]
     gate_ref[...] = jnp.broadcast_to(gate_row(gates), gate_ref.shape)
     pair_ref[0] = x0_ref[...]
-    pair_ref[1] = s0_ref[...]
+    pair_ref[1, 0 : count // 2, :] = s0_ref[...]
+    pair_ref[1, count // 2 :, :] = s1_ref[...]
     rest_ref[0:count, :] = x1_ref[...]
     rest_ref[count : count + rows, :] = y0_ref[...]
     rest_ref[count + rows :, :] = y1_ref[...]
@@ -390,10 +391,10 @@
     sum_ref[...] = near_own[...].astype(jnp.float32) + near_got[...].astype(jnp.float32)
 
 
-def pick_onward(after, pair, near_pair, near_x, other_x, near_y, chunk):
-    count, width = other_x.shape
+def pick_onward(after, pair, near_pair, near_x, other_x, near_y, chunk, held):
+    count, width = near_x[0].shape
     rows = near_y[0].shape[0]
-    operands = [*pair, *near_pair, *near_x, other_x, *near_y, *values_of(chunk)]
+    operands = [*pair, *near_pair, *near_x, *other_x, *near_y, *values_of(chunk), held]
     return pl.pallas_call(
         functools.partial(onward_kernel, kinds_of(chunk)),
         in_specs=[unread()] + [whole()] * len(operands),
@@ -407,7 +408,7 @@
             jax.ShapeDtypeStruct((8, 2 * count), jnp.float32),
         ],
         compiler_params=params(),
-        cost_estimate=cost(1000, 8 * other_x.size),
+        cost_estimate=cost(1000, 8 * near_x[0].size),
     )(after, *operands)
 
 
@@ -610,18 +611,19 @@
     along = [[(p, p ^ (2 if p % 2 == k else 4)) for p in range(n_data)] for k in (0, 1)]
     near_x = [lax.ppermute(x_own, "dp", pairs) for pairs in along]
     near_y = [lax.ppermute(y_own, "dp", pairs) for pairs in along]
-    send, token = partials(weights, token, [("x", near_x[0]), ("", near_x[1])], (2,), count)
+    other_x = [other(value) for value in passed_on(token, near_x[0], (count // 2, count // 2))]
+    early = [("x", value) for value in (near_x[1], *other_x)]
+    early_send, token = partials(weights, token, early, (4,), count)
+    send, token = partials(weights, token, [("x", near_x[0])], (2,), count)
     near_pair = (send, partner(send))
     x_pair, rest, picked, first_sum, near_sum, gate = pick_onward(
-        token, first_pair, near_pair, near_x, other(near_x[0]), near_y, first
+        token, first_pair, near_pair, near_x, other_x, near_y, first, early_send
     )
     far = lax.ppermute(picked, "dp", along[1])
     rest_other = other(rest)
-    early = [("x of xyy", rest), ("second x", x_pair)]
     late = [("y, y of xyy", rest), ("x, y, y", rest_other)]
-    send, token = partials(weights, picked, early, (4,), count)
-    early_pair = (send, partner(send))
-    send, token = partials(weights, token, late, (6,), count)
+    early_pair = (early_send, partner(early_send))
+    send, token = partials(weights, picked, late, (6,), count)
     late_pair = (send, partner(send))
     pieces = passed_on(token, far, (count // 2, count // 2, count // 2, count // 2 + slots))
     acc, early_sum, token = first_grads(

time: 43.3 us -> 45.3 us (1.046)
  waiting for transfers between devices: 11.8 us -> 13.9 us
    ppermute x14 -> x15, waiting for transfers between devices: 2.98 us -> 6.67 us  [from_masked(): return lax.ppermute(value, axis, pairs)]
    ppermute x2, waiting for transfers between devices: 2.35 us -> 0.59 us  [dense_plan(): near_y = [lax.ppermute(y_own, 'dp', pairs) for pairs in along]]
    ppermute x14 -> x15, starting transfers between devices: 13.1 us -> 13 us  [from_masked(): return lax.ppermute(value, axis, pairs)]
  transfers between devices with their start and end apart: 19 -> 20, of which waited for: 11 -> 12; matrix products, arithmetic and copies ran while one was open for 0% -> 0% of each run, Pallas kernels for 15% -> 14%
where the time goes in v13:
time: 45.3 us; the launch traced here: 45.1 us
  starting transfers between devices  20.5 us (45%)
  waiting for transfers between devices  13.9 us (31%)
  Pallas kernels  9.93 us (22%)
  between operations  0.76 us (2%)
    ppermute x15, starting transfers between devices, from_masked(): return lax.ppermute(value, axis, pairs)  13 us
    ppermute x15, waiting for transfers between devices, from_masked(): return lax.ppermute(value, axis, pairs)  6.67 us
    ppermute x1, waiting for transfers between devices, dense_plan(): far = lax.ppermute(picked, 'dp', along[1])  4.75 us
    ppermute x2, starting transfers between devices, dense_plan(): near_x = [lax.ppermute(x_own, 'dp', pairs) for pairs in along]  4.08 us
    pallas_call x3, Pallas kernels, update_piece(): pl.pallas_call(functools.partial(update_kernel, kinds, count, piece, last...  3.76 us
    pallas_call x4, Pallas kernels, partials(): pl.pallas_call(functools.partial(partial_kernel, kinds, count, tokened),...  1.98 us
    ppermute x2, starting transfers between devices, dense_plan(): near_y = [lax.ppermute(y_own, 'dp', pairs) for pairs in along]  1.86 us
    ppermute x2, waiting for transfers between devices, dense_plan(): near_x = [lax.ppermute(x_own, 'dp', pairs) for pairs in along]  1.86 us
  transfers between devices with their start and end apart: 20, of which 12 were waited for; matrix products, arithmetic and copies ran while one was open for 0% of the time, Pallas kernels for 14%

profile of v13, /device:TPU:0, one launch (start us, length us, event | category | flops | bytes accessed | tf_op | source)
XLA Modules:
  0.0 45.1 jit_solution(9414089941998205381)
XLA Ops:
  0.6 1.7 %shard_map.94 = (bf16[128,1024]{1,0:T(8,128)(2,1)S(1)}, bf16[144,1024]{1,0:T(8,128)(2,1)S(1)}, bf16[272,1024]{1,0:T(8,128)(2,1)S(1)}, bf16[3,192,1024]{2,1,0:T(8,128)(2,1)S(1)}) custom-call(s32[4,128]{1,0:T(4,128)} %bitcast.2, bf16[4,128]{1,0:T(4,128)(2,1)} %bitcast.3, bf16[128,2048]{1,0:T(8,128)(2,1)} %tokens_ref.1, bf16[128,2048]{1,0:T(8,128)(2,1)} %cot_ref.1, ...), custom_call_target="tpu_custom_call" | custom-call | flops 1000 | bytes 1048576 | tf_op jit(solution)/shard_map/pallas_call | solution.py:209
  2.8 2.6 %collective-permute-start.2 = (bf16[128,1024]{1,0:T(8,128)(2,1)S(1)}, bf16[128,1024]{1,0:T(8,128)(2,1)S(1)}, u32[]{:S(2)}, u32[]{:S(2)}) collective-permute-start(bf16[128,1024]{1,0:T(8,128)(2,1)S(1)} %get-tuple-element.45), channel_id=1, source_target_pairs={{0,2},{1,5},{2,0},{3,7},{4,6},{5,1},{6,4},{7,3},{8,10},{9,13},{10,... | collective-permute-start | bytes 786440 | tf_op jit(solution)/shard_map/ppermute | solution.py:612
  5.4 1.5 %collective-permute-start.1 = (bf16[128,1024]{1,0:T(8,128)(2,1)S(1)}, bf16[128,1024]{1,0:T(8,128)(2,1)S(1)}, u32[]{:S(2)}, u32[]{:S(2)}) collective-permute-start(bf16[128,1024]{1,0:T(8,128)(2,1)S(1)} %get-tuple-element.45), channel_id=1, source_target_pairs={{0,4},{1,3},{2,6},{3,1},{4,0},{5,7},{6,2},{7,5},{8,12},{9,11},{10,... | collective-permute-start | bytes 786440 | tf_op jit(solution)/shard_map/ppermute | solution.py:612
  7.5 1.6 %collective-permute-start.5 = (bf16[1168,128]{1,0:T(8,128)(2,1)S(1)}, bf16[1168,128]{1,0:T(8,128)(2,1)S(1)}, u32[]{:S(2)}, u32[]{:S(2)}) collective-permute-start(bf16[1168,128]{1,0:T(8,128)(2,1)S(1)} %get-tuple-element.50.own), channel_id=1, source_target_pairs={{0,8},{8,0},{16,24},{24,16},{1,9},{9,1},{17,25},{25,17},{2,10},{10... | collective-permute-start | bytes 897032 | tf_op jit(solution)/shard_map/ppermute | solution.py:593
  9.6 1.4 %collective-permute-start.7 = (bf16[144,1024]{1,0:T(8,128)(2,1)S(1)}, bf16[144,1024]{1,0:T(8,128)(2,1)S(1)}, u32[]{:S(2)}, u32[]{:S(2)}) collective-permute-start(bf16[144,1024]{1,0:T(8,128)(2,1)S(1)} %get-tuple-element.52), channel_id=1, source_target_pairs={{0,2},{1,5},{2,0},{3,7},{4,6},{5,1},{6,4},{7,3},{8,10},{9,13},{10,... | collective-permute-start | bytes 884744 | tf_op jit(solution)/shard_map/ppermute | solution.py:613
  11.6 1.4 %collective-permute-done.1.refs_0_.refs_1_ = bf16[128,1024]{1,0:T(8,128)(2,1)S(1)} collective-permute-done((bf16[128,1024]{1,0:T(8,128)(2,1)S(1)}, bf16[128,1024]{1,0:T(8,128)(2,1)S(1)}, u32[]{:S(2)}, u32[]{:S(2)}) %collective-permute-start.1) | collective-permute-done | bytes 262176 | tf_op jit(solution)/shard_map/ppermute | solution.py:612
  13.0 1.3 %collective-permute-done.4.refs_2_.refs_3_ = bf16[64,1024]{1,0:T(8,128)(2,1)S(1)} collective-permute-done((bf16[64,1024]{1,0:T(8,128)(2,1)S(1)}, bf16[64,1024]{1,0:T(8,128)(2,1)S(1)}, u32[]{:S(2)}, u32[]{:S(2)}) %collective-permute-start.4) | collective-permute-done | bytes 131104 | tf_op jit(solution)/shard_map/ppermute | solution.py:593
  15.1 3.2 %collective-permute-start.6 = (bf16[384,128]{1,0:T(8,128)(2,1)S(1)}, bf16[384,128]{1,0:T(8,128)(2,1)S(1)}, u32[]{:S(2)}, u32[]{:S(2)}) collective-permute-start(bf16[384,128]{1,0:T(8,128)(2,1)S(1)} %get-tuple-element.51.near_own), channel_id=1, source_target_pairs={{0,8},{8,0},{16,24},{24,16},{1,9},{9,1},{17,25},{25,17},{2,10},{10... | collective-permute-start | bytes 294920 | tf_op jit(solution)/shard_map/ppermute | solution.py:593
  18.9 2.5 %collective-permute-done.6.near_got = bf16[384,128]{1,0:T(8,128)(2,1)S(1)} collective-permute-done((bf16[384,128]{1,0:T(8,128)(2,1)S(1)}, bf16[384,128]{1,0:T(8,128)(2,1)S(1)}, u32[]{:S(2)}, u32[]{:S(2)}) %collective-permute-start.6) | collective-permute-done | bytes 98336 | tf_op jit(solution)/shard_map/ppermute | solution.py:593
  21.7 1.6 %collective-permute-start.10 = (bf16[272,1024]{1,0:T(8,128)(2,1)S(1)}, bf16[272,1024]{1,0:T(8,128)(2,1)S(1)}, u32[]{:S(2)}, u32[]{:S(2)}) collective-permute-start(bf16[272,1024]{1,0:T(8,128)(2,1)S(1)} %get-tuple-element.55.after_ref), channel_id=1, source_target_pairs={{0,4},{1,3},{2,6},{3,1},{4,0},{5,7},{6,2},{7,5},{8,12},{9,11},{10,... | collective-permute-start | bytes 1671176 | tf_op jit(solution)/shard_map/ppermute | solution.py:622
  23.3 1.7 %collective-permute-start.11 = (bf16[768,128]{1,0:T(8,128)(2,1)S(1)}, bf16[768,128]{1,0:T(8,128)(2,1)S(1)}, u32[]{:S(2)}, u32[]{:S(2)}) collective-permute-start(bf16[768,128]{1,0:T(8,128)(2,1)S(1)} %get-tuple-element.53.refs_8_.own), channel_id=1, source_target_pairs={{0,8},{8,0},{16,24},{24,16},{1,9},{9,1},{17,25},{25,17},{2,10},{10... | collective-permute-start | bytes 589832 | tf_op jit(solution)/shard_map/ppermute | solution.py:593
  25.0 0.7 %shard_map.100 = (bf16[1152,128]{1,0:T(8,128)(2,1)S(1)}, f32[8,128]{1,0:T(8,128)S(1)}) custom-call(bf16[3,192,1024]{2,1,0:T(8,128)(2,1)S(1)} %get-tuple-element.42.w_ref, bf16[272,1024]{1,0:T(8,128)(2,1)S(1)} %get-tuple-element.55.after_ref, bf16[416,1024]{1,0:T(8,128)(2,1)S(1)} %get-tuple-element.56.refs_0_.refs_1_, ...), custom_call_target="tpu_custom_call" | custom-call | flops 301989888 | bytes 884736 | tf_op jit(solution)/shard_map/pallas_call | solution.py:312
  25.7 0.8 %collective-permute-start.17 = (bf16[1152,128]{1,0:T(8,128)(2,1)S(1)}, bf16[1152,128]{1,0:T(8,128)(2,1)S(1)}, u32[]{:S(2)}, u32[]{:S(2)}) collective-permute-start(bf16[1152,128]{1,0:T(8,128)(2,1)S(1)} %get-tuple-element.67.own), channel_id=1, source_target_pairs={{0,8},{8,0},{16,24},{24,16},{1,9},{9,1},{17,25},{25,17},{2,10},{10... | collective-permute-start | bytes 884744 | tf_op jit(solution)/shard_map/ppermute | solution.py:593
  26.5 4.8 %collective-permute-done.10.in_ref = bf16[272,1024]{1,0:T(8,128)(2,1)S(1)} collective-permute-done((bf16[272,1024]{1,0:T(8,128)(2,1)S(1)}, bf16[272,1024]{1,0:T(8,128)(2,1)S(1)}, u32[]{:S(2)}, u32[]{:S(2)}) %collective-permute-start.10) | collective-permute-done | bytes 557088 | tf_op jit(solution)/shard_map/ppermute | solution.py:622
  32.4 0.5 %shard_map.102 = (f32[3,192,1024]{2,1,0:T(8,128)S(1)}, f32[768,128]{1,0:T(8,128)S(1)}, f32[8,128]{1,0:T(8,128)S(1)}) custom-call(f32[8,256]{1,0:T(8,128)S(1)} %get-tuple-element.54.gate_ref, bf16[64,1024]{1,0:T(8,128)(2,1)S(1)} %get-tuple-element.58.after_ref.refs_0_, f32[1152,128]{1,0:T(8,128)S(1)} %get-tuple-element.59.sum_ref, ...), custom_call_target="tpu_custom_call" | custom-call | flops 301989888 | bytes 2359296 | tf_op jit(solution)/shard_map/pallas_call | solution.py:449
  33.5 0.7 %shard_map.103 = (bf16[384,128]{1,0:T(8,128)(2,1)S(1)}, bf16[384,128]{1,0:T(8,128)(2,1)S(1)}, bf16[384,128]{1,0:T(8,128)(2,1)S(1)}) custom-call(bf16[3,192,1024]{2,1,0:T(8,128)(2,1)S(1)} %get-tuple-element.42.w_ref, f32[8,128]{1,0:T(8,128)S(1)} %get-tuple-element.60.after_ref, bf16[64,1024]{1,0:T(8,128)(2,1)S(1)} %get-tuple-element.58.after_ref.refs_0_, ...), custom_call_target="tpu_custom_call" | custom-call | flops 301989888 | bytes 884736 | tf_op jit(solution)/shard_map/pallas_call | solution.py:520
  34.1 1.8 %collective-permute-start.19 = (bf16[384,128]{1,0:T(8,128)(2,1)S(1)}, bf16[384,128]{1,0:T(8,128)(2,1)S(1)}, u32[]{:S(2)}, u32[]{:S(2)}) collective-permute-start(bf16[384,128]{1,0:T(8,128)(2,1)S(1)} %get-tuple-element.71.own), channel_id=1, source_target_pairs={{0,8},{8,0},{16,24},{24,16},{1,9},{9,1},{17,25},{25,17},{2,10},{10... | collective-permute-start | bytes 294920 | tf_op jit(solution)/shard_map/ppermute | solution.py:593
  36.2 1.7 %collective-permute-start.16 = (bf16[384,128]{1,0:T(8,128)(2,1)S(1)}, bf16[384,128]{1,0:T(8,128)(2,1)S(1)}, u32[]{:S(2)}, u32[]{:S(2)}) collective-permute-start(bf16[384,128]{1,0:T(8,128)(2,1)S(1)} %get-tuple-element.64.own), channel_id=1, source_target_pairs={{0,8},{8,0},{16,24},{24,16},{1,9},{9,1},{17,25},{25,17},{2,10},{10... | collective-permute-start | bytes 294920 | tf_op jit(solution)/shard_map/ppermute | solution.py:593
  38.0 1.0 %shard_map.104.refs_8_ = f32[3,192,1024]{2,1,0:T(8,128)S(1)} custom-call(f32[384,128]{1,0:T(8,128)S(1)} %get-tuple-element.65.sum_ref, f32[768,128]{1,0:T(8,128)S(1)} %get-tuple-element.66.more_ref, bf16[1152,128]{1,0:T(8,128)(2,1)S(1)} %get-tuple-element.67.own, bf16[1152,128]{1,0:T(8,128)(2,1)S(1)} %collective-permute-done.17.got, ...), custom_call_target="tpu_custom_call", output_to_operand_aliasing={{}: (8, {})} | custom-call | flops 603979776 | bytes 4718592 | tf_op jit(solution)/shard_map/pallas_call | solution.py:477
  39.0 0.8 %collective-permute-done.19.got = bf16[384,128]{1,0:T(8,128)(2,1)S(1)} collective-permute-done((bf16[384,128]{1,0:T(8,128)(2,1)S(1)}, bf16[384,128]{1,0:T(8,128)(2,1)S(1)}, u32[]{:S(2)}, u32[]{:S(2)}) %collective-permute-start.19) | collective-permute-done | bytes 98336 | tf_op jit(solution)/shard_map/ppermute | solution.py:593
  39.8 0.7 %shard_map.105 = (bf16[3,64,1024]{2,1,0:T(8,128)(2,1)S(1)}, bf16[3,64,1024]{2,1,0:T(8,128)(2,1)S(1)}, bf16[3,64,1024]{2,1,0:T(8,128)(2,1)S(1)}) custom-call(bf16[384,128]{1,0:T(8,128)(2,1)S(1)} %get-tuple-element.71.own, bf16[384,128]{1,0:T(8,128)(2,1)S(1)} %collective-permute-done.19.got, bf16[64,1024]{1,0:T(8,128)(2,1)S(1)} %get-tuple-element.58.after_ref.refs_0_, ...), custom_call_target="tpu_custom_call" | custom-call | flops 100663296 | bytes 2752512 | tf_op jit(solution)/shard_map/pallas_call | solution.py:578
  40.5 1.4 %collective-permute-done.18.got = bf16[384,128]{1,0:T(8,128)(2,1)S(1)} collective-permute-done((bf16[384,128]{1,0:T(8,128)(2,1)S(1)}, bf16[384,128]{1,0:T(8,128)(2,1)S(1)}, u32[]{:S(2)}, u32[]{:S(2)}) %collective-permute-start.18) | collective-permute-done | bytes 98336 | tf_op jit(solution)/shard_map/ppermute | solution.py:593
  41.9 1.4 %shard_map.106 = (bf16[3,192,1024]{2,1,0:T(8,128)(2,1)}, bf16[3,192,1024]{2,1,0:T(8,128)(2,1)}, bf16[3,192,1024]{2,1,0:T(8,128)(2,1)}, bf16[3,64,1024]{2,1,0:T(8...) custom-call(bf16[384,128]{1,0:T(8,128)(2,1)S(1)} %get-tuple-element.70.own, ...), custom_call_target="tpu_custom_call" | custom-call | flops 100663296 | bytes 2752512 | tf_op jit(solution)/shard_map/pallas_call | solution.py:578
  43.4 1.7 %shard_map.107 = (bf16[3,192,1024]{2,1,0:T(8,128)(2,1)}, bf16[3,192,1024]{2,1,0:T(8,128)(2,1)}, bf16[3,192,1024]{2,1,0:T(8,128)(2,1)}) custom-call(bf16[384,128]{1,0:T(8,128)(2,1)S(1)} %get-tuple-element.64.own, bf16[384,128]{1,0:T(8,128)(2,1)S(1)} %collective-permute-done.16.got, ...), custom_call_target="tpu_custom_call", output_to_operand_aliasing={{0}: (16, {}), {1}: (17, {}), {2}: (18, {})} | custom-call | flops 100663296 | bytes 2752512 | tf_op jit(solution)/shard_map/pallas_call | solution.py:578
  (34 shorter events, 5.7 us)
Async XLA Ops:
  2.3 4.6 %collective-permute-start = (bf16[272,1024]{1,0:T(8,128)(2,1)S(1)}, bf16[272,1024]{1,0:T(8,128)(2,1)S(1)}, u32[]{:S(2)}, u32[]{:S(2)}) collective-permute-start(bf16[272,1024]{1,0:T(8,128)(2,1)S(1)} %get-tuple-element.43.after_ref.refs_0_.refs_6_), channel_id=1, source_target_pairs={{0,1},{1,0},{2,3},{3,2},{4,5},{5,4},{6,7},{7,6},{8,9},{9,8},{10,11... | collective-permute-start | bytes 1671176 | tf_op jit(solution)/shard_map/ppermute | solution.py:593
  2.8 8.6 %collective-permute-start.2 = (bf16[128,1024]{1,0:T(8,128)(2,1)S(1)}, bf16[128,1024]{1,0:T(8,128)(2,1)S(1)}, u32[]{:S(2)}, u32[]{:S(2)}) collective-permute-start(bf16[128,1024]{1,0:T(8,128)(2,1)S(1)} %get-tuple-element.45), channel_id=1, source_target_pairs={{0,2},{1,5},{2,0},{3,7},{4,6},{5,1},{6,4},{7,3},{8,10},{9,13},{10,... | collective-permute-start | bytes 786440 | tf_op jit(solution)/shard_map/ppermute | solution.py:612
  5.4 7.5 %collective-permute-start.1 = (bf16[128,1024]{1,0:T(8,128)(2,1)S(1)}, bf16[128,1024]{1,0:T(8,128)(2,1)S(1)}, u32[]{:S(2)}, u32[]{:S(2)}) collective-permute-start(bf16[128,1024]{1,0:T(8,128)(2,1)S(1)} %get-tuple-element.45), channel_id=1, source_target_pairs={{0,4},{1,3},{2,6},{3,1},{4,0},{5,7},{6,2},{7,5},{8,12},{9,11},{10,... | collective-permute-start | bytes 786440 | tf_op jit(solution)/shard_map/ppermute | solution.py:612
  7.5 13.9 %collective-permute-start.5 = (bf16[1168,128]{1,0:T(8,128)(2,1)S(1)}, bf16[1168,128]{1,0:T(8,128)(2,1)S(1)}, u32[]{:S(2)}, u32[]{:S(2)}) collective-permute-start(bf16[1168,128]{1,0:T(8,128)(2,1)S(1)} %get-tuple-element.50.own), channel_id=1, source_target_pairs={{0,8},{8,0},{16,24},{24,16},{1,9},{9,1},{17,25},{25,17},{2,10},{10... | collective-permute-start | bytes 897032 | tf_op jit(solution)/shard_map/ppermute | solution.py:593
  9.1 9.5 %collective-permute-start.8 = (bf16[144,1024]{1,0:T(8,128)(2,1)S(1)}, bf16[144,1024]{1,0:T(8,128)(2,1)S(1)}, u32[]{:S(2)}, u32[]{:S(2)}) collective-permute-start(bf16[144,1024]{1,0:T(8,128)(2,1)S(1)} %get-tuple-element.52), channel_id=1, source_target_pairs={{0,4},{1,3},{2,6},{3,1},{4,0},{5,7},{6,2},{7,5},{8,12},{9,11},{10,... | collective-permute-start | bytes 884744 | tf_op jit(solution)/shard_map/ppermute | solution.py:613
  9.6 9.3 %collective-permute-start.7 = (bf16[144,1024]{1,0:T(8,128)(2,1)S(1)}, bf16[144,1024]{1,0:T(8,128)(2,1)S(1)}, u32[]{:S(2)}, u32[]{:S(2)}) collective-permute-start(bf16[144,1024]{1,0:T(8,128)(2,1)S(1)} %get-tuple-element.52), channel_id=1, source_target_pairs={{0,2},{1,5},{2,0},{3,7},{4,6},{5,1},{6,4},{7,3},{8,10},{9,13},{10,... | collective-permute-start | bytes 884744 | tf_op jit(solution)/shard_map/ppermute | solution.py:613
  11.5 1.5 %collective-permute-start.3 = (bf16[64,1024]{1,0:T(8,128)(2,1)S(1)}, bf16[64,1024]{1,0:T(8,128)(2,1)S(1)}, u32[]{:S(2)}, u32[]{:S(2)}) collective-permute-start(bf16[64,1024]{1,0:T(8,128)(2,1)S(1)} %get-tuple-element.46), channel_id=1, source_target_pairs={{0,1},{1,0},{2,3},{3,2},{4,5},{5,4},{6,7},{7,6},{8,9},{9,8},{10,11... | collective-permute-start | bytes 393224 | tf_op jit(solution)/shard_map/ppermute | solution.py:593
  13.0 1.3 %collective-permute-start.4 = (bf16[64,1024]{1,0:T(8,128)(2,1)S(1)}, bf16[64,1024]{1,0:T(8,128)(2,1)S(1)}, u32[]{:S(2)}, u32[]{:S(2)}) collective-permute-start(bf16[64,1024]{1,0:T(8,128)(2,1)S(1)} %get-tuple-element.47), channel_id=1, source_target_pairs={{0,1},{1,0},{2,3},{3,2},{4,5},{5,4},{6,7},{7,6},{8,9},{9,8},{10,11... | collective-permute-start | bytes 393224 | tf_op jit(solution)/shard_map/ppermute | solution.py:593
  15.1 6.3 %collective-permute-start.6 = (bf16[384,128]{1,0:T(8,128)(2,1)S(1)}, bf16[384,128]{1,0:T(8,128)(2,1)S(1)}, u32[]{:S(2)}, u32[]{:S(2)}) collective-permute-start(bf16[384,128]{1,0:T(8,128)(2,1)S(1)} %get-tuple-element.51.near_own), channel_id=1, source_target_pairs={{0,8},{8,0},{16,24},{24,16},{1,9},{9,1},{17,25},{25,17},{2,10},{10... | collective-permute-start | bytes 294920 | tf_op jit(solution)/shard_map/ppermute | solution.py:593
  21.6 3.4 %collective-permute-start.9 = (bf16[416,1024]{1,0:T(8,128)(2,1)S(1)}, bf16[416,1024]{1,0:T(8,128)(2,1)S(1)}, u32[]{:S(2)}, u32[]{:S(2)}) collective-permute-start(bf16[416,1024]{1,0:T(8,128)(2,1)S(1)} %get-tuple-element.56.refs_0_.refs_1_), channel_id=1, source_target_pairs={{0,1},{1,0},{2,3},{3,2},{4,5},{5,4},{6,7},{7,6},{8,9},{9,8},{10,11... | collective-permute-start | bytes 2555912 | tf_op jit(solution)/shard_map/ppermute | solution.py:593
  21.7 9.6 %collective-permute-start.10 = (bf16[272,1024]{1,0:T(8,128)(2,1)S(1)}, bf16[272,1024]{1,0:T(8,128)(2,1)S(1)}, u32[]{:S(2)}, u32[]{:S(2)}) collective-permute-start(bf16[272,1024]{1,0:T(8,128)(2,1)S(1)} %get-tuple-element.55.after_ref), channel_id=1, source_target_pairs={{0,4},{1,3},{2,6},{3,1},{4,0},{5,7},{6,2},{7,5},{8,12},{9,11},{10,... | collective-permute-start | bytes 1671176 | tf_op jit(solution)/shard_map/ppermute | solution.py:622
  23.3 8.7 %collective-permute-start.11 = (bf16[768,128]{1,0:T(8,128)(2,1)S(1)}, bf16[768,128]{1,0:T(8,128)(2,1)S(1)}, u32[]{:S(2)}, u32[]{:S(2)}) collective-permute-start(bf16[768,128]{1,0:T(8,128)(2,1)S(1)} %get-tuple-element.53.refs_8_.own), channel_id=1, source_target_pairs={{0,8},{8,0},{16,24},{24,16},{1,9},{9,1},{17,25},{25,17},{2,10},{10... | collective-permute-start | bytes 589832 | tf_op jit(solution)/shard_map/ppermute | solution.py:593
  25.7 12.3 %collective-permute-start.17 = (bf16[1152,128]{1,0:T(8,128)(2,1)S(1)}, bf16[1152,128]{1,0:T(8,128)(2,1)S(1)}, u32[]{:S(2)}, u32[]{:S(2)}) collective-permute-start(bf16[1152,128]{1,0:T(8,128)(2,1)S(1)} %get-tuple-element.67.own), channel_id=1, source_target_pairs={{0,8},{8,0},{16,24},{24,16},{1,9},{9,1},{17,25},{25,17},{2,10},{10... | collective-permute-start | bytes 884744 | tf_op jit(solution)/shard_map/ppermute | solution.py:593
  31.3 2.1 %collective-permute-start.15 = (bf16[80,1024]{1,0:T(8,128)(2,1)S(1)}, bf16[80,1024]{1,0:T(8,128)(2,1)S(1)}, u32[]{:S(2)}, u32[]{:S(2)}) collective-permute-start(bf16[80,1024]{1,0:T(8,128)(2,1)S(1)} %get-tuple-element.63.refs_3_), channel_id=1, source_target_pairs={{0,1},{1,0},{2,3},{3,2},{4,5},{5,4},{6,7},{7,6},{8,9},{9,8},{10,11... | collective-permute-start | bytes 491528 | tf_op jit(solution)/shard_map/ppermute | solution.py:593
  31.4 1.6 %collective-permute-start.13 = (bf16[64,1024]{1,0:T(8,128)(2,1)S(1)}, bf16[64,1024]{1,0:T(8,128)(2,1)S(1)}, u32[]{:S(2)}, u32[]{:S(2)}) collective-permute-start(bf16[64,1024]{1,0:T(8,128)(2,1)S(1)} %get-tuple-element.61.refs_1_), channel_id=1, source_target_pairs={{0,1},{1,0},{2,3},{3,2},{4,5},{5,4},{6,7},{7,6},{8,9},{9,8},{10,11... | collective-permute-start | bytes 393224 | tf_op jit(solution)/shard_map/ppermute | solution.py:593
  31.9 1.3 %collective-permute-start.14 = (bf16[64,1024]{1,0:T(8,128)(2,1)S(1)}, bf16[64,1024]{1,0:T(8,128)(2,1)S(1)}, u32[]{:S(2)}, u32[]{:S(2)}) collective-permute-start(bf16[64,1024]{1,0:T(8,128)(2,1)S(1)} %get-tuple-element.62.refs_2_), channel_id=1, source_target_pairs={{0,1},{1,0},{2,3},{3,2},{4,5},{5,4},{6,7},{7,6},{8,9},{9,8},{10,11... | collective-permute-start | bytes 393224 | tf_op jit(solution)/shard_map/ppermute | solution.py:593
  32.0 1.5 %collective-permute-start.12 = (bf16[64,1024]{1,0:T(8,128)(2,1)S(1)}, bf16[64,1024]{1,0:T(8,128)(2,1)S(1)}, u32[]{:S(2)}, u32[]{:S(2)}) collective-permute-start(bf16[64,1024]{1,0:T(8,128)(2,1)S(1)} %get-tuple-element.58.after_ref.refs_0_), channel_id=1, source_target_pairs={{0,1},{1,0},{2,3},{3,2},{4,5},{5,4},{6,7},{7,6},{8,9},{9,8},{10,11... | collective-permute-start | bytes 393224 | tf_op jit(solution)/shard_map/ppermute | solution.py:593
  34.1 5.7 %collective-permute-start.19 = (bf16[384,128]{1,0:T(8,128)(2,1)S(1)}, bf16[384,128]{1,0:T(8,128)(2,1)S(1)}, u32[]{:S(2)}, u32[]{:S(2)}) collective-permute-start(bf16[384,128]{1,0:T(8,128)(2,1)S(1)} %get-tuple-element.71.own), channel_id=1, source_target_pairs={{0,8},{8,0},{16,24},{24,16},{1,9},{9,1},{17,25},{25,17},{2,10},{10... | collective-permute-start | bytes 294920 | tf_op jit(solution)/shard_map/ppermute | solution.py:593
  35.9 6.0 %collective-permute-start.18 = (bf16[384,128]{1,0:T(8,128)(2,1)S(1)}, bf16[384,128]{1,0:T(8,128)(2,1)S(1)}, u32[]{:S(2)}, u32[]{:S(2)}) collective-permute-start(bf16[384,128]{1,0:T(8,128)(2,1)S(1)} %get-tuple-element.70.own), channel_id=1, source_target_pairs={{0,8},{8,0},{16,24},{24,16},{1,9},{9,1},{17,25},{25,17},{2,10},{10... | collective-permute-start | bytes 294920 | tf_op jit(solution)/shard_map/ppermute | solution.py:593
  36.2 7.2 %collective-permute-start.16 = (bf16[384,128]{1,0:T(8,128)(2,1)S(1)}, bf16[384,128]{1,0:T(8,128)(2,1)S(1)}, u32[]{:S(2)}, u32[]{:S(2)}) collective-permute-start(bf16[384,128]{1,0:T(8,128)(2,1)S(1)} %get-tuple-element.64.own), channel_id=1, source_target_pairs={{0,8},{8,0},{16,24},{24,16},{1,9},{9,1},{17,25},{25,17},{2,10},{10... | collective-permute-start | bytes 294920 | tf_op jit(solution)/shard_map/ppermute | solution.py:593
  38.0 1.9 %copy-start = (bf16[3,192,1024]{2,1,0:T(8,128)(2,1)S(1)}, bf16[3,192,1024]{2,1,0:T(8,128)(2,1)}, u32[]{:S(2)}) copy-start(bf16[3,192,1024]{2,1,0:T(8,128)(2,1)} %refs_9_.5) | copy-start | bytes 3538948
  38.0 1.9 %copy-start.1 = (bf16[3,192,1024]{2,1,0:T(8,128)(2,1)S(1)}, bf16[3,192,1024]{2,1,0:T(8,128)(2,1)}, u32[]{:S(2)}) copy-start(bf16[3,192,1024]{2,1,0:T(8,128)(2,1)} %refs_10_.5) | copy-start | bytes 3538948

commit v14 on v12

--- a/solution.py
+++ b/solution.py
@@ -374,7 +374,7 @@
 
 def onward_kernel(kinds, after_ref, own, got, near_own, near_got, *refs):
     x0_ref, x1_ref, s0_ref, y0_ref, y1_ref = refs[:5]
-    pair_ref, rest_ref, out_ref, first_ref, sum_ref, gate_ref = refs[5 + len(kinds) :]
+    pair_ref, rest_ref, out_ref, first_ref, sum_ref, gate_ref = refs[6 + len(kinds) :]
     count, rows = x0_ref.shape[0], y0_ref.shape[0]
     gates = views(refs[5 : 5 + len(kinds)], kinds, count)[2]
     gate_ref[...] = jnp.broadcast_to(gate_row(gates), gate_ref.shape)
@@ -390,10 +390,10 @@
     sum_ref[...] = near_own[...].astype(jnp.float32) + near_got[...].astype(jnp.float32)
 
 
-def pick_onward(after, pair, near_pair, near_x, other_x, near_y, chunk):
+def pick_onward(after, pair, near_pair, near_x, other_x, near_y, chunk, held):
     count, width = other_x.shape
     rows = near_y[0].shape[0]
-    operands = [*pair, *near_pair, *near_x, other_x, *near_y, *values_of(chunk)]
+    operands = [*pair, *near_pair, *near_x, other_x, *near_y, *values_of(chunk), held]
     return pl.pallas_call(
         functools.partial(onward_kernel, kinds_of(chunk)),
         in_specs=[unread()] + [whole()] * len(operands),
@@ -610,18 +610,19 @@
     along = [[(p, p ^ (2 if p % 2 == k else 4)) for p in range(n_data)] for k in (0, 1)]
     near_x = [lax.ppermute(x_own, "dp", pairs) for pairs in along]
     near_y = [lax.ppermute(y_own, "dp", pairs) for pairs in along]
+    other_x = other(near_x[0])
     send, token = partials(weights, token, [("x", near_x[0]), ("", near_x[1])], (2,), count)
     near_pair = (send, partner(send))
+    early = [("x", near_x[1]), ("x", other_x)]
+    early_send, token = partials(weights, token, early, (4,), count)
     x_pair, rest, picked, first_sum, near_sum, gate = pick_onward(
-        token, first_pair, near_pair, near_x, other(near_x[0]), near_y, first
+        token, first_pair, near_pair, near_x, other_x, near_y, first, early_send
     )
     far = lax.ppermute(picked, "dp", along[1])
     rest_other = other(rest)
-    early = [("x of xyy", rest), ("second x", x_pair)]
     late = [("y, y of xyy", rest), ("x, y, y", rest_other)]
-    send, token = partials(weights, picked, early, (4,), count)
-    early_pair = (send, partner(send))
-    send, token = partials(weights, token, late, (6,), count)
+    early_pair = (early_send, partner(early_send))
+    send, token = partials(weights, picked, late, (6,), count)
     late_pair = (send, partner(send))
     pieces = passed_on(token, far, (count // 2, count // 2, count // 2, count // 2 + slots))
     acc, early_sum, token = first_grads(

time: 43.3 us -> 43.3 us (level)
  waiting for transfers between devices: 11.8 us -> 11.3 us
where the time goes in v14:
time: 43.3 us; the launch traced here: 43.1 us
  starting transfers between devices  21 us (48%)
  waiting for transfers between devices  11.3 us (26%)
  Pallas kernels  9.9 us (23%)
  between operations  0.75 us (2%)
    ppermute x14, starting transfers between devices, from_masked(): return lax.ppermute(value, axis, pairs)  13.5 us
    ppermute x1, waiting for transfers between devices, dense_plan(): far = lax.ppermute(picked, 'dp', along[1])  4.47 us
    ppermute x2, starting transfers between devices, dense_plan(): near_x = [lax.ppermute(x_own, 'dp', pairs) for pairs in along]  4.08 us
    pallas_call x3, Pallas kernels, update_piece(): pl.pallas_call(functools.partial(update_kernel, kinds, count, piece, last...  3.76 us
    ppermute x14, waiting for transfers between devices, from_masked(): return lax.ppermute(value, axis, pairs)  2.97 us
    pallas_call x4, Pallas kernels, partials(): pl.pallas_call(functools.partial(partial_kernel, kinds, count, tokened),...  1.97 us
    ppermute x2, waiting for transfers between devices, dense_plan(): near_x = [lax.ppermute(x_own, 'dp', pairs) for pairs in along]  1.95 us
    ppermute x2, waiting for transfers between devices, dense_plan(): near_y = [lax.ppermute(y_own, 'dp', pairs) for pairs in along]  1.94 us
  transfers between devices with their start and end apart: 19, of which 11 were waited for; matrix products, arithmetic and copies ran while one was open for 0% of the time, Pallas kernels for 15%

profile of v14, /device:TPU:0, one launch (start us, length us, event | category | flops | bytes accessed | tf_op | source)
XLA Modules:
  0.0 43.1 jit_solution(16724459064771631130)
XLA Ops:
  0.6 1.7 %shard_map.94 = (bf16[128,1024]{1,0:T(8,128)(2,1)S(1)}, bf16[144,1024]{1,0:T(8,128)(2,1)S(1)}, bf16[272,1024]{1,0:T(8,128)(2,1)S(1)}, bf16[3,192,1024]{2,1,0:T(8,128)(2,1)S(1)}) custom-call(s32[4,128]{1,0:T(4,128)} %bitcast.2, bf16[4,128]{1,0:T(4,128)(2,1)} %bitcast.3, bf16[128,2048]{1,0:T(8,128)(2,1)} %tokens_ref.1, bf16[128,2048]{1,0:T(8,128)(2,1)} %cot_ref.1, ...), custom_call_target="tpu_custom_call" | custom-call | flops 1000 | bytes 1048576 | tf_op jit(solution)/shard_map/pallas_call | solution.py:209
  2.3 0.5 %collective-permute-start = (bf16[272,1024]{1,0:T(8,128)(2,1)S(1)}, bf16[272,1024]{1,0:T(8,128)(2,1)S(1)}, u32[]{:S(2)}, u32[]{:S(2)}) collective-permute-start(bf16[272,1024]{1,0:T(8,128)(2,1)S(1)} %get-tuple-element.41.after_ref.refs_0_.refs_5_), channel_id=1, source_target_pairs={{0,1},{1,0},{2,3},{3,2},{4,5},{5,4},{6,7},{7,6},{8,9},{9,8},{10,11... | collective-permute-start | bytes 1671176 | tf_op jit(solution)/shard_map/ppermute | solution.py:592
  2.8 2.6 %collective-permute-start.1 = (bf16[128,1024]{1,0:T(8,128)(2,1)S(1)}, bf16[128,1024]{1,0:T(8,128)(2,1)S(1)}, u32[]{:S(2)}, u32[]{:S(2)}) collective-permute-start(bf16[128,1024]{1,0:T(8,128)(2,1)S(1)} %get-tuple-element.43), channel_id=1, source_target_pairs={{0,2},{1,5},{2,0},{3,7},{4,6},{5,1},{6,4},{7,3},{8,10},{9,13},{10,... | collective-permute-start | bytes 786440 | tf_op jit(solution)/shard_map/ppermute | solution.py:611
  5.4 1.5 %collective-permute-start.2 = (bf16[128,1024]{1,0:T(8,128)(2,1)S(1)}, bf16[128,1024]{1,0:T(8,128)(2,1)S(1)}, u32[]{:S(2)}, u32[]{:S(2)}) collective-permute-start(bf16[128,1024]{1,0:T(8,128)(2,1)S(1)} %get-tuple-element.43), channel_id=1, source_target_pairs={{0,4},{1,3},{2,6},{3,1},{4,0},{5,7},{6,2},{7,5},{8,12},{9,11},{10,... | collective-permute-start | bytes 786440 | tf_op jit(solution)/shard_map/ppermute | solution.py:611
  6.9 0.5 %shard_map.95 = (bf16[1168,128]{1,0:T(8,128)(2,1)S(1)}, f32[8,128]{1,0:T(8,128)S(1)}) custom-call(bf16[3,192,1024]{2,1,0:T(8,128)(2,1)S(1)} %get-tuple-element.40.w_ref, bf16[272,1024]{1,0:T(8,128)(2,1)S(1)} %get-tuple-element.41.after_ref.refs_0_.refs_5_, bf16[272,1024]{1,0:T(8,128)(2,1)S(1)} %get-tuple-element.41.after_ref.refs_0_.refs_5_, ...), custom_call_target="tpu_custom_call" | custom-call | flops 301989888 | bytes 884736 | tf_op jit(solution)/shard_map/pallas_call | solution.py:312
  7.5 1.6 %collective-permute-start.4 = (bf16[1168,128]{1,0:T(8,128)(2,1)S(1)}, bf16[1168,128]{1,0:T(8,128)(2,1)S(1)}, u32[]{:S(2)}, u32[]{:S(2)}) collective-permute-start(bf16[1168,128]{1,0:T(8,128)(2,1)S(1)} %get-tuple-element.46.own), channel_id=1, source_target_pairs={{0,8},{8,0},{16,24},{24,16},{1,9},{9,1},{17,25},{25,17},{2,10},{10... | collective-permute-start | bytes 897032 | tf_op jit(solution)/shard_map/ppermute | solution.py:592
  9.6 1.4 %collective-permute-start.6 = (bf16[144,1024]{1,0:T(8,128)(2,1)S(1)}, bf16[144,1024]{1,0:T(8,128)(2,1)S(1)}, u32[]{:S(2)}, u32[]{:S(2)}) collective-permute-start(bf16[144,1024]{1,0:T(8,128)(2,1)S(1)} %get-tuple-element.48), channel_id=1, source_target_pairs={{0,2},{1,5},{2,0},{3,7},{4,6},{5,1},{6,4},{7,3},{8,10},{9,13},{10,... | collective-permute-start | bytes 884744 | tf_op jit(solution)/shard_map/ppermute | solution.py:612
  11.5 1.5 %collective-permute-done.2.refs_1_.refs_0_ = bf16[128,1024]{1,0:T(8,128)(2,1)S(1)} collective-permute-done((bf16[128,1024]{1,0:T(8,128)(2,1)S(1)}, bf16[128,1024]{1,0:T(8,128)(2,1)S(1)}, u32[]{:S(2)}, u32[]{:S(2)}) %collective-permute-start.2) | collective-permute-done | bytes 262176 | tf_op jit(solution)/shard_map/ppermute | solution.py:611
  13.3 3.2 %collective-permute-start.5 = (bf16[384,128]{1,0:T(8,128)(2,1)S(1)}, bf16[384,128]{1,0:T(8,128)(2,1)S(1)}, u32[]{:S(2)}, u32[]{:S(2)}) collective-permute-start(bf16[384,128]{1,0:T(8,128)(2,1)S(1)} %get-tuple-element.47.near_own), channel_id=1, source_target_pairs={{0,8},{8,0},{16,24},{24,16},{1,9},{9,1},{17,25},{25,17},{2,10},{10... | collective-permute-start | bytes 294920 | tf_op jit(solution)/shard_map/ppermute | solution.py:592
  16.9 1.7 %collective-permute-done.7.refs_4_ = bf16[144,1024]{1,0:T(8,128)(2,1)S(1)} collective-permute-done((bf16[144,1024]{1,0:T(8,128)(2,1)S(1)}, bf16[144,1024]{1,0:T(8,128)(2,1)S(1)}, u32[]{:S(2)}, u32[]{:S(2)}) %collective-permute-start.7) | collective-permute-done | bytes 294944 | tf_op jit(solution)/shard_map/ppermute | solution.py:612
  19.4 1.6 %collective-permute-start.9 = (bf16[272,1024]{1,0:T(8,128)(2,1)S(1)}, bf16[272,1024]{1,0:T(8,128)(2,1)S(1)}, u32[]{:S(2)}, u32[]{:S(2)}) collective-permute-start(bf16[272,1024]{1,0:T(8,128)(2,1)S(1)} %get-tuple-element.51.after_ref), channel_id=1, source_target_pairs={{0,4},{1,3},{2,6},{3,1},{4,0},{5,7},{6,2},{7,5},{8,12},{9,11},{10,... | collective-permute-start | bytes 1671176 | tf_op jit(solution)/shard_map/ppermute | solution.py:621
  21.0 2.0 %collective-permute-start.10 = (bf16[768,128]{1,0:T(8,128)(2,1)S(1)}, bf16[768,128]{1,0:T(8,128)(2,1)S(1)}, u32[]{:S(2)}, u32[]{:S(2)}) collective-permute-start(bf16[768,128]{1,0:T(8,128)(2,1)S(1)} %get-tuple-element.49.refs_7_.own), channel_id=1, source_target_pairs={{0,8},{8,0},{16,24},{24,16},{1,9},{9,1},{17,25},{25,17},{2,10},{10... | collective-permute-start | bytes 589832 | tf_op jit(solution)/shard_map/ppermute | solution.py:592
  23.0 0.7 %shard_map.99 = (bf16[1152,128]{1,0:T(8,128)(2,1)S(1)}, f32[8,128]{1,0:T(8,128)S(1)}) custom-call(bf16[3,192,1024]{2,1,0:T(8,128)(2,1)S(1)} %get-tuple-element.40.w_ref, bf16[272,1024]{1,0:T(8,128)(2,1)S(1)} %get-tuple-element.51.after_ref, bf16[416,1024]{1,0:T(8,128)(2,1)S(1)} %get-tuple-element.52.refs_0_.refs_1_, ...), custom_call_target="tpu_custom_call" | custom-call | flops 301989888 | bytes 884736 | tf_op jit(solution)/shard_map/pallas_call | solution.py:312
  23.7 0.8 %collective-permute-start.16 = (bf16[1152,128]{1,0:T(8,128)(2,1)S(1)}, bf16[1152,128]{1,0:T(8,128)(2,1)S(1)}, u32[]{:S(2)}, u32[]{:S(2)}) collective-permute-start(bf16[1152,128]{1,0:T(8,128)(2,1)S(1)} %get-tuple-element.63.own), channel_id=1, source_target_pairs={{0,8},{8,0},{16,24},{24,16},{1,9},{9,1},{17,25},{25,17},{2,10},{10... | collective-permute-start | bytes 884744 | tf_op jit(solution)/shard_map/ppermute | solution.py:592
  24.5 4.5 %collective-permute-done.9.in_ref = bf16[272,1024]{1,0:T(8,128)(2,1)S(1)} collective-permute-done((bf16[272,1024]{1,0:T(8,128)(2,1)S(1)}, bf16[272,1024]{1,0:T(8,128)(2,1)S(1)}, u32[]{:S(2)}, u32[]{:S(2)}) %collective-permute-start.9) | collective-permute-done | bytes 557088 | tf_op jit(solution)/shard_map/ppermute | solution.py:621
  30.1 0.5 %shard_map.101 = (f32[3,192,1024]{2,1,0:T(8,128)S(1)}, f32[768,128]{1,0:T(8,128)S(1)}, f32[8,128]{1,0:T(8,128)S(1)}) custom-call(f32[8,256]{1,0:T(8,128)S(1)} %get-tuple-element.50.gate_ref, bf16[64,1024]{1,0:T(8,128)(2,1)S(1)} %get-tuple-element.54.after_ref.refs_0_, f32[1152,128]{1,0:T(8,128)S(1)} %get-tuple-element.55.sum_ref, ...), custom_call_target="tpu_custom_call" | custom-call | flops 301989888 | bytes 2359296 | tf_op jit(solution)/shard_map/pallas_call | solution.py:448
  31.2 0.7 %shard_map.102 = (bf16[384,128]{1,0:T(8,128)(2,1)S(1)}, bf16[384,128]{1,0:T(8,128)(2,1)S(1)}, bf16[384,128]{1,0:T(8,128)(2,1)S(1)}) custom-call(bf16[3,192,1024]{2,1,0:T(8,128)(2,1)S(1)} %get-tuple-element.40.w_ref, f32[8,128]{1,0:T(8,128)S(1)} %get-tuple-element.56.after_ref, bf16[64,1024]{1,0:T(8,128)(2,1)S(1)} %get-tuple-element.54.after_ref.refs_0_, ...), custom_call_target="tpu_custom_call" | custom-call | flops 301989888 | bytes 884736 | tf_op jit(solution)/shard_map/pallas_call | solution.py:519
  31.9 2.1 %collective-permute-start.18 = (bf16[384,128]{1,0:T(8,128)(2,1)S(1)}, bf16[384,128]{1,0:T(8,128)(2,1)S(1)}, u32[]{:S(2)}, u32[]{:S(2)}) collective-permute-start(bf16[384,128]{1,0:T(8,128)(2,1)S(1)} %get-tuple-element.67.own), channel_id=1, source_target_pairs={{0,8},{8,0},{16,24},{24,16},{1,9},{9,1},{17,25},{25,17},{2,10},{10... | collective-permute-start | bytes 294920 | tf_op jit(solution)/shard_map/ppermute | solution.py:592
  34.0 1.9 %collective-permute-start.15 = (bf16[384,128]{1,0:T(8,128)(2,1)S(1)}, bf16[384,128]{1,0:T(8,128)(2,1)S(1)}, u32[]{:S(2)}, u32[]{:S(2)}) collective-permute-start(bf16[384,128]{1,0:T(8,128)(2,1)S(1)} %get-tuple-element.60.own), channel_id=1, source_target_pairs={{0,8},{8,0},{16,24},{24,16},{1,9},{9,1},{17,25},{25,17},{2,10},{10... | collective-permute-start | bytes 294920 | tf_op jit(solution)/shard_map/ppermute | solution.py:592
  36.0 1.0 %shard_map.103.refs_8_ = f32[3,192,1024]{2,1,0:T(8,128)S(1)} custom-call(f32[384,128]{1,0:T(8,128)S(1)} %get-tuple-element.61.sum_ref, f32[768,128]{1,0:T(8,128)S(1)} %get-tuple-element.62.more_ref, bf16[1152,128]{1,0:T(8,128)(2,1)S(1)} %get-tuple-element.63.own, bf16[1152,128]{1,0:T(8,128)(2,1)S(1)} %collective-permute-done.16.got, ...), custom_call_target="tpu_custom_call", output_to_operand_aliasing={{}: (8, {})} | custom-call | flops 603979776 | bytes 4718592 | tf_op jit(solution)/shard_map/pallas_call | solution.py:476
  37.6 0.7 %shard_map.104 = (bf16[3,64,1024]{2,1,0:T(8,128)(2,1)S(1)}, bf16[3,64,1024]{2,1,0:T(8,128)(2,1)S(1)}, bf16[3,64,1024]{2,1,0:T(8,128)(2,1)S(1)}) custom-call(bf16[384,128]{1,0:T(8,128)(2,1)S(1)} %get-tuple-element.67.own, bf16[384,128]{1,0:T(8,128)(2,1)S(1)} %collective-permute-done.18.got, bf16[64,1024]{1,0:T(8,128)(2,1)S(1)} %get-tuple-element.54.after_ref.refs_0_, ...), custom_call_target="tpu_custom_call" | custom-call | flops 100663296 | bytes 2752512 | tf_op jit(solution)/shard_map/pallas_call | solution.py:577
  38.3 1.4 %collective-permute-done.17.got = bf16[384,128]{1,0:T(8,128)(2,1)S(1)} collective-permute-done((bf16[384,128]{1,0:T(8,128)(2,1)S(1)}, bf16[384,128]{1,0:T(8,128)(2,1)S(1)}, u32[]{:S(2)}, u32[]{:S(2)}) %collective-permute-start.17) | collective-permute-done | bytes 98336 | tf_op jit(solution)/shard_map/ppermute | solution.py:592
  39.7 1.4 %shard_map.105 = (bf16[3,192,1024]{2,1,0:T(8,128)(2,1)}, bf16[3,192,1024]{2,1,0:T(8,128)(2,1)}, bf16[3,192,1024]{2,1,0:T(8,128)(2,1)}, bf16[3,64,1024]{2,1,0:T(8...) custom-call(bf16[384,128]{1,0:T(8,128)(2,1)S(1)} %get-tuple-element.66.own, ...), custom_call_target="tpu_custom_call" | custom-call | flops 100663296 | bytes 2752512 | tf_op jit(solution)/shard_map/pallas_call | solution.py:577
  41.4 1.7 %shard_map.106 = (bf16[3,192,1024]{2,1,0:T(8,128)(2,1)}, bf16[3,192,1024]{2,1,0:T(8,128)(2,1)}, bf16[3,192,1024]{2,1,0:T(8,128)(2,1)}) custom-call(bf16[384,128]{1,0:T(8,128)(2,1)S(1)} %get-tuple-element.60.own, bf16[384,128]{1,0:T(8,128)(2,1)S(1)} %collective-permute-done.15.got, ...), custom_call_target="tpu_custom_call", output_to_operand_aliasing={{0}: (16, {}), {1}: (17, {}), {2}: (18, {})} | custom-call | flops 100663296 | bytes 2752512 | tf_op jit(solution)/shard_map/pallas_call | solution.py:577
  (31 shorter events, 5.1 us)
Async XLA Ops:
  2.3 4.6 %collective-permute-start = (bf16[272,1024]{1,0:T(8,128)(2,1)S(1)}, bf16[272,1024]{1,0:T(8,128)(2,1)S(1)}, u32[]{:S(2)}, u32[]{:S(2)}) collective-permute-start(bf16[272,1024]{1,0:T(8,128)(2,1)S(1)} %get-tuple-element.41.after_ref.refs_0_.refs_5_), channel_id=1, source_target_pairs={{0,1},{1,0},{2,3},{3,2},{4,5},{5,4},{6,7},{7,6},{8,9},{9,8},{10,11... | collective-permute-start | bytes 1671176 | tf_op jit(solution)/shard_map/ppermute | solution.py:592
  2.8 8.6 %collective-permute-start.1 = (bf16[128,1024]{1,0:T(8,128)(2,1)S(1)}, bf16[128,1024]{1,0:T(8,128)(2,1)S(1)}, u32[]{:S(2)}, u32[]{:S(2)}) collective-permute-start(bf16[128,1024]{1,0:T(8,128)(2,1)S(1)} %get-tuple-element.43), channel_id=1, source_target_pairs={{0,2},{1,5},{2,0},{3,7},{4,6},{5,1},{6,4},{7,3},{8,10},{9,13},{10,... | collective-permute-start | bytes 786440 | tf_op jit(solution)/shard_map/ppermute | solution.py:611
  5.4 7.5 %collective-permute-start.2 = (bf16[128,1024]{1,0:T(8,128)(2,1)S(1)}, bf16[128,1024]{1,0:T(8,128)(2,1)S(1)}, u32[]{:S(2)}, u32[]{:S(2)}) collective-permute-start(bf16[128,1024]{1,0:T(8,128)(2,1)S(1)} %get-tuple-element.43), channel_id=1, source_target_pairs={{0,4},{1,3},{2,6},{3,1},{4,0},{5,7},{6,2},{7,5},{8,12},{9,11},{10,... | collective-permute-start | bytes 786440 | tf_op jit(solution)/shard_map/ppermute | solution.py:611
  7.5 11.7 %collective-permute-start.4 = (bf16[1168,128]{1,0:T(8,128)(2,1)S(1)}, bf16[1168,128]{1,0:T(8,128)(2,1)S(1)}, u32[]{:S(2)}, u32[]{:S(2)}) collective-permute-start(bf16[1168,128]{1,0:T(8,128)(2,1)S(1)} %get-tuple-element.46.own), channel_id=1, source_target_pairs={{0,8},{8,0},{16,24},{24,16},{1,9},{9,1},{17,25},{25,17},{2,10},{10... | collective-permute-start | bytes 897032 | tf_op jit(solution)/shard_map/ppermute | solution.py:592
  9.1 9.5 %collective-permute-start.7 = (bf16[144,1024]{1,0:T(8,128)(2,1)S(1)}, bf16[144,1024]{1,0:T(8,128)(2,1)S(1)}, u32[]{:S(2)}, u32[]{:S(2)}) collective-permute-start(bf16[144,1024]{1,0:T(8,128)(2,1)S(1)} %get-tuple-element.48), channel_id=1, source_target_pairs={{0,4},{1,3},{2,6},{3,1},{4,0},{5,7},{6,2},{7,5},{8,12},{9,11},{10,... | collective-permute-start | bytes 884744 | tf_op jit(solution)/shard_map/ppermute | solution.py:612
  9.6 9.3 %collective-permute-start.6 = (bf16[144,1024]{1,0:T(8,128)(2,1)S(1)}, bf16[144,1024]{1,0:T(8,128)(2,1)S(1)}, u32[]{:S(2)}, u32[]{:S(2)}) collective-permute-start(bf16[144,1024]{1,0:T(8,128)(2,1)S(1)} %get-tuple-element.48), channel_id=1, source_target_pairs={{0,2},{1,5},{2,0},{3,7},{4,6},{5,1},{6,4},{7,3},{8,10},{9,13},{10,... | collective-permute-start | bytes 884744 | tf_op jit(solution)/shard_map/ppermute | solution.py:612
  11.5 5.1 %collective-permute-start.3 = (bf16[128,1024]{1,0:T(8,128)(2,1)S(1)}, bf16[128,1024]{1,0:T(8,128)(2,1)S(1)}, u32[]{:S(2)}, u32[]{:S(2)}) collective-permute-start(bf16[128,1024]{1,0:T(8,128)(2,1)S(1)} %collective-permute-done.1.refs_0_), channel_id=1, source_target_pairs={{0,1},{1,0},{2,3},{3,2},{4,5},{5,4},{6,7},{7,6},{8,9},{9,8},{10,11... | collective-permute-start | bytes 786440 | tf_op jit(solution)/shard_map/ppermute | solution.py:592
  13.3 5.8 %collective-permute-start.5 = (bf16[384,128]{1,0:T(8,128)(2,1)S(1)}, bf16[384,128]{1,0:T(8,128)(2,1)S(1)}, u32[]{:S(2)}, u32[]{:S(2)}) collective-permute-start(bf16[384,128]{1,0:T(8,128)(2,1)S(1)} %get-tuple-element.47.near_own), channel_id=1, source_target_pairs={{0,8},{8,0},{16,24},{24,16},{1,9},{9,1},{17,25},{25,17},{2,10},{10... | collective-permute-start | bytes 294920 | tf_op jit(solution)/shard_map/ppermute | solution.py:592
  19.3 3.7 %collective-permute-start.8 = (bf16[416,1024]{1,0:T(8,128)(2,1)S(1)}, bf16[416,1024]{1,0:T(8,128)(2,1)S(1)}, u32[]{:S(2)}, u32[]{:S(2)}) collective-permute-start(bf16[416,1024]{1,0:T(8,128)(2,1)S(1)} %get-tuple-element.52.refs_0_.refs_1_), channel_id=1, source_target_pairs={{0,1},{1,0},{2,3},{3,2},{4,5},{5,4},{6,7},{7,6},{8,9},{9,8},{10,11... | collective-permute-start | bytes 2555912 | tf_op jit(solution)/shard_map/ppermute | solution.py:592
  19.4 9.6 %collective-permute-start.9 = (bf16[272,1024]{1,0:T(8,128)(2,1)S(1)}, bf16[272,1024]{1,0:T(8,128)(2,1)S(1)}, u32[]{:S(2)}, u32[]{:S(2)}) collective-permute-start(bf16[272,1024]{1,0:T(8,128)(2,1)S(1)} %get-tuple-element.51.after_ref), channel_id=1, source_target_pairs={{0,4},{1,3},{2,6},{3,1},{4,0},{5,7},{6,2},{7,5},{8,12},{9,11},{10,... | collective-permute-start | bytes 1671176 | tf_op jit(solution)/shard_map/ppermute | solution.py:621
  21.0 8.7 %collective-permute-start.10 = (bf16[768,128]{1,0:T(8,128)(2,1)S(1)}, bf16[768,128]{1,0:T(8,128)(2,1)S(1)}, u32[]{:S(2)}, u32[]{:S(2)}) collective-permute-start(bf16[768,128]{1,0:T(8,128)(2,1)S(1)} %get-tuple-element.49.refs_7_.own), channel_id=1, source_target_pairs={{0,8},{8,0},{16,24},{24,16},{1,9},{9,1},{17,25},{25,17},{2,10},{10... | collective-permute-start | bytes 589832 | tf_op jit(solution)/shard_map/ppermute | solution.py:592
  23.7 12.3 %collective-permute-start.16 = (bf16[1152,128]{1,0:T(8,128)(2,1)S(1)}, bf16[1152,128]{1,0:T(8,128)(2,1)S(1)}, u32[]{:S(2)}, u32[]{:S(2)}) collective-permute-start(bf16[1152,128]{1,0:T(8,128)(2,1)S(1)} %get-tuple-element.63.own), channel_id=1, source_target_pairs={{0,8},{8,0},{16,24},{24,16},{1,9},{9,1},{17,25},{25,17},{2,10},{10... | collective-permute-start | bytes 884744 | tf_op jit(solution)/shard_map/ppermute | solution.py:592
  29.1 2.1 %collective-permute-start.14 = (bf16[80,1024]{1,0:T(8,128)(2,1)S(1)}, bf16[80,1024]{1,0:T(8,128)(2,1)S(1)}, u32[]{:S(2)}, u32[]{:S(2)}) collective-permute-start(bf16[80,1024]{1,0:T(8,128)(2,1)S(1)} %get-tuple-element.59.refs_3_), channel_id=1, source_target_pairs={{0,1},{1,0},{2,3},{3,2},{4,5},{5,4},{6,7},{7,6},{8,9},{9,8},{10,11... | collective-permute-start | bytes 491528 | tf_op jit(solution)/shard_map/ppermute | solution.py:592
  29.1 1.6 %collective-permute-start.12 = (bf16[64,1024]{1,0:T(8,128)(2,1)S(1)}, bf16[64,1024]{1,0:T(8,128)(2,1)S(1)}, u32[]{:S(2)}, u32[]{:S(2)}) collective-permute-start(bf16[64,1024]{1,0:T(8,128)(2,1)S(1)} %get-tuple-element.57.refs_1_), channel_id=1, source_target_pairs={{0,1},{1,0},{2,3},{3,2},{4,5},{5,4},{6,7},{7,6},{8,9},{9,8},{10,11... | collective-permute-start | bytes 393224 | tf_op jit(solution)/shard_map/ppermute | solution.py:592
  29.6 1.3 %collective-permute-start.13 = (bf16[64,1024]{1,0:T(8,128)(2,1)S(1)}, bf16[64,1024]{1,0:T(8,128)(2,1)S(1)}, u32[]{:S(2)}, u32[]{:S(2)}) collective-permute-start(bf16[64,1024]{1,0:T(8,128)(2,1)S(1)} %get-tuple-element.58.refs_2_), channel_id=1, source_target_pairs={{0,1},{1,0},{2,3},{3,2},{4,5},{5,4},{6,7},{7,6},{8,9},{9,8},{10,11... | collective-permute-start | bytes 393224 | tf_op jit(solution)/shard_map/ppermute | solution.py:592
  29.7 1.5 %collective-permute-start.11 = (bf16[64,1024]{1,0:T(8,128)(2,1)S(1)}, bf16[64,1024]{1,0:T(8,128)(2,1)S(1)}, u32[]{:S(2)}, u32[]{:S(2)}) collective-permute-start(bf16[64,1024]{1,0:T(8,128)(2,1)S(1)} %get-tuple-element.54.after_ref.refs_0_), channel_id=1, source_target_pairs={{0,1},{1,0},{2,3},{3,2},{4,5},{5,4},{6,7},{7,6},{8,9},{9,8},{10,11... | collective-permute-start | bytes 393224 | tf_op jit(solution)/shard_map/ppermute | solution.py:592
  31.9 5.6 %collective-permute-start.18 = (bf16[384,128]{1,0:T(8,128)(2,1)S(1)}, bf16[384,128]{1,0:T(8,128)(2,1)S(1)}, u32[]{:S(2)}, u32[]{:S(2)}) collective-permute-start(bf16[384,128]{1,0:T(8,128)(2,1)S(1)} %get-tuple-element.67.own), channel_id=1, source_target_pairs={{0,8},{8,0},{16,24},{24,16},{1,9},{9,1},{17,25},{25,17},{2,10},{10... | collective-permute-start | bytes 294920 | tf_op jit(solution)/shard_map/ppermute | solution.py:592
  33.9 5.7 %collective-permute-start.17 = (bf16[384,128]{1,0:T(8,128)(2,1)S(1)}, bf16[384,128]{1,0:T(8,128)(2,1)S(1)}, u32[]{:S(2)}, u32[]{:S(2)}) collective-permute-start(bf16[384,128]{1,0:T(8,128)(2,1)S(1)} %get-tuple-element.66.own), channel_id=1, source_target_pairs={{0,8},{8,0},{16,24},{24,16},{1,9},{9,1},{17,25},{25,17},{2,10},{10... | collective-permute-start | bytes 294920 | tf_op jit(solution)/shard_map/ppermute | solution.py:592
  34.0 7.4 %collective-permute-start.15 = (bf16[384,128]{1,0:T(8,128)(2,1)S(1)}, bf16[384,128]{1,0:T(8,128)(2,1)S(1)}, u32[]{:S(2)}, u32[]{:S(2)}) collective-permute-start(bf16[384,128]{1,0:T(8,128)(2,1)S(1)} %get-tuple-element.60.own), channel_id=1, source_target_pairs={{0,8},{8,0},{16,24},{24,16},{1,9},{9,1},{17,25},{25,17},{2,10},{10... | collective-permute-start | bytes 294920 | tf_op jit(solution)/shard_map/ppermute | solution.py:592
  36.0 1.5 %copy-start = (bf16[3,192,1024]{2,1,0:T(8,128)(2,1)S(1)}, bf16[3,192,1024]{2,1,0:T(8,128)(2,1)}, u32[]{:S(2)}) copy-start(bf16[3,192,1024]{2,1,0:T(8,128)(2,1)} %refs_9_.5) | copy-start | bytes 3538948
  36.0 1.6 %copy-start.1 = (bf16[3,192,1024]{2,1,0:T(8,128)(2,1)S(1)}, bf16[3,192,1024]{2,1,0:T(8,128)(2,1)}, u32[]{:S(2)}) copy-start(bf16[3,192,1024]{2,1,0:T(8,128)(2,1)} %refs_10_.5) | copy-start | bytes 3538948

commit v15 on v14

--- a/solution.py
+++ b/solution.py
@@ -611,7 +611,7 @@
     near_x = [lax.ppermute(x_own, "dp", pairs) for pairs in along]
     near_y = [lax.ppermute(y_own, "dp", pairs) for pairs in along]
     other_x = other(near_x[0])
-    send, token = partials(weights, token, [("x", near_x[0]), ("", near_x[1])], (2,), count)
+    send, token = partials(weights, token, [("x", near_x[0])], (2,), count)
     near_pair = (send, partner(send))
     early = [("x", near_x[1]), ("x", other_x)]
     early_send, token = partials(weights, token, early, (4,), count)

time: 43.3 us -> 42.9 us (level)
    ppermute x2, waiting for transfers between devices: 1.94 us -> 2.38 us  [dense_plan(): near_y = [lax.ppermute(y_own, 'dp', pairs) for pairs in along]]
  transfers between devices with their start and end apart: 19 -> 19, of which waited for: 11 -> 10; matrix products, arithmetic and copies ran while one was open for 0% -> 0% of each run, Pallas kernels for 15% -> 15%
where the time goes in v15:
time: 42.9 us; the launch traced here: 42.7 us
  starting transfers between devices  20.6 us (48%)
  waiting for transfers between devices  11.4 us (27%)
  Pallas kernels  9.9 us (23%)
  between operations  0.76 us (2%)
    ppermute x14, starting transfers between devices, from_masked(): return lax.ppermute(value, axis, pairs)  13.1 us
    ppermute x1, waiting for transfers between devices, dense_plan(): far = lax.ppermute(picked, 'dp', along[1])  4.67 us
    ppermute x2, starting transfers between devices, dense_plan(): near_x = [lax.ppermute(x_own, 'dp', pairs) for pairs in along]  4.08 us
    pallas_call x3, Pallas kernels, update_piece(): pl.pallas_call(functools.partial(update_kernel, kinds, count, piece, last...  3.76 us
    ppermute x14, waiting for transfers between devices, from_masked(): return lax.ppermute(value, axis, pairs)  2.81 us
    ppermute x2, waiting for transfers between devices, dense_plan(): near_y = [lax.ppermute(y_own, 'dp', pairs) for pairs in along]  2.38 us
    pallas_call x4, Pallas kernels, partials(): pl.pallas_call(functools.partial(partial_kernel, kinds, count, tokened),...  1.97 us
    ppermute x2, starting transfers between devices, dense_plan(): near_y = [lax.ppermute(y_own, 'dp', pairs) for pairs in along]  1.86 us
  transfers between devices with their start and end apart: 19, of which 10 were waited for; matrix products, arithmetic and copies ran while one was open for 0% of the time, Pallas kernels for 15%

profile of v15, /device:TPU:0, one launch (start us, length us, event | category | flops | bytes accessed | tf_op | source)
XLA Modules:
  0.0 42.7 jit_solution(211555800872734895)
XLA Ops:
  0.6 1.7 %shard_map.94 = (bf16[128,1024]{1,0:T(8,128)(2,1)S(1)}, bf16[144,1024]{1,0:T(8,128)(2,1)S(1)}, bf16[272,1024]{1,0:T(8,128)(2,1)S(1)}, bf16[3,192,1024]{2,1,0:T(8,128)(2,1)S(1)}) custom-call(s32[4,128]{1,0:T(4,128)} %bitcast.2, bf16[4,128]{1,0:T(4,128)(2,1)} %bitcast.3, bf16[128,2048]{1,0:T(8,128)(2,1)} %tokens_ref.1, bf16[128,2048]{1,0:T(8,128)(2,1)} %cot_ref.1, ...), custom_call_target="tpu_custom_call" | custom-call | flops 1000 | bytes 1048576 | tf_op jit(solution)/shard_map/pallas_call | solution.py:209
  2.8 2.6 %collective-permute-start.1 = (bf16[128,1024]{1,0:T(8,128)(2,1)S(1)}, bf16[128,1024]{1,0:T(8,128)(2,1)S(1)}, u32[]{:S(2)}, u32[]{:S(2)}) collective-permute-start(bf16[128,1024]{1,0:T(8,128)(2,1)S(1)} %get-tuple-element.43), channel_id=1, source_target_pairs={{0,2},{1,5},{2,0},{3,7},{4,6},{5,1},{6,4},{7,3},{8,10},{9,13},{10,... | collective-permute-start | bytes 786440 | tf_op jit(solution)/shard_map/ppermute | solution.py:611
  5.4 1.5 %collective-permute-start.2 = (bf16[128,1024]{1,0:T(8,128)(2,1)S(1)}, bf16[128,1024]{1,0:T(8,128)(2,1)S(1)}, u32[]{:S(2)}, u32[]{:S(2)}) collective-permute-start(bf16[128,1024]{1,0:T(8,128)(2,1)S(1)} %get-tuple-element.43), channel_id=1, source_target_pairs={{0,4},{1,3},{2,6},{3,1},{4,0},{5,7},{6,2},{7,5},{8,12},{9,11},{10,... | collective-permute-start | bytes 786440 | tf_op jit(solution)/shard_map/ppermute | solution.py:611
  6.9 0.5 %shard_map.95 = (bf16[1168,128]{1,0:T(8,128)(2,1)S(1)}, f32[8,128]{1,0:T(8,128)S(1)}) custom-call(bf16[3,192,1024]{2,1,0:T(8,128)(2,1)S(1)} %get-tuple-element.40.w_ref, bf16[272,1024]{1,0:T(8,128)(2,1)S(1)} %get-tuple-element.41.after_ref.refs_0_.refs_5_, bf16[272,1024]{1,0:T(8,128)(2,1)S(1)} %get-tuple-element.41.after_ref.refs_0_.refs_5_, ...), custom_call_target="tpu_custom_call" | custom-call | flops 301989888 | bytes 884736 | tf_op jit(solution)/shard_map/pallas_call | solution.py:312
  7.5 1.6 %collective-permute-start.4 = (bf16[1168,128]{1,0:T(8,128)(2,1)S(1)}, bf16[1168,128]{1,0:T(8,128)(2,1)S(1)}, u32[]{:S(2)}, u32[]{:S(2)}) collective-permute-start(bf16[1168,128]{1,0:T(8,128)(2,1)S(1)} %get-tuple-element.46.own), channel_id=1, source_target_pairs={{0,8},{8,0},{16,24},{24,16},{1,9},{9,1},{17,25},{25,17},{2,10},{10... | collective-permute-start | bytes 897032 | tf_op jit(solution)/shard_map/ppermute | solution.py:592
  9.6 1.4 %collective-permute-start.6 = (bf16[144,1024]{1,0:T(8,128)(2,1)S(1)}, bf16[144,1024]{1,0:T(8,128)(2,1)S(1)}, u32[]{:S(2)}, u32[]{:S(2)}) collective-permute-start(bf16[144,1024]{1,0:T(8,128)(2,1)S(1)} %get-tuple-element.48), channel_id=1, source_target_pairs={{0,2},{1,5},{2,0},{3,7},{4,6},{5,1},{6,4},{7,3},{8,10},{9,13},{10,... | collective-permute-start | bytes 884744 | tf_op jit(solution)/shard_map/ppermute | solution.py:612
  11.8 1.1 %collective-permute-done.2.refs_0_.refs_1_ = bf16[128,1024]{1,0:T(8,128)(2,1)S(1)} collective-permute-done((bf16[128,1024]{1,0:T(8,128)(2,1)S(1)}, bf16[128,1024]{1,0:T(8,128)(2,1)S(1)}, u32[]{:S(2)}, u32[]{:S(2)}) %collective-permute-start.2) | collective-permute-done | bytes 262176 | tf_op jit(solution)/shard_map/ppermute | solution.py:611
  12.9 3.2 %collective-permute-start.5 = (bf16[384,128]{1,0:T(8,128)(2,1)S(1)}, bf16[384,128]{1,0:T(8,128)(2,1)S(1)}, u32[]{:S(2)}, u32[]{:S(2)}) collective-permute-start(bf16[384,128]{1,0:T(8,128)(2,1)S(1)} %get-tuple-element.47.near_own), channel_id=1, source_target_pairs={{0,8},{8,0},{16,24},{24,16},{1,9},{9,1},{17,25},{25,17},{2,10},{10... | collective-permute-start | bytes 294920 | tf_op jit(solution)/shard_map/ppermute | solution.py:592
  16.5 2.1 %collective-permute-done.7.refs_4_ = bf16[144,1024]{1,0:T(8,128)(2,1)S(1)} collective-permute-done((bf16[144,1024]{1,0:T(8,128)(2,1)S(1)}, bf16[144,1024]{1,0:T(8,128)(2,1)S(1)}, u32[]{:S(2)}, u32[]{:S(2)}) %collective-permute-start.7) | collective-permute-done | bytes 294944 | tf_op jit(solution)/shard_map/ppermute | solution.py:612
  19.2 1.6 %collective-permute-start.9 = (bf16[272,1024]{1,0:T(8,128)(2,1)S(1)}, bf16[272,1024]{1,0:T(8,128)(2,1)S(1)}, u32[]{:S(2)}, u32[]{:S(2)}) collective-permute-start(bf16[272,1024]{1,0:T(8,128)(2,1)S(1)} %get-tuple-element.51.after_ref), channel_id=1, source_target_pairs={{0,4},{1,3},{2,6},{3,1},{4,0},{5,7},{6,2},{7,5},{8,12},{9,11},{10,... | collective-permute-start | bytes 1671176 | tf_op jit(solution)/shard_map/ppermute | solution.py:621
  20.8 1.8 %collective-permute-start.10 = (bf16[768,128]{1,0:T(8,128)(2,1)S(1)}, bf16[768,128]{1,0:T(8,128)(2,1)S(1)}, u32[]{:S(2)}, u32[]{:S(2)}) collective-permute-start(bf16[768,128]{1,0:T(8,128)(2,1)S(1)} %get-tuple-element.49.refs_7_.own), channel_id=1, source_target_pairs={{0,8},{8,0},{16,24},{24,16},{1,9},{9,1},{17,25},{25,17},{2,10},{10... | collective-permute-start | bytes 589832 | tf_op jit(solution)/shard_map/ppermute | solution.py:592
  22.6 0.7 %shard_map.99 = (bf16[1152,128]{1,0:T(8,128)(2,1)S(1)}, f32[8,128]{1,0:T(8,128)S(1)}) custom-call(bf16[3,192,1024]{2,1,0:T(8,128)(2,1)S(1)} %get-tuple-element.40.w_ref, bf16[272,1024]{1,0:T(8,128)(2,1)S(1)} %get-tuple-element.51.after_ref, bf16[416,1024]{1,0:T(8,128)(2,1)S(1)} %get-tuple-element.52.refs_0_.refs_1_, ...), custom_call_target="tpu_custom_call" | custom-call | flops 301989888 | bytes 884736 | tf_op jit(solution)/shard_map/pallas_call | solution.py:312
  23.3 0.8 %collective-permute-start.16 = (bf16[1152,128]{1,0:T(8,128)(2,1)S(1)}, bf16[1152,128]{1,0:T(8,128)(2,1)S(1)}, u32[]{:S(2)}, u32[]{:S(2)}) collective-permute-start(bf16[1152,128]{1,0:T(8,128)(2,1)S(1)} %get-tuple-element.63.own), channel_id=1, source_target_pairs={{0,8},{8,0},{16,24},{24,16},{1,9},{9,1},{17,25},{25,17},{2,10},{10... | collective-permute-start | bytes 884744 | tf_op jit(solution)/shard_map/ppermute | solution.py:592
  24.1 4.7 %collective-permute-done.9.in_ref = bf16[272,1024]{1,0:T(8,128)(2,1)S(1)} collective-permute-done((bf16[272,1024]{1,0:T(8,128)(2,1)S(1)}, bf16[272,1024]{1,0:T(8,128)(2,1)S(1)}, u32[]{:S(2)}, u32[]{:S(2)}) %collective-permute-start.9) | collective-permute-done | bytes 557088 | tf_op jit(solution)/shard_map/ppermute | solution.py:621
  29.9 0.6 %shard_map.101 = (f32[3,192,1024]{2,1,0:T(8,128)S(1)}, f32[768,128]{1,0:T(8,128)S(1)}, f32[8,128]{1,0:T(8,128)S(1)}) custom-call(f32[8,256]{1,0:T(8,128)S(1)} %get-tuple-element.50.gate_ref, bf16[64,1024]{1,0:T(8,128)(2,1)S(1)} %get-tuple-element.54.after_ref.refs_0_, f32[1152,128]{1,0:T(8,128)S(1)} %get-tuple-element.55.sum_ref, ...), custom_call_target="tpu_custom_call" | custom-call | flops 301989888 | bytes 2359296 | tf_op jit(solution)/shard_map/pallas_call | solution.py:448
  30.9 0.7 %shard_map.102 = (bf16[384,128]{1,0:T(8,128)(2,1)S(1)}, bf16[384,128]{1,0:T(8,128)(2,1)S(1)}, bf16[384,128]{1,0:T(8,128)(2,1)S(1)}) custom-call(bf16[3,192,1024]{2,1,0:T(8,128)(2,1)S(1)} %get-tuple-element.40.w_ref, f32[8,128]{1,0:T(8,128)S(1)} %get-tuple-element.56.after_ref, bf16[64,1024]{1,0:T(8,128)(2,1)S(1)} %get-tuple-element.54.after_ref.refs_0_, ...), custom_call_target="tpu_custom_call" | custom-call | flops 301989888 | bytes 884736 | tf_op jit(solution)/shard_map/pallas_call | solution.py:519
  31.6 1.9 %collective-permute-start.18 = (bf16[384,128]{1,0:T(8,128)(2,1)S(1)}, bf16[384,128]{1,0:T(8,128)(2,1)S(1)}, u32[]{:S(2)}, u32[]{:S(2)}) collective-permute-start(bf16[384,128]{1,0:T(8,128)(2,1)S(1)} %get-tuple-element.67.own), channel_id=1, source_target_pairs={{0,8},{8,0},{16,24},{24,16},{1,9},{9,1},{17,25},{25,17},{2,10},{10... | collective-permute-start | bytes 294920 | tf_op jit(solution)/shard_map/ppermute | solution.py:592
  33.7 1.9 %collective-permute-start.15 = (bf16[384,128]{1,0:T(8,128)(2,1)S(1)}, bf16[384,128]{1,0:T(8,128)(2,1)S(1)}, u32[]{:S(2)}, u32[]{:S(2)}) collective-permute-start(bf16[384,128]{1,0:T(8,128)(2,1)S(1)} %get-tuple-element.60.own), channel_id=1, source_target_pairs={{0,8},{8,0},{16,24},{24,16},{1,9},{9,1},{17,25},{25,17},{2,10},{10... | collective-permute-start | bytes 294920 | tf_op jit(solution)/shard_map/ppermute | solution.py:592
  35.6 1.0 %shard_map.103.refs_8_ = f32[3,192,1024]{2,1,0:T(8,128)S(1)} custom-call(f32[384,128]{1,0:T(8,128)S(1)} %get-tuple-element.61.sum_ref, f32[768,128]{1,0:T(8,128)S(1)} %get-tuple-element.62.more_ref, bf16[1152,128]{1,0:T(8,128)(2,1)S(1)} %get-tuple-element.63.own, bf16[1152,128]{1,0:T(8,128)(2,1)S(1)} %collective-permute-done.16.got, ...), custom_call_target="tpu_custom_call", output_to_operand_aliasing={{}: (8, {})} | custom-call | flops 603979776 | bytes 4718592 | tf_op jit(solution)/shard_map/pallas_call | solution.py:476
  36.6 0.7 %collective-permute-done.18.got = bf16[384,128]{1,0:T(8,128)(2,1)S(1)} collective-permute-done((bf16[384,128]{1,0:T(8,128)(2,1)S(1)}, bf16[384,128]{1,0:T(8,128)(2,1)S(1)}, u32[]{:S(2)}, u32[]{:S(2)}) %collective-permute-start.18) | collective-permute-done | bytes 98336 | tf_op jit(solution)/shard_map/ppermute | solution.py:592
  37.3 0.7 %shard_map.104 = (bf16[3,64,1024]{2,1,0:T(8,128)(2,1)S(1)}, bf16[3,64,1024]{2,1,0:T(8,128)(2,1)S(1)}, bf16[3,64,1024]{2,1,0:T(8,128)(2,1)S(1)}) custom-call(bf16[384,128]{1,0:T(8,128)(2,1)S(1)} %get-tuple-element.67.own, bf16[384,128]{1,0:T(8,128)(2,1)S(1)} %collective-permute-done.18.got, bf16[64,1024]{1,0:T(8,128)(2,1)S(1)} %get-tuple-element.54.after_ref.refs_0_, ...), custom_call_target="tpu_custom_call" | custom-call | flops 100663296 | bytes 2752512 | tf_op jit(solution)/shard_map/pallas_call | solution.py:577
  38.0 1.4 %collective-permute-done.17.got = bf16[384,128]{1,0:T(8,128)(2,1)S(1)} collective-permute-done((bf16[384,128]{1,0:T(8,128)(2,1)S(1)}, bf16[384,128]{1,0:T(8,128)(2,1)S(1)}, u32[]{:S(2)}, u32[]{:S(2)}) %collective-permute-start.17) | collective-permute-done | bytes 98336 | tf_op jit(solution)/shard_map/ppermute | solution.py:592
  39.4 1.4 %shard_map.105 = (bf16[3,192,1024]{2,1,0:T(8,128)(2,1)}, bf16[3,192,1024]{2,1,0:T(8,128)(2,1)}, bf16[3,192,1024]{2,1,0:T(8,128)(2,1)}, bf16[3,64,1024]{2,1,0:T(8...) custom-call(bf16[384,128]{1,0:T(8,128)(2,1)S(1)} %get-tuple-element.66.own, ...), custom_call_target="tpu_custom_call" | custom-call | flops 100663296 | bytes 2752512 | tf_op jit(solution)/shard_map/pallas_call | solution.py:577
  41.1 1.7 %shard_map.106 = (bf16[3,192,1024]{2,1,0:T(8,128)(2,1)}, bf16[3,192,1024]{2,1,0:T(8,128)(2,1)}, bf16[3,192,1024]{2,1,0:T(8,128)(2,1)}) custom-call(bf16[384,128]{1,0:T(8,128)(2,1)S(1)} %get-tuple-element.60.own, bf16[384,128]{1,0:T(8,128)(2,1)S(1)} %collective-permute-done.15.got, ...), custom_call_target="tpu_custom_call", output_to_operand_aliasing={{0}: (16, {}), {1}: (17, {}), {2}: (18, {})} | custom-call | flops 100663296 | bytes 2752512 | tf_op jit(solution)/shard_map/pallas_call | solution.py:577
  (31 shorter events, 4.7 us)
Async XLA Ops:
  2.3 4.6 %collective-permute-start = (bf16[272,1024]{1,0:T(8,128)(2,1)S(1)}, bf16[272,1024]{1,0:T(8,128)(2,1)S(1)}, u32[]{:S(2)}, u32[]{:S(2)}) collective-permute-start(bf16[272,1024]{1,0:T(8,128)(2,1)S(1)} %get-tuple-element.41.after_ref.refs_0_.refs_5_), channel_id=1, source_target_pairs={{0,1},{1,0},{2,3},{3,2},{4,5},{5,4},{6,7},{7,6},{8,9},{9,8},{10,11... | collective-permute-start | bytes 1671176 | tf_op jit(solution)/shard_map/ppermute | solution.py:592
  2.8 8.6 %collective-permute-start.1 = (bf16[128,1024]{1,0:T(8,128)(2,1)S(1)}, bf16[128,1024]{1,0:T(8,128)(2,1)S(1)}, u32[]{:S(2)}, u32[]{:S(2)}) collective-permute-start(bf16[128,1024]{1,0:T(8,128)(2,1)S(1)} %get-tuple-element.43), channel_id=1, source_target_pairs={{0,2},{1,5},{2,0},{3,7},{4,6},{5,1},{6,4},{7,3},{8,10},{9,13},{10,... | collective-permute-start | bytes 786440 | tf_op jit(solution)/shard_map/ppermute | solution.py:611
  5.4 7.5 %collective-permute-start.2 = (bf16[128,1024]{1,0:T(8,128)(2,1)S(1)}, bf16[128,1024]{1,0:T(8,128)(2,1)S(1)}, u32[]{:S(2)}, u32[]{:S(2)}) collective-permute-start(bf16[128,1024]{1,0:T(8,128)(2,1)S(1)} %get-tuple-element.43), channel_id=1, source_target_pairs={{0,4},{1,3},{2,6},{3,1},{4,0},{5,7},{6,2},{7,5},{8,12},{9,11},{10,... | collective-permute-start | bytes 786440 | tf_op jit(solution)/shard_map/ppermute | solution.py:611
  7.5 11.4 %collective-permute-start.4 = (bf16[1168,128]{1,0:T(8,128)(2,1)S(1)}, bf16[1168,128]{1,0:T(8,128)(2,1)S(1)}, u32[]{:S(2)}, u32[]{:S(2)}) collective-permute-start(bf16[1168,128]{1,0:T(8,128)(2,1)S(1)} %get-tuple-element.46.own), channel_id=1, source_target_pairs={{0,8},{8,0},{16,24},{24,16},{1,9},{9,1},{17,25},{25,17},{2,10},{10... | collective-permute-start | bytes 897032 | tf_op jit(solution)/shard_map/ppermute | solution.py:592
  9.1 9.5 %collective-permute-start.7 = (bf16[144,1024]{1,0:T(8,128)(2,1)S(1)}, bf16[144,1024]{1,0:T(8,128)(2,1)S(1)}, u32[]{:S(2)}, u32[]{:S(2)}) collective-permute-start(bf16[144,1024]{1,0:T(8,128)(2,1)S(1)} %get-tuple-element.48), channel_id=1, source_target_pairs={{0,4},{1,3},{2,6},{3,1},{4,0},{5,7},{6,2},{7,5},{8,12},{9,11},{10,... | collective-permute-start | bytes 884744 | tf_op jit(solution)/shard_map/ppermute | solution.py:612
  9.6 9.3 %collective-permute-start.6 = (bf16[144,1024]{1,0:T(8,128)(2,1)S(1)}, bf16[144,1024]{1,0:T(8,128)(2,1)S(1)}, u32[]{:S(2)}, u32[]{:S(2)}) collective-permute-start(bf16[144,1024]{1,0:T(8,128)(2,1)S(1)} %get-tuple-element.48), channel_id=1, source_target_pairs={{0,2},{1,5},{2,0},{3,7},{4,6},{5,1},{6,4},{7,3},{8,10},{9,13},{10,... | collective-permute-start | bytes 884744 | tf_op jit(solution)/shard_map/ppermute | solution.py:612
  11.5 4.6 %collective-permute-start.3 = (bf16[128,1024]{1,0:T(8,128)(2,1)S(1)}, bf16[128,1024]{1,0:T(8,128)(2,1)S(1)}, u32[]{:S(2)}, u32[]{:S(2)}) collective-permute-start(bf16[128,1024]{1,0:T(8,128)(2,1)S(1)} %collective-permute-done.1.refs_0_), channel_id=1, source_target_pairs={{0,1},{1,0},{2,3},{3,2},{4,5},{5,4},{6,7},{7,6},{8,9},{9,8},{10,11... | collective-permute-start | bytes 786440 | tf_op jit(solution)/shard_map/ppermute | solution.py:592
  12.9 6.0 %collective-permute-start.5 = (bf16[384,128]{1,0:T(8,128)(2,1)S(1)}, bf16[384,128]{1,0:T(8,128)(2,1)S(1)}, u32[]{:S(2)}, u32[]{:S(2)}) collective-permute-start(bf16[384,128]{1,0:T(8,128)(2,1)S(1)} %get-tuple-element.47.near_own), channel_id=1, source_target_pairs={{0,8},{8,0},{16,24},{24,16},{1,9},{9,1},{17,25},{25,17},{2,10},{10... | collective-permute-start | bytes 294920 | tf_op jit(solution)/shard_map/ppermute | solution.py:592
  19.1 3.5 %collective-permute-start.8 = (bf16[416,1024]{1,0:T(8,128)(2,1)S(1)}, bf16[416,1024]{1,0:T(8,128)(2,1)S(1)}, u32[]{:S(2)}, u32[]{:S(2)}) collective-permute-start(bf16[416,1024]{1,0:T(8,128)(2,1)S(1)} %get-tuple-element.52.refs_0_.refs_1_), channel_id=1, source_target_pairs={{0,1},{1,0},{2,3},{3,2},{4,5},{5,4},{6,7},{7,6},{8,9},{9,8},{10,11... | collective-permute-start | bytes 2555912 | tf_op jit(solution)/shard_map/ppermute | solution.py:592
  19.2 9.6 %collective-permute-start.9 = (bf16[272,1024]{1,0:T(8,128)(2,1)S(1)}, bf16[272,1024]{1,0:T(8,128)(2,1)S(1)}, u32[]{:S(2)}, u32[]{:S(2)}) collective-permute-start(bf16[272,1024]{1,0:T(8,128)(2,1)S(1)} %get-tuple-element.51.after_ref), channel_id=1, source_target_pairs={{0,4},{1,3},{2,6},{3,1},{4,0},{5,7},{6,2},{7,5},{8,12},{9,11},{10,... | collective-permute-start | bytes 1671176 | tf_op jit(solution)/shard_map/ppermute | solution.py:621
  20.8 8.7 %collective-permute-start.10 = (bf16[768,128]{1,0:T(8,128)(2,1)S(1)}, bf16[768,128]{1,0:T(8,128)(2,1)S(1)}, u32[]{:S(2)}, u32[]{:S(2)}) collective-permute-start(bf16[768,128]{1,0:T(8,128)(2,1)S(1)} %get-tuple-element.49.refs_7_.own), channel_id=1, source_target_pairs={{0,8},{8,0},{16,24},{24,16},{1,9},{9,1},{17,25},{25,17},{2,10},{10... | collective-permute-start | bytes 589832 | tf_op jit(solution)/shard_map/ppermute | solution.py:592
  23.3 12.3 %collective-permute-start.16 = (bf16[1152,128]{1,0:T(8,128)(2,1)S(1)}, bf16[1152,128]{1,0:T(8,128)(2,1)S(1)}, u32[]{:S(2)}, u32[]{:S(2)}) collective-permute-start(bf16[1152,128]{1,0:T(8,128)(2,1)S(1)} %get-tuple-element.63.own), channel_id=1, source_target_pairs={{0,8},{8,0},{16,24},{24,16},{1,9},{9,1},{17,25},{25,17},{2,10},{10... | collective-permute-start | bytes 884744 | tf_op jit(solution)/shard_map/ppermute | solution.py:592
  28.8 2.1 %collective-permute-start.14 = (bf16[80,1024]{1,0:T(8,128)(2,1)S(1)}, bf16[80,1024]{1,0:T(8,128)(2,1)S(1)}, u32[]{:S(2)}, u32[]{:S(2)}) collective-permute-start(bf16[80,1024]{1,0:T(8,128)(2,1)S(1)} %get-tuple-element.59.refs_3_), channel_id=1, source_target_pairs={{0,1},{1,0},{2,3},{3,2},{4,5},{5,4},{6,7},{7,6},{8,9},{9,8},{10,11... | collective-permute-start | bytes 491528 | tf_op jit(solution)/shard_map/ppermute | solution.py:592
  28.9 1.6 %collective-permute-start.12 = (bf16[64,1024]{1,0:T(8,128)(2,1)S(1)}, bf16[64,1024]{1,0:T(8,128)(2,1)S(1)}, u32[]{:S(2)}, u32[]{:S(2)}) collective-permute-start(bf16[64,1024]{1,0:T(8,128)(2,1)S(1)} %get-tuple-element.57.refs_1_), channel_id=1, source_target_pairs={{0,1},{1,0},{2,3},{3,2},{4,5},{5,4},{6,7},{7,6},{8,9},{9,8},{10,11... | collective-permute-start | bytes 393224 | tf_op jit(solution)/shard_map/ppermute | solution.py:592
  29.4 1.3 %collective-permute-start.13 = (bf16[64,1024]{1,0:T(8,128)(2,1)S(1)}, bf16[64,1024]{1,0:T(8,128)(2,1)S(1)}, u32[]{:S(2)}, u32[]{:S(2)}) collective-permute-start(bf16[64,1024]{1,0:T(8,128)(2,1)S(1)} %get-tuple-element.58.refs_2_), channel_id=1, source_target_pairs={{0,1},{1,0},{2,3},{3,2},{4,5},{5,4},{6,7},{7,6},{8,9},{9,8},{10,11... | collective-permute-start | bytes 393224 | tf_op jit(solution)/shard_map/ppermute | solution.py:592
  29.5 1.5 %collective-permute-start.11 = (bf16[64,1024]{1,0:T(8,128)(2,1)S(1)}, bf16[64,1024]{1,0:T(8,128)(2,1)S(1)}, u32[]{:S(2)}, u32[]{:S(2)}) collective-permute-start(bf16[64,1024]{1,0:T(8,128)(2,1)S(1)} %get-tuple-element.54.after_ref.refs_0_), channel_id=1, source_target_pairs={{0,1},{1,0},{2,3},{3,2},{4,5},{5,4},{6,7},{7,6},{8,9},{9,8},{10,11... | collective-permute-start | bytes 393224 | tf_op jit(solution)/shard_map/ppermute | solution.py:592
  31.6 5.7 %collective-permute-start.18 = (bf16[384,128]{1,0:T(8,128)(2,1)S(1)}, bf16[384,128]{1,0:T(8,128)(2,1)S(1)}, u32[]{:S(2)}, u32[]{:S(2)}) collective-permute-start(bf16[384,128]{1,0:T(8,128)(2,1)S(1)} %get-tuple-element.67.own), channel_id=1, source_target_pairs={{0,8},{8,0},{16,24},{24,16},{1,9},{9,1},{17,25},{25,17},{2,10},{10... | collective-permute-start | bytes 294920 | tf_op jit(solution)/shard_map/ppermute | solution.py:592
  33.6 5.8 %collective-permute-start.17 = (bf16[384,128]{1,0:T(8,128)(2,1)S(1)}, bf16[384,128]{1,0:T(8,128)(2,1)S(1)}, u32[]{:S(2)}, u32[]{:S(2)}) collective-permute-start(bf16[384,128]{1,0:T(8,128)(2,1)S(1)} %get-tuple-element.66.own), channel_id=1, source_target_pairs={{0,8},{8,0},{16,24},{24,16},{1,9},{9,1},{17,25},{25,17},{2,10},{10... | collective-permute-start | bytes 294920 | tf_op jit(solution)/shard_map/ppermute | solution.py:592
  33.7 7.4 %collective-permute-start.15 = (bf16[384,128]{1,0:T(8,128)(2,1)S(1)}, bf16[384,128]{1,0:T(8,128)(2,1)S(1)}, u32[]{:S(2)}, u32[]{:S(2)}) collective-permute-start(bf16[384,128]{1,0:T(8,128)(2,1)S(1)} %get-tuple-element.60.own), channel_id=1, source_target_pairs={{0,8},{8,0},{16,24},{24,16},{1,9},{9,1},{17,25},{25,17},{2,10},{10... | collective-permute-start | bytes 294920 | tf_op jit(solution)/shard_map/ppermute | solution.py:592
  35.6 1.7 %copy-start = (bf16[3,192,1024]{2,1,0:T(8,128)(2,1)S(1)}, bf16[3,192,1024]{2,1,0:T(8,128)(2,1)}, u32[]{:S(2)}) copy-start(bf16[3,192,1024]{2,1,0:T(8,128)(2,1)} %refs_9_.5) | copy-start | bytes 3538948
  35.6 1.7 %copy-start.1 = (bf16[3,192,1024]{2,1,0:T(8,128)(2,1)S(1)}, bf16[3,192,1024]{2,1,0:T(8,128)(2,1)}, u32[]{:S(2)}) copy-start(bf16[3,192,1024]{2,1,0:T(8,128)(2,1)} %refs_10_.5) | copy-start | bytes 3538948

commit v16 on v15

--- a/solution.py
+++ b/solution.py
@@ -183,7 +183,7 @@
         pltpu.make_async_copy(cot_ref.at[:, columns], y_ref.at[0:count, :], sems.at[3]),
         pltpu.make_async_copy(tokens_ref.at[:, columns], own_ref.at[0:count, :], sems.at[4]),
         pltpu.make_async_copy(cot_ref.at[:, columns], own_ref.at[count : 2 * count, :], sems.at[5]),
-        pltpu.make_async_copy(w_hbm, w_ref, sems.at[6]),
+        *[pltpu.make_async_copy(w_hbm.at[m], w_ref.at[m], sems.at[6 + m]) for m in range(3)],
     ]
     for copy in copies:
         copy.start()
@@ -218,7 +218,7 @@
         scratch_shapes=[
             pltpu.VMEM((top, count), ids.dtype),
             pltpu.VMEM((top, count), gates.dtype),
-            pltpu.SemaphoreType.DMA((7,)),
+            pltpu.SemaphoreType.DMA((9,)),
         ],
         compiler_params=params(),
         cost_estimate=cost(1000, 8 * count * width),

time: 42.9 us -> 42.9 us (level)
  no operation moved by 1% of the time
where the time goes in v16:
time: 42.9 us; the launch traced here: 42.7 us
  starting transfers between devices  20.6 us (48%)
  waiting for transfers between devices  11.4 us (27%)
  Pallas kernels  9.87 us (23%)
  between operations  0.75 us (2%)
    ppermute x14, starting transfers between devices, from_masked(): return lax.ppermute(value, axis, pairs)  13.1 us
    ppermute x1, waiting for transfers between devices, dense_plan(): far = lax.ppermute(picked, 'dp', along[1])  4.67 us
    ppermute x2, starting transfers between devices, dense_plan(): near_x = [lax.ppermute(x_own, 'dp', pairs) for pairs in along]  4.08 us
    pallas_call x3, Pallas kernels, update_piece(): pl.pallas_call(functools.partial(update_kernel, kinds, count, piece, last...  3.76 us
    ppermute x14, waiting for transfers between devices, from_masked(): return lax.ppermute(value, axis, pairs)  2.82 us
    ppermute x2, waiting for transfers between devices, dense_plan(): near_y = [lax.ppermute(y_own, 'dp', pairs) for pairs in along]  2.38 us
    pallas_call x4, Pallas kernels, partials(): pl.pallas_call(functools.partial(partial_kernel, kinds, count, tokened),...  1.97 us
    ppermute x2, starting transfers between devices, dense_plan(): near_y = [lax.ppermute(y_own, 'dp', pairs) for pairs in along]  1.88 us
  transfers between devices with their start and end apart: 19, of which 10 were waited for; matrix products, arithmetic and copies ran while one was open for 0% of the time, Pallas kernels for 15%

profile of v16, /device:TPU:0, one launch (start us, length us, event | category | flops | bytes accessed | tf_op | source)
XLA Modules:
  0.0 42.7 jit_solution(724822412132199516)
XLA Ops:
  0.6 1.7 %shard_map.94 = (bf16[128,1024]{1,0:T(8,128)(2,1)S(1)}, bf16[144,1024]{1,0:T(8,128)(2,1)S(1)}, bf16[272,1024]{1,0:T(8,128)(2,1)S(1)}, bf16[3,192,1024]{2,1,0:T(8,128)(2,1)S(1)}) custom-call(s32[4,128]{1,0:T(4,128)} %bitcast.2, bf16[4,128]{1,0:T(4,128)(2,1)} %bitcast.3, bf16[128,2048]{1,0:T(8,128)(2,1)} %tokens_ref.1, bf16[128,2048]{1,0:T(8,128)(2,1)} %cot_ref.1, ...), custom_call_target="tpu_custom_call" | custom-call | flops 1000 | bytes 1048576 | tf_op jit(solution)/shard_map/pallas_call | solution.py:209
  2.8 2.6 %collective-permute-start.1 = (bf16[128,1024]{1,0:T(8,128)(2,1)S(1)}, bf16[128,1024]{1,0:T(8,128)(2,1)S(1)}, u32[]{:S(2)}, u32[]{:S(2)}) collective-permute-start(bf16[128,1024]{1,0:T(8,128)(2,1)S(1)} %get-tuple-element.43), channel_id=1, source_target_pairs={{0,2},{1,5},{2,0},{3,7},{4,6},{5,1},{6,4},{7,3},{8,10},{9,13},{10,... | collective-permute-start | bytes 786440 | tf_op jit(solution)/shard_map/ppermute | solution.py:611
  5.4 1.5 %collective-permute-start.2 = (bf16[128,1024]{1,0:T(8,128)(2,1)S(1)}, bf16[128,1024]{1,0:T(8,128)(2,1)S(1)}, u32[]{:S(2)}, u32[]{:S(2)}) collective-permute-start(bf16[128,1024]{1,0:T(8,128)(2,1)S(1)} %get-tuple-element.43), channel_id=1, source_target_pairs={{0,4},{1,3},{2,6},{3,1},{4,0},{5,7},{6,2},{7,5},{8,12},{9,11},{10,... | collective-permute-start | bytes 786440 | tf_op jit(solution)/shard_map/ppermute | solution.py:611
  6.9 0.5 %shard_map.95 = (bf16[1168,128]{1,0:T(8,128)(2,1)S(1)}, f32[8,128]{1,0:T(8,128)S(1)}) custom-call(bf16[3,192,1024]{2,1,0:T(8,128)(2,1)S(1)} %get-tuple-element.40.w_ref, bf16[272,1024]{1,0:T(8,128)(2,1)S(1)} %get-tuple-element.41.after_ref.refs_0_.refs_5_, bf16[272,1024]{1,0:T(8,128)(2,1)S(1)} %get-tuple-element.41.after_ref.refs_0_.refs_5_, ...), custom_call_target="tpu_custom_call" | custom-call | flops 301989888 | bytes 884736 | tf_op jit(solution)/shard_map/pallas_call | solution.py:312
  7.5 1.6 %collective-permute-start.4 = (bf16[1168,128]{1,0:T(8,128)(2,1)S(1)}, bf16[1168,128]{1,0:T(8,128)(2,1)S(1)}, u32[]{:S(2)}, u32[]{:S(2)}) collective-permute-start(bf16[1168,128]{1,0:T(8,128)(2,1)S(1)} %get-tuple-element.46.own), channel_id=1, source_target_pairs={{0,8},{8,0},{16,24},{24,16},{1,9},{9,1},{17,25},{25,17},{2,10},{10... | collective-permute-start | bytes 897032 | tf_op jit(solution)/shard_map/ppermute | solution.py:592
  9.6 1.4 %collective-permute-start.6 = (bf16[144,1024]{1,0:T(8,128)(2,1)S(1)}, bf16[144,1024]{1,0:T(8,128)(2,1)S(1)}, u32[]{:S(2)}, u32[]{:S(2)}) collective-permute-start(bf16[144,1024]{1,0:T(8,128)(2,1)S(1)} %get-tuple-element.48), channel_id=1, source_target_pairs={{0,2},{1,5},{2,0},{3,7},{4,6},{5,1},{6,4},{7,3},{8,10},{9,13},{10,... | collective-permute-start | bytes 884744 | tf_op jit(solution)/shard_map/ppermute | solution.py:612
  11.8 1.1 %collective-permute-done.2.refs_0_.refs_1_ = bf16[128,1024]{1,0:T(8,128)(2,1)S(1)} collective-permute-done((bf16[128,1024]{1,0:T(8,128)(2,1)S(1)}, bf16[128,1024]{1,0:T(8,128)(2,1)S(1)}, u32[]{:S(2)}, u32[]{:S(2)}) %collective-permute-start.2) | collective-permute-done | bytes 262176 | tf_op jit(solution)/shard_map/ppermute | solution.py:611
  12.9 3.1 %collective-permute-start.5 = (bf16[384,128]{1,0:T(8,128)(2,1)S(1)}, bf16[384,128]{1,0:T(8,128)(2,1)S(1)}, u32[]{:S(2)}, u32[]{:S(2)}) collective-permute-start(bf16[384,128]{1,0:T(8,128)(2,1)S(1)} %get-tuple-element.47.near_own), channel_id=1, source_target_pairs={{0,8},{8,0},{16,24},{24,16},{1,9},{9,1},{17,25},{25,17},{2,10},{10... | collective-permute-start | bytes 294920 | tf_op jit(solution)/shard_map/ppermute | solution.py:592
  16.5 2.1 %collective-permute-done.7.refs_4_ = bf16[144,1024]{1,0:T(8,128)(2,1)S(1)} collective-permute-done((bf16[144,1024]{1,0:T(8,128)(2,1)S(1)}, bf16[144,1024]{1,0:T(8,128)(2,1)S(1)}, u32[]{:S(2)}, u32[]{:S(2)}) %collective-permute-start.7) | collective-permute-done | bytes 294944 | tf_op jit(solution)/shard_map/ppermute | solution.py:612
  19.2 1.6 %collective-permute-start.9 = (bf16[272,1024]{1,0:T(8,128)(2,1)S(1)}, bf16[272,1024]{1,0:T(8,128)(2,1)S(1)}, u32[]{:S(2)}, u32[]{:S(2)}) collective-permute-start(bf16[272,1024]{1,0:T(8,128)(2,1)S(1)} %get-tuple-element.51.after_ref), channel_id=1, source_target_pairs={{0,4},{1,3},{2,6},{3,1},{4,0},{5,7},{6,2},{7,5},{8,12},{9,11},{10,... | collective-permute-start | bytes 1671176 | tf_op jit(solution)/shard_map/ppermute | solution.py:621
  20.7 1.8 %collective-permute-start.10 = (bf16[768,128]{1,0:T(8,128)(2,1)S(1)}, bf16[768,128]{1,0:T(8,128)(2,1)S(1)}, u32[]{:S(2)}, u32[]{:S(2)}) collective-permute-start(bf16[768,128]{1,0:T(8,128)(2,1)S(1)} %get-tuple-element.49.refs_7_.own), channel_id=1, source_target_pairs={{0,8},{8,0},{16,24},{24,16},{1,9},{9,1},{17,25},{25,17},{2,10},{10... | collective-permute-start | bytes 589832 | tf_op jit(solution)/shard_map/ppermute | solution.py:592
  22.6 0.7 %shard_map.99 = (bf16[1152,128]{1,0:T(8,128)(2,1)S(1)}, f32[8,128]{1,0:T(8,128)S(1)}) custom-call(bf16[3,192,1024]{2,1,0:T(8,128)(2,1)S(1)} %get-tuple-element.40.w_ref, bf16[272,1024]{1,0:T(8,128)(2,1)S(1)} %get-tuple-element.51.after_ref, bf16[416,1024]{1,0:T(8,128)(2,1)S(1)} %get-tuple-element.52.refs_0_.refs_1_, ...), custom_call_target="tpu_custom_call" | custom-call | flops 301989888 | bytes 884736 | tf_op jit(solution)/shard_map/pallas_call | solution.py:312
  23.2 0.8 %collective-permute-start.16 = (bf16[1152,128]{1,0:T(8,128)(2,1)S(1)}, bf16[1152,128]{1,0:T(8,128)(2,1)S(1)}, u32[]{:S(2)}, u32[]{:S(2)}) collective-permute-start(bf16[1152,128]{1,0:T(8,128)(2,1)S(1)} %get-tuple-element.63.own), channel_id=1, source_target_pairs={{0,8},{8,0},{16,24},{24,16},{1,9},{9,1},{17,25},{25,17},{2,10},{10... | collective-permute-start | bytes 884744 | tf_op jit(solution)/shard_map/ppermute | solution.py:592
  24.1 4.7 %collective-permute-done.9.in_ref = bf16[272,1024]{1,0:T(8,128)(2,1)S(1)} collective-permute-done((bf16[272,1024]{1,0:T(8,128)(2,1)S(1)}, bf16[272,1024]{1,0:T(8,128)(2,1)S(1)}, u32[]{:S(2)}, u32[]{:S(2)}) %collective-permute-start.9) | collective-permute-done | bytes 557088 | tf_op jit(solution)/shard_map/ppermute | solution.py:621
  29.9 0.5 %shard_map.101 = (f32[3,192,1024]{2,1,0:T(8,128)S(1)}, f32[768,128]{1,0:T(8,128)S(1)}, f32[8,128]{1,0:T(8,128)S(1)}) custom-call(f32[8,256]{1,0:T(8,128)S(1)} %get-tuple-element.50.gate_ref, bf16[64,1024]{1,0:T(8,128)(2,1)S(1)} %get-tuple-element.54.after_ref.refs_0_, f32[1152,128]{1,0:T(8,128)S(1)} %get-tuple-element.55.sum_ref, ...), custom_call_target="tpu_custom_call" | custom-call | flops 301989888 | bytes 2359296 | tf_op jit(solution)/shard_map/pallas_call | solution.py:448
  30.9 0.7 %shard_map.102 = (bf16[384,128]{1,0:T(8,128)(2,1)S(1)}, bf16[384,128]{1,0:T(8,128)(2,1)S(1)}, bf16[384,128]{1,0:T(8,128)(2,1)S(1)}) custom-call(bf16[3,192,1024]{2,1,0:T(8,128)(2,1)S(1)} %get-tuple-element.40.w_ref, f32[8,128]{1,0:T(8,128)S(1)} %get-tuple-element.56.after_ref, bf16[64,1024]{1,0:T(8,128)(2,1)S(1)} %get-tuple-element.54.after_ref.refs_0_, ...), custom_call_target="tpu_custom_call" | custom-call | flops 301989888 | bytes 884736 | tf_op jit(solution)/shard_map/pallas_call | solution.py:519
  31.6 1.9 %collective-permute-start.18 = (bf16[384,128]{1,0:T(8,128)(2,1)S(1)}, bf16[384,128]{1,0:T(8,128)(2,1)S(1)}, u32[]{:S(2)}, u32[]{:S(2)}) collective-permute-start(bf16[384,128]{1,0:T(8,128)(2,1)S(1)} %get-tuple-element.67.own), channel_id=1, source_target_pairs={{0,8},{8,0},{16,24},{24,16},{1,9},{9,1},{17,25},{25,17},{2,10},{10... | collective-permute-start | bytes 294920 | tf_op jit(solution)/shard_map/ppermute | solution.py:592
  33.7 1.9 %collective-permute-start.15 = (bf16[384,128]{1,0:T(8,128)(2,1)S(1)}, bf16[384,128]{1,0:T(8,128)(2,1)S(1)}, u32[]{:S(2)}, u32[]{:S(2)}) collective-permute-start(bf16[384,128]{1,0:T(8,128)(2,1)S(1)} %get-tuple-element.60.own), channel_id=1, source_target_pairs={{0,8},{8,0},{16,24},{24,16},{1,9},{9,1},{17,25},{25,17},{2,10},{10... | collective-permute-start | bytes 294920 | tf_op jit(solution)/shard_map/ppermute | solution.py:592
  35.6 1.0 %shard_map.103.refs_8_ = f32[3,192,1024]{2,1,0:T(8,128)S(1)} custom-call(f32[384,128]{1,0:T(8,128)S(1)} %get-tuple-element.61.sum_ref, f32[768,128]{1,0:T(8,128)S(1)} %get-tuple-element.62.more_ref, bf16[1152,128]{1,0:T(8,128)(2,1)S(1)} %get-tuple-element.63.own, bf16[1152,128]{1,0:T(8,128)(2,1)S(1)} %collective-permute-done.16.got, ...), custom_call_target="tpu_custom_call", output_to_operand_aliasing={{}: (8, {})} | custom-call | flops 603979776 | bytes 4718592 | tf_op jit(solution)/shard_map/pallas_call | solution.py:476
  36.6 0.7 %collective-permute-done.18.got = bf16[384,128]{1,0:T(8,128)(2,1)S(1)} collective-permute-done((bf16[384,128]{1,0:T(8,128)(2,1)S(1)}, bf16[384,128]{1,0:T(8,128)(2,1)S(1)}, u32[]{:S(2)}, u32[]{:S(2)}) %collective-permute-start.18) | collective-permute-done | bytes 98336 | tf_op jit(solution)/shard_map/ppermute | solution.py:592
  37.3 0.7 %shard_map.104 = (bf16[3,64,1024]{2,1,0:T(8,128)(2,1)S(1)}, bf16[3,64,1024]{2,1,0:T(8,128)(2,1)S(1)}, bf16[3,64,1024]{2,1,0:T(8,128)(2,1)S(1)}) custom-call(bf16[384,128]{1,0:T(8,128)(2,1)S(1)} %get-tuple-element.67.own, bf16[384,128]{1,0:T(8,128)(2,1)S(1)} %collective-permute-done.18.got, bf16[64,1024]{1,0:T(8,128)(2,1)S(1)} %get-tuple-element.54.after_ref.refs_0_, ...), custom_call_target="tpu_custom_call" | custom-call | flops 100663296 | bytes 2752512 | tf_op jit(solution)/shard_map/pallas_call | solution.py:577
  37.9 1.4 %collective-permute-done.17.got = bf16[384,128]{1,0:T(8,128)(2,1)S(1)} collective-permute-done((bf16[384,128]{1,0:T(8,128)(2,1)S(1)}, bf16[384,128]{1,0:T(8,128)(2,1)S(1)}, u32[]{:S(2)}, u32[]{:S(2)}) %collective-permute-start.17) | collective-permute-done | bytes 98336 | tf_op jit(solution)/shard_map/ppermute | solution.py:592
  39.4 1.4 %shard_map.105 = (bf16[3,192,1024]{2,1,0:T(8,128)(2,1)}, bf16[3,192,1024]{2,1,0:T(8,128)(2,1)}, bf16[3,192,1024]{2,1,0:T(8,128)(2,1)}, bf16[3,64,1024]{2,1,0:T(8...) custom-call(bf16[384,128]{1,0:T(8,128)(2,1)S(1)} %get-tuple-element.66.own, ...), custom_call_target="tpu_custom_call" | custom-call | flops 100663296 | bytes 2752512 | tf_op jit(solution)/shard_map/pallas_call | solution.py:577
  41.0 1.7 %shard_map.106 = (bf16[3,192,1024]{2,1,0:T(8,128)(2,1)}, bf16[3,192,1024]{2,1,0:T(8,128)(2,1)}, bf16[3,192,1024]{2,1,0:T(8,128)(2,1)}) custom-call(bf16[384,128]{1,0:T(8,128)(2,1)S(1)} %get-tuple-element.60.own, bf16[384,128]{1,0:T(8,128)(2,1)S(1)} %collective-permute-done.15.got, ...), custom_call_target="tpu_custom_call", output_to_operand_aliasing={{0}: (16, {}), {1}: (17, {}), {2}: (18, {})} | custom-call | flops 100663296 | bytes 2752512 | tf_op jit(solution)/shard_map/pallas_call | solution.py:577
  (31 shorter events, 4.7 us)
Async XLA Ops:
  2.3 4.6 %collective-permute-start = (bf16[272,1024]{1,0:T(8,128)(2,1)S(1)}, bf16[272,1024]{1,0:T(8,128)(2,1)S(1)}, u32[]{:S(2)}, u32[]{:S(2)}) collective-permute-start(bf16[272,1024]{1,0:T(8,128)(2,1)S(1)} %get-tuple-element.41.after_ref.refs_0_.refs_5_), channel_id=1, source_target_pairs={{0,1},{1,0},{2,3},{3,2},{4,5},{5,4},{6,7},{7,6},{8,9},{9,8},{10,11... | collective-permute-start | bytes 1671176 | tf_op jit(solution)/shard_map/ppermute | solution.py:592
  2.8 8.6 %collective-permute-start.1 = (bf16[128,1024]{1,0:T(8,128)(2,1)S(1)}, bf16[128,1024]{1,0:T(8,128)(2,1)S(1)}, u32[]{:S(2)}, u32[]{:S(2)}) collective-permute-start(bf16[128,1024]{1,0:T(8,128)(2,1)S(1)} %get-tuple-element.43), channel_id=1, source_target_pairs={{0,2},{1,5},{2,0},{3,7},{4,6},{5,1},{6,4},{7,3},{8,10},{9,13},{10,... | collective-permute-start | bytes 786440 | tf_op jit(solution)/shard_map/ppermute | solution.py:611
  5.4 7.5 %collective-permute-start.2 = (bf16[128,1024]{1,0:T(8,128)(2,1)S(1)}, bf16[128,1024]{1,0:T(8,128)(2,1)S(1)}, u32[]{:S(2)}, u32[]{:S(2)}) collective-permute-start(bf16[128,1024]{1,0:T(8,128)(2,1)S(1)} %get-tuple-element.43), channel_id=1, source_target_pairs={{0,4},{1,3},{2,6},{3,1},{4,0},{5,7},{6,2},{7,5},{8,12},{9,11},{10,... | collective-permute-start | bytes 786440 | tf_op jit(solution)/shard_map/ppermute | solution.py:611
  7.5 11.4 %collective-permute-start.4 = (bf16[1168,128]{1,0:T(8,128)(2,1)S(1)}, bf16[1168,128]{1,0:T(8,128)(2,1)S(1)}, u32[]{:S(2)}, u32[]{:S(2)}) collective-permute-start(bf16[1168,128]{1,0:T(8,128)(2,1)S(1)} %get-tuple-element.46.own), channel_id=1, source_target_pairs={{0,8},{8,0},{16,24},{24,16},{1,9},{9,1},{17,25},{25,17},{2,10},{10... | collective-permute-start | bytes 897032 | tf_op jit(solution)/shard_map/ppermute | solution.py:592
  9.1 9.5 %collective-permute-start.7 = (bf16[144,1024]{1,0:T(8,128)(2,1)S(1)}, bf16[144,1024]{1,0:T(8,128)(2,1)S(1)}, u32[]{:S(2)}, u32[]{:S(2)}) collective-permute-start(bf16[144,1024]{1,0:T(8,128)(2,1)S(1)} %get-tuple-element.48), channel_id=1, source_target_pairs={{0,4},{1,3},{2,6},{3,1},{4,0},{5,7},{6,2},{7,5},{8,12},{9,11},{10,... | collective-permute-start | bytes 884744 | tf_op jit(solution)/shard_map/ppermute | solution.py:612
  9.6 9.3 %collective-permute-start.6 = (bf16[144,1024]{1,0:T(8,128)(2,1)S(1)}, bf16[144,1024]{1,0:T(8,128)(2,1)S(1)}, u32[]{:S(2)}, u32[]{:S(2)}) collective-permute-start(bf16[144,1024]{1,0:T(8,128)(2,1)S(1)} %get-tuple-element.48), channel_id=1, source_target_pairs={{0,2},{1,5},{2,0},{3,7},{4,6},{5,1},{6,4},{7,3},{8,10},{9,13},{10,... | collective-permute-start | bytes 884744 | tf_op jit(solution)/shard_map/ppermute | solution.py:612
  11.4 4.6 %collective-permute-start.3 = (bf16[128,1024]{1,0:T(8,128)(2,1)S(1)}, bf16[128,1024]{1,0:T(8,128)(2,1)S(1)}, u32[]{:S(2)}, u32[]{:S(2)}) collective-permute-start(bf16[128,1024]{1,0:T(8,128)(2,1)S(1)} %collective-permute-done.1.refs_0_), channel_id=1, source_target_pairs={{0,1},{1,0},{2,3},{3,2},{4,5},{5,4},{6,7},{7,6},{8,9},{9,8},{10,11... | collective-permute-start | bytes 786440 | tf_op jit(solution)/shard_map/ppermute | solution.py:592
  12.9 5.9 %collective-permute-start.5 = (bf16[384,128]{1,0:T(8,128)(2,1)S(1)}, bf16[384,128]{1,0:T(8,128)(2,1)S(1)}, u32[]{:S(2)}, u32[]{:S(2)}) collective-permute-start(bf16[384,128]{1,0:T(8,128)(2,1)S(1)} %get-tuple-element.47.near_own), channel_id=1, source_target_pairs={{0,8},{8,0},{16,24},{24,16},{1,9},{9,1},{17,25},{25,17},{2,10},{10... | collective-permute-start | bytes 294920 | tf_op jit(solution)/shard_map/ppermute | solution.py:592
  19.1 3.5 %collective-permute-start.8 = (bf16[416,1024]{1,0:T(8,128)(2,1)S(1)}, bf16[416,1024]{1,0:T(8,128)(2,1)S(1)}, u32[]{:S(2)}, u32[]{:S(2)}) collective-permute-start(bf16[416,1024]{1,0:T(8,128)(2,1)S(1)} %get-tuple-element.52.refs_0_.refs_1_), channel_id=1, source_target_pairs={{0,1},{1,0},{2,3},{3,2},{4,5},{5,4},{6,7},{7,6},{8,9},{9,8},{10,11... | collective-permute-start | bytes 2555912 | tf_op jit(solution)/shard_map/ppermute | solution.py:592
  19.2 9.6 %collective-permute-start.9 = (bf16[272,1024]{1,0:T(8,128)(2,1)S(1)}, bf16[272,1024]{1,0:T(8,128)(2,1)S(1)}, u32[]{:S(2)}, u32[]{:S(2)}) collective-permute-start(bf16[272,1024]{1,0:T(8,128)(2,1)S(1)} %get-tuple-element.51.after_ref), channel_id=1, source_target_pairs={{0,4},{1,3},{2,6},{3,1},{4,0},{5,7},{6,2},{7,5},{8,12},{9,11},{10,... | collective-permute-start | bytes 1671176 | tf_op jit(solution)/shard_map/ppermute | solution.py:621
  20.7 8.7 %collective-permute-start.10 = (bf16[768,128]{1,0:T(8,128)(2,1)S(1)}, bf16[768,128]{1,0:T(8,128)(2,1)S(1)}, u32[]{:S(2)}, u32[]{:S(2)}) collective-permute-start(bf16[768,128]{1,0:T(8,128)(2,1)S(1)} %get-tuple-element.49.refs_7_.own), channel_id=1, source_target_pairs={{0,8},{8,0},{16,24},{24,16},{1,9},{9,1},{17,25},{25,17},{2,10},{10... | collective-permute-start | bytes 589832 | tf_op jit(solution)/shard_map/ppermute | solution.py:592
  23.2 12.3 %collective-permute-start.16 = (bf16[1152,128]{1,0:T(8,128)(2,1)S(1)}, bf16[1152,128]{1,0:T(8,128)(2,1)S(1)}, u32[]{:S(2)}, u32[]{:S(2)}) collective-permute-start(bf16[1152,128]{1,0:T(8,128)(2,1)S(1)} %get-tuple-element.63.own), channel_id=1, source_target_pairs={{0,8},{8,0},{16,24},{24,16},{1,9},{9,1},{17,25},{25,17},{2,10},{10... | collective-permute-start | bytes 884744 | tf_op jit(solution)/shard_map/ppermute | solution.py:592
  28.8 2.1 %collective-permute-start.14 = (bf16[80,1024]{1,0:T(8,128)(2,1)S(1)}, bf16[80,1024]{1,0:T(8,128)(2,1)S(1)}, u32[]{:S(2)}, u32[]{:S(2)}) collective-permute-start(bf16[80,1024]{1,0:T(8,128)(2,1)S(1)} %get-tuple-element.59.refs_3_), channel_id=1, source_target_pairs={{0,1},{1,0},{2,3},{3,2},{4,5},{5,4},{6,7},{7,6},{8,9},{9,8},{10,11... | collective-permute-start | bytes 491528 | tf_op jit(solution)/shard_map/ppermute | solution.py:592
  28.9 1.6 %collective-permute-start.12 = (bf16[64,1024]{1,0:T(8,128)(2,1)S(1)}, bf16[64,1024]{1,0:T(8,128)(2,1)S(1)}, u32[]{:S(2)}, u32[]{:S(2)}) collective-permute-start(bf16[64,1024]{1,0:T(8,128)(2,1)S(1)} %get-tuple-element.57.refs_1_), channel_id=1, source_target_pairs={{0,1},{1,0},{2,3},{3,2},{4,5},{5,4},{6,7},{7,6},{8,9},{9,8},{10,11... | collective-permute-start | bytes 393224 | tf_op jit(solution)/shard_map/ppermute | solution.py:592
  29.4 1.3 %collective-permute-start.13 = (bf16[64,1024]{1,0:T(8,128)(2,1)S(1)}, bf16[64,1024]{1,0:T(8,128)(2,1)S(1)}, u32[]{:S(2)}, u32[]{:S(2)}) collective-permute-start(bf16[64,1024]{1,0:T(8,128)(2,1)S(1)} %get-tuple-element.58.refs_2_), channel_id=1, source_target_pairs={{0,1},{1,0},{2,3},{3,2},{4,5},{5,4},{6,7},{7,6},{8,9},{9,8},{10,11... | collective-permute-start | bytes 393224 | tf_op jit(solution)/shard_map/ppermute | solution.py:592
  29.4 1.5 %collective-permute-start.11 = (bf16[64,1024]{1,0:T(8,128)(2,1)S(1)}, bf16[64,1024]{1,0:T(8,128)(2,1)S(1)}, u32[]{:S(2)}, u32[]{:S(2)}) collective-permute-start(bf16[64,1024]{1,0:T(8,128)(2,1)S(1)} %get-tuple-element.54.after_ref.refs_0_), channel_id=1, source_target_pairs={{0,1},{1,0},{2,3},{3,2},{4,5},{5,4},{6,7},{7,6},{8,9},{9,8},{10,11... | collective-permute-start | bytes 393224 | tf_op jit(solution)/shard_map/ppermute | solution.py:592
  31.6 5.7 %collective-permute-start.18 = (bf16[384,128]{1,0:T(8,128)(2,1)S(1)}, bf16[384,128]{1,0:T(8,128)(2,1)S(1)}, u32[]{:S(2)}, u32[]{:S(2)}) collective-permute-start(bf16[384,128]{1,0:T(8,128)(2,1)S(1)} %get-tuple-element.67.own), channel_id=1, source_target_pairs={{0,8},{8,0},{16,24},{24,16},{1,9},{9,1},{17,25},{25,17},{2,10},{10... | collective-permute-start | bytes 294920 | tf_op jit(solution)/shard_map/ppermute | solution.py:592
  33.5 5.8 %collective-permute-start.17 = (bf16[384,128]{1,0:T(8,128)(2,1)S(1)}, bf16[384,128]{1,0:T(8,128)(2,1)S(1)}, u32[]{:S(2)}, u32[]{:S(2)}) collective-permute-start(bf16[384,128]{1,0:T(8,128)(2,1)S(1)} %get-tuple-element.66.own), channel_id=1, source_target_pairs={{0,8},{8,0},{16,24},{24,16},{1,9},{9,1},{17,25},{25,17},{2,10},{10... | collective-permute-start | bytes 294920 | tf_op jit(solution)/shard_map/ppermute | solution.py:592
  33.7 7.3 %collective-permute-start.15 = (bf16[384,128]{1,0:T(8,128)(2,1)S(1)}, bf16[384,128]{1,0:T(8,128)(2,1)S(1)}, u32[]{:S(2)}, u32[]{:S(2)}) collective-permute-start(bf16[384,128]{1,0:T(8,128)(2,1)S(1)} %get-tuple-element.60.own), channel_id=1, source_target_pairs={{0,8},{8,0},{16,24},{24,16},{1,9},{9,1},{17,25},{25,17},{2,10},{10... | collective-permute-start | bytes 294920 | tf_op jit(solution)/shard_map/ppermute | solution.py:592
  35.6 1.7 %copy-start = (bf16[3,192,1024]{2,1,0:T(8,128)(2,1)S(1)}, bf16[3,192,1024]{2,1,0:T(8,128)(2,1)}, u32[]{:S(2)}) copy-start(bf16[3,192,1024]{2,1,0:T(8,128)(2,1)} %refs_9_.5) | copy-start | bytes 3538948
  35.6 1.7 %copy-start.1 = (bf16[3,192,1024]{2,1,0:T(8,128)(2,1)S(1)}, bf16[3,192,1024]{2,1,0:T(8,128)(2,1)}, u32[]{:S(2)}) copy-start(bf16[3,192,1024]{2,1,0:T(8,128)(2,1)} %refs_10_.5) | copy-start | bytes 3538948
